TPU v7x, 32 devices: a whole 2x2x4 slice. The times are simulated.
32 devices in a mesh: rows: 8 (over z, y), cols: 4 (over x, core).
Axes of the slice: x: 2, y: 2, z: 4, core: 2. Of those that a mesh axis runs over, the one named last changes fastest.
Arguments:
- user_factors: float32 [128, 16384], P('cols', 'rows'), may hold values from -6 to 6
- item_factors: bfloat16 [128, 65536], P('cols', 'rows'), may hold values from -0.0234375 to 0.0234375
- tile_user: int32 [576], P('rows'), may hold values from 0 to 7
- tile_item: int32 [576], P('rows'), may hold values from 0 to 255, as said below
- tile_count: int32 [8], P('rows'), may hold values from 36 to 72, as said below
- tile_mask: bfloat16 [576, 256, 256], P('rows'), may hold values from 0 to 2, as said below
Outputs:
- solution_field: float32 [128, 16384], P('cols', 'rows')
- residual: float32 [128, 16384], P('cols', 'rows')
Inputs may be any that keep to these rules, and one draw needn't show every extreme that they name: `tile_item`: item block b is held by index b // 32 of rows. Among the live slots of one index of rows at most 9 name item blocks held by one index of rows, and in every draw some index reaches 9. `tile_count`: some index of rows has all 72 slots live in every draw. `tile_mask`: each entry is zero or a strength of 0.5 or more.
All inputs are finite; a program needn't handle non-finite values.
Results may differ from a plain program's by a relative error of at most 0.0008.
Values may be sent and summed in bfloat16 or wider, within the bound.
No kernel may reach another device: no remote copies, remote signals or barrier semaphores. Data moves between devices by JAX's collectives and lax.ppermute only.
A program may use at most 128 MiB of HBM per device.

v0:
```python
import jax
import jax.numpy as jnp
from jax import lax
from jax.sharding import PartitionSpec as P

ITERS = 2


ridge = 0.5
confidence = 40.0
highest = lax.Precision.HIGHEST


def lookup(table, wanted):
    picked = table[jnp.maximum(wanted, 0)]
    return jnp.where((wanted >= 0)[:, :, None, None], picked, jnp.zeros_like(picked))


def squares(vector):
    return lax.psum(jnp.sum(vector * vector), ("rows", "cols"))


def on_device(user_factors, item_factors, tile_user, tile_item, tile_count, tile_mask):
    tile_rows = tile_mask.shape[1]
    col_width = user_factors.shape[0]
    column = lax.axis_index("cols")
    row_devs = lax.axis_size("rows")
    tile_total = tile_user.shape[0]
    user_blocks = user_factors.shape[1] // tile_rows
    item_blocks = item_factors.shape[1] // tile_rows
    capacity = max(2, (tile_total + row_devs - 1) // row_devs)
    order = jnp.arange(tile_total, dtype=jnp.int32)
    live = (order < tile_count[0]).astype(jnp.int32)
    holder = tile_item // item_blocks
    local_block = tile_item % item_blocks
    earlier = (
        (holder[None, :] == holder[:, None])
        & (order[None, :] < order[:, None])
        & (live[None, :] > 0)
    )
    rank = jnp.sum(earlier.astype(jnp.int32), axis=1)
    slot_ids = jnp.minimum(holder * capacity + rank, row_devs * capacity - 1)
    slot_range = jnp.arange(row_devs * capacity, dtype=jnp.int32)
    hits = ((slot_ids[None, :] == slot_range[:, None]) & (live[None, :] > 0)).astype(jnp.int32)
    requests = (jnp.sum(hits * (local_block + 1)[None, :], axis=1) - 1).reshape(row_devs, capacity)
    own_full = lax.all_gather(item_factors, "cols", axis=0, tiled=True)
    own_float = own_full.astype(jnp.float32)
    own_cols = lax.dynamic_slice_in_dim(own_float, column * col_width, col_width, 0)
    gram_part = jnp.dot(own_cols, own_float.T, precision=highest)
    gram_rows = lax.psum(gram_part, "rows")
    table_full = jnp.transpose(
        own_full.reshape(own_full.shape[0], item_blocks, tile_rows), (1, 0, 2)
    )
    fetched = lax.all_to_all(
        lookup(
            table_full, lax.all_to_all(requests, "rows", split_axis=0, concat_axis=0, tiled=True)
        ),
        "rows",
        split_axis=0,
        concat_axis=0,
        tiled=True,
    )
    full_width = fetched.shape[2]
    item_tiles = fetched.reshape(row_devs * capacity, full_width, tile_rows)[slot_ids].astype(
        jnp.float32
    )
    item_cols = lax.dynamic_slice_in_dim(item_tiles, column * col_width, col_width, 1)
    masks = tile_mask * live.astype(jnp.bfloat16)[:, None, None]
    select = (tile_user[None, :] == jnp.arange(user_blocks, dtype=jnp.int32)[:, None]).astype(
        jnp.float32
    )

    def collect(terms):
        summed = jnp.einsum("bt,tcu->cbu", select, terms, precision=highest)
        return summed.reshape(col_width, user_blocks * tile_rows)

    right_side = (1.0 + confidence) * collect(
        jnp.einsum("tui,tci->tcu", masks.astype(jnp.float32), item_cols, precision=highest)
    )

    def apply_op(dirs):
        dirs_full = lax.all_gather(dirs, "cols", axis=0, tiled=True)
        dir_tiles = dirs_full.reshape(full_width, user_blocks, tile_rows)[:, tile_user]
        scores = jnp.einsum(
            "ktu,tki->tui", dir_tiles, item_tiles, precision=highest
        ) * masks.astype(jnp.float32)
        sparse = collect(jnp.einsum("tui,tci->tcu", scores, item_cols, precision=highest))
        return jnp.dot(gram_rows, dirs_full, precision=highest) + ridge * dirs + confidence * sparse

    solution_field = user_factors
    residual = right_side - apply_op(user_factors)
    direction = residual
    norm_now = squares(residual)
    for iteration in range(ITERS):
        image = apply_op(direction)
        alpha = norm_now / lax.psum(jnp.sum(direction * image), ("rows", "cols"))
        solution_field = solution_field + alpha * direction
        residual = residual - alpha * image
        norm_next = squares(residual)
        direction = residual + norm_next / norm_now * direction
        norm_now = norm_next
    return (solution_field, residual)


def solution(mesh):
    return jax.shard_map(
        on_device,
        mesh=mesh,
        in_specs=(
            P("cols", "rows"),
            P("cols", "rows"),
            P("rows"),
            P("rows"),
            P("rows"),
            P("rows", None, None),
        ),
        out_specs=(P("cols", "rows"), P("cols", "rows")),
        check_vma=False,
    )
```

profile of v0, /device:TPU:0, one launch (start us, length us, event | category | flops | bytes accessed | tf_op | source)
XLA Modules:
  0.0 487.3 jit_solution(8477559864119070177)
XLA Ops:
  9.6 13.5 %all_to_all.11 = s32[8,1,9]{2,1,0:T(1,128)S(1)} all-to-all(s32[8,1,9]{2,1,0:T(1,128)S(1)} %bitcast.78), channel_id=1, replica_groups=mesh['rows'=8,'cols'=4] {'rows'}, dimensions={0} | all-to-all | bytes 576 | tf_op jit(solution)/shard_map/all_to_all | solution.py:56
  23.3 11.6 %all-gather.5.cloned.1.call-done = bf16[128,8192]{1,0:T(8,128)(2,1)} async-done(((bf16[32,8192]{1,0:T(8,128)(2,1)}), bf16[128,8192]{1,0:T(8,128)(2,1)}) %all-gather.5.cloned.1.call-update) | async-done | bytes 2097168 | tf_op jit(solution)/shard_map/all_gather | solution.py:46
  34.9 4.1 copy.41
  42.2 5.5 %gather_fusion = bf16[72,128,256]{2,1,0:T(8,128)(2,1)} fusion(bf16[32,128,256]{2,1,0:T(8,128)(2,1)S(1)} %bitcast.62, s32[1024]{0:T(1024)S(1)} %pad_clamp_fusion.2), kind=kCustom, calls=%fused_computation | custom fusion | bytes 9437472 | tf_op jit(solution)/shard_map/gather | solution.py:15
  47.7 4.9 %broadcast_select_fusion = bf16[8,9,128,256]{3,2,1,0:T(8,128)(2,1)} fusion(bf16[8,9,128,256]{3,2,1,0:T(8,128)(2,1)} %bitcast.63, pred[8,9]{1,0:T(8,128)(4,1)S(1)} %compare_bitcast_fusion), kind=kLoop, calls=%fused_computation.26 | loop fusion | flops 2359296 | bytes 9437256 | tf_op jit(solution)/shard_map/jit(_where)/select_n | solution.py:16
  52.6 5.7 %all-to-all-start.1 = ((bf16[8,9,128,256]{3,2,1,0:T(8,128)(2,1)}), bf16[8,9,128,256]{3,2,1,0:T(8,128)(2,1)}, u32[]{:S(2)}, u32[]{:S(2)}) async-start(bf16[8,9,128,256]{3,2,1,0:T(8,128)(2,1)} %broadcast_select_fusion), calls=%async_computation.1 | async-start | bytes 9437184 | tf_op jit(solution)/shard_map/all_to_all | solution.py:54
  59.1 18.8 %all-gather.7.cloned.1.call-done = f32[128,2048]{1,0:T(8,128)} async-done(((f32[32,2048]{1,0:T(8,128)}), f32[128,2048]{1,0:T(8,128)}) %all-gather.7.cloned.1.call-update) | async-done | bytes 1048592 | tf_op jit(solution)/shard_map/all_gather | solution.py:82
  79.8 4.9 %gather_fusion.2 = f32[72,128,256]{2,1,0:T(8,128)} fusion(f32[128,8,256]{2,0,1:T(8,128)S(1)} %copy.46, s32[1024]{0:T(1024)S(1)} %pad_clamp_fusion), kind=kCustom, calls=%fused_computation.2 | custom fusion | bytes 18874656 | tf_op jit(solution)/shard_map/gather | solution.py:83
  85.5 100.9 %psum.35 = f32[32,128]{1,0:T(8,128)S(1)} all-reduce(f32[32,128]{1,0:T(8,128)S(1)} %fusion.46), channel_id=1, replica_groups=mesh['rows'=8,'cols'=4] {'rows'}, use_global_device_ids=true, to_apply=%region_2.3 | all-reduce | flops 4096 | bytes 32768 | tf_op jit(solution)/shard_map/psum | solution.py:50
  186.4 7.8 %gather_fusion.1 = bf16[72,128,256]{2,1,0:T(8,128)(2,1)} fusion(bf16[72,128,256]{2,1,0:T(8,128)(2,1)} %bitcast.8, s32[1024]{0:T(1024)S(1)} %pad_clamp_fusion.1), kind=kCustom, calls=%fused_computation.1 | custom fusion | bytes 9437472 | tf_op jit(solution)/shard_map/gather | solution.py:64
  194.2 7.1 %fusion.12 = f32[72,32,256]{2,1,0:T(8,128)S(1)} fusion(bf16[72,256,256]{2,1,0:T(8,128)(2,1)} %param.11, bf16[72]{0:T(256)(128)(2,1)S(1)} %fusion.61, bf16[72,128,256]{2,1,0:T(8,128)(2,1)} %gather_fusion.1, s32[]{:T(128)S(6)} %select_n.33), kind=kOutput, calls=%fused_computation.20 | convolution fusion | flops 306708480 | bytes 12976276 | tf_op jit(solution)/shard_map/tui,tci->tcu/dot_general | solution.py:78
  204.4 14.4 %fusion.7 = f32[72,256,256]{2,1,0:T(8,128)} fusion(bf16[72,128,256]{2,1,0:T(8,128)(2,1)S(1)} %copy-done, f32[72,128,256]{2,1,0:T(8,128)} %gather_fusion.2), kind=kOutput, calls=%fused_computation.15 | convolution fusion | flops 7247757312 | bytes 33030144 | tf_op jit(solution)/shard_map/ktu,tki->tui/dot_general | solution.py:84
  218.7 15.9 %fusion = f32[72,32,256]{2,1,0:T(8,128)S(1)} fusion(f32[72,256,256]{2,1,0:T(8,128)} %fusion.7, bf16[72,256,256]{2,1,0:T(8,128)(2,1)} %param.11, bf16[72]{0:T(256)(128)(2,1)S(1)} %fusion.61, bf16[72,128,256]{2,1,0:T(8,128)(2,1)} %gather_fusion.1, s32[]{:T(128)S(6)} %select_n.33), kind=kOutput, calls=%fused_computation.8 | convolution fusion | flops 1826095104 | bytes 31850644 | tf_op jit(solution)/shard_map/tui,tci->tcu/dot_general | solution.py:87
  239.4 13.2 %all-gather.9.cloned.1.call-done = f32[128,2048]{1,0:T(8,128)} async-done(((f32[32,2048]{1,0:T(8,128)}), f32[128,2048]{1,0:T(8,128)}) %all-gather.9.cloned.1.call-update) | async-done | bytes 1048592 | tf_op jit(solution)/shard_map/all_gather | solution.py:82
  253.9 4.9 %gather_fusion.3 = f32[72,128,256]{2,1,0:T(8,128)} fusion(f32[128,8,256]{2,0,1:T(8,128)S(1)} %bitcast.61, s32[1024]{0:T(1024)S(1)} %pad_clamp_fusion), kind=kCustom, calls=%fused_computation.3 | custom fusion | bytes 18874656 | tf_op jit(solution)/shard_map/gather | solution.py:83
  258.7 15.6 %fusion.5 = f32[72,256,256]{2,1,0:T(8,128)} fusion(bf16[72,128,256]{2,1,0:T(8,128)(2,1)} %gather_fusion.1, f32[72,128,256]{2,1,0:T(8,128)} %gather_fusion.3), kind=kOutput, calls=%fused_computation.13 | convolution fusion | flops 7247757312 | bytes 33030144 | tf_op jit(solution)/shard_map/ktu,tki->tui/dot_general | solution.py:84
  274.3 15.6 %fusion.1 = f32[72,32,256]{2,1,0:T(8,128)S(1)} fusion(f32[72,256,256]{2,1,0:T(8,128)} %fusion.5, bf16[72,256,256]{2,1,0:T(8,128)(2,1)} %param.11, bf16[72]{0:T(256)(128)(2,1)S(1)} %fusion.61, bf16[72,128,256]{2,1,0:T(8,128)(2,1)} %gather_fusion.1, s32[]{:T(128)S(6)} %select_n.33), kind=kOutput, calls=%fused_computation.9 | convolution fusion | flops 1826095104 | bytes 31850644 | tf_op jit(solution)/shard_map/tui,tci->tcu/dot_general | solution.py:87
  294.8 39.6 %all-reduce = (f32[]{:T(128)}, f32[]{:T(128)}) all-reduce(f32[]{:T(128)} %get-tuple-element.3, f32[]{:T(128)} %get-tuple-element.2), channel_id=1, replica_groups=mesh['rows'=8,'cols'=4] {'rows','cols'}, use_global_device_ids=true, to_apply=%region_4.5 | all-reduce | flops 2 | bytes 16 | tf_op jit(solution)/shard_map/psum | solution.py:20
  336.4 41.5 %psum.38 = f32[]{:T(128)} all-reduce(f32[]{:T(128)} %multiply_reduce_fusion.1), channel_id=1, replica_groups=mesh['rows'=8,'cols'=4] {'rows','cols'}, use_global_device_ids=true, to_apply=%region_8.9 | all-reduce | flops 1 | bytes 8 | tf_op jit(solution)/shard_map/psum | solution.py:20
  380.0 16.9 %all-gather.11.cloned.1.call-done = f32[128,2048]{1,0:T(8,128)} async-done(((f32[32,2048]{1,0:T(8,128)}), f32[128,2048]{1,0:T(8,128)}) %all-gather.11.cloned.1.call-update) | async-done | bytes 1048592 | tf_op jit(solution)/shard_map/all_gather | solution.py:82
  398.3 4.9 %gather_fusion.4 = f32[72,128,256]{2,1,0:T(8,128)} fusion(f32[128,8,256]{2,0,1:T(8,128)S(1)} %bitcast.60, s32[1024]{0:T(1024)S(1)} %pad_clamp_fusion), kind=kCustom, calls=%fused_computation.4 | custom fusion | bytes 18874656 | tf_op jit(solution)/shard_map/gather | solution.py:83
  403.2 15.2 %fusion.3 = f32[72,256,256]{2,1,0:T(8,128)} fusion(bf16[72,128,256]{2,1,0:T(8,128)(2,1)} %gather_fusion.1, f32[72,128,256]{2,1,0:T(8,128)} %gather_fusion.4), kind=kOutput, calls=%fused_computation.11 | convolution fusion | flops 7247757312 | bytes 33030144 | tf_op jit(solution)/shard_map/ktu,tki->tui/dot_general | solution.py:84
  418.4 15.6 %fusion.2 = f32[72,32,256]{2,1,0:T(8,128)S(1)} fusion(f32[72,256,256]{2,1,0:T(8,128)} %fusion.3, bf16[72,256,256]{2,1,0:T(8,128)(2,1)} %param.11, bf16[72]{0:T(256)(128)(2,1)S(1)} %fusion.61, bf16[72,128,256]{2,1,0:T(8,128)(2,1)} %gather_fusion.1, s32[]{:T(128)S(6)} %select_n.33), kind=kOutput, calls=%fused_computation.10 | convolution fusion | flops 1826095104 | bytes 31850644 | tf_op jit(solution)/shard_map/tui,tci->tcu/dot_general | solution.py:87
  438.8 39.5 %psum.39 = f32[]{:T(128)} all-reduce(f32[]{:T(128)} %get-tuple-element.13), channel_id=1, replica_groups=mesh['rows'=8,'cols'=4] {'rows','cols'}, use_global_device_ids=true, to_apply=%region_10.11 | all-reduce | flops 1 | bytes 8 | tf_op jit(solution)/shard_map/psum | solution.py:96
  (58 shorter events, 30.8 us)
Async XLA Ops:
  7.2 27.7 %all-gather.5.cloned.1.call-start = ((), (), s32[]{:S(2)}) async-start(), calls=%async_computation.2 | async-start | bytes 2621440 | tf_op jit(solution)/shard_map/all_gather | solution.py:46
  52.6 6.5 %copy-start.6 = (s32[72]{0:T(128)S(1)}, s32[72]{0:T(128)}, u32[]{:S(2)}) copy-start(s32[72]{0:T(128)} %param.8) | copy-start | bytes 868
  52.6 133.8 %all-to-all-start.1 = ((bf16[8,9,128,256]{3,2,1,0:T(8,128)(2,1)}), bf16[8,9,128,256]{3,2,1,0:T(8,128)(2,1)}, u32[]{:S(2)}, u32[]{:S(2)}) async-start(bf16[8,9,128,256]{3,2,1,0:T(8,128)(2,1)} %broadcast_select_fusion), calls=%async_computation.1 | async-start | bytes 9437184 | tf_op jit(solution)/shard_map/all_to_all | solution.py:54
  58.3 19.6 %all-gather.7.cloned.1.call-start = ((), (), s32[]{:S(2)}) async-start(), calls=%async_computation.3 | async-start | bytes 1310720 | tf_op jit(solution)/shard_map/all_gather | solution.py:82
  59.0 193.5 %all-gather.9.cloned.1.call-start = ((), (), s32[]{:S(2)}) async-start(), calls=%async_computation.4 | async-start | bytes 1310720 | tf_op jit(solution)/shard_map/all_gather | solution.py:82
  79.8 4.9 %copy-start.2 = (bf16[128,8192]{1,0:T(8,128)(2,1)S(1)}, bf16[128,8192]{1,0:T(8,128)(2,1)}, u32[]{:S(2)}) copy-start(bf16[128,8192]{1,0:T(8,128)(2,1)} %all-gather.5.cloned.1.call-done) | copy-start | bytes 6291460
  194.2 10.1 %copy-start = (bf16[72,128,256]{2,1,0:T(8,128)(2,1)S(1)}, bf16[72,128,256]{2,1,0:T(8,128)(2,1)}, u32[]{:S(2)}) copy-start(bf16[72,128,256]{2,1,0:T(8,128)(2,1)} %gather_fusion.1) | copy-start | bytes 14155780
  218.7 18.2 %copy-start.3 = (f32[128,2048]{1,0:T(8,128)S(1)}, f32[128,2048]{1,0:T(8,128)}, u32[]{:S(2)}) copy-start(f32[128,2048]{1,0:T(8,128)} %all-gather.7.cloned.1.call-done) | copy-start | bytes 3145732
  239.3 157.6 %all-gather.11.cloned.1.call-start = ((), (), s32[]{:S(2)}) async-start(), calls=%async_computation.5 | async-start | bytes 1310720 | tf_op jit(solution)/shard_map/all_gather | solution.py:82
  274.3 17.9 %copy-start.1 = (f32[32,2048]{1,0:T(8,128)S(1)}, f32[32,2048]{1,0:T(8,128)}, u32[]{:S(2)}) copy-start(f32[32,2048]{1,0:T(8,128)} %fusion.29) | copy-start | bytes 786436
  418.4 17.9 %copy-start.4 = (f32[32,2048]{1,0:T(8,128)S(1)}, f32[32,2048]{1,0:T(8,128)}, u32[]{:S(2)}) copy-start(f32[32,2048]{1,0:T(8,128)} %multiply_add_fusion.1) | copy-start | bytes 786436
  434.0 45.7 %copy-start.5 = (f32[32,2048]{1,0:T(8,128)S(1)}, f32[32,2048]{1,0:T(8,128)}, u32[]{:S(2)}) copy-start(f32[32,2048]{1,0:T(8,128)} %param.6) | copy-start | bytes 786436
Sparse Core Ops, SparseCore 0:
  9.6 25.2 all-gather.4
  60.7 17.1 all-gather.6
  239.5 13.0 all-gather.8
  380.2 16.7 all-gather.10
where the time goes:
time: 492 us; the launch traced here: 487 us
  blocking collectives  235 us (48%)
  matrix products  116 us (24%)
  waiting for transfers between devices  61.9 us (13%)
  local copies, waits for them, and re-layouts  41 us (8%)
  between operations  18.9 us (4%)
  other arithmetic  8.17 us (2%)
  starting transfers between devices  5.81 us (1%)
    psum x1, blocking collectives, on_device(): gram_rows = lax.psum(gram_part, 'rows')  101 us
    psum x2, blocking collectives, squares(): return lax.psum(jnp.sum(vector * vector), ('rows', 'cols'))  81.1 us
    all_gather x3, waiting for transfers between devices, apply_op(): dirs_full = lax.all_gather(dirs, 'cols', axis=0, tiled=True)  48.9 us
    dot_general x3, matrix products, apply_op(): jnp.einsum('tui,tci->tcu', scores, item_cols, precision=highest)  47.1 us
    dot_general x3, matrix products, apply_op(): jnp.einsum('ktu,tki->tui', dir_tiles, item_tiles, precision=highest)  45.2 us
    psum x1, blocking collectives, on_device(): alpha = norm_now / lax.psum(jnp.sum(direction * image), ('rows', 'cols'))  39.5 us
    gather x3, local copies, waits for them, and re-layouts, apply_op(): dirs_full.reshape(full_width, user_blocks, tile_rows)[:, tile_user]  14.6 us
    all_to_all x1, blocking collectives, on_device(): lax.all_to_all(requests, 'rows', split_axis=0, concat_axis=0, tiled=True)  13.5 us
  transfers between devices with their start and end apart: 5, of which 4 were waited for; matrix products, arithmetic and copies ran while one was open for 2% of the time, Pallas kernels for 0%

commit v1 on v0

v1 whole, which is shorter than its diff:
```python
import functools

import jax
import jax.numpy as jnp
from jax import lax
from jax.experimental import pallas as pl
from jax.experimental.pallas import tpu as pltpu
from jax.sharding import PartitionSpec as P

ridge = 0.5
confidence = 40.0
UNROLL = 8
LIMIT = 24 * 1024 * 1024
f32 = jnp.float32
bf16 = jnp.bfloat16


def matmul(left, right):
    return jnp.dot(left, right, preferred_element_type=f32)


def split(value):
    high = value.astype(bf16)
    low = (value - high.astype(f32)).astype(bf16)
    return high, low


def prepare_kernel(info_ref, x_ref, items_ref, mask_hbm, x_out, items_out, mask, sem):
    column = info_ref[1]
    n_cols, _, span = items_out.shape
    tiles, share, side = mask.shape
    copy = pltpu.make_async_copy(
        mask_hbm.at[:, pl.ds(pl.multiple_of(column * share, share), share), :], mask, sem
    )
    copy.start()
    for m in range(n_cols):
        place = pl.multiple_of((column ^ m) * span, span)
        items_out[m] = items_ref[:, pl.ds(place, span)]
        blocks = x_ref.shape[1] // side
        x_out[column ^ m] = jnp.concatenate(
            [
                x_ref[:, b * side + m * share : b * side + (m + 1) * share]
                for b in range(blocks)
            ],
            axis=1,
        )
    copy.wait()

    def clear(t, carry):
        mask[t] = jnp.zeros((share, side), bf16)
        return carry

    lax.fori_loop(info_ref[0], tiles, clear, 0)


def pick_kernel(side, items_ref, *refs):
    half = len(refs) // 2
    for wanted_ref, out_ref in zip(refs[:half], refs[half:]):
        for r in range(out_ref.shape[0]):
            block = jnp.maximum(wanted_ref[r], 0)
            start = pl.multiple_of(block * side, side)
            out_ref[r] = items_ref[:, pl.ds(start, side)]


def gram_kernel(info_ref, *refs):
    column = info_ref[1]
    pieces, out_ref, items = refs[:-2], refs[-2], refs[-1]
    width = pieces[0].shape[0]
    for m, piece in enumerate(pieces):
        items[pl.ds(pl.multiple_of((column ^ m) * width, width), width), :] = piece[...]
    out_ref[...] = lax.dot_general(
        items[...], items[...], (((1,), (1,)), ((), ())), preferred_element_type=f32
    )


def load(p_hl, vector):
    blocks, both, width = p_hl.shape
    share = both // 2
    high, low = split(vector)
    p_hl[:, :share] = high.reshape(blocks, share, width)
    p_hl[:, share:] = low.reshape(blocks, share, width)


def dense(p_hl, gram_ref, vector):
    blocks, both, width = p_hl.shape
    gram_high, gram_low = split(gram_ref[...])
    product = matmul(
        p_hl[...].reshape(blocks * both, width),
        jnp.concatenate([gram_high, gram_low], axis=1),
    ).reshape(blocks, 2, both // 2, 2 * width)
    product = product[:, 0] + product[:, 1]
    product = product[:, :, :width] + product[:, :, width:]
    return product.reshape(vector.shape) + ridge * vector


def sparse(starting, slot_ref, user_ref, y, mask, p_hl, acc, held):
    tiles, share, side = mask.shape
    groups = tiles // UNROLL
    acc[...] = jnp.zeros_like(acc)

    def score(group):
        for j in range(UNROLL):
            t = group * UNROLL + j
            scores = matmul(p_hl[user_ref[t]], y[slot_ref[t]])
            scores = scores[:share] + scores[share:]
            if starting:
                scores = (1.0 + confidence) - confidence * scores
            high, low = split(mask[t].astype(f32) * scores)
            held[group % 2, j, :share] = high
            held[group % 2, j, share:] = low

    def collect(group):
        terms = []
        for j in range(UNROLL):
            t = group * UNROLL + j
            term = lax.dot_general(
                held[group % 2, j],
                y[slot_ref[t]],
                (((1,), (1,)), ((), ())),
                preferred_element_type=f32,
            )
            terms.append(term[:share] + term[share:])
        return terms

    def add(group, terms):
        for j, term in enumerate(terms):
            acc[user_ref[group * UNROLL + j]] += term

    score(0)

    def step(group, carry):
        terms = collect(group - 1)
        score(group)
        add(group - 1, terms)
        return carry

    lax.fori_loop(1, groups, step, 0)
    add(groups - 1, collect(groups - 1))


def put(column, ref, vector):
    n_cols, piece_width, _ = ref.shape
    turned = vector.T
    for m in range(n_cols):
        ref[column ^ m] = turned[m * piece_width : (m + 1) * piece_width]


def start_kernel(n_cols, slot_ref, user_ref, info_ref, gram_ref, mask, *refs):
    n_pieces = len(refs) - 8
    x_pieces, pieces = refs[:n_cols], refs[n_cols:n_pieces]
    sent_ref, field_ref, y, x, p_hl, acc, held, sems = refs[n_pieces:]
    piece_width = y.shape[1] // n_cols
    column = info_ref[1]
    copies = []
    base = 0
    for k in range(0, len(pieces), 2):
        own, other = pieces[k], pieces[k + 1]
        slots = other.shape[0] // 2
        for m in range(n_cols):
            place = pl.multiple_of((column ^ m) * piece_width, piece_width)
            source = (other if m % 2 else own).at[pl.ds(m // 2 * slots, slots)]
            copies.append(
                pltpu.make_async_copy(
                    source,
                    y.at[pl.ds(base, slots), pl.ds(place, piece_width), :],
                    sems.at[len(copies)],
                )
            )
        base += slots
    for copy in copies:
        copy.start()
    for m, piece in enumerate(x_pieces):
        x[pl.ds(pl.multiple_of((column ^ m) * piece_width, piece_width), piece_width), :] = piece[...]
    start = x[...].T
    load(p_hl, start)
    rest = dense(p_hl, gram_ref, start)
    for copy in copies:
        copy.wait()
    sparse(True, slot_ref, user_ref, y, mask, p_hl, acc, held)
    field = acc[...].reshape(start.shape) - rest
    field_ref[...] = field
    put(column, sent_ref, field)


def first_kernel(
    slot_ref, user_ref, info_ref, field_ref, gram_ref, y, mask, sent_ref, first_ref, p_hl, acc, held
):
    field = field_ref[...]
    load(p_hl, field)
    sparse(False, slot_ref, user_ref, y, mask, p_hl, acc, held)
    first = confidence * acc[...].reshape(field.shape) + dense(p_hl, gram_ref, field)
    first_ref[...] = first
    put(info_ref[1], sent_ref, first)


def second_kernel(
    slot_ref, user_ref, info_ref, field_ref, first_ref, gram_ref, y, mask, sent_ref, dots_ref, p_hl, acc, held
):
    field = field_ref[...]
    first = first_ref[...]
    load(p_hl, first)
    sparse(False, slot_ref, user_ref, y, mask, p_hl, acc, held)
    second = confidence * acc[...].reshape(field.shape) + dense(p_hl, gram_ref, first)
    put(info_ref[1], sent_ref, second)

    def total(left, right):
        return jnp.sum(left * right)

    aa, ab, bb = total(field, field), total(field, first), total(first, first)
    guess = jnp.where(bb > 0.0, ab / jnp.where(bb > 0.0, bb, 1.0), 0.0)
    near = field - guess * first
    near_image = first - guess * second
    values = (
        aa,
        ab,
        bb,
        guess,
        total(near, near),
        total(near, first),
        total(near, near_image),
        total(near, second) + total(first, near_image),
        total(first, second),
    )
    lane = lax.broadcasted_iota(jnp.int32, dots_ref.shape, 1)
    dots = jnp.zeros(dots_ref.shape, f32)
    for j, value in enumerate(values):
        dots = jnp.where(lane == j, value, dots)
    dots_ref[...] = dots


def finish_kernel(share, info_ref, dots_ref, x_ref, *refs):
    n_cols = (len(refs) - 5) // 3
    x_out, r_out, field_ref, first_ref, second_ref = refs[3 * n_cols :]
    for v, ref in enumerate((field_ref, first_ref, second_ref)):
        for m in range(n_cols):
            ref[info_ref[1] ^ m] = refs[v * n_cols + m][...]
    dots = dots_ref[...]

    def column(j):
        return dots[:, j : j + 1]

    def total(value):
        return jnp.sum(value, axis=0, keepdims=True)

    rr0 = total(column(0))
    ab = total(column(1))
    alpha0 = rr0 / ab
    delta = alpha0 - column(3)
    rr1 = total(column(4) - 2.0 * delta * column(5) + delta * delta * column(2))
    curved = total(column(6) - delta * column(7) + delta * delta * column(8))
    crossed = total(column(5) - delta * column(2))
    beta = rr1 / rr0
    alpha1 = rr1 / (curved + 2.0 * beta * crossed + beta * beta * ab)
    along = alpha0 + alpha1 * (1.0 + beta)
    across = alpha1 * alpha0
    blocks = x_ref.shape[1] // (share * n_cols)
    for b in range(blocks):

        def gather(ref):
            return jnp.concatenate(
                [ref[m, :, b * share : (b + 1) * share] for m in range(n_cols)], axis=1
            )

        field, first, second = gather(field_ref), gather(first_ref), gather(second_ref)
        here = slice(b * share * n_cols, (b + 1) * share * n_cols)
        x_out[:, here] = x_ref[:, here] + along * field - across * first
        r_out[:, here] = field - along * first + across * second


def flip(value, axis, bit):
    size = lax.axis_size(axis)
    return lax.ppermute(value, axis, [(i, i ^ bit) for i in range(size)])


def swap(sent):
    return [sent[0]] + [flip(sent[m], "cols", m) for m in range(1, sent.shape[0])]


def after(value, other):
    return lax.optimization_barrier((value, other))[0]


def add_all(value):
    for axis in ("cols", "rows"):
        bit = 1
        while bit < lax.axis_size(axis):
            value = value + flip(value, axis, bit)
            bit *= 2
    return value


def on_device(user_factors, item_factors, tile_user, tile_item, tile_count, tile_mask):
    side = tile_mask.shape[1]
    col_width = user_factors.shape[0]
    column = lax.axis_index("cols").astype(jnp.int32)
    row = lax.axis_index("rows").astype(jnp.int32)
    row_devs = lax.axis_size("rows")
    n_cols = lax.axis_size("cols")
    devices = row_devs * n_cols
    width = col_width * n_cols
    tile_total = tile_user.shape[0]
    users = user_factors.shape[1]
    user_blocks = users // side
    item_blocks = item_factors.shape[1] // side
    share = side // n_cols
    own_users = users // n_cols
    capacity = max(2, (tile_total + row_devs - 1) // row_devs)
    direct = row_devs == 8
    vmem = pl.BlockSpec(memory_space=pltpu.VMEM)
    smem = pl.BlockSpec(memory_space=pltpu.SMEM)
    anywhere = pl.BlockSpec(memory_space=pl.ANY)
    params = pltpu.CompilerParams(vmem_limit_bytes=LIMIT)

    def call(kernel, out_shape, in_specs, name, scratch=(), flops=0):
        return pl.pallas_call(
            kernel,
            out_shape=out_shape,
            in_specs=in_specs,
            out_specs=jax.tree.map(lambda _: vmem, out_shape),
            scratch_shapes=scratch,
            compiler_params=params,
            cost_estimate=pl.CostEstimate(
                flops=flops, bytes_accessed=0, transcendentals=0
            ),
            name=name,
        )

    info = jnp.stack([tile_count[0], column])
    order = jnp.arange(tile_total, dtype=jnp.int32)
    live = (order < tile_count[0]).astype(jnp.int32)
    holder = tile_item // item_blocks
    local_block = tile_item % item_blocks
    earlier = (
        (holder[None, :] == holder[:, None])
        & (order[None, :] < order[:, None])
        & (live[None, :] > 0)
    )
    rank = jnp.sum(earlier.astype(jnp.int32), axis=1)
    near = row if direct else 0
    places = (holder ^ near) * capacity + jnp.minimum(rank, capacity - 1)
    slot_range = jnp.arange(row_devs * capacity, dtype=jnp.int32)
    hits = ((places[None, :] == slot_range[:, None]) & (live[None, :] > 0)).astype(jnp.int32)
    requests = (jnp.sum(hits * (local_block + 1)[None, :], axis=1) - 1).reshape(row_devs, capacity)
    places = jnp.where(live > 0, places, places[0])
    tile_users = jnp.where(live > 0, tile_user, tile_user[0])
    if direct:
        wanted = [flip(requests[j], "rows", j) if j else requests[j] for j in range(row_devs)]
    else:
        wanted = [lax.all_to_all(requests, "rows", split_axis=0, concat_axis=0, tiled=True).reshape(-1)]

    span = item_factors.shape[1] // n_cols
    sent = jax.ShapeDtypeStruct((n_cols, col_width, own_users), f32)
    strengths = jax.ShapeDtypeStruct((tile_total, share, side), bf16)
    start, own_items, mask = call(
        prepare_kernel,
        [sent, jax.ShapeDtypeStruct((n_cols, col_width, span), bf16), strengths],
        [smem, vmem, vmem, pl.BlockSpec(memory_space=pltpu.HBM)],
        "prepare",
        [pltpu.SemaphoreType.DMA],
        10**9,
    )(info, user_factors, item_factors, tile_mask)
    own_items = swap(own_items)
    start = swap(start)

    picked = call(
        functools.partial(pick_kernel, side),
        [jax.ShapeDtypeStruct((len(value), col_width, side), bf16) for value in wanted],
        [vmem] + [smem] * len(wanted),
        "pick",
        flops=10**9,
    )(item_factors, *wanted)
    if direct:
        far = [flip(picked[j], "rows", j) for j in (4, 5)]
        close = [flip(picked[j], "rows", j) for j in (1, 2, 3)]
        last = [flip(after(picked[j + 2], far[j - 4]), "rows", j + 2) for j in (4, 5)]
        groups = [[picked[0]], close, far, last]
        groups = [jnp.concatenate(group, axis=0) for group in groups]
    else:
        groups = [lax.all_to_all(picked[0], "rows", split_axis=0, concat_axis=0, tiled=True)]
    pieces = []
    for own in groups:
        bit = n_cols // 2
        while bit > 1:
            own = jnp.concatenate([own, flip(own, "cols", bit)], axis=0)
            bit //= 2
        pieces += [own, flip(own, "cols", 1)]

    square = jax.ShapeDtypeStruct((width, width), f32)
    gram = call(
        gram_kernel,
        square,
        [smem] + [vmem] * n_cols,
        "gram",
        [pltpu.VMEM((width, span), bf16)],
        10**9,
    )(info, *own_items)
    gram = add_all(gram)

    vector = jax.ShapeDtypeStruct((own_users, width), f32)
    held = jax.ShapeDtypeStruct((row_devs * capacity, width, side), bf16)
    work = [
        pltpu.VMEM((user_blocks, 2 * share, width), bf16),
        pltpu.VMEM((user_blocks, share, width), f32),
        pltpu.VMEM((2, UNROLL, 2 * share, side), bf16),
    ]
    lists = (places, tile_users, info)
    field_sent, field, y = call(
        functools.partial(start_kernel, n_cols),
        [sent, vector, held],
        [smem] * 3 + [vmem] * (2 + n_cols) + [anywhere] * len(pieces),
        "start",
        [pltpu.VMEM((width, own_users), f32)]
        + work
        + [pltpu.SemaphoreType.DMA((n_cols * len(groups),))],
        8 * 10**9,
    )(*lists, gram, mask, *start, *pieces)
    first_sent, first = call(
        first_kernel, [sent, vector], [smem] * 3 + [vmem] * 4, "first", work, 8 * 10**9
    )(*lists, field, gram, y, mask)
    second_sent, dots = call(
        second_kernel,
        [sent, jax.ShapeDtypeStruct((devices, 128), f32)],
        [smem] * 3 + [vmem] * 5,
        "second",
        work,
        8 * 10**9,
    )(*lists, field, first, gram, y, mask)

    turned = swap(field_sent) + swap(first_sent) + swap(second_sent)
    dots = lax.all_to_all(dots, ("rows", "cols"), split_axis=0, concat_axis=0, tiled=True)
    result = jax.ShapeDtypeStruct((col_width, users), f32)
    return tuple(
        call(
            functools.partial(finish_kernel, share),
            [result, result],
            [smem] + [vmem] * (2 + 3 * n_cols),
            "finish",
            [pltpu.VMEM((n_cols, col_width, own_users), f32)] * 3,
            10**9,
        )(info, dots, user_factors, *turned)
    )


def solution(mesh):
    return jax.shard_map(
        on_device,
        mesh=mesh,
        in_specs=(
            P("cols", "rows"),
            P("cols", "rows"),
            P("rows"),
            P("rows"),
            P("rows"),
            P("rows", None, None),
        ),
        out_specs=(P("cols", "rows"), P("cols", "rows")),
        check_vma=False,
    )
```

time: 492 us -> 131 us (0.27)
  blocking collectives: 235 us -> 9.95 us
  matrix products: 116 us -> 0 us
  starting transfers between devices: 5.81 us -> 45.6 us
  local copies, waits for them, and re-layouts: 41 us -> 6.77 us
  Pallas kernels: 0 us -> 21.5 us
  between operations: 18.9 us -> 1.67 us
  waiting for transfers between devices: 61.9 us -> 44.8 us
  other arithmetic: 8.17 us -> 0.58 us
    psum x4 -> x0, blocking collectives: 222 us -> none  [the longest x1 101 us: on_device(): gram_rows = lax.psum(gram_part, 'rows')]
    dot_general x15 -> x0, matrix products: 116 us -> none  [the longest x3 47.1 us: apply_op(): jnp.einsum('tui,tci->tcu', scores, item_cols, precision=highest)]
    all_gather x4 -> x0, waiting for transfers between devices: 60.5 us -> none  [the longest x3 48.9 us: apply_op(): dirs_full = lax.all_gather(dirs, 'cols', axis=0, tiled=True)]
    ppermute x0 -> x42, starting transfers between devices: none -> 45.6 us  [flip(): return lax.ppermute(value, axis, [(i, i ^ bit) for i in range(size)])]
    ppermute x0 -> x42, waiting for transfers between devices: none -> 44.8 us  [flip(): return lax.ppermute(value, axis, [(i, i ^ bit) for i in range(size)])]
    gather x5 -> x0, local copies, waits for them, and re-layouts: 27.9 us -> none  [the longest x3 14.6 us: apply_op(): dirs_full.reshape(full_width, user_blocks, tile_rows)[:, tile_user]]
    pallas_call x0 -> x7, Pallas kernels: none -> 21.5 us  [the longest x1 6.21 us: on_device(): call(functools.partial(start_kernel, n_cols), [sent, vector, held], [smem...]
    reshape x4 -> x0, local copies, waits for them, and re-layouts: 6.23 us -> none  [the longest x1 3.27 us: on_device(): own_full.reshape(own_full.shape[0], item_blocks, tile_rows)]
  transfers between devices with their start and end apart: 5 -> 42, of which waited for: 4 -> 16; matrix products, arithmetic and copies ran while one was open for 2% -> 1% of each run, Pallas kernels for 0% -> 9%
where the time goes in v1:
time: 131 us
  starting transfers between devices  45.6 us (35%)
  waiting for transfers between devices  44.8 us (34%)
  Pallas kernels  21.5 us (16%)
  blocking collectives  9.95 us (8%)
  local copies, waits for them, and re-layouts  6.77 us (5%)
  between operations  1.67 us (1%)
    ppermute x42, starting transfers between devices, flip(): return lax.ppermute(value, axis, [(i, i ^ bit) for i in range(size)])  45.6 us
    ppermute x42, waiting for transfers between devices, flip(): return lax.ppermute(value, axis, [(i, i ^ bit) for i in range(size)])  44.8 us
    all_to_all x1, blocking collectives, on_device(): lax.all_to_all(dots, ('rows', 'cols'), split_axis=0, concat_axis=0, tiled...  9.95 us
    pallas_call x1, Pallas kernels, on_device(): call(functools.partial(start_kernel, n_cols), [sent, vector, held], [smem...  6.21 us
    unnamed x22, local copies, waits for them, and re-layouts  5.78 us
    pallas_call x1, Pallas kernels, on_device(): call(second_kernel, [sent, jax.ShapeDtypeStruct((devices, 128), f32)], [s...  5.21 us
    pallas_call x1, Pallas kernels, on_device(): call(first_kernel, [sent, vector], [smem] * 3 + [vmem] * 4, 'first', work...  5.04 us
  transfers between devices with their start and end apart: 42, of which 16 were waited for; matrix products, arithmetic and copies ran while one was open for 1% of the time, Pallas kernels for 9%

profile of v1, /device:TPU:0, one launch (start us, length us, event | category | flops | bytes accessed | tf_op | source)
XLA Modules:
  0.0 131.0 jit_solution(8821556971259141801)
XLA Ops:
  1.4 3.7 %copy-done = bf16[72,256,256]{2,1,0:T(8,128)(2,1)S(1)} copy-done((bf16[72,256,256]{2,1,0:T(8,128)(2,1)S(1)}, bf16[72,256,256]{2,1,0:T(8,128)(2,1)}, u32[]{:S(2)}) %copy-start) | copy-done | bytes 9437208
  8.8 2.4 %collective-permute-start.2 = (bf16[32,2048]{1,0:T(8,128)(2,1)}, bf16[32,2048]{1,0:T(8,128)(2,1)S(1)}, u32[]{:S(2)}, u32[]{:S(2)}) collective-permute-start(bf16[32,2048]{1,0:T(8,128)(2,1)} %get-tuple-element.42), channel_id=1, source_target_pairs={{0,3},{1,2},{2,1},{3,0},{4,7},{5,6},{6,5},{7,4},{8,11},{9,10},{10,... | collective-permute-start | bytes 393224 | tf_op jit(solution)/shard_map/ppermute | solution.py:272
  12.3 4.8 %collective-permute-start.17 = (s32[9]{0:T(128)S(1)}, s32[9]{0:T(128)S(1)}, u32[]{:S(2)}, u32[]{:S(2)}) collective-permute-start(s32[9]{0:T(128)S(1)} %get-tuple-element.62), channel_id=1, source_target_pairs={{0,28},{4,24},{8,20},{12,16},{16,12},{20,8},{24,4},{28,0},{1,29},{... | collective-permute-start | bytes 116 | tf_op jit(solution)/shard_map/ppermute | solution.py:272
  18.6 1.9 %collective-permute-start.15 = (s32[9]{0:T(128)S(1)}, s32[9]{0:T(128)S(1)}, u32[]{:S(2)}, u32[]{:S(2)}) collective-permute-start(s32[9]{0:T(128)S(1)} %get-tuple-element.64), channel_id=1, source_target_pairs={{0,20},{4,16},{8,28},{12,24},{16,4},{20,0},{24,12},{28,8},{1,21},{... | collective-permute-start | bytes 116 | tf_op jit(solution)/shard_map/ppermute | solution.py:272
  20.5 1.9 %collective-permute-done.16.refs_6_ = s32[9]{0:T(128)S(1)} collective-permute-done((s32[9]{0:T(128)S(1)}, s32[9]{0:T(128)S(1)}, u32[]{:S(2)}, u32[]{:S(2)}) %collective-permute-start.16) | collective-permute-done | bytes 68 | tf_op jit(solution)/shard_map/ppermute | solution.py:272
  28.4 1.8 %collective-permute-start.11 = (s32[9]{0:T(128)S(1)}, s32[9]{0:T(128)S(1)}, u32[]{:S(2)}, u32[]{:S(2)}) collective-permute-start(s32[9]{0:T(128)S(1)} %get-tuple-element.68), channel_id=1, source_target_pairs={{0,4},{4,0},{8,12},{12,8},{16,20},{20,16},{24,28},{28,24},{1,5},{5... | collective-permute-start | bytes 116 | tf_op jit(solution)/shard_map/ppermute | solution.py:272
  32.7 2.4 %collective-permute-start.25 = (bf16[9,32,256]{2,1,0:T(8,128)(2,1)S(1)}, bf16[9,32,256]{2,1,0:T(8,128)(2,1)S(1)}, u32[]{:S(2)}, u32[]{:S(2)}) collective-permute-start(bf16[9,32,256]{2,1,0:T(8,128)(2,1)S(1)} %get-tuple-element.29), channel_id=1, source_target_pairs={{0,16},{4,20},{8,24},{12,28},{16,0},{20,4},{24,8},{28,12},{1,17},{... | collective-permute-start | bytes 442376 | tf_op jit(solution)/shard_map/ppermute | solution.py:272
  35.1 1.8 %collective-permute-start.26 = (bf16[9,32,256]{2,1,0:T(8,128)(2,1)S(1)}, bf16[9,32,256]{2,1,0:T(8,128)(2,1)S(1)}, u32[]{:S(2)}, u32[]{:S(2)}) collective-permute-start(bf16[9,32,256]{2,1,0:T(8,128)(2,1)S(1)} %get-tuple-element.30), channel_id=1, source_target_pairs={{0,20},{4,16},{8,28},{12,24},{16,4},{20,0},{24,12},{28,8},{1,21},{... | collective-permute-start | bytes 442376 | tf_op jit(solution)/shard_map/ppermute | solution.py:272
  38.7 1.8 %collective-permute-start.22 = (bf16[9,32,256]{2,1,0:T(8,128)(2,1)S(1)}, bf16[9,32,256]{2,1,0:T(8,128)(2,1)S(1)}, u32[]{:S(2)}, u32[]{:S(2)}) collective-permute-start(bf16[9,32,256]{2,1,0:T(8,128)(2,1)S(1)} %get-tuple-element.28), channel_id=1, source_target_pairs={{0,12},{4,8},{8,4},{12,0},{16,28},{20,24},{24,20},{28,16},{1,13},{... | collective-permute-start | bytes 442376 | tf_op jit(solution)/shard_map/ppermute | solution.py:272
  43.3 2.6 %collective-permute-done.26 = bf16[9,32,256]{2,1,0:T(8,128)(2,1)S(1)} collective-permute-done((bf16[9,32,256]{2,1,0:T(8,128)(2,1)S(1)}, bf16[9,32,256]{2,1,0:T(8,128)(2,1)S(1)}, u32[]{:S(2)}, u32[]{:S(2)}) %collective-permute-start.26) | collective-permute-done | bytes 147488 | tf_op jit(solution)/shard_map/ppermute | solution.py:272
  45.9 2.7 %collective-permute-start.29 = (bf16[9,32,256]{2,1,0:T(8,128)(2,1)S(1)}, bf16[9,32,256]{2,1,0:T(8,128)(2,1)S(1)}, u32[]{:S(2)}, u32[]{:S(2)}) collective-permute-start(bf16[9,32,256]{2,1,0:T(8,128)(2,1)S(1)} %get-tuple-element.32), channel_id=1, source_target_pairs={{0,24},{4,28},{8,16},{12,20},{16,8},{20,12},{24,0},{28,4},{1,25},{... | collective-permute-start | bytes 442376 | tf_op jit(solution)/shard_map/ppermute | solution.py:272
  52.2 11.2 %collective-permute-done.4 = f32[128,128]{1,0:T(8,128)S(1)} collective-permute-done((f32[128,128]{1,0:T(8,128)S(1)}, f32[128,128]{1,0:T(8,128)S(1)}, u32[]{:S(2)}, u32[]{:S(2)}) %collective-permute-start.4) | collective-permute-done | bytes 65568 | tf_op jit(solution)/shard_map/ppermute | solution.py:272
  67.1 6.3 %collective-permute-done.27 = bf16[18,32,256]{2,1,0:T(8,128)(2,1)S(1)} collective-permute-done((bf16[18,32,256]{2,1,0:T(8,128)(2,1)S(1)}, bf16[18,32,256]{2,1,0:T(8,128)(2,1)S(1)}, u32[]{:S(2)}, u32[]{:S(2)}) %collective-permute-start.27) | collective-permute-done | bytes 294944 | tf_op jit(solution)/shard_map/ppermute | solution.py:272
  73.5 4.3 %collective-permute-done.31 = bf16[18,32,256]{2,1,0:T(8,128)(2,1)S(1)} collective-permute-done((bf16[18,32,256]{2,1,0:T(8,128)(2,1)S(1)}, bf16[18,32,256]{2,1,0:T(8,128)(2,1)S(1)}, u32[]{:S(2)}, u32[]{:S(2)}) %collective-permute-start.31) | collective-permute-done | bytes 294944 | tf_op jit(solution)/shard_map/ppermute | solution.py:272
  77.9 1.6 %collective-permute-start.10 = (f32[32,512]{1,0:T(8,128)S(1)}, f32[32,512]{1,0:T(8,128)S(1)}, u32[]{:S(2)}, u32[]{:S(2)}) collective-permute-start(f32[32,512]{1,0:T(8,128)S(1)} %get-tuple-element.58), channel_id=1, source_target_pairs={{0,3},{1,2},{2,1},{3,0},{4,7},{5,6},{6,5},{7,4},{8,11},{9,10},{10,... | collective-permute-start | bytes 196616 | tf_op jit(solution)/shard_map/ppermute | solution.py:272
  79.5 2.2 %collective-permute-done.10.refs_3_ = f32[32,512]{1,0:T(8,128)S(1)} collective-permute-done((f32[32,512]{1,0:T(8,128)S(1)}, f32[32,512]{1,0:T(8,128)S(1)}, u32[]{:S(2)}, u32[]{:S(2)}) %collective-permute-start.10) | collective-permute-done | bytes 65568 | tf_op jit(solution)/shard_map/ppermute | solution.py:272
  83.2 4.2 %collective-permute-done.6 = f32[128,128]{1,0:T(8,128)S(1)} collective-permute-done((f32[128,128]{1,0:T(8,128)S(1)}, f32[128,128]{1,0:T(8,128)S(1)}, u32[]{:S(2)}, u32[]{:S(2)}) %collective-permute-start.6) | collective-permute-done | bytes 65568 | tf_op jit(solution)/shard_map/ppermute | solution.py:272
  87.4 1.8 %collective-permute-start.7 = (f32[128,128]{1,0:T(8,128)S(1)}, f32[128,128]{1,0:T(8,128)S(1)}, u32[]{:S(2)}, u32[]{:S(2)}) collective-permute-start(f32[128,128]{1,0:T(8,128)S(1)} %add.33), channel_id=1, source_target_pairs={{0,16},{4,20},{8,24},{12,28},{16,0},{20,4},{24,8},{28,12},{1,17},{... | collective-permute-start | bytes 196616 | tf_op jit(solution)/shard_map/ppermute | solution.py:272
  89.2 5.1 %collective-permute-done.7 = f32[128,128]{1,0:T(8,128)S(1)} collective-permute-done((f32[128,128]{1,0:T(8,128)S(1)}, f32[128,128]{1,0:T(8,128)S(1)}, u32[]{:S(2)}, u32[]{:S(2)}) %collective-permute-start.7) | collective-permute-done | bytes 65568 | tf_op jit(solution)/shard_map/ppermute | solution.py:272
  95.6 6.2 %start.1 = (f32[4,32,512]{2,1,0:T(8,128)S(1)}, f32[512,128]{1,0:T(8,128)S(1)}, bf16[72,128,256]{2,1,0:T(8,128)(2,1)S(1)}) custom-call(s32[72]{0:T(128)S(1)} %get-tuple-element.73.slot_ref, s32[72]{0:T(128)S(1)} %get-tuple-element.72.user_ref, s32[2]{0:T(128)S(1)} %pad_add_fusion.info_ref, f32[128,128]{1,0:T(8,128)S(1)} %add.34.gram_ref, ...), custom_call_target="tpu_custom_call" | custom-call | flops 8000000000 | tf_op jit(solution)/shard_map/start/pallas_call | solution.py:407
  103.8 5.0 %first.1 = (f32[4,32,512]{2,1,0:T(8,128)S(1)}, f32[512,128]{1,0:T(8,128)S(1)}) custom-call(s32[72]{0:T(128)S(1)} %get-tuple-element.73.slot_ref, s32[72]{0:T(128)S(1)} %get-tuple-element.72.user_ref, s32[2]{0:T(128)S(1)} %pad_add_fusion.info_ref, f32[512,128]{1,0:T(8,128)S(1)} %get-tuple-element.35.field_ref, f32[128,128]{1,0:T(8,128)S(1)} %add.34.gram_ref, ...), custom_call_target="tpu_custom_call" | custom-call | flops 8000000000 | tf_op jit(solution)/shard_map/first/pallas_call | solution.py:417
  108.8 5.2 %second.1 = (f32[4,32,512]{2,1,0:T(8,128)S(1)}, f32[32,128]{1,0:T(8,128)S(1)}) custom-call(s32[72]{0:T(128)S(1)} %get-tuple-element.73.slot_ref, s32[72]{0:T(128)S(1)} %get-tuple-element.72.user_ref, s32[2]{0:T(128)S(1)} %pad_add_fusion.info_ref, f32[512,128]{1,0:T(8,128)S(1)} %get-tuple-element.35.field_ref, f32[512,128]{1,0:T(8,128)S(1)} %get-tuple-element.37.first_ref, ...), custom_call_target="tpu_custom_call" | custom-call | flops 8000000000 | tf_op jit(solution)/shard_map/second/pallas_call | solution.py:420
  118.9 10.0 %all_to_all.11 = f32[32,1,128]{2,1,0:T(1,128)S(1)} all-to-all(f32[32,1,128]{2,1,0:T(1,128)S(1)} %bitcast.52), channel_id=1, replica_groups=mesh['rows'=8,'cols'=4] {'rows','cols'}, dimensions={0} | all-to-all | bytes 32768 | tf_op jit(solution)/shard_map/all_to_all | solution.py:430
  128.9 2.0 %finish.1 = (f32[32,2048]{1,0:T(8,128)}, f32[32,2048]{1,0:T(8,128)}) custom-call(s32[2]{0:T(128)S(1)} %pad_add_fusion.info_ref, f32[32,128]{1,0:T(8,128)S(1)} %bitcast.53, f32[32,2048]{1,0:T(8,128)S(1)} %copy-done.4, f32[32,512]{1,0:T(8,128)S(1)} %get-tuple-element.57.refs_0_, f32[32,512]{1,0:T(8,128)S(1)} %collective-permute-done.33.refs_1_, ...), custom_call_target="tpu_custom_call" | custom-call | flops 1000000000 | tf_op jit(solution)/shard_map/finish/pallas_call | solution.py:433
  (116 shorter events, 36.4 us)
Async XLA Ops:
  8.8 28.2 %collective-permute-start.2 = (bf16[32,2048]{1,0:T(8,128)(2,1)}, bf16[32,2048]{1,0:T(8,128)(2,1)S(1)}, u32[]{:S(2)}, u32[]{:S(2)}) collective-permute-start(bf16[32,2048]{1,0:T(8,128)(2,1)} %get-tuple-element.42), channel_id=1, source_target_pairs={{0,3},{1,2},{2,1},{3,0},{4,7},{5,6},{6,5},{7,4},{8,11},{9,10},{10,... | collective-permute-start | bytes 393224 | tf_op jit(solution)/shard_map/ppermute | solution.py:272
  11.2 26.0 %collective-permute-start.1 = (bf16[32,2048]{1,0:T(8,128)(2,1)}, bf16[32,2048]{1,0:T(8,128)(2,1)S(1)}, u32[]{:S(2)}, u32[]{:S(2)}) collective-permute-start(bf16[32,2048]{1,0:T(8,128)(2,1)} %get-tuple-element.43), channel_id=1, source_target_pairs={{0,2},{1,3},{2,0},{3,1},{4,6},{5,7},{6,4},{7,5},{8,10},{9,11},{10,... | collective-permute-start | bytes 393224 | tf_op jit(solution)/shard_map/ppermute | solution.py:272
  11.8 26.9 %collective-permute-start = (bf16[32,2048]{1,0:T(8,128)(2,1)}, bf16[32,2048]{1,0:T(8,128)(2,1)}, u32[]{:S(2)}, u32[]{:S(2)}) collective-permute-start(bf16[32,2048]{1,0:T(8,128)(2,1)} %get-tuple-element.44), channel_id=1, source_target_pairs={{0,1},{1,0},{2,3},{3,2},{4,5},{5,4},{6,7},{7,6},{8,9},{9,8},{10,11... | collective-permute-start | bytes 393224 | tf_op jit(solution)/shard_map/ppermute | solution.py:272
  35.1 10.7 %collective-permute-start.26 = (bf16[9,32,256]{2,1,0:T(8,128)(2,1)S(1)}, bf16[9,32,256]{2,1,0:T(8,128)(2,1)S(1)}, u32[]{:S(2)}, u32[]{:S(2)}) collective-permute-start(bf16[9,32,256]{2,1,0:T(8,128)(2,1)S(1)} %get-tuple-element.30), channel_id=1, source_target_pairs={{0,20},{4,16},{8,28},{12,24},{16,4},{20,0},{24,12},{28,8},{1,21},{... | collective-permute-start | bytes 442376 | tf_op jit(solution)/shard_map/ppermute | solution.py:272
  37.2 11.4 %collective-permute-start.21 = (bf16[9,32,256]{2,1,0:T(8,128)(2,1)S(1)}, bf16[9,32,256]{2,1,0:T(8,128)(2,1)S(1)}, u32[]{:S(2)}, u32[]{:S(2)}) collective-permute-start(bf16[9,32,256]{2,1,0:T(8,128)(2,1)S(1)} %get-tuple-element.27), channel_id=1, source_target_pairs={{0,8},{4,12},{8,0},{12,4},{16,24},{20,28},{24,16},{28,20},{1,9},{5... | collective-permute-start | bytes 442376 | tf_op jit(solution)/shard_map/ppermute | solution.py:272
  38.7 11.2 %collective-permute-start.22 = (bf16[9,32,256]{2,1,0:T(8,128)(2,1)S(1)}, bf16[9,32,256]{2,1,0:T(8,128)(2,1)S(1)}, u32[]{:S(2)}, u32[]{:S(2)}) collective-permute-start(bf16[9,32,256]{2,1,0:T(8,128)(2,1)S(1)} %get-tuple-element.28), channel_id=1, source_target_pairs={{0,12},{4,8},{8,4},{12,0},{16,28},{20,24},{24,20},{28,16},{1,13},{... | collective-permute-start | bytes 442376 | tf_op jit(solution)/shard_map/ppermute | solution.py:272
  41.9 41.3 %collective-permute-start.18 = (bf16[9,32,256]{2,1,0:T(8,128)(2,1)S(1)}, bf16[9,32,256]{2,1,0:T(8,128)(2,1)S(1)}, u32[]{:S(2)}, u32[]{:S(2)}) collective-permute-start(bf16[9,32,256]{2,1,0:T(8,128)(2,1)S(1)} %get-tuple-element.25), channel_id=1, source_target_pairs={{0,2},{1,3},{2,0},{3,1},{4,6},{5,7},{6,4},{7,5},{8,10},{9,11},{10,... | collective-permute-start | bytes 442376 | tf_op jit(solution)/shard_map/ppermute | solution.py:272
  45.9 19.0 %collective-permute-start.29 = (bf16[9,32,256]{2,1,0:T(8,128)(2,1)S(1)}, bf16[9,32,256]{2,1,0:T(8,128)(2,1)S(1)}, u32[]{:S(2)}, u32[]{:S(2)}) collective-permute-start(bf16[9,32,256]{2,1,0:T(8,128)(2,1)S(1)} %get-tuple-element.32), channel_id=1, source_target_pairs={{0,24},{4,28},{8,16},{12,20},{16,8},{20,12},{24,0},{28,4},{1,25},{... | collective-permute-start | bytes 442376 | tf_op jit(solution)/shard_map/ppermute | solution.py:272
  48.6 17.6 %collective-permute-start.30 = (bf16[9,32,256]{2,1,0:T(8,128)(2,1)S(1)}, bf16[9,32,256]{2,1,0:T(8,128)(2,1)S(1)}, u32[]{:S(2)}, u32[]{:S(2)}) collective-permute-start(bf16[9,32,256]{2,1,0:T(8,128)(2,1)S(1)} %get-tuple-element.34), channel_id=1, source_target_pairs={{0,28},{4,24},{8,20},{12,16},{16,12},{20,8},{24,4},{28,0},{1,29},{... | collective-permute-start | bytes 442376 | tf_op jit(solution)/shard_map/ppermute | solution.py:272
  49.9 17.0 %collective-permute-start.23 = (bf16[27,32,256]{2,1,0:T(8,128)(2,1)S(1)}, bf16[27,32,256]{2,1,0:T(8,128)(2,1)S(1)}, u32[]{:S(2)}, u32[]{:S(2)}) collective-permute-start(bf16[27,32,256]{2,1,0:T(8,128)(2,1)S(1)} %pad_maximum_fusion), channel_id=1, source_target_pairs={{0,2},{1,3},{2,0},{3,1},{4,6},{5,7},{6,4},{7,5},{8,10},{9,11},{10,... | collective-permute-start | bytes 1327112 | tf_op jit(solution)/shard_map/ppermute | solution.py:272
  51.6 11.9 %collective-permute-start.4 = (f32[128,128]{1,0:T(8,128)S(1)}, f32[128,128]{1,0:T(8,128)S(1)}, u32[]{:S(2)}, u32[]{:S(2)}) collective-permute-start(f32[128,128]{1,0:T(8,128)S(1)} %add.30), channel_id=1, source_target_pairs={{0,2},{1,3},{2,0},{3,1},{4,6},{5,7},{6,4},{7,5},{8,10},{9,11},{10,... | collective-permute-start | bytes 196616 | tf_op jit(solution)/shard_map/ppermute | solution.py:272
  64.9 13.0 %collective-permute-start.5 = (f32[128,128]{1,0:T(8,128)S(1)}, f32[128,128]{1,0:T(8,128)S(1)}, u32[]{:S(2)}, u32[]{:S(2)}) collective-permute-start(f32[128,128]{1,0:T(8,128)S(1)} %add.31), channel_id=1, source_target_pairs={{0,4},{4,0},{8,12},{12,8},{16,20},{20,16},{24,28},{28,24},{1,5},{5... | collective-permute-start | bytes 196616 | tf_op jit(solution)/shard_map/ppermute | solution.py:272
  66.3 11.5 %collective-permute-start.31 = (bf16[18,32,256]{2,1,0:T(8,128)(2,1)S(1)}, bf16[18,32,256]{2,1,0:T(8,128)(2,1)S(1)}, u32[]{:S(2)}, u32[]{:S(2)}) collective-permute-start(bf16[18,32,256]{2,1,0:T(8,128)(2,1)S(1)} %pad_maximum_fusion.2), channel_id=1, source_target_pairs={{0,2},{1,3},{2,0},{3,1},{4,6},{5,7},{6,4},{7,5},{8,10},{9,11},{10,... | collective-permute-start | bytes 884744 | tf_op jit(solution)/shard_map/ppermute | solution.py:272
  67.0 28.6 %collective-permute-start.24 = (bf16[54,32,256]{2,1,0:T(8,128)(2,1)S(1)}, bf16[54,32,256]{2,1,0:T(8,128)(2,1)S(1)}, u32[]{:S(2)}, u32[]{:S(2)}) collective-permute-start(bf16[54,32,256]{2,1,0:T(8,128)(2,1)S(1)} %constant_dynamic-update-slice_fusion.2.refs_6_), channel_id=1, source_target_pairs={{0,1},{1,0},{2,3},{3,2},{4,5},{5,4},{6,7},{7,6},{8,9},{9,8},{10,11... | collective-permute-start | bytes 2654216 | tf_op jit(solution)/shard_map/ppermute | solution.py:272
  73.4 22.2 %collective-permute-start.28 = (bf16[36,32,256]{2,1,0:T(8,128)(2,1)S(1)}, bf16[36,32,256]{2,1,0:T(8,128)(2,1)S(1)}, u32[]{:S(2)}, u32[]{:S(2)}) collective-permute-start(bf16[36,32,256]{2,1,0:T(8,128)(2,1)S(1)} %constant_dynamic-update-slice_fusion.6.refs_8_), channel_id=1, source_target_pairs={{0,1},{1,0},{2,3},{3,2},{4,5},{5,4},{6,7},{7,6},{8,9},{9,8},{10,11... | collective-permute-start | bytes 1769480 | tf_op jit(solution)/shard_map/ppermute | solution.py:272
  77.8 17.8 %collective-permute-start.32 = (bf16[36,32,256]{2,1,0:T(8,128)(2,1)S(1)}, bf16[36,32,256]{2,1,0:T(8,128)(2,1)S(1)}, u32[]{:S(2)}, u32[]{:S(2)}) collective-permute-start(bf16[36,32,256]{2,1,0:T(8,128)(2,1)S(1)} %constant_dynamic-update-slice_fusion.9.refs_10_), channel_id=1, source_target_pairs={{0,1},{1,0},{2,3},{3,2},{4,5},{5,4},{6,7},{7,6},{8,9},{9,8},{10,11... | collective-permute-start | bytes 1769480 | tf_op jit(solution)/shard_map/ppermute | solution.py:272
  101.8 14.4 %collective-permute-start.35 = (f32[32,512]{1,0:T(8,128)S(1)}, f32[32,512]{1,0:T(8,128)S(1)}, u32[]{:S(2)}, u32[]{:S(2)}) collective-permute-start(f32[32,512]{1,0:T(8,128)S(1)} %get-tuple-element.54), channel_id=1, source_target_pairs={{0,3},{1,2},{2,1},{3,0},{4,7},{5,6},{6,5},{7,4},{8,11},{9,10},{10,... | collective-permute-start | bytes 196616 | tf_op jit(solution)/shard_map/ppermute | solution.py:272
  102.3 14.1 %collective-permute-start.34 = (f32[32,512]{1,0:T(8,128)S(1)}, f32[32,512]{1,0:T(8,128)S(1)}, u32[]{:S(2)}, u32[]{:S(2)}) collective-permute-start(f32[32,512]{1,0:T(8,128)S(1)} %get-tuple-element.55), channel_id=1, source_target_pairs={{0,2},{1,3},{2,0},{3,1},{4,6},{5,7},{6,4},{7,5},{8,10},{9,11},{10,... | collective-permute-start | bytes 196616 | tf_op jit(solution)/shard_map/ppermute | solution.py:272
  103.7 13.3 %collective-permute-start.33 = (f32[32,512]{1,0:T(8,128)S(1)}, f32[32,512]{1,0:T(8,128)S(1)}, u32[]{:S(2)}, u32[]{:S(2)}) collective-permute-start(f32[32,512]{1,0:T(8,128)S(1)} %get-tuple-element.56), channel_id=1, source_target_pairs={{0,1},{1,0},{2,3},{3,2},{4,5},{5,4},{6,7},{7,6},{8,9},{9,8},{10,11... | collective-permute-start | bytes 196616 | tf_op jit(solution)/shard_map/ppermute | solution.py:272
  114.8 14.1 %collective-permute-start.40 = (f32[32,512]{1,0:T(8,128)S(1)}, f32[32,512]{1,0:T(8,128)S(1)}, u32[]{:S(2)}, u32[]{:S(2)}) collective-permute-start(f32[32,512]{1,0:T(8,128)S(1)} %get-tuple-element.47), channel_id=1, source_target_pairs={{0,2},{1,3},{2,0},{3,1},{4,6},{5,7},{6,4},{7,5},{8,10},{9,11},{10,... | collective-permute-start | bytes 196616 | tf_op jit(solution)/shard_map/ppermute | solution.py:272
  116.2 12.6 %collective-permute-start.39 = (f32[32,512]{1,0:T(8,128)S(1)}, f32[32,512]{1,0:T(8,128)S(1)}, u32[]{:S(2)}, u32[]{:S(2)}) collective-permute-start(f32[32,512]{1,0:T(8,128)S(1)} %get-tuple-element.48), channel_id=1, source_target_pairs={{0,1},{1,0},{2,3},{3,2},{4,5},{5,4},{6,7},{7,6},{8,9},{9,8},{10,11... | collective-permute-start | bytes 196616 | tf_op jit(solution)/shard_map/ppermute | solution.py:272
  116.3 12.5 %collective-permute-start.38 = (f32[32,512]{1,0:T(8,128)S(1)}, f32[32,512]{1,0:T(8,128)S(1)}, u32[]{:S(2)}, u32[]{:S(2)}) collective-permute-start(f32[32,512]{1,0:T(8,128)S(1)} %get-tuple-element.50), channel_id=1, source_target_pairs={{0,3},{1,2},{2,1},{3,0},{4,7},{5,6},{6,5},{7,4},{8,11},{9,10},{10,... | collective-permute-start | bytes 196616 | tf_op jit(solution)/shard_map/ppermute | solution.py:272
  117.0 11.8 %collective-permute-start.37 = (f32[32,512]{1,0:T(8,128)S(1)}, f32[32,512]{1,0:T(8,128)S(1)}, u32[]{:S(2)}, u32[]{:S(2)}) collective-permute-start(f32[32,512]{1,0:T(8,128)S(1)} %get-tuple-element.51), channel_id=1, source_target_pairs={{0,2},{1,3},{2,0},{3,1},{4,6},{5,7},{6,4},{7,5},{8,10},{9,11},{10,... | collective-permute-start | bytes 196616 | tf_op jit(solution)/shard_map/ppermute | solution.py:272
  118.5 10.4 %collective-permute-start.36 = (f32[32,512]{1,0:T(8,128)S(1)}, f32[32,512]{1,0:T(8,128)S(1)}, u32[]{:S(2)}, u32[]{:S(2)}) collective-permute-start(f32[32,512]{1,0:T(8,128)S(1)} %get-tuple-element.52), channel_id=1, source_target_pairs={{0,1},{1,0},{2,3},{3,2},{4,5},{5,4},{6,7},{7,6},{8,9},{9,8},{10,11... | collective-permute-start | bytes 196616 | tf_op jit(solution)/shard_map/ppermute | solution.py:272
  (25 other events, 209.3 us)

commit v2 on v1

--- a/solution.py
+++ b/solution.py
@@ -25,25 +25,45 @@
     return high, low
 
 
-def prepare_kernel(info_ref, x_ref, items_ref, mask_hbm, x_out, items_out, mask, sem):
+def prepare_kernel(n_cols, side, info_ref, x_hbm, items_hbm, *refs):
+    sent, (x_ref, x_pieces, sems) = refs[:n_cols], refs[n_cols:]
     column = info_ref[1]
-    n_cols, _, span = items_out.shape
+    share = side // n_cols
+    blocks = x_ref.shape[1] // side
+    own_users = blocks * share
+    span = sent[0].shape[1] - 2 * own_users
+    copies = [
+        pltpu.make_async_copy(
+            items_hbm.at[:, pl.ds(pl.multiple_of((column ^ m) * span, span), span)],
+            sent[m].at[:, pl.ds(2 * own_users, span)],
+            sems.at[m],
+        )
+        for m in range(n_cols)
+    ]
+    fetch = pltpu.make_async_copy(x_hbm, x_ref, sems.at[n_cols])
+    fetch.start()
+    for copy in copies:
+        copy.start()
+    fetch.wait()
+    for m in range(n_cols):
+        x_pieces[m] = jnp.concatenate(
+            [x_ref[:, b * side + m * share : b * side + (m + 1) * share] for b in range(blocks)],
+            axis=1,
+        )
+    for m in range(n_cols):
+        high, low = split(x_pieces[column ^ m])
+        sent[m][:, :own_users] = high
+        sent[m][:, own_users : 2 * own_users] = low
+    for copy in copies:
+        copy.wait()
+
+
+def mask_kernel(info_ref, mask_hbm, mask, sem):
     tiles, share, side = mask.shape
     copy = pltpu.make_async_copy(
-        mask_hbm.at[:, pl.ds(pl.multiple_of(column * share, share), share), :], mask, sem
+        mask_hbm.at[:, pl.ds(pl.multiple_of(info_ref[1] * share, share), share), :], mask, sem
     )
     copy.start()
-    for m in range(n_cols):
-        place = pl.multiple_of((column ^ m) * span, span)
-        items_out[m] = items_ref[:, pl.ds(place, span)]
-        blocks = x_ref.shape[1] // side
-        x_out[column ^ m] = jnp.concatenate(
-            [
-                x_ref[:, b * side + m * share : b * side + (m + 1) * share]
-                for b in range(blocks)
-            ],
-            axis=1,
-        )
     copy.wait()
 
     def clear(t, carry):
@@ -53,24 +73,62 @@
     lax.fori_loop(info_ref[0], tiles, clear, 0)
 
 
-def pick_kernel(side, items_ref, *refs):
-    half = len(refs) // 2
-    for wanted_ref, out_ref in zip(refs[:half], refs[half:]):
-        for r in range(out_ref.shape[0]):
-            block = jnp.maximum(wanted_ref[r], 0)
-            start = pl.multiple_of(block * side, side)
-            out_ref[r] = items_ref[:, pl.ds(start, side)]
-
-
-def gram_kernel(info_ref, *refs):
+def pick_kernel(direct, info_ref, wanted_ref, items_ref, *out_refs):
+    capacity = wanted_ref.shape[1]
+    side = out_refs[0].shape[2]
+    for o, out_ref in enumerate(out_refs):
+        for i in range(out_ref.shape[0] // capacity):
+            dest = info_ref[2] ^ o if direct else i
+            for r in range(capacity):
+                block = jnp.maximum(wanted_ref[dest, r], 0)
+                start = pl.multiple_of(block * side, side)
+                out_ref[i * capacity + r] = items_ref[:, pl.ds(start, side)]
+
+
+def pack(ref, gram):
+    high, low = split(gram)
+    both = jnp.concatenate([high, low], axis=1)
+    for k in range(ref.shape[0]):
+        ref[k] = both[k * ref.shape[1] : (k + 1) * ref.shape[1]]
+
+
+def unpack(blocks):
+    both = jnp.concatenate([blocks[k] for k in range(blocks.shape[0])], axis=0).astype(f32)
+    width = both.shape[1] // 2
+    return both[:, :width] + both[:, width:]
+
+
+def gram_kernel(own_users, info_ref, *refs):
     column = info_ref[1]
-    pieces, out_ref, items = refs[:-2], refs[-2], refs[-1]
+    pieces = refs[:-6]
+    out_ref, pack_ref, start_ref, starts, items, sems = refs[-6:]
     width = pieces[0].shape[0]
+    span = items.shape[1]
+    copies = []
     for m, piece in enumerate(pieces):
-        items[pl.ds(pl.multiple_of((column ^ m) * width, width), width), :] = piece[...]
-    out_ref[...] = lax.dot_general(
+        place = pl.ds(pl.multiple_of((column ^ m) * width, width), width)
+        for source, target in (
+            (piece.at[:, pl.ds(0, 2 * own_users)], starts.at[place, :]),
+            (piece.at[:, pl.ds(2 * own_users, span)], items.at[place, :]),
+        ):
+            copies.append(pltpu.make_async_copy(source, target, sems.at[len(copies)]))
+            copies[-1].start()
+    for copy in copies:
+        copy.wait()
+    both = starts[...].astype(f32)
+    start_ref[...] = both[:, :own_users] + both[:, own_users:]
+    gram = lax.dot_general(
         items[...], items[...], (((1,), (1,)), ((), ())), preferred_element_type=f32
     )
+    out_ref[...] = gram
+    pack(pack_ref, gram)
+
+
+def add_kernel(gram_ref, arrived_ref, out_ref, pack_ref):
+    extra = pack_ref.shape[0]
+    total = gram_ref[...] + unpack(arrived_ref[arrived_ref.shape[0] - extra :])
+    out_ref[...] = total
+    pack(pack_ref, total)
 
 
 def load(p_hl, vector):
@@ -138,59 +196,66 @@
     add(groups - 1, collect(groups - 1))
 
 
-def put(column, ref, vector):
-    n_cols, piece_width, _ = ref.shape
+def put(column, ref, vector, part=0):
+    n_cols, rows, _ = ref.shape
     turned = vector.T
+    width = turned.shape[0] // n_cols
     for m in range(n_cols):
-        ref[column ^ m] = turned[m * piece_width : (m + 1) * piece_width]
-
-
-def start_kernel(n_cols, slot_ref, user_ref, info_ref, gram_ref, mask, *refs):
-    n_pieces = len(refs) - 8
-    x_pieces, pieces = refs[:n_cols], refs[n_cols:n_pieces]
-    sent_ref, field_ref, y, x, p_hl, acc, held, sems = refs[n_pieces:]
+        ref[column ^ m, part * width : (part + 1) * width] = turned[m * width : (m + 1) * width]
+
+
+def start_kernel(
+    n_cols, slots, extra, slot_ref, user_ref, info_ref, x_ref, gram_ref, mask, *refs
+):
+    pieces = refs[: 2 * len(slots)]
+    sent_ref, field_ref, gram_out, y, tail, p_hl, acc, held, sems = refs[2 * len(slots) :]
     piece_width = y.shape[1] // n_cols
     column = info_ref[1]
     copies = []
     base = 0
-    for k in range(0, len(pieces), 2):
-        own, other = pieces[k], pieces[k + 1]
-        slots = other.shape[0] // 2
+    for k, count in enumerate(slots):
         for m in range(n_cols):
             place = pl.multiple_of((column ^ m) * piece_width, piece_width)
-            source = (other if m % 2 else own).at[pl.ds(m // 2 * slots, slots)]
+            source = pieces[2 * k + m % 2].at[pl.ds(m // 2 * count, count)]
             copies.append(
                 pltpu.make_async_copy(
                     source,
-                    y.at[pl.ds(base, slots), pl.ds(place, piece_width), :],
+                    y.at[pl.ds(base, count), pl.ds(place, piece_width), :],
                     sems.at[len(copies)],
                 )
             )
-        base += slots
+        base += count
+    if extra:
+        blocks = pieces[-1].shape[0]
+        copies.append(
+            pltpu.make_async_copy(
+                pieces[-1].at[pl.ds(blocks - extra, extra)], tail, sems.at[len(copies)]
+            )
+        )
     for copy in copies:
         copy.start()
-    for m, piece in enumerate(x_pieces):
-        x[pl.ds(pl.multiple_of((column ^ m) * piece_width, piece_width), piece_width), :] = piece[...]
-    start = x[...].T
+    start = x_ref[...].T
     load(p_hl, start)
-    rest = dense(p_hl, gram_ref, start)
     for copy in copies:
         copy.wait()
+    gram = gram_ref[...]
+    if extra:
+        gram = gram + unpack(tail)
+    gram_out[...] = gram
     sparse(True, slot_ref, user_ref, y, mask, p_hl, acc, held)
-    field = acc[...].reshape(start.shape) - rest
+    field = acc[...].reshape(start.shape) - dense(p_hl, gram_out, start)
     field_ref[...] = field
     put(column, sent_ref, field)
 
 
 def first_kernel(
-    slot_ref, user_ref, info_ref, field_ref, gram_ref, y, mask, sent_ref, first_ref, p_hl, acc, held
+    slot_ref, user_ref, info_ref, field_ref, gram_ref, y, mask, first_ref, p_hl, acc, held
 ):
     field = field_ref[...]
     load(p_hl, field)
     sparse(False, slot_ref, user_ref, y, mask, p_hl, acc, held)
     first = confidence * acc[...].reshape(field.shape) + dense(p_hl, gram_ref, field)
     first_ref[...] = first
-    put(info_ref[1], sent_ref, first)
 
 
 def second_kernel(
@@ -201,7 +266,8 @@
     load(p_hl, first)
     sparse(False, slot_ref, user_ref, y, mask, p_hl, acc, held)
     second = confidence * acc[...].reshape(field.shape) + dense(p_hl, gram_ref, first)
-    put(info_ref[1], sent_ref, second)
+    put(info_ref[1], sent_ref, first)
+    put(info_ref[1], sent_ref, second, 1)
 
     def total(left, right):
         return jnp.sum(left * right)
@@ -229,11 +295,14 @@
 
 
 def finish_kernel(share, info_ref, dots_ref, x_ref, *refs):
-    n_cols = (len(refs) - 5) // 3
-    x_out, r_out, field_ref, first_ref, second_ref = refs[3 * n_cols :]
-    for v, ref in enumerate((field_ref, first_ref, second_ref)):
-        for m in range(n_cols):
-            ref[info_ref[1] ^ m] = refs[v * n_cols + m][...]
+    n_cols = (len(refs) - 5) // 2
+    x_out, r_out, field_ref, first_ref, second_ref = refs[2 * n_cols :]
+    width = field_ref.shape[1]
+    for m in range(n_cols):
+        place = info_ref[1] ^ m
+        field_ref[place] = refs[m][...]
+        first_ref[place] = refs[n_cols + m][:width]
+        second_ref[place] = refs[n_cols + m][width:]
     dots = dots_ref[...]
 
     def column(j):
@@ -273,11 +342,11 @@
 
 
 def swap(sent):
-    return [sent[0]] + [flip(sent[m], "cols", m) for m in range(1, sent.shape[0])]
-
-
-def after(value, other):
-    return lax.optimization_barrier((value, other))[0]
+    return [sent[0]] + [flip(sent[m], "cols", m) for m in range(1, len(sent))]
+
+
+def after(value, *others):
+    return lax.optimization_barrier((value, *others))[0]
 
 
 def add_all(value):
@@ -305,7 +374,7 @@
     share = side // n_cols
     own_users = users // n_cols
     capacity = max(2, (tile_total + row_devs - 1) // row_devs)
-    direct = row_devs == 8
+    direct = row_devs == 8 and 2 * width == side
     vmem = pl.BlockSpec(memory_space=pltpu.VMEM)
     smem = pl.BlockSpec(memory_space=pltpu.SMEM)
     anywhere = pl.BlockSpec(memory_space=pl.ANY)
@@ -325,9 +394,29 @@
             name=name,
         )
 
-    info = jnp.stack([tile_count[0], column])
+    info = jnp.stack([tile_count[0], column, row])
+    span = item_factors.shape[1] // n_cols
+    sent = call(
+        functools.partial(prepare_kernel, n_cols, side),
+        [jax.ShapeDtypeStruct((col_width, 2 * own_users + span), bf16)] * n_cols,
+        [smem, anywhere, anywhere],
+        "prepare",
+        [
+            pltpu.VMEM(user_factors.shape, f32),
+            pltpu.VMEM((n_cols, col_width, own_users), f32),
+            pltpu.SemaphoreType.DMA((n_cols + 1,)),
+        ],
+        10**9,
+    )(
+        info,
+        pltpu.with_memory_space_constraint(user_factors, pltpu.HBM),
+        pltpu.with_memory_space_constraint(item_factors, pltpu.HBM),
+    )
+    shared = swap(sent)
+
     order = jnp.arange(tile_total, dtype=jnp.int32)
     live = (order < tile_count[0]).astype(jnp.int32)
+    tile_item = after(tile_item, sent[0])
     holder = tile_item // item_blocks
     local_block = tile_item % item_blocks
     earlier = (
@@ -336,65 +425,93 @@
         & (live[None, :] > 0)
     )
     rank = jnp.sum(earlier.astype(jnp.int32), axis=1)
-    near = row if direct else 0
-    places = (holder ^ near) * capacity + jnp.minimum(rank, capacity - 1)
+    slot_ids = jnp.minimum(holder * capacity + rank, row_devs * capacity - 1)
     slot_range = jnp.arange(row_devs * capacity, dtype=jnp.int32)
-    hits = ((places[None, :] == slot_range[:, None]) & (live[None, :] > 0)).astype(jnp.int32)
+    hits = ((slot_ids[None, :] == slot_range[:, None]) & (live[None, :] > 0)).astype(jnp.int32)
     requests = (jnp.sum(hits * (local_block + 1)[None, :], axis=1) - 1).reshape(row_devs, capacity)
+    wanted = lax.all_to_all(requests, "rows", split_axis=0, concat_axis=0, tiled=True)
+    block = holder
+    if direct:
+        step = holder ^ row
+        block = step
+        for j, spot in ((1, 1), (3, 2), (2, 3), (5, 4), (6, 5), (7, 6), (4, 7)):
+            block = jnp.where(step == j, spot, block)
+    places = block * capacity + jnp.minimum(rank, capacity - 1)
     places = jnp.where(live > 0, places, places[0])
     tile_users = jnp.where(live > 0, tile_user, tile_user[0])
+
+    picked = call(
+        functools.partial(pick_kernel, direct),
+        [jax.ShapeDtypeStruct((capacity, col_width, side), bf16)] * row_devs
+        if direct
+        else [jax.ShapeDtypeStruct((row_devs * capacity, col_width, side), bf16)],
+        [smem, smem, vmem],
+        "pick",
+        flops=10**9,
+    )(after(info, *shared), wanted, item_factors)
+
+    def join(*arrays):
+        return jnp.concatenate(arrays, axis=0)
+
+    def add(gram, arrived):
+        return call(add_kernel, [square, packed], [vmem] * 2, "add")(gram, arrived)
+
+    got = {0: picked[0]}
     if direct:
-        wanted = [flip(requests[j], "rows", j) if j else requests[j] for j in range(row_devs)]
-    else:
-        wanted = [lax.all_to_all(requests, "rows", split_axis=0, concat_axis=0, tiled=True).reshape(-1)]
-
-    span = item_factors.shape[1] // n_cols
-    sent = jax.ShapeDtypeStruct((n_cols, col_width, own_users), f32)
+        for j, ready in ((1, None), (3, None), (2, None), (5, None), (6, None), (7, 3), (4, 5)):
+            message = picked[j] if ready is None else after(picked[j], got[ready])
+            got[j] = flip(message, "rows", j)
+
     strengths = jax.ShapeDtypeStruct((tile_total, share, side), bf16)
-    start, own_items, mask = call(
-        prepare_kernel,
-        [sent, jax.ShapeDtypeStruct((n_cols, col_width, span), bf16), strengths],
-        [smem, vmem, vmem, pl.BlockSpec(memory_space=pltpu.HBM)],
-        "prepare",
+    (mask,) = call(
+        mask_kernel,
+        [strengths],
+        [smem, anywhere],
+        "mask",
         [pltpu.SemaphoreType.DMA],
         10**9,
-    )(info, user_factors, item_factors, tile_mask)
-    own_items = swap(own_items)
-    start = swap(start)
-
-    picked = call(
-        functools.partial(pick_kernel, side),
-        [jax.ShapeDtypeStruct((len(value), col_width, side), bf16) for value in wanted],
-        [vmem] + [smem] * len(wanted),
-        "pick",
-        flops=10**9,
-    )(item_factors, *wanted)
+    )(
+        after(info, got[1] if direct else picked[0]),
+        pltpu.with_memory_space_constraint(tile_mask, pltpu.HBM),
+    )
+    square = jax.ShapeDtypeStruct((width, width), f32)
+    extra = width // col_width
+    packed = jax.ShapeDtypeStruct((extra, col_width, 2 * width), bf16)
+    gram, carried, start = call(
+        functools.partial(gram_kernel, own_users),
+        [square, packed, jax.ShapeDtypeStruct((width, own_users), f32)],
+        [smem] + [anywhere] * n_cols,
+        "gram",
+        [
+            pltpu.VMEM((width, 2 * own_users), bf16),
+            pltpu.VMEM((width, span), bf16),
+            pltpu.SemaphoreType.DMA((2 * n_cols,)),
+        ],
+        10**9,
+    )(after(info, got[1] if direct else picked[0]), *shared)
     if direct:
-        far = [flip(picked[j], "rows", j) for j in (4, 5)]
-        close = [flip(picked[j], "rows", j) for j in (1, 2, 3)]
-        last = [flip(after(picked[j + 2], far[j - 4]), "rows", j + 2) for j in (4, 5)]
-        groups = [[picked[0]], close, far, last]
-        groups = [jnp.concatenate(group, axis=0) for group in groups]
+        slots = (3 * capacity, 3 * capacity, 2 * capacity)
+        pieces = []
+        for group in ((0, 1, 3), (2, 5, 6)):
+            own = join(*[got[j] for j in group])
+            own = after(own, got[6], *pieces[:1])
+            own = join(own, flip(own, "cols", 2))
+            pieces += [own, flip(own, "cols", 1)]
+        carried = after(carried, got[7])
+        for bit in (1, 2, 4):
+            gram, carried = add(gram, flip(carried, "rows", bit))
+        own = join(got[7], got[4])
+        arrived = flip(join(own, carried), "cols", 2)
+        gram, carried = add(gram, arrived)
+        own = join(own, arrived[: 2 * capacity], carried)
+        pieces += [own, flip(own, "cols", 1)]
     else:
-        groups = [lax.all_to_all(picked[0], "rows", split_axis=0, concat_axis=0, tiled=True)]
-    pieces = []
-    for own in groups:
-        bit = n_cols // 2
-        while bit > 1:
-            own = jnp.concatenate([own, flip(own, "cols", bit)], axis=0)
-            bit //= 2
-        pieces += [own, flip(own, "cols", 1)]
-
-    square = jax.ShapeDtypeStruct((width, width), f32)
-    gram = call(
-        gram_kernel,
-        square,
-        [smem] + [vmem] * n_cols,
-        "gram",
-        [pltpu.VMEM((width, span), bf16)],
-        10**9,
-    )(info, *own_items)
-    gram = add_all(gram)
+        slots = (row_devs * capacity,)
+        extra = 0
+        gram = add_all(gram)
+        own = lax.all_to_all(picked[0], "rows", split_axis=0, concat_axis=0, tiled=True)
+        own = join(own, flip(own, "cols", 2))
+        pieces = [own, flip(own, "cols", 1)]
 
     vector = jax.ShapeDtypeStruct((own_users, width), f32)
     held = jax.ShapeDtypeStruct((row_devs * capacity, width, side), bf16)
@@ -404,36 +521,46 @@
         pltpu.VMEM((2, UNROLL, 2 * share, side), bf16),
     ]
     lists = (places, tile_users, info)
-    field_sent, field, y = call(
-        functools.partial(start_kernel, n_cols),
-        [sent, vector, held],
-        [smem] * 3 + [vmem] * (2 + n_cols) + [anywhere] * len(pieces),
+    field_sent, field, gram, y = call(
+        functools.partial(start_kernel, n_cols, slots, extra),
+        [
+            jax.ShapeDtypeStruct((n_cols, col_width, own_users), f32),
+            vector,
+            square,
+            held,
+        ],
+        [smem] * 3 + [vmem] * 3 + [anywhere] * len(pieces),
         "start",
-        [pltpu.VMEM((width, own_users), f32)]
+        [pltpu.VMEM(packed.shape, bf16)]
         + work
-        + [pltpu.SemaphoreType.DMA((n_cols * len(groups),))],
+        + [pltpu.SemaphoreType.DMA((n_cols * len(slots) + 1,))],
         8 * 10**9,
-    )(*lists, gram, mask, *start, *pieces)
-    first_sent, first = call(
-        first_kernel, [sent, vector], [smem] * 3 + [vmem] * 4, "first", work, 8 * 10**9
+    )(*lists, start, gram, mask, *pieces)
+    (first,) = call(
+        first_kernel, [vector], [smem] * 3 + [vmem] * 4, "first", work, 8 * 10**9
     )(*lists, field, gram, y, mask)
+    turned = swap(field_sent)
+    field = after(field, *turned)
     second_sent, dots = call(
         second_kernel,
-        [sent, jax.ShapeDtypeStruct((devices, 128), f32)],
+        [
+            jax.ShapeDtypeStruct((n_cols, 2 * col_width, own_users), f32),
+            jax.ShapeDtypeStruct((devices, 128), f32),
+        ],
         [smem] * 3 + [vmem] * 5,
         "second",
         work,
         8 * 10**9,
     )(*lists, field, first, gram, y, mask)
 
-    turned = swap(field_sent) + swap(first_sent) + swap(second_sent)
+    turned += swap(second_sent)
     dots = lax.all_to_all(dots, ("rows", "cols"), split_axis=0, concat_axis=0, tiled=True)
     result = jax.ShapeDtypeStruct((col_width, users), f32)
     return tuple(
         call(
             functools.partial(finish_kernel, share),
             [result, result],
-            [smem] + [vmem] * (2 + 3 * n_cols),
+            [smem] + [vmem] * (2 + 2 * n_cols),
             "finish",
             [pltpu.VMEM((n_cols, col_width, own_users), f32)] * 3,
             10**9,

time: 131 us -> 106 us (0.81)
  starting transfers between devices: 45.6 us -> 32.6 us
  waiting for transfers between devices: 44.8 us -> 32.6 us
  local copies, waits for them, and re-layouts: 6.77 us -> 1.93 us
  Pallas kernels: 21.5 us -> 24.2 us
  blocking collectives: 9.95 us -> 11.9 us
    ppermute x42 -> x25, starting transfers between devices: 45.6 us -> 26.5 us  [flip(): return lax.ppermute(value, axis, [(i, i ^ bit) for i in range(size)])]
    ppermute x42 -> x25, waiting for transfers between devices: 44.8 us -> 27.9 us  [flip(): return lax.ppermute(value, axis, [(i, i ^ bit) for i in range(size)])]
    all_to_all x0 -> x1, starting transfers between devices: none -> 6.07 us  [on_device(): lax.all_to_all(requests, 'rows', split_axis=0, concat_axis=0, tiled=True)]
    all_to_all x0 -> x1, waiting for transfers between devices: none -> 4.76 us  [on_device(): lax.all_to_all(requests, 'rows', split_axis=0, concat_axis=0, tiled=True)]
    unnamed x22 -> x8, local copies, waits for them, and re-layouts: 5.78 us -> 1.11 us
    pallas_call x6 -> x11, Pallas kernels: 19.5 us -> 22.1 us  [the longest x1 5.89 us: on_device(): call(functools.partial(start_kernel, n_cols, slots, extra), [jax.ShapeDty...]
    all_to_all x1, blocking collectives: 9.95 us -> 11.9 us  [on_device(): lax.all_to_all(dots, ('rows', 'cols'), split_axis=0, concat_axis=0, tiled...]
  transfers between devices with their start and end apart: 42 -> 26, of which waited for: 16 -> 9; matrix products, arithmetic and copies ran while one was open for 1% -> 2% of each run, Pallas kernels for 9% -> 8%
where the time goes in v2:
time: 106 us
  starting transfers between devices  32.6 us (31%)
  waiting for transfers between devices  32.6 us (31%)
  Pallas kernels  24.2 us (23%)
  blocking collectives  11.9 us (11%)
  local copies, waits for them, and re-layouts  1.93 us (2%)
  between operations  1.61 us (2%)
  other arithmetic  1.32 us (1%)
    ppermute x25, waiting for transfers between devices, flip(): return lax.ppermute(value, axis, [(i, i ^ bit) for i in range(size)])  27.9 us
    ppermute x25, starting transfers between devices, flip(): return lax.ppermute(value, axis, [(i, i ^ bit) for i in range(size)])  26.5 us
    all_to_all x1, blocking collectives, on_device(): lax.all_to_all(dots, ('rows', 'cols'), split_axis=0, concat_axis=0, tiled...  11.9 us
    all_to_all x1, starting transfers between devices, on_device(): lax.all_to_all(requests, 'rows', split_axis=0, concat_axis=0, tiled=True)  6.07 us
    pallas_call x1, Pallas kernels, on_device(): call(functools.partial(start_kernel, n_cols, slots, extra), [jax.ShapeDty...  5.89 us
    pallas_call x1, Pallas kernels, on_device(): call(second_kernel, [jax.ShapeDtypeStruct((n_cols, 2 * col_width, own_use...  5.22 us
    pallas_call x1, Pallas kernels, on_device(): call(first_kernel, [vector], [smem] * 3 + [vmem] * 4, 'first', work, 8 *...  4.96 us
    all_to_all x1, waiting for transfers between devices, on_device(): lax.all_to_all(requests, 'rows', split_axis=0, concat_axis=0, tiled=True)  4.76 us
  transfers between devices with their start and end apart: 26, of which 9 were waited for; matrix products, arithmetic and copies ran while one was open for 2% of the time, Pallas kernels for 8%

profile of v2, /device:TPU:0, one launch (start us, length us, event | category | flops | bytes accessed | tf_op | source)
XLA Modules:
  0.0 106.1 jit_solution(10490589070577757298)
XLA Ops:
  1.4 1.7 %prepare.1 = (bf16[32,3072]{1,0:T(8,128)(2,1)S(1)}, bf16[32,3072]{1,0:T(8,128)(2,1)S(1)}, bf16[32,3072]{1,0:T(8,128)(2,1)S(1)}, bf16[32,3072]{1,0:T(8,128)(2,1)S(1)}) custom-call(s32[3]{0:T(128)S(1)} %pad_add_fusion.info_ref, f32[32,2048]{1,0:T(8,128)} %x_ref.1, bf16[32,8192]{1,0:T(8,128)(2,1)} %items_ref.1), custom_call_target="tpu_custom_call" | custom-call | flops 1000000000 | tf_op jit(solution)/shard_map/prepare/pallas_call | solution.py:399
  3.6 2.6 %collective-permute-start.1 = (bf16[32,3072]{1,0:T(8,128)(2,1)S(1)}, bf16[32,3072]{1,0:T(8,128)(2,1)S(1)}, u32[]{:S(2)}, u32[]{:S(2)}) collective-permute-start(bf16[32,3072]{1,0:T(8,128)(2,1)S(1)} %get-tuple-element.43), channel_id=1, source_target_pairs={{0,2},{1,3},{2,0},{3,1},{4,6},{5,7},{6,4},{7,5},{8,10},{9,11},{10,... | collective-permute-start | bytes 589832 | tf_op jit(solution)/shard_map/ppermute | solution.py:341
  7.9 6.1 %all-to-all-start = ((s32[8,1,9]{2,1,0:T(1,128)}), s32[8,1,9]{2,1,0:T(1,128)S(1)}, u32[]{:S(2)}, u32[]{:S(2)}) async-start(s32[8,1,9]{2,1,0:T(1,128)} %bitcast.5), calls=%async_computation | async-start | bytes 8192 | tf_op jit(solution)/shard_map/all_to_all | solution.py:432
  14.0 1.6 %collective-permute-done.2.refs_3_ = bf16[32,3072]{1,0:T(8,128)(2,1)S(1)} collective-permute-done((bf16[32,3072]{1,0:T(8,128)(2,1)S(1)}, bf16[32,3072]{1,0:T(8,128)(2,1)S(1)}, u32[]{:S(2)}, u32[]{:S(2)}) %collective-permute-start.2) | collective-permute-done | bytes 196640 | tf_op jit(solution)/shard_map/ppermute | solution.py:341
  15.6 4.8 %all-to-all-done = s32[8,1,9]{2,1,0:T(1,128)S(1)} async-done(((s32[8,1,9]{2,1,0:T(1,128)}), s32[8,1,9]{2,1,0:T(1,128)S(1)}, u32[]{:S(2)}, u32[]{:S(2)}) %all-to-all-start) | async-done | bytes 320 | tf_op jit(solution)/shard_map/all_to_all | solution.py:432
  24.3 1.5 %collective-permute-start.12 = (bf16[9,32,256]{2,1,0:T(8,128)(2,1)S(1)}, bf16[9,32,256]{2,1,0:T(8,128)(2,1)S(1)}, u32[]{:S(2)}, u32[]{:S(2)}) collective-permute-start(bf16[9,32,256]{2,1,0:T(8,128)(2,1)S(1)} %get-tuple-element.66), channel_id=1, source_target_pairs={{0,24},{4,28},{8,16},{12,20},{16,8},{20,12},{24,0},{28,4},{1,25},{... | collective-permute-start | bytes 442376 | tf_op jit(solution)/shard_map/ppermute | solution.py:341
  25.8 3.8 %collective-permute-done.3 = bf16[9,32,256]{2,1,0:T(8,128)(2,1)S(1)} collective-permute-done((bf16[9,32,256]{2,1,0:T(8,128)(2,1)S(1)}, bf16[9,32,256]{2,1,0:T(8,128)(2,1)S(1)}, u32[]{:S(2)}, u32[]{:S(2)}) %collective-permute-start.3) | collective-permute-done | bytes 147488 | tf_op jit(solution)/shard_map/ppermute | solution.py:341
  29.6 2.3 %collective-permute-done.4 = bf16[9,32,256]{2,1,0:T(8,128)(2,1)S(1)} collective-permute-done((bf16[9,32,256]{2,1,0:T(8,128)(2,1)S(1)}, bf16[9,32,256]{2,1,0:T(8,128)(2,1)S(1)}, u32[]{:S(2)}, u32[]{:S(2)}) %collective-permute-start.4) | collective-permute-done | bytes 147488 | tf_op jit(solution)/shard_map/ppermute | solution.py:341
  32.0 1.6 %collective-permute-start.13 = (bf16[27,32,256]{2,1,0:T(8,128)(2,1)S(1)}, bf16[27,32,256]{2,1,0:T(8,128)(2,1)S(1)}, u32[]{:S(2)}, u32[]{:S(2)}) collective-permute-start(bf16[27,32,256]{2,1,0:T(8,128)(2,1)S(1)} %pad_maximum_fusion.1), channel_id=1, source_target_pairs={{0,2},{1,3},{2,0},{3,1},{4,6},{5,7},{6,4},{7,5},{8,10},{9,11},{10,... | collective-permute-start | bytes 1327112 | tf_op jit(solution)/shard_map/ppermute | solution.py:341
  35.9 3.0 %collective-permute-start.5 = (bf16[9,32,256]{2,1,0:T(8,128)(2,1)S(1)}, bf16[9,32,256]{2,1,0:T(8,128)(2,1)S(1)}, u32[]{:S(2)}, u32[]{:S(2)}) collective-permute-start(bf16[9,32,256]{2,1,0:T(8,128)(2,1)S(1)} %get-tuple-element.53), channel_id=1, source_target_pairs={{0,28},{4,24},{8,20},{12,16},{16,12},{20,8},{24,4},{28,0},{1,29},{... | collective-permute-start | bytes 442376 | tf_op jit(solution)/shard_map/ppermute | solution.py:341
  40.2 5.4 %collective-permute-done.9 = bf16[9,32,256]{2,1,0:T(8,128)(2,1)S(1)} collective-permute-done((bf16[9,32,256]{2,1,0:T(8,128)(2,1)S(1)}, bf16[9,32,256]{2,1,0:T(8,128)(2,1)S(1)}, u32[]{:S(2)}, u32[]{:S(2)}) %collective-permute-start.9) | collective-permute-done | bytes 147488 | tf_op jit(solution)/shard_map/ppermute | solution.py:341
  46.9 2.7 %collective-permute-start.10 = (bf16[9,32,256]{2,1,0:T(8,128)(2,1)S(1)}, bf16[9,32,256]{2,1,0:T(8,128)(2,1)S(1)}, u32[]{:S(2)}, u32[]{:S(2)}) collective-permute-start(bf16[9,32,256]{2,1,0:T(8,128)(2,1)S(1)} %get-tuple-element.62), channel_id=1, source_target_pairs={{0,16},{4,20},{8,24},{12,28},{16,0},{20,4},{24,8},{28,12},{1,17},{... | collective-permute-start | bytes 442376 | tf_op jit(solution)/shard_map/ppermute | solution.py:341
  50.0 3.5 %collective-permute-start.7 = (bf16[4,32,256]{2,1,0:T(8,128)(2,1)S(1)}, bf16[4,32,256]{2,1,0:T(8,128)(2,1)S(1)}, u32[]{:S(2)}, u32[]{:S(2)}) collective-permute-start(bf16[4,32,256]{2,1,0:T(8,128)(2,1)S(1)} %get-tuple-element.56), channel_id=1, source_target_pairs={{0,8},{4,12},{8,0},{12,4},{16,24},{20,28},{24,16},{28,20},{1,9},{5... | collective-permute-start | bytes 196616 | tf_op jit(solution)/shard_map/ppermute | solution.py:341
  53.5 2.7 %collective-permute-done.7.arrived_ref = bf16[4,32,256]{2,1,0:T(8,128)(2,1)S(1)} collective-permute-done((bf16[4,32,256]{2,1,0:T(8,128)(2,1)S(1)}, bf16[4,32,256]{2,1,0:T(8,128)(2,1)S(1)}, u32[]{:S(2)}, u32[]{:S(2)}) %collective-permute-start.7) | collective-permute-done | bytes 65568 | tf_op jit(solution)/shard_map/ppermute | solution.py:341
  56.5 5.0 %collective-permute-done.8.arrived_ref = bf16[4,32,256]{2,1,0:T(8,128)(2,1)S(1)} collective-permute-done((bf16[4,32,256]{2,1,0:T(8,128)(2,1)S(1)}, bf16[4,32,256]{2,1,0:T(8,128)(2,1)S(1)}, u32[]{:S(2)}, u32[]{:S(2)}) %collective-permute-start.8) | collective-permute-done | bytes 65568 | tf_op jit(solution)/shard_map/ppermute | solution.py:341
  62.4 6.7 %collective-permute-done.11.arrived_ref = bf16[22,32,256]{2,1,0:T(8,128)(2,1)S(1)} collective-permute-done((bf16[22,32,256]{2,1,0:T(8,128)(2,1)S(1)}, bf16[22,32,256]{2,1,0:T(8,128)(2,1)S(1)}, u32[]{:S(2)}, u32[]{:S(2)}) %collective-permute-start.11) | collective-permute-done | bytes 360480 | tf_op jit(solution)/shard_map/ppermute | solution.py:341
  69.3 2.2 %mask.1 = bf16[72,64,256]{2,1,0:T(8,128)(2,1)S(1)} custom-call(s32[3]{0:T(128)S(1)} %pad_add_fusion.info_ref, bf16[72,256,256]{2,1,0:T(8,128)(2,1)} %mask_hbm.1), custom_call_target="tpu_custom_call" | custom-call | flops 1000000000 | tf_op jit(solution)/shard_map/mask/pallas_call | solution.py:466
  71.6 5.9 %start.1 = (f32[4,32,512]{2,1,0:T(8,128)S(1)}, f32[512,128]{1,0:T(8,128)S(1)}, f32[128,128]{1,0:T(8,128)S(1)}, bf16[72,128,256]{2,1,0:T(8,128)(2,1)S(1)}) custom-call(s32[72]{0:T(128)S(1)} %get-tuple-element.91.slot_ref, s32[72]{0:T(128)S(1)} %get-tuple-element.90.user_ref, s32[3]{0:T(128)S(1)} %pad_add_fusion.info_ref, ...), custom_call_target="tpu_custom_call" | custom-call | flops 8000000000 | tf_op jit(solution)/shard_map/start/pallas_call | solution.py:524
  77.7 2.0 %collective-permute-start.20 = (f32[32,512]{1,0:T(8,128)S(1)}, f32[32,512]{1,0:T(8,128)S(1)}, u32[]{:S(2)}, u32[]{:S(2)}) collective-permute-start(f32[32,512]{1,0:T(8,128)S(1)} %get-tuple-element.83), channel_id=1, source_target_pairs={{0,2},{1,3},{2,0},{3,1},{4,6},{5,7},{6,4},{7,5},{8,10},{9,11},{10,... | collective-permute-start | bytes 196616 | tf_op jit(solution)/shard_map/ppermute | solution.py:341
  79.7 5.0 %first.1.first_ref = f32[512,128]{1,0:T(8,128)S(1)} custom-call(s32[72]{0:T(128)S(1)} %get-tuple-element.91.slot_ref, s32[72]{0:T(128)S(1)} %get-tuple-element.90.user_ref, s32[3]{0:T(128)S(1)} %pad_add_fusion.info_ref, f32[512,128]{1,0:T(8,128)S(1)} %get-tuple-element.73.field_ref, f32[128,128]{1,0:T(8,128)S(1)} %get-tuple-element.74.gram_ref, ...), custom_call_target="tpu_custom_call" | custom-call | flops 8000000000 | tf_op jit(solution)/shard_map/first/pallas_call | solution.py:539
  84.8 5.2 %second.1 = (f32[4,64,512]{2,1,0:T(8,128)S(1)}, f32[32,128]{1,0:T(8,128)S(1)}) custom-call(s32[72]{0:T(128)S(1)} %get-tuple-element.91.slot_ref, s32[72]{0:T(128)S(1)} %get-tuple-element.90.user_ref, s32[3]{0:T(128)S(1)} %pad_add_fusion.info_ref, f32[512,128]{1,0:T(8,128)S(1)} %get-tuple-element.73.field_ref, f32[512,128]{1,0:T(8,128)S(1)} %first.1.first_ref, ...), custom_call_target="tpu_custom_call" | custom-call | flops 8000000000 | tf_op jit(solution)/shard_map/second/pallas_call | solution.py:544
  90.2 2.0 %collective-permute-start.23 = (f32[64,512]{1,0:T(8,128)S(1)}, f32[64,512]{1,0:T(8,128)S(1)}, u32[]{:S(2)}, u32[]{:S(2)}) collective-permute-start(f32[64,512]{1,0:T(8,128)S(1)} %get-tuple-element.79), channel_id=1, source_target_pairs={{0,2},{1,3},{2,0},{3,1},{4,6},{5,7},{6,4},{7,5},{8,10},{9,11},{10,... | collective-permute-start | bytes 393224 | tf_op jit(solution)/shard_map/ppermute | solution.py:341
  92.2 11.9 %all_to_all.19 = f32[32,1,128]{2,1,0:T(1,128)S(1)} all-to-all(f32[32,1,128]{2,1,0:T(1,128)S(1)} %bitcast.31), channel_id=1, replica_groups=mesh['rows'=8,'cols'=4] {'rows','cols'}, dimensions={0} | all-to-all | bytes 32768 | tf_op jit(solution)/shard_map/all_to_all | solution.py:557
  104.1 2.0 %finish.1 = (f32[32,2048]{1,0:T(8,128)}, f32[32,2048]{1,0:T(8,128)}) custom-call(s32[3]{0:T(128)S(1)} %pad_add_fusion.info_ref, f32[32,128]{1,0:T(8,128)S(1)} %bitcast.32, f32[32,2048]{1,0:T(8,128)S(1)} %copy-done.1, f32[32,512]{1,0:T(8,128)S(1)} %get-tuple-element.85.refs_0_, f32[32,512]{1,0:T(8,128)S(1)} %collective-permute-done.19.refs_1_, ...), custom_call_target="tpu_custom_call" | custom-call | flops 1000000000 | tf_op jit(solution)/shard_map/finish/pallas_call | solution.py:560
  (67 shorter events, 13.4 us)
Async XLA Ops:
  3.1 10.9 %collective-permute-start = (bf16[32,3072]{1,0:T(8,128)(2,1)S(1)}, bf16[32,3072]{1,0:T(8,128)(2,1)S(1)}, u32[]{:S(2)}, u32[]{:S(2)}) collective-permute-start(bf16[32,3072]{1,0:T(8,128)(2,1)S(1)} %get-tuple-element.42), channel_id=1, source_target_pairs={{0,1},{1,0},{2,3},{3,2},{4,5},{5,4},{6,7},{7,6},{8,9},{9,8},{10,11... | collective-permute-start | bytes 589832 | tf_op jit(solution)/shard_map/ppermute | solution.py:341
  3.6 10.4 %collective-permute-start.1 = (bf16[32,3072]{1,0:T(8,128)(2,1)S(1)}, bf16[32,3072]{1,0:T(8,128)(2,1)S(1)}, u32[]{:S(2)}, u32[]{:S(2)}) collective-permute-start(bf16[32,3072]{1,0:T(8,128)(2,1)S(1)} %get-tuple-element.43), channel_id=1, source_target_pairs={{0,2},{1,3},{2,0},{3,1},{4,6},{5,7},{6,4},{7,5},{8,10},{9,11},{10,... | collective-permute-start | bytes 589832 | tf_op jit(solution)/shard_map/ppermute | solution.py:341
  6.2 9.4 %collective-permute-start.2 = (bf16[32,3072]{1,0:T(8,128)(2,1)S(1)}, bf16[32,3072]{1,0:T(8,128)(2,1)S(1)}, u32[]{:S(2)}, u32[]{:S(2)}) collective-permute-start(bf16[32,3072]{1,0:T(8,128)(2,1)S(1)} %get-tuple-element.44), channel_id=1, source_target_pairs={{0,3},{1,2},{2,1},{3,0},{4,7},{5,6},{6,5},{7,4},{8,11},{9,10},{10,... | collective-permute-start | bytes 589832 | tf_op jit(solution)/shard_map/ppermute | solution.py:341
  7.9 12.5 %all-to-all-start = ((s32[8,1,9]{2,1,0:T(1,128)}), s32[8,1,9]{2,1,0:T(1,128)S(1)}, u32[]{:S(2)}, u32[]{:S(2)}) async-start(s32[8,1,9]{2,1,0:T(1,128)} %bitcast.5), calls=%async_computation | async-start | bytes 8192 | tf_op jit(solution)/shard_map/all_to_all | solution.py:432
  22.2 7.4 %collective-permute-start.3 = (bf16[9,32,256]{2,1,0:T(8,128)(2,1)S(1)}, bf16[9,32,256]{2,1,0:T(8,128)(2,1)S(1)}, u32[]{:S(2)}, u32[]{:S(2)}) collective-permute-start(bf16[9,32,256]{2,1,0:T(8,128)(2,1)S(1)} %get-tuple-element.46), channel_id=1, source_target_pairs={{0,4},{4,0},{8,12},{12,8},{16,20},{20,16},{24,28},{28,24},{1,5},{5... | collective-permute-start | bytes 442376 | tf_op jit(solution)/shard_map/ppermute | solution.py:341
  22.8 9.1 %collective-permute-start.4 = (bf16[9,32,256]{2,1,0:T(8,128)(2,1)S(1)}, bf16[9,32,256]{2,1,0:T(8,128)(2,1)S(1)}, u32[]{:S(2)}, u32[]{:S(2)}) collective-permute-start(bf16[9,32,256]{2,1,0:T(8,128)(2,1)S(1)} %get-tuple-element.52), channel_id=1, source_target_pairs={{0,12},{4,8},{8,4},{12,0},{16,28},{20,24},{24,20},{28,16},{1,13},{... | collective-permute-start | bytes 442376 | tf_op jit(solution)/shard_map/ppermute | solution.py:341
  24.3 7.7 %collective-permute-start.12 = (bf16[9,32,256]{2,1,0:T(8,128)(2,1)S(1)}, bf16[9,32,256]{2,1,0:T(8,128)(2,1)S(1)}, u32[]{:S(2)}, u32[]{:S(2)}) collective-permute-start(bf16[9,32,256]{2,1,0:T(8,128)(2,1)S(1)} %get-tuple-element.66), channel_id=1, source_target_pairs={{0,24},{4,28},{8,16},{12,20},{16,8},{20,12},{24,0},{28,4},{1,25},{... | collective-permute-start | bytes 442376 | tf_op jit(solution)/shard_map/ppermute | solution.py:341
  32.0 14.3 %collective-permute-start.13 = (bf16[27,32,256]{2,1,0:T(8,128)(2,1)S(1)}, bf16[27,32,256]{2,1,0:T(8,128)(2,1)S(1)}, u32[]{:S(2)}, u32[]{:S(2)}) collective-permute-start(bf16[27,32,256]{2,1,0:T(8,128)(2,1)S(1)} %pad_maximum_fusion.1), channel_id=1, source_target_pairs={{0,2},{1,3},{2,0},{3,1},{4,6},{5,7},{6,4},{7,5},{8,10},{9,11},{10,... | collective-permute-start | bytes 1327112 | tf_op jit(solution)/shard_map/ppermute | solution.py:341
  33.5 12.0 %collective-permute-start.9 = (bf16[9,32,256]{2,1,0:T(8,128)(2,1)S(1)}, bf16[9,32,256]{2,1,0:T(8,128)(2,1)S(1)}, u32[]{:S(2)}, u32[]{:S(2)}) collective-permute-start(bf16[9,32,256]{2,1,0:T(8,128)(2,1)S(1)} %get-tuple-element.61), channel_id=1, source_target_pairs={{0,20},{4,16},{8,28},{12,24},{16,4},{20,0},{24,12},{28,8},{1,21},{... | collective-permute-start | bytes 442376 | tf_op jit(solution)/shard_map/ppermute | solution.py:341
  34.6 10.9 %collective-permute-start.15 = (bf16[9,32,256]{2,1,0:T(8,128)(2,1)S(1)}, bf16[9,32,256]{2,1,0:T(8,128)(2,1)S(1)}, u32[]{:S(2)}, u32[]{:S(2)}) collective-permute-start(bf16[9,32,256]{2,1,0:T(8,128)(2,1)S(1)} %get-tuple-element.68), channel_id=1, source_target_pairs={{0,8},{4,12},{8,0},{12,4},{16,24},{20,28},{24,16},{28,20},{1,9},{5... | collective-permute-start | bytes 442376 | tf_op jit(solution)/shard_map/ppermute | solution.py:341
  35.9 9.7 %collective-permute-start.5 = (bf16[9,32,256]{2,1,0:T(8,128)(2,1)S(1)}, bf16[9,32,256]{2,1,0:T(8,128)(2,1)S(1)}, u32[]{:S(2)}, u32[]{:S(2)}) collective-permute-start(bf16[9,32,256]{2,1,0:T(8,128)(2,1)S(1)} %get-tuple-element.53), channel_id=1, source_target_pairs={{0,28},{4,24},{8,20},{12,16},{16,12},{20,8},{24,4},{28,0},{1,29},{... | collective-permute-start | bytes 442376 | tf_op jit(solution)/shard_map/ppermute | solution.py:341
  46.3 15.5 %collective-permute-start.16 = (bf16[27,32,256]{2,1,0:T(8,128)(2,1)S(1)}, bf16[27,32,256]{2,1,0:T(8,128)(2,1)S(1)}, u32[]{:S(2)}, u32[]{:S(2)}) collective-permute-start(bf16[27,32,256]{2,1,0:T(8,128)(2,1)S(1)} %pad_maximum_fusion.2), channel_id=1, source_target_pairs={{0,2},{1,3},{2,0},{3,1},{4,6},{5,7},{6,4},{7,5},{8,10},{9,11},{10,... | collective-permute-start | bytes 1327112 | tf_op jit(solution)/shard_map/ppermute | solution.py:341
  46.9 14.6 %collective-permute-start.10 = (bf16[9,32,256]{2,1,0:T(8,128)(2,1)S(1)}, bf16[9,32,256]{2,1,0:T(8,128)(2,1)S(1)}, u32[]{:S(2)}, u32[]{:S(2)}) collective-permute-start(bf16[9,32,256]{2,1,0:T(8,128)(2,1)S(1)} %get-tuple-element.62), channel_id=1, source_target_pairs={{0,16},{4,20},{8,24},{12,28},{16,0},{20,4},{24,8},{28,12},{1,17},{... | collective-permute-start | bytes 442376 | tf_op jit(solution)/shard_map/ppermute | solution.py:341
  50.0 6.3 %collective-permute-start.7 = (bf16[4,32,256]{2,1,0:T(8,128)(2,1)S(1)}, bf16[4,32,256]{2,1,0:T(8,128)(2,1)S(1)}, u32[]{:S(2)}, u32[]{:S(2)}) collective-permute-start(bf16[4,32,256]{2,1,0:T(8,128)(2,1)S(1)} %get-tuple-element.56), channel_id=1, source_target_pairs={{0,8},{4,12},{8,0},{12,4},{16,24},{20,28},{24,16},{28,20},{1,9},{5... | collective-permute-start | bytes 196616 | tf_op jit(solution)/shard_map/ppermute | solution.py:341
  56.2 5.2 %collective-permute-start.8 = (bf16[4,32,256]{2,1,0:T(8,128)(2,1)S(1)}, bf16[4,32,256]{2,1,0:T(8,128)(2,1)S(1)}, u32[]{:S(2)}, u32[]{:S(2)}) collective-permute-start(bf16[4,32,256]{2,1,0:T(8,128)(2,1)S(1)} %get-tuple-element.58), channel_id=1, source_target_pairs={{0,16},{4,20},{8,24},{12,28},{16,0},{20,4},{24,8},{28,12},{1,17},{... | collective-permute-start | bytes 196616 | tf_op jit(solution)/shard_map/ppermute | solution.py:341
  61.6 7.5 %collective-permute-start.11 = (bf16[22,32,256]{2,1,0:T(8,128)(2,1)S(1)}, bf16[22,32,256]{2,1,0:T(8,128)(2,1)S(1)}, u32[]{:S(2)}, u32[]{:S(2)}) collective-permute-start(bf16[22,32,256]{2,1,0:T(8,128)(2,1)S(1)} %pad_maximum_fusion.3), channel_id=1, source_target_pairs={{0,2},{1,3},{2,0},{3,1},{4,6},{5,7},{6,4},{7,5},{8,10},{9,11},{10,... | collective-permute-start | bytes 1081352 | tf_op jit(solution)/shard_map/ppermute | solution.py:341
  61.6 9.9 %collective-permute-start.14 = (bf16[54,32,256]{2,1,0:T(8,128)(2,1)S(1)}, bf16[54,32,256]{2,1,0:T(8,128)(2,1)S(1)}, u32[]{:S(2)}, u32[]{:S(2)}) collective-permute-start(bf16[54,32,256]{2,1,0:T(8,128)(2,1)S(1)} %constant_dynamic-update-slice_fusion.refs_0_), channel_id=1, source_target_pairs={{0,1},{1,0},{2,3},{3,2},{4,5},{5,4},{6,7},{7,6},{8,9},{9,8},{10,11... | collective-permute-start | bytes 2654216 | tf_op jit(solution)/shard_map/ppermute | solution.py:341
  61.8 9.8 %collective-permute-start.17 = (bf16[54,32,256]{2,1,0:T(8,128)(2,1)S(1)}, bf16[54,32,256]{2,1,0:T(8,128)(2,1)S(1)}, u32[]{:S(2)}, u32[]{:S(2)}) collective-permute-start(bf16[54,32,256]{2,1,0:T(8,128)(2,1)S(1)} %constant_dynamic-update-slice_fusion.2.refs_2_), channel_id=1, source_target_pairs={{0,1},{1,0},{2,3},{3,2},{4,5},{5,4},{6,7},{7,6},{8,9},{9,8},{10,11... | collective-permute-start | bytes 2654216 | tf_op jit(solution)/shard_map/ppermute | solution.py:341
  77.5 7.2 %collective-permute-start.21 = (f32[32,512]{1,0:T(8,128)S(1)}, f32[32,512]{1,0:T(8,128)S(1)}, u32[]{:S(2)}, u32[]{:S(2)}) collective-permute-start(f32[32,512]{1,0:T(8,128)S(1)} %get-tuple-element.82), channel_id=1, source_target_pairs={{0,3},{1,2},{2,1},{3,0},{4,7},{5,6},{6,5},{7,4},{8,11},{9,10},{10,... | collective-permute-start | bytes 196616 | tf_op jit(solution)/shard_map/ppermute | solution.py:341
  77.7 7.0 %collective-permute-start.20 = (f32[32,512]{1,0:T(8,128)S(1)}, f32[32,512]{1,0:T(8,128)S(1)}, u32[]{:S(2)}, u32[]{:S(2)}) collective-permute-start(f32[32,512]{1,0:T(8,128)S(1)} %get-tuple-element.83), channel_id=1, source_target_pairs={{0,2},{1,3},{2,0},{3,1},{4,6},{5,7},{6,4},{7,5},{8,10},{9,11},{10,... | collective-permute-start | bytes 196616 | tf_op jit(solution)/shard_map/ppermute | solution.py:341
  79.7 5.0 %collective-permute-start.19 = (f32[32,512]{1,0:T(8,128)S(1)}, f32[32,512]{1,0:T(8,128)S(1)}, u32[]{:S(2)}, u32[]{:S(2)}) collective-permute-start(f32[32,512]{1,0:T(8,128)S(1)} %get-tuple-element.84), channel_id=1, source_target_pairs={{0,1},{1,0},{2,3},{3,2},{4,5},{5,4},{6,7},{7,6},{8,9},{9,8},{10,11... | collective-permute-start | bytes 196616 | tf_op jit(solution)/shard_map/ppermute | solution.py:341
  90.0 14.1 %collective-permute-start.24 = (f32[64,512]{1,0:T(8,128)S(1)}, f32[64,512]{1,0:T(8,128)S(1)}, u32[]{:S(2)}, u32[]{:S(2)}) collective-permute-start(f32[64,512]{1,0:T(8,128)S(1)} %get-tuple-element.78), channel_id=1, source_target_pairs={{0,3},{1,2},{2,1},{3,0},{4,7},{5,6},{6,5},{7,4},{8,11},{9,10},{10,... | collective-permute-start | bytes 393224 | tf_op jit(solution)/shard_map/ppermute | solution.py:341
  90.2 13.8 %collective-permute-start.23 = (f32[64,512]{1,0:T(8,128)S(1)}, f32[64,512]{1,0:T(8,128)S(1)}, u32[]{:S(2)}, u32[]{:S(2)}) collective-permute-start(f32[64,512]{1,0:T(8,128)S(1)} %get-tuple-element.79), channel_id=1, source_target_pairs={{0,2},{1,3},{2,0},{3,1},{4,6},{5,7},{6,4},{7,5},{8,10},{9,11},{10,... | collective-permute-start | bytes 393224 | tf_op jit(solution)/shard_map/ppermute | solution.py:341
  92.2 11.9 %collective-permute-start.22 = (f32[64,512]{1,0:T(8,128)S(1)}, f32[64,512]{1,0:T(8,128)S(1)}, u32[]{:S(2)}, u32[]{:S(2)}) collective-permute-start(f32[64,512]{1,0:T(8,128)S(1)} %get-tuple-element.80), channel_id=1, source_target_pairs={{0,1},{1,0},{2,3},{3,2},{4,5},{5,4},{6,7},{7,6},{8,9},{9,8},{10,11... | collective-permute-start | bytes 393224 | tf_op jit(solution)/shard_map/ppermute | solution.py:341
  (5 other events, 60.5 us)

commit v3 on v2

--- a/solution.py
+++ b/solution.py
@@ -131,6 +131,21 @@
     pack(pack_ref, total)
 
 
+def join_kernel(*refs):
+    sources, out_ref, sems = refs[:-2], refs[-2], refs[-1]
+    copies = []
+    base = 0
+    for source in sources:
+        rows = source.shape[0]
+        copies.append(
+            pltpu.make_async_copy(source, out_ref.at[pl.ds(base, rows)], sems.at[len(copies)])
+        )
+        copies[-1].start()
+        base += rows
+    for copy in copies:
+        copy.wait()
+
+
 def load(p_hl, vector):
     blocks, both, width = p_hl.shape
     share = both // 2
@@ -204,11 +219,9 @@
         ref[column ^ m, part * width : (part + 1) * width] = turned[m * width : (m + 1) * width]
 
 
-def start_kernel(
-    n_cols, slots, extra, slot_ref, user_ref, info_ref, x_ref, gram_ref, mask, *refs
-):
+def start_kernel(n_cols, slots, slot_ref, user_ref, info_ref, x_ref, mask, *refs):
     pieces = refs[: 2 * len(slots)]
-    sent_ref, field_ref, gram_out, y, tail, p_hl, acc, held, sems = refs[2 * len(slots) :]
+    part_ref, y, p_hl, acc, held, sems = refs[2 * len(slots) :]
     piece_width = y.shape[1] // n_cols
     column = info_ref[1]
     copies = []
@@ -225,37 +238,29 @@
                 )
             )
         base += count
-    if extra:
-        blocks = pieces[-1].shape[0]
-        copies.append(
-            pltpu.make_async_copy(
-                pieces[-1].at[pl.ds(blocks - extra, extra)], tail, sems.at[len(copies)]
-            )
-        )
     for copy in copies:
         copy.start()
+    load(p_hl, x_ref[...].T)
+    for copy in copies:
+        copy.wait()
+    sparse(True, slot_ref, user_ref, y, mask, p_hl, acc, held)
+    part_ref[...] = acc[...].reshape(part_ref.shape)
+
+
+def first_kernel(
+    slot_ref, user_ref, info_ref, x_ref, part_ref, gram_ref, y, mask,
+    sent_ref, field_ref, first_ref, p_hl, acc, held,
+):
     start = x_ref[...].T
     load(p_hl, start)
-    for copy in copies:
-        copy.wait()
-    gram = gram_ref[...]
-    if extra:
-        gram = gram + unpack(tail)
-    gram_out[...] = gram
-    sparse(True, slot_ref, user_ref, y, mask, p_hl, acc, held)
-    field = acc[...].reshape(start.shape) - dense(p_hl, gram_out, start)
+    field = part_ref[...] - dense(p_hl, gram_ref, start)
     field_ref[...] = field
-    put(column, sent_ref, field)
-
-
-def first_kernel(
-    slot_ref, user_ref, info_ref, field_ref, gram_ref, y, mask, first_ref, p_hl, acc, held
-):
-    field = field_ref[...]
+    put(info_ref[1], sent_ref, field)
     load(p_hl, field)
     sparse(False, slot_ref, user_ref, y, mask, p_hl, acc, held)
     first = confidence * acc[...].reshape(field.shape) + dense(p_hl, gram_ref, field)
     first_ref[...] = first
+    put(info_ref[1], sent_ref, first, 1)
 
 
 def second_kernel(
@@ -266,8 +271,7 @@
     load(p_hl, first)
     sparse(False, slot_ref, user_ref, y, mask, p_hl, acc, held)
     second = confidence * acc[...].reshape(field.shape) + dense(p_hl, gram_ref, first)
-    put(info_ref[1], sent_ref, first)
-    put(info_ref[1], sent_ref, second, 1)
+    put(info_ref[1], sent_ref, second)
 
     def total(left, right):
         return jnp.sum(left * right)
@@ -300,9 +304,9 @@
     width = field_ref.shape[1]
     for m in range(n_cols):
         place = info_ref[1] ^ m
-        field_ref[place] = refs[m][...]
-        first_ref[place] = refs[n_cols + m][:width]
-        second_ref[place] = refs[n_cols + m][width:]
+        field_ref[place] = refs[m][:width]
+        first_ref[place] = refs[m][width:]
+        second_ref[place] = refs[n_cols + m][...]
     dots = dots_ref[...]
 
     def column(j):
@@ -453,13 +457,24 @@
     def join(*arrays):
         return jnp.concatenate(arrays, axis=0)
 
+    def gather(*arrays):
+        rows = sum(array.shape[0] for array in arrays)
+        return call(
+            join_kernel,
+            [jax.ShapeDtypeStruct((rows, *arrays[0].shape[1:]), bf16)],
+            [anywhere] * len(arrays),
+            "join",
+            [pltpu.SemaphoreType.DMA((len(arrays),))],
+            2 * 10**10,
+        )(*arrays)[0]
+
     def add(gram, arrived):
         return call(add_kernel, [square, packed], [vmem] * 2, "add")(gram, arrived)
 
     got = {0: picked[0]}
     if direct:
-        for j, ready in ((1, None), (3, None), (2, None), (5, None), (6, None), (7, 3), (4, 5)):
-            message = picked[j] if ready is None else after(picked[j], got[ready])
+        for j in (1, 3, 5, 6, 2, 7, 4):
+            message = picked[j] if j not in (4, 7) else after(picked[j], got[5], got[6])
             got[j] = flip(message, "rows", j)
 
     strengths = jax.ShapeDtypeStruct((tile_total, share, side), bf16)
@@ -491,23 +506,28 @@
     )(after(info, got[1] if direct else picked[0]), *shared)
     if direct:
         slots = (3 * capacity, 3 * capacity, 2 * capacity)
-        pieces = []
-        for group in ((0, 1, 3), (2, 5, 6)):
-            own = join(*[got[j] for j in group])
-            own = after(own, got[6], *pieces[:1])
-            own = join(own, flip(own, "cols", 2))
-            pieces += [own, flip(own, "cols", 1)]
-        carried = after(carried, got[7])
+        own = gather(got[0], got[1], got[3])
+        early = join(own, flip(own, "cols", 2))
+        pieces = [early, flip(early, "cols", 1)]
+
+        own = after(gather(got[2], got[5], got[6], carried), early)
+        arrived = flip(own, "cols", 2)
+        gram, carried = add(gram, arrived)
+        own = join(own[: 3 * capacity], arrived[: 3 * capacity], carried)
+        arrived = flip(own, "cols", 1)
+        gram, carried = add(gram, arrived)
+        pieces += [own, arrived]
+
+        own = gather(got[7], got[4])
+        arrived = flip(own, "cols", 2)
         for bit in (1, 2, 4):
             gram, carried = add(gram, flip(carried, "rows", bit))
-        own = join(got[7], got[4])
-        arrived = flip(join(own, carried), "cols", 2)
-        gram, carried = add(gram, arrived)
-        own = join(own, arrived[: 2 * capacity], carried)
+            if bit == 1:
+                own = after(own, carried, mask)
+        own = join(own, arrived)
         pieces += [own, flip(own, "cols", 1)]
     else:
         slots = (row_devs * capacity,)
-        extra = 0
         gram = add_all(gram)
         own = lax.all_to_all(picked[0], "rows", split_axis=0, concat_axis=0, tiled=True)
         own = join(own, flip(own, "cols", 2))
@@ -521,30 +541,27 @@
         pltpu.VMEM((2, UNROLL, 2 * share, side), bf16),
     ]
     lists = (places, tile_users, info)
-    field_sent, field, gram, y = call(
-        functools.partial(start_kernel, n_cols, slots, extra),
-        [
-            jax.ShapeDtypeStruct((n_cols, col_width, own_users), f32),
-            vector,
-            square,
-            held,
-        ],
-        [smem] * 3 + [vmem] * 3 + [anywhere] * len(pieces),
+    part, y = call(
+        functools.partial(start_kernel, n_cols, slots),
+        [vector, held],
+        [smem] * 3 + [vmem] * 2 + [anywhere] * len(pieces),
         "start",
-        [pltpu.VMEM(packed.shape, bf16)]
-        + work
-        + [pltpu.SemaphoreType.DMA((n_cols * len(slots) + 1,))],
+        work + [pltpu.SemaphoreType.DMA((n_cols * len(slots),))],
         8 * 10**9,
-    )(*lists, start, gram, mask, *pieces)
-    (first,) = call(
-        first_kernel, [vector], [smem] * 3 + [vmem] * 4, "first", work, 8 * 10**9
-    )(*lists, field, gram, y, mask)
-    turned = swap(field_sent)
-    field = after(field, *turned)
+    )(*lists, start, mask, *pieces)
+    pair = jax.ShapeDtypeStruct((n_cols, 2 * col_width, own_users), f32)
+    pair_sent, field, first = call(
+        first_kernel,
+        [pair, vector, vector],
+        [smem] * 3 + [vmem] * 5,
+        "first",
+        work,
+        8 * 10**9,
+    )(*lists, start, part, gram, y, mask)
     second_sent, dots = call(
         second_kernel,
         [
-            jax.ShapeDtypeStruct((n_cols, 2 * col_width, own_users), f32),
+            jax.ShapeDtypeStruct((n_cols, col_width, own_users), f32),
             jax.ShapeDtypeStruct((devices, 128), f32),
         ],
         [smem] * 3 + [vmem] * 5,
@@ -553,6 +570,8 @@
         8 * 10**9,
     )(*lists, field, first, gram, y, mask)
 
+    turned = swap(pair_sent)
+    dots = after(dots, *turned)
     turned += swap(second_sent)
     dots = lax.all_to_all(dots, ("rows", "cols"), split_axis=0, concat_axis=0, tiled=True)
     result = jax.ShapeDtypeStruct((col_width, users), f32)

time: 106 us -> 108 us (1.019)
  waiting for transfers between devices: 32.6 us -> 45.7 us
  blocking collectives: 11.9 us -> 0 us
  Pallas kernels: 24.2 us -> 27.4 us
  starting transfers between devices: 32.6 us -> 30.1 us
    all_to_all x1 -> x0, blocking collectives: 11.9 us -> none  [on_device(): lax.all_to_all(dots, ('rows', 'cols'), split_axis=0, concat_axis=0, tiled...]
    all_to_all x0 -> x1, waiting for transfers between devices: none -> 7.04 us  [on_device(): lax.all_to_all(dots, ('rows', 'cols'), split_axis=0, concat_axis=0, tiled...]
    ppermute x25, starting transfers between devices: 26.5 us -> 19.9 us  [flip(): return lax.ppermute(value, axis, [(i, i ^ bit) for i in range(size)])]
    ppermute x25, waiting for transfers between devices: 27.9 us -> 33.9 us  [flip(): return lax.ppermute(value, axis, [(i, i ^ bit) for i in range(size)])]
    all_to_all x0 -> x1, starting transfers between devices: none -> 4.09 us  [on_device(): lax.all_to_all(dots, ('rows', 'cols'), split_axis=0, concat_axis=0, tiled...]
    pallas_call x3 -> x6, Pallas kernels: 16.1 us -> 18.6 us  [the longest x1 5.81 us: on_device(): call(second_kernel, [jax.ShapeDtypeStruct((n_cols, col_width, own_users),...]
  transfers between devices with their start and end apart: 26 -> 27, of which waited for: 9 -> 14; matrix products, arithmetic and copies ran while one was open for 2% -> 2% of each run, Pallas kernels for 8% -> 11%
where the time goes in v3:
time: 108 us
  waiting for transfers between devices  45.7 us (42%)
  starting transfers between devices  30.1 us (28%)
  Pallas kernels  27.4 us (25%)
  local copies, waits for them, and re-layouts  1.89 us (2%)
  between operations  1.54 us (1%)
  other arithmetic  1.29 us (1%)
    ppermute x25, waiting for transfers between devices, flip(): return lax.ppermute(value, axis, [(i, i ^ bit) for i in range(size)])  33.9 us
    ppermute x25, starting transfers between devices, flip(): return lax.ppermute(value, axis, [(i, i ^ bit) for i in range(size)])  19.9 us
    all_to_all x1, waiting for transfers between devices, on_device(): lax.all_to_all(dots, ('rows', 'cols'), split_axis=0, concat_axis=0, tiled...  7.04 us
    all_to_all x1, starting transfers between devices, on_device(): lax.all_to_all(requests, 'rows', split_axis=0, concat_axis=0, tiled=True)  6.07 us
    pallas_call x1, Pallas kernels, on_device(): call(second_kernel, [jax.ShapeDtypeStruct((n_cols, col_width, own_users),...  5.81 us
    pallas_call x1, Pallas kernels, on_device(): call(first_kernel, [pair, vector, vector], [smem] * 3 + [vmem] * 5, 'firs...  5.65 us
    pallas_call x1, Pallas kernels, on_device(): call(functools.partial(start_kernel, n_cols, slots), [vector, held], [sme...  5.55 us
    all_to_all x1, waiting for transfers between devices, on_device(): lax.all_to_all(requests, 'rows', split_axis=0, concat_axis=0, tiled=True)  4.76 us
  transfers between devices with their start and end apart: 27, of which 14 were waited for; matrix products, arithmetic and copies ran while one was open for 2% of the time, Pallas kernels for 11%

profile of v3, /device:TPU:0, one launch (start us, length us, event | category | flops | bytes accessed | tf_op | source)
XLA Modules:
  0.0 107.9 jit_solution(17831922329901368043)
XLA Ops:
  1.4 1.7 %prepare.1 = (bf16[32,3072]{1,0:T(8,128)(2,1)S(1)}, bf16[32,3072]{1,0:T(8,128)(2,1)S(1)}, bf16[32,3072]{1,0:T(8,128)(2,1)S(1)}, bf16[32,3072]{1,0:T(8,128)(2,1)S(1)}) custom-call(s32[3]{0:T(128)S(1)} %pad_add_fusion.info_ref, f32[32,2048]{1,0:T(8,128)} %x_ref.1, bf16[32,8192]{1,0:T(8,128)(2,1)} %items_ref.1), custom_call_target="tpu_custom_call" | custom-call | flops 1000000000 | tf_op jit(solution)/shard_map/prepare/pallas_call | solution.py:403
  3.6 2.6 %collective-permute-start.1 = (bf16[32,3072]{1,0:T(8,128)(2,1)S(1)}, bf16[32,3072]{1,0:T(8,128)(2,1)S(1)}, u32[]{:S(2)}, u32[]{:S(2)}) collective-permute-start(bf16[32,3072]{1,0:T(8,128)(2,1)S(1)} %get-tuple-element.44), channel_id=1, source_target_pairs={{0,2},{1,3},{2,0},{3,1},{4,6},{5,7},{6,4},{7,5},{8,10},{9,11},{10,... | collective-permute-start | bytes 589832 | tf_op jit(solution)/shard_map/ppermute | solution.py:345
  7.9 6.1 %all-to-all-start = ((s32[8,1,9]{2,1,0:T(1,128)}), s32[8,1,9]{2,1,0:T(1,128)S(1)}, u32[]{:S(2)}, u32[]{:S(2)}) async-start(s32[8,1,9]{2,1,0:T(1,128)} %bitcast.5), calls=%async_computation | async-start | bytes 8192 | tf_op jit(solution)/shard_map/all_to_all | solution.py:436
  14.0 1.6 %collective-permute-done.2.refs_3_ = bf16[32,3072]{1,0:T(8,128)(2,1)S(1)} collective-permute-done((bf16[32,3072]{1,0:T(8,128)(2,1)S(1)}, bf16[32,3072]{1,0:T(8,128)(2,1)S(1)}, u32[]{:S(2)}, u32[]{:S(2)}) %collective-permute-start.2) | collective-permute-done | bytes 196640 | tf_op jit(solution)/shard_map/ppermute | solution.py:345
  15.6 4.8 %all-to-all-done = s32[8,1,9]{2,1,0:T(1,128)S(1)} async-done(((s32[8,1,9]{2,1,0:T(1,128)}), s32[8,1,9]{2,1,0:T(1,128)S(1)}, u32[]{:S(2)}, u32[]{:S(2)}) %all-to-all-start) | async-done | bytes 320 | tf_op jit(solution)/shard_map/all_to_all | solution.py:436
  26.3 2.4 %collective-permute-start.9 = (bf16[9,32,256]{2,1,0:T(8,128)(2,1)S(1)}, bf16[9,32,256]{2,1,0:T(8,128)(2,1)S(1)}, u32[]{:S(2)}, u32[]{:S(2)}) collective-permute-start(bf16[9,32,256]{2,1,0:T(8,128)(2,1)S(1)} %get-tuple-element.54), channel_id=1, source_target_pairs={{0,24},{4,28},{8,16},{12,20},{16,8},{20,12},{24,0},{28,4},{1,25},{... | collective-permute-start | bytes 442376 | tf_op jit(solution)/shard_map/ppermute | solution.py:345
  28.7 3.1 %collective-permute-done.3.refs_1_ = bf16[9,32,256]{2,1,0:T(8,128)(2,1)S(1)} collective-permute-done((bf16[9,32,256]{2,1,0:T(8,128)(2,1)S(1)}, bf16[9,32,256]{2,1,0:T(8,128)(2,1)S(1)}, u32[]{:S(2)}, u32[]{:S(2)}) %collective-permute-start.3) | collective-permute-done | bytes 147488 | tf_op jit(solution)/shard_map/ppermute | solution.py:345
  32.4 1.6 %collective-permute-start.5 = (bf16[27,32,256]{2,1,0:T(8,128)(2,1)S(1)}, bf16[27,32,256]{2,1,0:T(8,128)(2,1)S(1)}, u32[]{:S(2)}, u32[]{:S(2)}) collective-permute-start(bf16[27,32,256]{2,1,0:T(8,128)(2,1)S(1)} %join.3), channel_id=1, source_target_pairs={{0,2},{1,3},{2,0},{3,1},{4,6},{5,7},{6,4},{7,5},{8,10},{9,11},{10,... | collective-permute-start | bytes 1327112 | tf_op jit(solution)/shard_map/ppermute | solution.py:345
  35.4 3.9 %collective-permute-done.8.refs_1_ = bf16[9,32,256]{2,1,0:T(8,128)(2,1)S(1)} collective-permute-done((bf16[9,32,256]{2,1,0:T(8,128)(2,1)S(1)}, bf16[9,32,256]{2,1,0:T(8,128)(2,1)S(1)}, u32[]{:S(2)}, u32[]{:S(2)}) %collective-permute-start.8) | collective-permute-done | bytes 147488 | tf_op jit(solution)/shard_map/ppermute | solution.py:345
  40.0 2.7 %collective-permute-done.5 = bf16[27,32,256]{2,1,0:T(8,128)(2,1)S(1)} collective-permute-done((bf16[27,32,256]{2,1,0:T(8,128)(2,1)S(1)}, bf16[27,32,256]{2,1,0:T(8,128)(2,1)S(1)}, u32[]{:S(2)}, u32[]{:S(2)}) %collective-permute-start.5) | collective-permute-done | bytes 442400 | tf_op jit(solution)/shard_map/ppermute | solution.py:345
  42.7 1.6 %collective-permute-start.10 = (bf16[31,32,256]{2,1,0:T(8,128)(2,1)S(1)}, bf16[31,32,256]{2,1,0:T(8,128)(2,1)S(1)}, u32[]{:S(2)}, u32[]{:S(2)}) collective-permute-start(bf16[31,32,256]{2,1,0:T(8,128)(2,1)S(1)} %join.4), channel_id=1, source_target_pairs={{0,2},{1,3},{2,0},{3,1},{4,6},{5,7},{6,4},{7,5},{8,10},{9,11},{10,... | collective-permute-start | bytes 1523720 | tf_op jit(solution)/shard_map/ppermute | solution.py:345
  44.3 1.9 %collective-permute-start.12 = (bf16[9,32,256]{2,1,0:T(8,128)(2,1)S(1)}, bf16[9,32,256]{2,1,0:T(8,128)(2,1)S(1)}, u32[]{:S(2)}, u32[]{:S(2)}) collective-permute-start(bf16[9,32,256]{2,1,0:T(8,128)(2,1)S(1)} %get-tuple-element.60), channel_id=1, source_target_pairs={{0,28},{4,24},{8,20},{12,16},{16,12},{20,8},{24,4},{28,0},{1,29},{... | collective-permute-start | bytes 442376 | tf_op jit(solution)/shard_map/ppermute | solution.py:345
  46.2 5.6 %collective-permute-done.10.arrived_ref = bf16[31,32,256]{2,1,0:T(8,128)(2,1)S(1)} collective-permute-done((bf16[31,32,256]{2,1,0:T(8,128)(2,1)S(1)}, bf16[31,32,256]{2,1,0:T(8,128)(2,1)S(1)}, u32[]{:S(2)}, u32[]{:S(2)}) %collective-permute-start.10) | collective-permute-done | bytes 507936 | tf_op jit(solution)/shard_map/ppermute | solution.py:345
  52.2 3.1 %collective-permute-done.13.refs_1_ = bf16[9,32,256]{2,1,0:T(8,128)(2,1)S(1)} collective-permute-done((bf16[9,32,256]{2,1,0:T(8,128)(2,1)S(1)}, bf16[9,32,256]{2,1,0:T(8,128)(2,1)S(1)}, u32[]{:S(2)}, u32[]{:S(2)}) %collective-permute-start.13) | collective-permute-done | bytes 147488 | tf_op jit(solution)/shard_map/ppermute | solution.py:345
  56.7 2.3 %mask.1 = bf16[72,64,256]{2,1,0:T(8,128)(2,1)S(1)} custom-call(s32[3]{0:T(128)S(1)} %pad_add_fusion.info_ref, bf16[72,256,256]{2,1,0:T(8,128)(2,1)} %mask_hbm.1), custom_call_target="tpu_custom_call" | custom-call | flops 1000000000 | tf_op jit(solution)/shard_map/mask/pallas_call | solution.py:481
  58.9 2.0 %collective-permute-done.14.arrived_ref = bf16[4,32,256]{2,1,0:T(8,128)(2,1)S(1)} collective-permute-done((bf16[4,32,256]{2,1,0:T(8,128)(2,1)S(1)}, bf16[4,32,256]{2,1,0:T(8,128)(2,1)S(1)}, u32[]{:S(2)}, u32[]{:S(2)}) %collective-permute-start.14) | collective-permute-done | bytes 65568 | tf_op jit(solution)/shard_map/ppermute | solution.py:345
  62.7 4.4 %collective-permute-done.17.arrived_ref = bf16[4,32,256]{2,1,0:T(8,128)(2,1)S(1)} collective-permute-done((bf16[4,32,256]{2,1,0:T(8,128)(2,1)S(1)}, bf16[4,32,256]{2,1,0:T(8,128)(2,1)S(1)}, u32[]{:S(2)}, u32[]{:S(2)}) %collective-permute-start.17) | collective-permute-done | bytes 65568 | tf_op jit(solution)/shard_map/ppermute | solution.py:345
  67.5 5.5 %collective-permute-done.18.arrived_ref = bf16[4,32,256]{2,1,0:T(8,128)(2,1)S(1)} collective-permute-done((bf16[4,32,256]{2,1,0:T(8,128)(2,1)S(1)}, bf16[4,32,256]{2,1,0:T(8,128)(2,1)S(1)}, u32[]{:S(2)}, u32[]{:S(2)}) %collective-permute-start.18) | collective-permute-done | bytes 65568 | tf_op jit(solution)/shard_map/ppermute | solution.py:345
  73.7 5.5 %start.1 = (f32[512,128]{1,0:T(8,128)S(1)}, bf16[72,128,256]{2,1,0:T(8,128)(2,1)S(1)}) custom-call(s32[72]{0:T(128)S(1)} %get-tuple-element.93.slot_ref, s32[72]{0:T(128)S(1)} %get-tuple-element.92.user_ref, s32[3]{0:T(128)S(1)} %pad_add_fusion.info_ref, f32[128,512]{1,0:T(8,128)S(1)} %get-tuple-element.49.x_ref, bf16[72,64,256]{2,1,0:T(8,128)(2,1)S(1)} %mask.1, ...), custom_call_target="tpu_custom_call" | custom-call | flops 8000000000 | tf_op jit(solution)/shard_map/start/pallas_call | solution.py:544
  79.3 5.6 %first.1 = (f32[4,64,512]{2,1,0:T(8,128)S(1)}, f32[512,128]{1,0:T(8,128)S(1)}, f32[512,128]{1,0:T(8,128)S(1)}) custom-call(s32[72]{0:T(128)S(1)} %get-tuple-element.93.slot_ref, s32[72]{0:T(128)S(1)} %get-tuple-element.92.user_ref, s32[3]{0:T(128)S(1)} %pad_add_fusion.info_ref, f32[128,512]{1,0:T(8,128)S(1)} %get-tuple-element.49.x_ref, ...), custom_call_target="tpu_custom_call" | custom-call | flops 8000000000 | tf_op jit(solution)/shard_map/first/pallas_call | solution.py:553
  86.9 5.8 %second.1 = (f32[4,32,512]{2,1,0:T(8,128)S(1)}, f32[32,128]{1,0:T(8,128)}) custom-call(s32[72]{0:T(128)S(1)} %get-tuple-element.93.slot_ref, s32[72]{0:T(128)S(1)} %get-tuple-element.92.user_ref, s32[3]{0:T(128)S(1)} %pad_add_fusion.info_ref, f32[512,128]{1,0:T(8,128)S(1)} %get-tuple-element.74.field_ref, f32[512,128]{1,0:T(8,128)S(1)} %get-tuple-element.75.first_ref, ...), custom_call_target="tpu_custom_call" | custom-call | flops 8000000000 | tf_op jit(solution)/shard_map/second/pallas_call | solution.py:561
  94.7 4.1 %all-to-all-start.1 = ((f32[32,1,128]{2,1,0:T(1,128)}), f32[32,1,128]{2,1,0:T(1,128)S(1)}, u32[]{:S(2)}, u32[]{:S(2)}) async-start(f32[32,1,128]{2,1,0:T(1,128)} %bitcast.12), calls=%async_computation.1 | async-start | bytes 32768 | tf_op jit(solution)/shard_map/all_to_all | solution.py:576
  98.8 7.0 %all-to-all-done.1 = f32[32,1,128]{2,1,0:T(1,128)S(1)} async-done(((f32[32,1,128]{2,1,0:T(1,128)}), f32[32,1,128]{2,1,0:T(1,128)S(1)}, u32[]{:S(2)}, u32[]{:S(2)}) %all-to-all-start.1) | async-done | bytes 16416 | tf_op jit(solution)/shard_map/all_to_all | solution.py:576
  105.8 2.0 %finish.1 = (f32[32,2048]{1,0:T(8,128)}, f32[32,2048]{1,0:T(8,128)}) custom-call(s32[3]{0:T(128)S(1)} %pad_add_fusion.info_ref, f32[32,128]{1,0:T(8,128)S(1)} %bitcast.31, f32[32,2048]{1,0:T(8,128)S(1)} %copy-done.1, f32[64,512]{1,0:T(8,128)S(1)} %get-tuple-element.83.refs_0_, f32[64,512]{1,0:T(8,128)S(1)} %collective-permute-done.19.refs_1_, ...), custom_call_target="tpu_custom_call" | custom-call | flops 1000000000 | tf_op jit(solution)/shard_map/finish/pallas_call | solution.py:579
  (69 shorter events, 19.4 us)
Async XLA Ops:
  3.1 10.9 %collective-permute-start = (bf16[32,3072]{1,0:T(8,128)(2,1)S(1)}, bf16[32,3072]{1,0:T(8,128)(2,1)S(1)}, u32[]{:S(2)}, u32[]{:S(2)}) collective-permute-start(bf16[32,3072]{1,0:T(8,128)(2,1)S(1)} %get-tuple-element.43), channel_id=1, source_target_pairs={{0,1},{1,0},{2,3},{3,2},{4,5},{5,4},{6,7},{7,6},{8,9},{9,8},{10,11... | collective-permute-start | bytes 589832 | tf_op jit(solution)/shard_map/ppermute | solution.py:345
  3.6 10.4 %collective-permute-start.1 = (bf16[32,3072]{1,0:T(8,128)(2,1)S(1)}, bf16[32,3072]{1,0:T(8,128)(2,1)S(1)}, u32[]{:S(2)}, u32[]{:S(2)}) collective-permute-start(bf16[32,3072]{1,0:T(8,128)(2,1)S(1)} %get-tuple-element.44), channel_id=1, source_target_pairs={{0,2},{1,3},{2,0},{3,1},{4,6},{5,7},{6,4},{7,5},{8,10},{9,11},{10,... | collective-permute-start | bytes 589832 | tf_op jit(solution)/shard_map/ppermute | solution.py:345
  6.2 9.4 %collective-permute-start.2 = (bf16[32,3072]{1,0:T(8,128)(2,1)S(1)}, bf16[32,3072]{1,0:T(8,128)(2,1)S(1)}, u32[]{:S(2)}, u32[]{:S(2)}) collective-permute-start(bf16[32,3072]{1,0:T(8,128)(2,1)S(1)} %get-tuple-element.45), channel_id=1, source_target_pairs={{0,3},{1,2},{2,1},{3,0},{4,7},{5,6},{6,5},{7,4},{8,11},{9,10},{10,... | collective-permute-start | bytes 589832 | tf_op jit(solution)/shard_map/ppermute | solution.py:345
  7.9 12.5 %all-to-all-start = ((s32[8,1,9]{2,1,0:T(1,128)}), s32[8,1,9]{2,1,0:T(1,128)S(1)}, u32[]{:S(2)}, u32[]{:S(2)}) async-start(s32[8,1,9]{2,1,0:T(1,128)} %bitcast.5), calls=%async_computation | async-start | bytes 8192 | tf_op jit(solution)/shard_map/all_to_all | solution.py:436
  22.2 9.6 %collective-permute-start.3 = (bf16[9,32,256]{2,1,0:T(8,128)(2,1)S(1)}, bf16[9,32,256]{2,1,0:T(8,128)(2,1)S(1)}, u32[]{:S(2)}, u32[]{:S(2)}) collective-permute-start(bf16[9,32,256]{2,1,0:T(8,128)(2,1)S(1)} %get-tuple-element.47), channel_id=1, source_target_pairs={{0,4},{4,0},{8,12},{12,8},{16,20},{20,16},{24,28},{28,24},{1,5},{5... | collective-permute-start | bytes 442376 | tf_op jit(solution)/shard_map/ppermute | solution.py:345
  22.8 9.0 %collective-permute-start.4 = (bf16[9,32,256]{2,1,0:T(8,128)(2,1)S(1)}, bf16[9,32,256]{2,1,0:T(8,128)(2,1)S(1)}, u32[]{:S(2)}, u32[]{:S(2)}) collective-permute-start(bf16[9,32,256]{2,1,0:T(8,128)(2,1)S(1)} %get-tuple-element.51), channel_id=1, source_target_pairs={{0,12},{4,8},{8,4},{12,0},{16,28},{20,24},{24,20},{28,16},{1,13},{... | collective-permute-start | bytes 442376 | tf_op jit(solution)/shard_map/ppermute | solution.py:345
  24.3 11.1 %collective-permute-start.7 = (bf16[9,32,256]{2,1,0:T(8,128)(2,1)S(1)}, bf16[9,32,256]{2,1,0:T(8,128)(2,1)S(1)}, u32[]{:S(2)}, u32[]{:S(2)}) collective-permute-start(bf16[9,32,256]{2,1,0:T(8,128)(2,1)S(1)} %get-tuple-element.52), channel_id=1, source_target_pairs={{0,8},{4,12},{8,0},{12,4},{16,24},{20,28},{24,16},{28,20},{1,9},{5... | collective-permute-start | bytes 442376 | tf_op jit(solution)/shard_map/ppermute | solution.py:345
  25.8 13.5 %collective-permute-start.8 = (bf16[9,32,256]{2,1,0:T(8,128)(2,1)S(1)}, bf16[9,32,256]{2,1,0:T(8,128)(2,1)S(1)}, u32[]{:S(2)}, u32[]{:S(2)}) collective-permute-start(bf16[9,32,256]{2,1,0:T(8,128)(2,1)S(1)} %get-tuple-element.53), channel_id=1, source_target_pairs={{0,20},{4,16},{8,28},{12,24},{16,4},{20,0},{24,12},{28,8},{1,21},{... | collective-permute-start | bytes 442376 | tf_op jit(solution)/shard_map/ppermute | solution.py:345
  26.3 13.0 %collective-permute-start.9 = (bf16[9,32,256]{2,1,0:T(8,128)(2,1)S(1)}, bf16[9,32,256]{2,1,0:T(8,128)(2,1)S(1)}, u32[]{:S(2)}, u32[]{:S(2)}) collective-permute-start(bf16[9,32,256]{2,1,0:T(8,128)(2,1)S(1)} %get-tuple-element.54), channel_id=1, source_target_pairs={{0,24},{4,28},{8,16},{12,20},{16,8},{20,12},{24,0},{28,4},{1,25},{... | collective-permute-start | bytes 442376 | tf_op jit(solution)/shard_map/ppermute | solution.py:345
  32.4 10.2 %collective-permute-start.5 = (bf16[27,32,256]{2,1,0:T(8,128)(2,1)S(1)}, bf16[27,32,256]{2,1,0:T(8,128)(2,1)S(1)}, u32[]{:S(2)}, u32[]{:S(2)}) collective-permute-start(bf16[27,32,256]{2,1,0:T(8,128)(2,1)S(1)} %join.3), channel_id=1, source_target_pairs={{0,2},{1,3},{2,0},{3,1},{4,6},{5,7},{6,4},{7,5},{8,10},{9,11},{10,... | collective-permute-start | bytes 1327112 | tf_op jit(solution)/shard_map/ppermute | solution.py:345
  42.7 9.1 %collective-permute-start.10 = (bf16[31,32,256]{2,1,0:T(8,128)(2,1)S(1)}, bf16[31,32,256]{2,1,0:T(8,128)(2,1)S(1)}, u32[]{:S(2)}, u32[]{:S(2)}) collective-permute-start(bf16[31,32,256]{2,1,0:T(8,128)(2,1)S(1)} %join.4), channel_id=1, source_target_pairs={{0,2},{1,3},{2,0},{3,1},{4,6},{5,7},{6,4},{7,5},{8,10},{9,11},{10,... | collective-permute-start | bytes 1523720 | tf_op jit(solution)/shard_map/ppermute | solution.py:345
  44.3 7.9 %collective-permute-start.12 = (bf16[9,32,256]{2,1,0:T(8,128)(2,1)S(1)}, bf16[9,32,256]{2,1,0:T(8,128)(2,1)S(1)}, u32[]{:S(2)}, u32[]{:S(2)}) collective-permute-start(bf16[9,32,256]{2,1,0:T(8,128)(2,1)S(1)} %get-tuple-element.60), channel_id=1, source_target_pairs={{0,28},{4,24},{8,20},{12,16},{16,12},{20,8},{24,4},{28,0},{1,29},{... | collective-permute-start | bytes 442376 | tf_op jit(solution)/shard_map/ppermute | solution.py:345
  46.1 9.2 %collective-permute-start.13 = (bf16[9,32,256]{2,1,0:T(8,128)(2,1)S(1)}, bf16[9,32,256]{2,1,0:T(8,128)(2,1)S(1)}, u32[]{:S(2)}, u32[]{:S(2)}) collective-permute-start(bf16[9,32,256]{2,1,0:T(8,128)(2,1)S(1)} %get-tuple-element.62), channel_id=1, source_target_pairs={{0,16},{4,20},{8,24},{12,28},{16,0},{20,4},{24,8},{28,12},{1,17},{... | collective-permute-start | bytes 442376 | tf_op jit(solution)/shard_map/ppermute | solution.py:345
  55.7 6.8 %collective-permute-start.15 = (bf16[18,32,256]{2,1,0:T(8,128)(2,1)S(1)}, bf16[18,32,256]{2,1,0:T(8,128)(2,1)S(1)}, u32[]{:S(2)}, u32[]{:S(2)}) collective-permute-start(bf16[18,32,256]{2,1,0:T(8,128)(2,1)S(1)} %join.5), channel_id=1, source_target_pairs={{0,2},{1,3},{2,0},{3,1},{4,6},{5,7},{6,4},{7,5},{8,10},{9,11},{10,... | collective-permute-start | bytes 884744 | tf_op jit(solution)/shard_map/ppermute | solution.py:345
  56.3 17.4 %collective-permute-start.6 = (bf16[54,32,256]{2,1,0:T(8,128)(2,1)S(1)}, bf16[54,32,256]{2,1,0:T(8,128)(2,1)S(1)}, u32[]{:S(2)}, u32[]{:S(2)}) collective-permute-start(bf16[54,32,256]{2,1,0:T(8,128)(2,1)S(1)} %pad_maximum_fusion.1.refs_0_), channel_id=1, source_target_pairs={{0,1},{1,0},{2,3},{3,2},{4,5},{5,4},{6,7},{7,6},{8,9},{9,8},{10,11... | collective-permute-start | bytes 2654216 | tf_op jit(solution)/shard_map/ppermute | solution.py:345
  56.4 4.6 %collective-permute-start.14 = (bf16[4,32,256]{2,1,0:T(8,128)(2,1)S(1)}, bf16[4,32,256]{2,1,0:T(8,128)(2,1)S(1)}, u32[]{:S(2)}, u32[]{:S(2)}) collective-permute-start(bf16[4,32,256]{2,1,0:T(8,128)(2,1)S(1)} %get-tuple-element.65), channel_id=1, source_target_pairs={{0,4},{4,0},{8,12},{12,8},{16,20},{20,16},{24,28},{28,24},{1,5},{5... | collective-permute-start | bytes 196616 | tf_op jit(solution)/shard_map/ppermute | solution.py:345
  62.5 11.2 %collective-permute-start.16 = (bf16[36,32,256]{2,1,0:T(8,128)(2,1)S(1)}, bf16[36,32,256]{2,1,0:T(8,128)(2,1)S(1)}, u32[]{:S(2)}, u32[]{:S(2)}) collective-permute-start(bf16[36,32,256]{2,1,0:T(8,128)(2,1)S(1)} %constant_dynamic-update-slice_fusion.refs_4_), channel_id=1, source_target_pairs={{0,1},{1,0},{2,3},{3,2},{4,5},{5,4},{6,7},{7,6},{8,9},{9,8},{10,11... | collective-permute-start | bytes 1769480 | tf_op jit(solution)/shard_map/ppermute | solution.py:345
  67.1 5.9 %collective-permute-start.18 = (bf16[4,32,256]{2,1,0:T(8,128)(2,1)S(1)}, bf16[4,32,256]{2,1,0:T(8,128)(2,1)S(1)}, u32[]{:S(2)}, u32[]{:S(2)}) collective-permute-start(bf16[4,32,256]{2,1,0:T(8,128)(2,1)S(1)} %get-tuple-element.71), channel_id=1, source_target_pairs={{0,16},{4,20},{8,24},{12,28},{16,0},{20,4},{24,8},{28,12},{1,17},{... | collective-permute-start | bytes 196616 | tf_op jit(solution)/shard_map/ppermute | solution.py:345
  85.0 9.5 %collective-permute-start.21 = (f32[64,512]{1,0:T(8,128)S(1)}, f32[64,512]{1,0:T(8,128)S(1)}, u32[]{:S(2)}, u32[]{:S(2)}) collective-permute-start(f32[64,512]{1,0:T(8,128)S(1)} %get-tuple-element.80), channel_id=1, source_target_pairs={{0,3},{1,2},{2,1},{3,0},{4,7},{5,6},{6,5},{7,4},{8,11},{9,10},{10,... | collective-permute-start | bytes 393224 | tf_op jit(solution)/shard_map/ppermute | solution.py:345
  85.2 9.4 %collective-permute-start.20 = (f32[64,512]{1,0:T(8,128)S(1)}, f32[64,512]{1,0:T(8,128)S(1)}, u32[]{:S(2)}, u32[]{:S(2)}) collective-permute-start(f32[64,512]{1,0:T(8,128)S(1)} %get-tuple-element.81), channel_id=1, source_target_pairs={{0,2},{1,3},{2,0},{3,1},{4,6},{5,7},{6,4},{7,5},{8,10},{9,11},{10,... | collective-permute-start | bytes 393224 | tf_op jit(solution)/shard_map/ppermute | solution.py:345
  86.3 8.3 %collective-permute-start.19 = (f32[64,512]{1,0:T(8,128)S(1)}, f32[64,512]{1,0:T(8,128)S(1)}, u32[]{:S(2)}, u32[]{:S(2)}) collective-permute-start(f32[64,512]{1,0:T(8,128)S(1)} %get-tuple-element.82), channel_id=1, source_target_pairs={{0,1},{1,0},{2,3},{3,2},{4,5},{5,4},{6,7},{7,6},{8,9},{9,8},{10,11... | collective-permute-start | bytes 393224 | tf_op jit(solution)/shard_map/ppermute | solution.py:345
  92.7 6.0 %collective-permute-start.24 = (f32[32,512]{1,0:T(8,128)S(1)}, f32[32,512]{1,0:T(8,128)S(1)}, u32[]{:S(2)}, u32[]{:S(2)}) collective-permute-start(f32[32,512]{1,0:T(8,128)S(1)} %get-tuple-element.84), channel_id=1, source_target_pairs={{0,3},{1,2},{2,1},{3,0},{4,7},{5,6},{6,5},{7,4},{8,11},{9,10},{10,... | collective-permute-start | bytes 196616 | tf_op jit(solution)/shard_map/ppermute | solution.py:345
  93.3 5.4 %collective-permute-start.23 = (f32[32,512]{1,0:T(8,128)S(1)}, f32[32,512]{1,0:T(8,128)S(1)}, u32[]{:S(2)}, u32[]{:S(2)}) collective-permute-start(f32[32,512]{1,0:T(8,128)S(1)} %get-tuple-element.85), channel_id=1, source_target_pairs={{0,2},{1,3},{2,0},{3,1},{4,6},{5,7},{6,4},{7,5},{8,10},{9,11},{10,... | collective-permute-start | bytes 196616 | tf_op jit(solution)/shard_map/ppermute | solution.py:345
  94.7 11.2 %all-to-all-start.1 = ((f32[32,1,128]{2,1,0:T(1,128)}), f32[32,1,128]{2,1,0:T(1,128)S(1)}, u32[]{:S(2)}, u32[]{:S(2)}) async-start(f32[32,1,128]{2,1,0:T(1,128)} %bitcast.12), calls=%async_computation.1 | async-start | bytes 32768 | tf_op jit(solution)/shard_map/all_to_all | solution.py:576
  (6 other events, 44.3 us)

commit v4 on v3

--- a/solution.py
+++ b/solution.py
@@ -454,6 +454,9 @@
         flops=10**9,
     )(after(info, *shared), wanted, item_factors)
 
+    def add(gram, arrived):
+        return call(add_kernel, [square, packed], [vmem] * 2, "add")(gram, arrived)
+
     def join(*arrays):
         return jnp.concatenate(arrays, axis=0)
 
@@ -467,9 +470,6 @@
             [pltpu.SemaphoreType.DMA((len(arrays),))],
             2 * 10**10,
         )(*arrays)[0]
-
-    def add(gram, arrived):
-        return call(add_kernel, [square, packed], [vmem] * 2, "add")(gram, arrived)
 
     got = {0: picked[0]}
     if direct:
@@ -489,6 +489,8 @@
         after(info, got[1] if direct else picked[0]),
         pltpu.with_memory_space_constraint(tile_mask, pltpu.HBM),
     )
+    if direct:
+        own = gather(got[0], got[1], got[3])
     square = jax.ShapeDtypeStruct((width, width), f32)
     extra = width // col_width
     packed = jax.ShapeDtypeStruct((extra, col_width, 2 * width), bf16)
@@ -503,29 +505,30 @@
             pltpu.SemaphoreType.DMA((2 * n_cols,)),
         ],
         10**9,
-    )(after(info, got[1] if direct else picked[0]), *shared)
+    )(after(info, own if direct else picked[0]), *shared)
     if direct:
         slots = (3 * capacity, 3 * capacity, 2 * capacity)
-        own = gather(got[0], got[1], got[3])
         early = join(own, flip(own, "cols", 2))
         pieces = [early, flip(early, "cols", 1)]
 
-        own = after(gather(got[2], got[5], got[6], carried), early)
+        middle = after(gather(after(got[2], mask), got[5], got[6]), early)
+        own = middle
+        own = join(own, flip(own, "cols", 2))
+        pieces += [own, flip(own, "cols", 1)]
+
+        for bit in (1, 2, 4):
+            gram, carried = add(gram, flip(carried, "rows", bit))
+            if bit == 1:
+                carried = after(carried, got[5], got[6])
+            if bit == 2:
+                carried = after(carried, middle)
+        own = gather(got[7], got[4], carried)
         arrived = flip(own, "cols", 2)
         gram, carried = add(gram, arrived)
-        own = join(own[: 3 * capacity], arrived[: 3 * capacity], carried)
+        own = join(own[: 2 * capacity], arrived[: 2 * capacity], carried)
         arrived = flip(own, "cols", 1)
         gram, carried = add(gram, arrived)
         pieces += [own, arrived]
-
-        own = gather(got[7], got[4])
-        arrived = flip(own, "cols", 2)
-        for bit in (1, 2, 4):
-            gram, carried = add(gram, flip(carried, "rows", bit))
-            if bit == 1:
-                own = after(own, carried, mask)
-        own = join(own, arrived)
-        pieces += [own, flip(own, "cols", 1)]
     else:
         slots = (row_devs * capacity,)
         gram = add_all(gram)

time: 108 us -> 106 us (0.981)
  waiting for transfers between devices: 45.7 us -> 36.5 us
  starting transfers between devices: 30.1 us -> 37.2 us
    ppermute x25, waiting for transfers between devices: 33.9 us -> 25.2 us  [flip(): return lax.ppermute(value, axis, [(i, i ^ bit) for i in range(size)])]
    ppermute x25, starting transfers between devices: 19.9 us -> 28 us  [flip(): return lax.ppermute(value, axis, [(i, i ^ bit) for i in range(size)])]
  transfers between devices with their start and end apart: 27 -> 27, of which waited for: 14 -> 11; matrix products, arithmetic and copies ran while one was open for 2% -> 2% of each run, Pallas kernels for 11% -> 11%
where the time goes in v4:
time: 106 us
  starting transfers between devices  37.2 us (35%)
  waiting for transfers between devices  36.5 us (34%)
  Pallas kernels  27.6 us (26%)
  local copies, waits for them, and re-layouts  1.89 us (2%)
  between operations  1.59 us (2%)
  other arithmetic  1.25 us (1%)
    ppermute x25, starting transfers between devices, flip(): return lax.ppermute(value, axis, [(i, i ^ bit) for i in range(size)])  28 us
    ppermute x25, waiting for transfers between devices, flip(): return lax.ppermute(value, axis, [(i, i ^ bit) for i in range(size)])  25.2 us
    all_to_all x1, waiting for transfers between devices, on_device(): lax.all_to_all(dots, ('rows', 'cols'), split_axis=0, concat_axis=0, tiled...  6.52 us
    all_to_all x1, starting transfers between devices, on_device(): lax.all_to_all(requests, 'rows', split_axis=0, concat_axis=0, tiled=True)  6.07 us
    pallas_call x1, Pallas kernels, on_device(): call(second_kernel, [jax.ShapeDtypeStruct((n_cols, col_width, own_users),...  5.81 us
    pallas_call x1, Pallas kernels, on_device(): call(first_kernel, [pair, vector, vector], [smem] * 3 + [vmem] * 5, 'firs...  5.65 us
    pallas_call x1, Pallas kernels, on_device(): call(functools.partial(start_kernel, n_cols, slots), [vector, held], [sme...  5.55 us
    all_to_all x1, waiting for transfers between devices, on_device(): lax.all_to_all(requests, 'rows', split_axis=0, concat_axis=0, tiled=True)  4.76 us
  transfers between devices with their start and end apart: 27, of which 11 were waited for; matrix products, arithmetic and copies ran while one was open for 2% of the time, Pallas kernels for 11%

profile of v4, /device:TPU:0, one launch (start us, length us, event | category | flops | bytes accessed | tf_op | source)
XLA Modules:
  0.0 106.0 jit_solution(4584963265379983538)
XLA Ops:
  1.4 1.7 %prepare.1 = (bf16[32,3072]{1,0:T(8,128)(2,1)S(1)}, bf16[32,3072]{1,0:T(8,128)(2,1)S(1)}, bf16[32,3072]{1,0:T(8,128)(2,1)S(1)}, bf16[32,3072]{1,0:T(8,128)(2,1)S(1)}) custom-call(s32[3]{0:T(128)S(1)} %pad_add_fusion.info_ref, f32[32,2048]{1,0:T(8,128)} %x_ref.1, bf16[32,8192]{1,0:T(8,128)(2,1)} %items_ref.1), custom_call_target="tpu_custom_call" | custom-call | flops 1000000000 | tf_op jit(solution)/shard_map/prepare/pallas_call | solution.py:403
  3.6 2.6 %collective-permute-start.1 = (bf16[32,3072]{1,0:T(8,128)(2,1)S(1)}, bf16[32,3072]{1,0:T(8,128)(2,1)S(1)}, u32[]{:S(2)}, u32[]{:S(2)}) collective-permute-start(bf16[32,3072]{1,0:T(8,128)(2,1)S(1)} %get-tuple-element.47), channel_id=1, source_target_pairs={{0,2},{1,3},{2,0},{3,1},{4,6},{5,7},{6,4},{7,5},{8,10},{9,11},{10,... | collective-permute-start | bytes 589832 | tf_op jit(solution)/shard_map/ppermute | solution.py:345
  7.9 6.1 %all-to-all-start = ((s32[8,1,9]{2,1,0:T(1,128)}), s32[8,1,9]{2,1,0:T(1,128)S(1)}, u32[]{:S(2)}, u32[]{:S(2)}) async-start(s32[8,1,9]{2,1,0:T(1,128)} %bitcast.5), calls=%async_computation | async-start | bytes 8192 | tf_op jit(solution)/shard_map/all_to_all | solution.py:436
  14.0 1.6 %collective-permute-done.2.refs_3_ = bf16[32,3072]{1,0:T(8,128)(2,1)S(1)} collective-permute-done((bf16[32,3072]{1,0:T(8,128)(2,1)S(1)}, bf16[32,3072]{1,0:T(8,128)(2,1)S(1)}, u32[]{:S(2)}, u32[]{:S(2)}) %collective-permute-start.2) | collective-permute-done | bytes 196640 | tf_op jit(solution)/shard_map/ppermute | solution.py:345
  15.6 4.8 %all-to-all-done = s32[8,1,9]{2,1,0:T(1,128)S(1)} async-done(((s32[8,1,9]{2,1,0:T(1,128)}), s32[8,1,9]{2,1,0:T(1,128)S(1)}, u32[]{:S(2)}, u32[]{:S(2)}) %all-to-all-start) | async-done | bytes 320 | tf_op jit(solution)/shard_map/all_to_all | solution.py:436
  26.3 2.4 %collective-permute-start.9 = (bf16[9,32,256]{2,1,0:T(8,128)(2,1)S(1)}, bf16[9,32,256]{2,1,0:T(8,128)(2,1)S(1)}, u32[]{:S(2)}, u32[]{:S(2)}) collective-permute-start(bf16[9,32,256]{2,1,0:T(8,128)(2,1)S(1)} %get-tuple-element.59), channel_id=1, source_target_pairs={{0,24},{4,28},{8,16},{12,20},{16,8},{20,12},{24,0},{28,4},{1,25},{... | collective-permute-start | bytes 442376 | tf_op jit(solution)/shard_map/ppermute | solution.py:345
  28.7 3.1 %collective-permute-done.3.refs_1_ = bf16[9,32,256]{2,1,0:T(8,128)(2,1)S(1)} collective-permute-done((bf16[9,32,256]{2,1,0:T(8,128)(2,1)S(1)}, bf16[9,32,256]{2,1,0:T(8,128)(2,1)S(1)}, u32[]{:S(2)}, u32[]{:S(2)}) %collective-permute-start.3) | collective-permute-done | bytes 147488 | tf_op jit(solution)/shard_map/ppermute | solution.py:345
  32.4 1.6 %collective-permute-start.5 = (bf16[27,32,256]{2,1,0:T(8,128)(2,1)S(1)}, bf16[27,32,256]{2,1,0:T(8,128)(2,1)S(1)}, u32[]{:S(2)}, u32[]{:S(2)}) collective-permute-start(bf16[27,32,256]{2,1,0:T(8,128)(2,1)S(1)} %join.3), channel_id=1, source_target_pairs={{0,2},{1,3},{2,0},{3,1},{4,6},{5,7},{6,4},{7,5},{8,10},{9,11},{10,... | collective-permute-start | bytes 1327112 | tf_op jit(solution)/shard_map/ppermute | solution.py:345
  36.6 2.8 %collective-permute-done.8.refs_1_ = bf16[9,32,256]{2,1,0:T(8,128)(2,1)S(1)} collective-permute-done((bf16[9,32,256]{2,1,0:T(8,128)(2,1)S(1)}, bf16[9,32,256]{2,1,0:T(8,128)(2,1)S(1)}, u32[]{:S(2)}, u32[]{:S(2)}) %collective-permute-start.8) | collective-permute-done | bytes 147488 | tf_op jit(solution)/shard_map/ppermute | solution.py:345
  40.1 7.2 %collective-permute-start.13 = (bf16[9,32,256]{2,1,0:T(8,128)(2,1)S(1)}, bf16[9,32,256]{2,1,0:T(8,128)(2,1)S(1)}, u32[]{:S(2)}, u32[]{:S(2)}) collective-permute-start(bf16[9,32,256]{2,1,0:T(8,128)(2,1)S(1)} %get-tuple-element.64), channel_id=1, source_target_pairs={{0,16},{4,20},{8,24},{12,28},{16,0},{20,4},{24,8},{28,12},{1,17},{... | collective-permute-start | bytes 442376 | tf_op jit(solution)/shard_map/ppermute | solution.py:345
  47.4 2.4 %mask.1 = bf16[72,64,256]{2,1,0:T(8,128)(2,1)S(1)} custom-call(s32[3]{0:T(128)S(1)} %pad_add_fusion.info_ref, bf16[72,256,256]{2,1,0:T(8,128)(2,1)} %mask_hbm.1), custom_call_target="tpu_custom_call" | custom-call | flops 1000000000 | tf_op jit(solution)/shard_map/mask/pallas_call | solution.py:481
  50.5 5.3 %collective-permute-done.15.arrived_ref = bf16[4,32,256]{2,1,0:T(8,128)(2,1)S(1)} collective-permute-done((bf16[4,32,256]{2,1,0:T(8,128)(2,1)S(1)}, bf16[4,32,256]{2,1,0:T(8,128)(2,1)S(1)}, u32[]{:S(2)}, u32[]{:S(2)}) %collective-permute-start.15) | collective-permute-done | bytes 65568 | tf_op jit(solution)/shard_map/ppermute | solution.py:345
  55.9 1.6 %collective-permute-start.10 = (bf16[27,32,256]{2,1,0:T(8,128)(2,1)S(1)}, bf16[27,32,256]{2,1,0:T(8,128)(2,1)S(1)}, u32[]{:S(2)}, u32[]{:S(2)}) collective-permute-start(bf16[27,32,256]{2,1,0:T(8,128)(2,1)S(1)} %join.4), channel_id=1, source_target_pairs={{0,2},{1,3},{2,0},{3,1},{4,6},{5,7},{6,4},{7,5},{8,10},{9,11},{10,... | collective-permute-start | bytes 1327112 | tf_op jit(solution)/shard_map/ppermute | solution.py:345
  57.5 3.6 %collective-permute-done.16.arrived_ref = bf16[4,32,256]{2,1,0:T(8,128)(2,1)S(1)} collective-permute-done((bf16[4,32,256]{2,1,0:T(8,128)(2,1)S(1)}, bf16[4,32,256]{2,1,0:T(8,128)(2,1)S(1)}, u32[]{:S(2)}, u32[]{:S(2)}) %collective-permute-start.16) | collective-permute-done | bytes 65568 | tf_op jit(solution)/shard_map/ppermute | solution.py:345
  63.2 2.5 %collective-permute-done.10 = bf16[27,32,256]{2,1,0:T(8,128)(2,1)S(1)} collective-permute-done((bf16[27,32,256]{2,1,0:T(8,128)(2,1)S(1)}, bf16[27,32,256]{2,1,0:T(8,128)(2,1)S(1)}, u32[]{:S(2)}, u32[]{:S(2)}) %collective-permute-start.10) | collective-permute-done | bytes 442400 | tf_op jit(solution)/shard_map/ppermute | solution.py:345
  65.8 3.7 %collective-permute-done.17.arrived_ref = bf16[22,32,256]{2,1,0:T(8,128)(2,1)S(1)} collective-permute-done((bf16[22,32,256]{2,1,0:T(8,128)(2,1)S(1)}, bf16[22,32,256]{2,1,0:T(8,128)(2,1)S(1)}, u32[]{:S(2)}, u32[]{:S(2)}) %collective-permute-start.17) | collective-permute-done | bytes 360480 | tf_op jit(solution)/shard_map/ppermute | solution.py:345
  69.8 2.0 %collective-permute-done.18.refs_5_.arrived_ref = bf16[40,32,256]{2,1,0:T(8,128)(2,1)S(1)} collective-permute-done((bf16[40,32,256]{2,1,0:T(8,128)(2,1)S(1)}, bf16[40,32,256]{2,1,0:T(8,128)(2,1)S(1)}, u32[]{:S(2)}, u32[]{:S(2)}) %collective-permute-start.18) | collective-permute-done | bytes 655392 | tf_op jit(solution)/shard_map/ppermute | solution.py:345
  72.5 5.5 %start.1 = (f32[512,128]{1,0:T(8,128)S(1)}, bf16[72,128,256]{2,1,0:T(8,128)(2,1)S(1)}) custom-call(s32[72]{0:T(128)S(1)} %get-tuple-element.99.slot_ref, s32[72]{0:T(128)S(1)} %get-tuple-element.98.user_ref, s32[3]{0:T(128)S(1)} %pad_add_fusion.info_ref, f32[128,512]{1,0:T(8,128)S(1)} %get-tuple-element.54.x_ref, bf16[72,64,256]{2,1,0:T(8,128)(2,1)S(1)} %mask.1, ...), custom_call_target="tpu_custom_call" | custom-call | flops 8000000000 | tf_op jit(solution)/shard_map/start/pallas_call | solution.py:547
  78.1 5.6 %first.1 = (f32[4,64,512]{2,1,0:T(8,128)S(1)}, f32[512,128]{1,0:T(8,128)S(1)}, f32[512,128]{1,0:T(8,128)S(1)}) custom-call(s32[72]{0:T(128)S(1)} %get-tuple-element.99.slot_ref, s32[72]{0:T(128)S(1)} %get-tuple-element.98.user_ref, s32[3]{0:T(128)S(1)} %pad_add_fusion.info_ref, f32[128,512]{1,0:T(8,128)S(1)} %get-tuple-element.54.x_ref, ...), custom_call_target="tpu_custom_call" | custom-call | flops 8000000000 | tf_op jit(solution)/shard_map/first/pallas_call | solution.py:556
  85.7 5.8 %second.1 = (f32[4,32,512]{2,1,0:T(8,128)S(1)}, f32[32,128]{1,0:T(8,128)}) custom-call(s32[72]{0:T(128)S(1)} %get-tuple-element.99.slot_ref, s32[72]{0:T(128)S(1)} %get-tuple-element.98.user_ref, s32[3]{0:T(128)S(1)} %pad_add_fusion.info_ref, f32[512,128]{1,0:T(8,128)S(1)} %get-tuple-element.80.field_ref, f32[512,128]{1,0:T(8,128)S(1)} %get-tuple-element.81.first_ref, ...), custom_call_target="tpu_custom_call" | custom-call | flops 8000000000 | tf_op jit(solution)/shard_map/second/pallas_call | solution.py:564
  91.5 1.6 %collective-permute-start.24 = (f32[32,512]{1,0:T(8,128)S(1)}, f32[32,512]{1,0:T(8,128)S(1)}, u32[]{:S(2)}, u32[]{:S(2)}) collective-permute-start(f32[32,512]{1,0:T(8,128)S(1)} %get-tuple-element.90), channel_id=1, source_target_pairs={{0,3},{1,2},{2,1},{3,0},{4,7},{5,6},{6,5},{7,4},{8,11},{9,10},{10,... | collective-permute-start | bytes 196616 | tf_op jit(solution)/shard_map/ppermute | solution.py:345
  93.7 3.2 %all-to-all-start.1 = ((f32[32,1,128]{2,1,0:T(1,128)}), f32[32,1,128]{2,1,0:T(1,128)S(1)}, u32[]{:S(2)}, u32[]{:S(2)}) async-start(f32[32,1,128]{2,1,0:T(1,128)} %bitcast.12), calls=%async_computation.1 | async-start | bytes 32768 | tf_op jit(solution)/shard_map/all_to_all | solution.py:579
  97.4 6.5 %all-to-all-done.1 = f32[32,1,128]{2,1,0:T(1,128)S(1)} async-done(((f32[32,1,128]{2,1,0:T(1,128)}), f32[32,1,128]{2,1,0:T(1,128)S(1)}, u32[]{:S(2)}, u32[]{:S(2)}) %all-to-all-start.1) | async-done | bytes 16416 | tf_op jit(solution)/shard_map/all_to_all | solution.py:579
  104.0 2.0 %finish.1 = (f32[32,2048]{1,0:T(8,128)}, f32[32,2048]{1,0:T(8,128)}) custom-call(s32[3]{0:T(128)S(1)} %pad_add_fusion.info_ref, f32[32,128]{1,0:T(8,128)S(1)} %bitcast.31, f32[32,2048]{1,0:T(8,128)S(1)} %copy-done.1, f32[64,512]{1,0:T(8,128)S(1)} %get-tuple-element.89.refs_0_, f32[64,512]{1,0:T(8,128)S(1)} %collective-permute-done.19.refs_1_, ...), custom_call_target="tpu_custom_call" | custom-call | flops 1000000000 | tf_op jit(solution)/shard_map/finish/pallas_call | solution.py:582
  (69 shorter events, 19.2 us)
Async XLA Ops:
  3.1 10.9 %collective-permute-start = (bf16[32,3072]{1,0:T(8,128)(2,1)S(1)}, bf16[32,3072]{1,0:T(8,128)(2,1)S(1)}, u32[]{:S(2)}, u32[]{:S(2)}) collective-permute-start(bf16[32,3072]{1,0:T(8,128)(2,1)S(1)} %get-tuple-element.46), channel_id=1, source_target_pairs={{0,1},{1,0},{2,3},{3,2},{4,5},{5,4},{6,7},{7,6},{8,9},{9,8},{10,11... | collective-permute-start | bytes 589832 | tf_op jit(solution)/shard_map/ppermute | solution.py:345
  3.6 10.4 %collective-permute-start.1 = (bf16[32,3072]{1,0:T(8,128)(2,1)S(1)}, bf16[32,3072]{1,0:T(8,128)(2,1)S(1)}, u32[]{:S(2)}, u32[]{:S(2)}) collective-permute-start(bf16[32,3072]{1,0:T(8,128)(2,1)S(1)} %get-tuple-element.47), channel_id=1, source_target_pairs={{0,2},{1,3},{2,0},{3,1},{4,6},{5,7},{6,4},{7,5},{8,10},{9,11},{10,... | collective-permute-start | bytes 589832 | tf_op jit(solution)/shard_map/ppermute | solution.py:345
  6.2 9.4 %collective-permute-start.2 = (bf16[32,3072]{1,0:T(8,128)(2,1)S(1)}, bf16[32,3072]{1,0:T(8,128)(2,1)S(1)}, u32[]{:S(2)}, u32[]{:S(2)}) collective-permute-start(bf16[32,3072]{1,0:T(8,128)(2,1)S(1)} %get-tuple-element.48), channel_id=1, source_target_pairs={{0,3},{1,2},{2,1},{3,0},{4,7},{5,6},{6,5},{7,4},{8,11},{9,10},{10,... | collective-permute-start | bytes 589832 | tf_op jit(solution)/shard_map/ppermute | solution.py:345
  7.9 12.5 %all-to-all-start = ((s32[8,1,9]{2,1,0:T(1,128)}), s32[8,1,9]{2,1,0:T(1,128)S(1)}, u32[]{:S(2)}, u32[]{:S(2)}) async-start(s32[8,1,9]{2,1,0:T(1,128)} %bitcast.5), calls=%async_computation | async-start | bytes 8192 | tf_op jit(solution)/shard_map/all_to_all | solution.py:436
  22.2 9.6 %collective-permute-start.3 = (bf16[9,32,256]{2,1,0:T(8,128)(2,1)S(1)}, bf16[9,32,256]{2,1,0:T(8,128)(2,1)S(1)}, u32[]{:S(2)}, u32[]{:S(2)}) collective-permute-start(bf16[9,32,256]{2,1,0:T(8,128)(2,1)S(1)} %get-tuple-element.51), channel_id=1, source_target_pairs={{0,4},{4,0},{8,12},{12,8},{16,20},{20,16},{24,28},{28,24},{1,5},{5... | collective-permute-start | bytes 442376 | tf_op jit(solution)/shard_map/ppermute | solution.py:345
  22.8 9.0 %collective-permute-start.4 = (bf16[9,32,256]{2,1,0:T(8,128)(2,1)S(1)}, bf16[9,32,256]{2,1,0:T(8,128)(2,1)S(1)}, u32[]{:S(2)}, u32[]{:S(2)}) collective-permute-start(bf16[9,32,256]{2,1,0:T(8,128)(2,1)S(1)} %get-tuple-element.52), channel_id=1, source_target_pairs={{0,12},{4,8},{8,4},{12,0},{16,28},{20,24},{24,20},{28,16},{1,13},{... | collective-permute-start | bytes 442376 | tf_op jit(solution)/shard_map/ppermute | solution.py:345
  24.3 25.5 %collective-permute-start.7 = (bf16[9,32,256]{2,1,0:T(8,128)(2,1)S(1)}, bf16[9,32,256]{2,1,0:T(8,128)(2,1)S(1)}, u32[]{:S(2)}, u32[]{:S(2)}) collective-permute-start(bf16[9,32,256]{2,1,0:T(8,128)(2,1)S(1)} %get-tuple-element.56), channel_id=1, source_target_pairs={{0,8},{4,12},{8,0},{12,4},{16,24},{20,28},{24,16},{28,20},{1,9},{5... | collective-permute-start | bytes 442376 | tf_op jit(solution)/shard_map/ppermute | solution.py:345
  25.8 13.6 %collective-permute-start.8 = (bf16[9,32,256]{2,1,0:T(8,128)(2,1)S(1)}, bf16[9,32,256]{2,1,0:T(8,128)(2,1)S(1)}, u32[]{:S(2)}, u32[]{:S(2)}) collective-permute-start(bf16[9,32,256]{2,1,0:T(8,128)(2,1)S(1)} %get-tuple-element.58), channel_id=1, source_target_pairs={{0,20},{4,16},{8,28},{12,24},{16,4},{20,0},{24,12},{28,8},{1,21},{... | collective-permute-start | bytes 442376 | tf_op jit(solution)/shard_map/ppermute | solution.py:345
  26.3 13.1 %collective-permute-start.9 = (bf16[9,32,256]{2,1,0:T(8,128)(2,1)S(1)}, bf16[9,32,256]{2,1,0:T(8,128)(2,1)S(1)}, u32[]{:S(2)}, u32[]{:S(2)}) collective-permute-start(bf16[9,32,256]{2,1,0:T(8,128)(2,1)S(1)} %get-tuple-element.59), channel_id=1, source_target_pairs={{0,24},{4,28},{8,16},{12,20},{16,8},{20,12},{24,0},{28,4},{1,25},{... | collective-permute-start | bytes 442376 | tf_op jit(solution)/shard_map/ppermute | solution.py:345
  32.4 23.3 %collective-permute-start.5 = (bf16[27,32,256]{2,1,0:T(8,128)(2,1)S(1)}, bf16[27,32,256]{2,1,0:T(8,128)(2,1)S(1)}, u32[]{:S(2)}, u32[]{:S(2)}) collective-permute-start(bf16[27,32,256]{2,1,0:T(8,128)(2,1)S(1)} %join.3), channel_id=1, source_target_pairs={{0,2},{1,3},{2,0},{3,1},{4,6},{5,7},{6,4},{7,5},{8,10},{9,11},{10,... | collective-permute-start | bytes 1327112 | tf_op jit(solution)/shard_map/ppermute | solution.py:345
  35.2 14.5 %collective-permute-start.14 = (bf16[4,32,256]{2,1,0:T(8,128)(2,1)S(1)}, bf16[4,32,256]{2,1,0:T(8,128)(2,1)S(1)}, u32[]{:S(2)}, u32[]{:S(2)}) collective-permute-start(bf16[4,32,256]{2,1,0:T(8,128)(2,1)S(1)} %get-tuple-element.66), channel_id=1, source_target_pairs={{0,4},{4,0},{8,12},{12,8},{16,20},{20,16},{24,28},{28,24},{1,5},{5... | collective-permute-start | bytes 196616 | tf_op jit(solution)/shard_map/ppermute | solution.py:345
  39.4 21.7 %collective-permute-start.12 = (bf16[9,32,256]{2,1,0:T(8,128)(2,1)S(1)}, bf16[9,32,256]{2,1,0:T(8,128)(2,1)S(1)}, u32[]{:S(2)}, u32[]{:S(2)}) collective-permute-start(bf16[9,32,256]{2,1,0:T(8,128)(2,1)S(1)} %get-tuple-element.62), channel_id=1, source_target_pairs={{0,28},{4,24},{8,20},{12,16},{16,12},{20,8},{24,4},{28,0},{1,29},{... | collective-permute-start | bytes 442376 | tf_op jit(solution)/shard_map/ppermute | solution.py:345
  40.1 21.0 %collective-permute-start.13 = (bf16[9,32,256]{2,1,0:T(8,128)(2,1)S(1)}, bf16[9,32,256]{2,1,0:T(8,128)(2,1)S(1)}, u32[]{:S(2)}, u32[]{:S(2)}) collective-permute-start(bf16[9,32,256]{2,1,0:T(8,128)(2,1)S(1)} %get-tuple-element.64), channel_id=1, source_target_pairs={{0,16},{4,20},{8,24},{12,28},{16,0},{20,4},{24,8},{28,12},{1,17},{... | collective-permute-start | bytes 442376 | tf_op jit(solution)/shard_map/ppermute | solution.py:345
  49.8 6.0 %collective-permute-start.15 = (bf16[4,32,256]{2,1,0:T(8,128)(2,1)S(1)}, bf16[4,32,256]{2,1,0:T(8,128)(2,1)S(1)}, u32[]{:S(2)}, u32[]{:S(2)}) collective-permute-start(bf16[4,32,256]{2,1,0:T(8,128)(2,1)S(1)} %get-tuple-element.69), channel_id=1, source_target_pairs={{0,8},{4,12},{8,0},{12,4},{16,24},{20,28},{24,16},{28,20},{1,9},{5... | collective-permute-start | bytes 196616 | tf_op jit(solution)/shard_map/ppermute | solution.py:345
  55.9 5.2 %collective-permute-start.16 = (bf16[4,32,256]{2,1,0:T(8,128)(2,1)S(1)}, bf16[4,32,256]{2,1,0:T(8,128)(2,1)S(1)}, u32[]{:S(2)}, u32[]{:S(2)}) collective-permute-start(bf16[4,32,256]{2,1,0:T(8,128)(2,1)S(1)} %get-tuple-element.72), channel_id=1, source_target_pairs={{0,16},{4,20},{8,24},{12,28},{16,0},{20,4},{24,8},{28,12},{1,17},{... | collective-permute-start | bytes 196616 | tf_op jit(solution)/shard_map/ppermute | solution.py:345
  55.9 9.8 %collective-permute-start.10 = (bf16[27,32,256]{2,1,0:T(8,128)(2,1)S(1)}, bf16[27,32,256]{2,1,0:T(8,128)(2,1)S(1)}, u32[]{:S(2)}, u32[]{:S(2)}) collective-permute-start(bf16[27,32,256]{2,1,0:T(8,128)(2,1)S(1)} %join.4), channel_id=1, source_target_pairs={{0,2},{1,3},{2,0},{3,1},{4,6},{5,7},{6,4},{7,5},{8,10},{9,11},{10,... | collective-permute-start | bytes 1327112 | tf_op jit(solution)/shard_map/ppermute | solution.py:345
  61.7 7.9 %collective-permute-start.17 = (bf16[22,32,256]{2,1,0:T(8,128)(2,1)S(1)}, bf16[22,32,256]{2,1,0:T(8,128)(2,1)S(1)}, u32[]{:S(2)}, u32[]{:S(2)}) collective-permute-start(bf16[22,32,256]{2,1,0:T(8,128)(2,1)S(1)} %join.5), channel_id=1, source_target_pairs={{0,2},{1,3},{2,0},{3,1},{4,6},{5,7},{6,4},{7,5},{8,10},{9,11},{10,... | collective-permute-start | bytes 1081352 | tf_op jit(solution)/shard_map/ppermute | solution.py:345
  63.2 9.3 %collective-permute-start.6 = (bf16[54,32,256]{2,1,0:T(8,128)(2,1)S(1)}, bf16[54,32,256]{2,1,0:T(8,128)(2,1)S(1)}, u32[]{:S(2)}, u32[]{:S(2)}) collective-permute-start(bf16[54,32,256]{2,1,0:T(8,128)(2,1)S(1)} %pad_maximum_fusion.refs_0_), channel_id=1, source_target_pairs={{0,1},{1,0},{2,3},{3,2},{4,5},{5,4},{6,7},{7,6},{8,9},{9,8},{10,11... | collective-permute-start | bytes 2654216 | tf_op jit(solution)/shard_map/ppermute | solution.py:345
  65.7 6.8 %collective-permute-start.11 = (bf16[54,32,256]{2,1,0:T(8,128)(2,1)S(1)}, bf16[54,32,256]{2,1,0:T(8,128)(2,1)S(1)}, u32[]{:S(2)}, u32[]{:S(2)}) collective-permute-start(bf16[54,32,256]{2,1,0:T(8,128)(2,1)S(1)} %constant_dynamic-update-slice_fusion.refs_2_), channel_id=1, source_target_pairs={{0,1},{1,0},{2,3},{3,2},{4,5},{5,4},{6,7},{7,6},{8,9},{9,8},{10,11... | collective-permute-start | bytes 2654216 | tf_op jit(solution)/shard_map/ppermute | solution.py:345
  83.8 9.9 %collective-permute-start.21 = (f32[64,512]{1,0:T(8,128)S(1)}, f32[64,512]{1,0:T(8,128)S(1)}, u32[]{:S(2)}, u32[]{:S(2)}) collective-permute-start(f32[64,512]{1,0:T(8,128)S(1)} %get-tuple-element.86), channel_id=1, source_target_pairs={{0,3},{1,2},{2,1},{3,0},{4,7},{5,6},{6,5},{7,4},{8,11},{9,10},{10,... | collective-permute-start | bytes 393224 | tf_op jit(solution)/shard_map/ppermute | solution.py:345
  85.1 8.6 %collective-permute-start.20 = (f32[64,512]{1,0:T(8,128)S(1)}, f32[64,512]{1,0:T(8,128)S(1)}, u32[]{:S(2)}, u32[]{:S(2)}) collective-permute-start(f32[64,512]{1,0:T(8,128)S(1)} %get-tuple-element.87), channel_id=1, source_target_pairs={{0,2},{1,3},{2,0},{3,1},{4,6},{5,7},{6,4},{7,5},{8,10},{9,11},{10,... | collective-permute-start | bytes 393224 | tf_op jit(solution)/shard_map/ppermute | solution.py:345
  85.6 8.1 %collective-permute-start.19 = (f32[64,512]{1,0:T(8,128)S(1)}, f32[64,512]{1,0:T(8,128)S(1)}, u32[]{:S(2)}, u32[]{:S(2)}) collective-permute-start(f32[64,512]{1,0:T(8,128)S(1)} %get-tuple-element.88), channel_id=1, source_target_pairs={{0,1},{1,0},{2,3},{3,2},{4,5},{5,4},{6,7},{7,6},{8,9},{9,8},{10,11... | collective-permute-start | bytes 393224 | tf_op jit(solution)/shard_map/ppermute | solution.py:345
  91.5 5.3 %collective-permute-start.24 = (f32[32,512]{1,0:T(8,128)S(1)}, f32[32,512]{1,0:T(8,128)S(1)}, u32[]{:S(2)}, u32[]{:S(2)}) collective-permute-start(f32[32,512]{1,0:T(8,128)S(1)} %get-tuple-element.90), channel_id=1, source_target_pairs={{0,3},{1,2},{2,1},{3,0},{4,7},{5,6},{6,5},{7,4},{8,11},{9,10},{10,... | collective-permute-start | bytes 196616 | tf_op jit(solution)/shard_map/ppermute | solution.py:345
  93.7 10.2 %all-to-all-start.1 = ((f32[32,1,128]{2,1,0:T(1,128)}), f32[32,1,128]{2,1,0:T(1,128)S(1)}, u32[]{:S(2)}, u32[]{:S(2)}) async-start(f32[32,1,128]{2,1,0:T(1,128)} %bitcast.12), calls=%async_computation.1 | async-start | bytes 32768 | tf_op jit(solution)/shard_map/all_to_all | solution.py:579
  (6 other events, 38.1 us)

commit v5 on v3

--- a/solution.py
+++ b/solution.py
@@ -147,23 +147,26 @@
 
 
 def load(p_hl, vector):
-    blocks, both, width = p_hl.shape
-    share = both // 2
+    blocks, share, both = p_hl.shape
+    width = both // 2
     high, low = split(vector)
-    p_hl[:, :share] = high.reshape(blocks, share, width)
-    p_hl[:, share:] = low.reshape(blocks, share, width)
+    p_hl[:, :, :width] = high.reshape(blocks, share, width)
+    p_hl[:, :, width:] = low.reshape(blocks, share, width)
 
 
 def dense(p_hl, gram_ref, vector):
-    blocks, both, width = p_hl.shape
-    gram_high, gram_low = split(gram_ref[...])
-    product = matmul(
-        p_hl[...].reshape(blocks * both, width),
-        jnp.concatenate([gram_high, gram_low], axis=1),
-    ).reshape(blocks, 2, both // 2, 2 * width)
-    product = product[:, 0] + product[:, 1]
-    product = product[:, :, :width] + product[:, :, width:]
-    return product.reshape(vector.shape) + ridge * vector
+    blocks, share, both = p_hl.shape
+    width = both // 2
+    high, low = split(gram_ref[...])
+    table = jnp.concatenate(
+        [
+            jnp.concatenate([high, low], axis=1),
+            jnp.concatenate([high, jnp.zeros_like(low)], axis=1),
+        ],
+        axis=0,
+    )
+    product = matmul(p_hl[...].reshape(blocks * share, both), table)
+    return product[:, :width] + product[:, width:] + ridge * vector
 
 
 def sparse(starting, slot_ref, user_ref, y, mask, p_hl, acc, held):
@@ -174,8 +177,8 @@
     def score(group):
         for j in range(UNROLL):
             t = group * UNROLL + j
-            scores = matmul(p_hl[user_ref[t]], y[slot_ref[t]])
-            scores = scores[:share] + scores[share:]
+            tile = y[slot_ref[t]]
+            scores = matmul(p_hl[user_ref[t]], jnp.concatenate([tile, tile], axis=0))
             if starting:
                 scores = (1.0 + confidence) - confidence * scores
             high, low = split(mask[t].astype(f32) * scores)
@@ -514,18 +517,16 @@
         arrived = flip(own, "cols", 2)
         gram, carried = add(gram, arrived)
         own = join(own[: 3 * capacity], arrived[: 3 * capacity], carried)
-        arrived = flip(own, "cols", 1)
+        arrived = flip(after(own, mask), "cols", 1)
         gram, carried = add(gram, arrived)
         pieces += [own, arrived]
 
         own = gather(got[7], got[4])
-        arrived = flip(own, "cols", 2)
-        for bit in (1, 2, 4):
-            gram, carried = add(gram, flip(carried, "rows", bit))
-            if bit == 1:
-                own = after(own, carried, mask)
-        own = join(own, arrived)
-        pieces += [own, flip(own, "cols", 1)]
+        own = join(own, flip(own, "cols", 2))
+        gram, carried = add(gram, flip(carried, "rows", 1))
+        pieces += [own, flip(after(own, carried), "cols", 1)]
+        gram, carried = add(gram, flip(carried, "rows", 2))
+        arrived = flip(carried, "rows", 4)
     else:
         slots = (row_devs * capacity,)
         gram = add_all(gram)
@@ -536,7 +537,7 @@
     vector = jax.ShapeDtypeStruct((own_users, width), f32)
     held = jax.ShapeDtypeStruct((row_devs * capacity, width, side), bf16)
     work = [
-        pltpu.VMEM((user_blocks, 2 * share, width), bf16),
+        pltpu.VMEM((user_blocks, share, 2 * width), bf16),
         pltpu.VMEM((user_blocks, share, width), f32),
         pltpu.VMEM((2, UNROLL, 2 * share, side), bf16),
     ]
@@ -549,6 +550,8 @@
         work + [pltpu.SemaphoreType.DMA((n_cols * len(slots),))],
         8 * 10**9,
     )(*lists, start, mask, *pieces)
+    if direct:
+        gram, _ = add(gram, after(arrived, part))
     pair = jax.ShapeDtypeStruct((n_cols, 2 * col_width, own_users), f32)
     pair_sent, field, first = call(
         first_kernel,

time: 108 us -> 104 us (0.963)
  waiting for transfers between devices: 45.7 us -> 40 us
    ppermute x25, waiting for transfers between devices: 33.9 us -> 28.2 us  [flip(): return lax.ppermute(value, axis, [(i, i ^ bit) for i in range(size)])]
  transfers between devices with their start and end apart: 27 -> 27, of which waited for: 14 -> 12; matrix products, arithmetic and copies ran while one was open for 2% -> 2% of each run, Pallas kernels for 11% -> 16%
where the time goes in v5:
time: 104 us; the launch traced here: 103 us
  waiting for transfers between devices  40 us (38%)
  starting transfers between devices  31.1 us (30%)
  Pallas kernels  27.4 us (26%)
  local copies, waits for them, and re-layouts  1.85 us (2%)
  between operations  1.54 us (1%)
  other arithmetic  1.34 us (1%)
    ppermute x25, waiting for transfers between devices, flip(): return lax.ppermute(value, axis, [(i, i ^ bit) for i in range(size)])  28.2 us
    ppermute x25, starting transfers between devices, flip(): return lax.ppermute(value, axis, [(i, i ^ bit) for i in range(size)])  20 us
    all_to_all x1, waiting for transfers between devices, on_device(): lax.all_to_all(dots, ('rows', 'cols'), split_axis=0, concat_axis=0, tiled...  7.04 us
    all_to_all x1, starting transfers between devices, on_device(): lax.all_to_all(requests, 'rows', split_axis=0, concat_axis=0, tiled=True)  6.07 us
    pallas_call x1, Pallas kernels, on_device(): call(second_kernel, [jax.ShapeDtypeStruct((n_cols, col_width, own_users),...  5.84 us
    pallas_call x1, Pallas kernels, on_device(): call(functools.partial(start_kernel, n_cols, slots), [vector, held], [sme...  5.7 us
    pallas_call x1, Pallas kernels, on_device(): call(first_kernel, [pair, vector, vector], [smem] * 3 + [vmem] * 5, 'firs...  5.38 us
    all_to_all x1, starting transfers between devices, on_device(): lax.all_to_all(dots, ('rows', 'cols'), split_axis=0, concat_axis=0, tiled...  5.01 us
  transfers between devices with their start and end apart: 27, of which 12 were waited for; matrix products, arithmetic and copies ran while one was open for 2% of the time, Pallas kernels for 16%

profile of v5, /device:TPU:0, one launch (start us, length us, event | category | flops | bytes accessed | tf_op | source)
XLA Modules:
  0.0 103.2 jit_solution(8479216262707824773)
XLA Ops:
  1.4 1.7 %prepare.1 = (bf16[32,3072]{1,0:T(8,128)(2,1)S(1)}, bf16[32,3072]{1,0:T(8,128)(2,1)S(1)}, bf16[32,3072]{1,0:T(8,128)(2,1)S(1)}, bf16[32,3072]{1,0:T(8,128)(2,1)S(1)}) custom-call(s32[3]{0:T(128)S(1)} %pad_add_fusion.info_ref, f32[32,2048]{1,0:T(8,128)} %x_ref.1, bf16[32,8192]{1,0:T(8,128)(2,1)} %items_ref.1), custom_call_target="tpu_custom_call" | custom-call | flops 1000000000 | tf_op jit(solution)/shard_map/prepare/pallas_call | solution.py:406
  3.6 2.6 %collective-permute-start.1 = (bf16[32,3072]{1,0:T(8,128)(2,1)S(1)}, bf16[32,3072]{1,0:T(8,128)(2,1)S(1)}, u32[]{:S(2)}, u32[]{:S(2)}) collective-permute-start(bf16[32,3072]{1,0:T(8,128)(2,1)S(1)} %get-tuple-element.46), channel_id=1, source_target_pairs={{0,2},{1,3},{2,0},{3,1},{4,6},{5,7},{6,4},{7,5},{8,10},{9,11},{10,... | collective-permute-start | bytes 589832 | tf_op jit(solution)/shard_map/ppermute | solution.py:348
  7.9 6.1 %all-to-all-start = ((s32[8,1,9]{2,1,0:T(1,128)}), s32[8,1,9]{2,1,0:T(1,128)S(1)}, u32[]{:S(2)}, u32[]{:S(2)}) async-start(s32[8,1,9]{2,1,0:T(1,128)} %bitcast.5), calls=%async_computation | async-start | bytes 8192 | tf_op jit(solution)/shard_map/all_to_all | solution.py:439
  14.0 1.6 %collective-permute-done.2.refs_3_ = bf16[32,3072]{1,0:T(8,128)(2,1)S(1)} collective-permute-done((bf16[32,3072]{1,0:T(8,128)(2,1)S(1)}, bf16[32,3072]{1,0:T(8,128)(2,1)S(1)}, u32[]{:S(2)}, u32[]{:S(2)}) %collective-permute-start.2) | collective-permute-done | bytes 196640 | tf_op jit(solution)/shard_map/ppermute | solution.py:348
  15.6 4.8 %all-to-all-done = s32[8,1,9]{2,1,0:T(1,128)S(1)} async-done(((s32[8,1,9]{2,1,0:T(1,128)}), s32[8,1,9]{2,1,0:T(1,128)S(1)}, u32[]{:S(2)}, u32[]{:S(2)}) %all-to-all-start) | async-done | bytes 320 | tf_op jit(solution)/shard_map/all_to_all | solution.py:439
  24.3 1.5 %collective-permute-start.7 = (bf16[9,32,256]{2,1,0:T(8,128)(2,1)S(1)}, bf16[9,32,256]{2,1,0:T(8,128)(2,1)S(1)}, u32[]{:S(2)}, u32[]{:S(2)}) collective-permute-start(bf16[9,32,256]{2,1,0:T(8,128)(2,1)S(1)} %get-tuple-element.54), channel_id=1, source_target_pairs={{0,8},{4,12},{8,0},{12,4},{16,24},{20,28},{24,16},{28,20},{1,9},{5... | collective-permute-start | bytes 442376 | tf_op jit(solution)/shard_map/ppermute | solution.py:348
  26.3 2.4 %collective-permute-start.9 = (bf16[9,32,256]{2,1,0:T(8,128)(2,1)S(1)}, bf16[9,32,256]{2,1,0:T(8,128)(2,1)S(1)}, u32[]{:S(2)}, u32[]{:S(2)}) collective-permute-start(bf16[9,32,256]{2,1,0:T(8,128)(2,1)S(1)} %get-tuple-element.56), channel_id=1, source_target_pairs={{0,24},{4,28},{8,16},{12,20},{16,8},{20,12},{24,0},{28,4},{1,25},{... | collective-permute-start | bytes 442376 | tf_op jit(solution)/shard_map/ppermute | solution.py:348
  28.7 3.1 %collective-permute-done.3.refs_1_ = bf16[9,32,256]{2,1,0:T(8,128)(2,1)S(1)} collective-permute-done((bf16[9,32,256]{2,1,0:T(8,128)(2,1)S(1)}, bf16[9,32,256]{2,1,0:T(8,128)(2,1)S(1)}, u32[]{:S(2)}, u32[]{:S(2)}) %collective-permute-start.3) | collective-permute-done | bytes 147488 | tf_op jit(solution)/shard_map/ppermute | solution.py:348
  32.4 1.6 %collective-permute-start.5 = (bf16[27,32,256]{2,1,0:T(8,128)(2,1)S(1)}, bf16[27,32,256]{2,1,0:T(8,128)(2,1)S(1)}, u32[]{:S(2)}, u32[]{:S(2)}) collective-permute-start(bf16[27,32,256]{2,1,0:T(8,128)(2,1)S(1)} %join.3), channel_id=1, source_target_pairs={{0,2},{1,3},{2,0},{3,1},{4,6},{5,7},{6,4},{7,5},{8,10},{9,11},{10,... | collective-permute-start | bytes 1327112 | tf_op jit(solution)/shard_map/ppermute | solution.py:348
  35.4 3.9 %collective-permute-done.8.refs_1_ = bf16[9,32,256]{2,1,0:T(8,128)(2,1)S(1)} collective-permute-done((bf16[9,32,256]{2,1,0:T(8,128)(2,1)S(1)}, bf16[9,32,256]{2,1,0:T(8,128)(2,1)S(1)}, u32[]{:S(2)}, u32[]{:S(2)}) %collective-permute-start.8) | collective-permute-done | bytes 147488 | tf_op jit(solution)/shard_map/ppermute | solution.py:348
  40.0 2.7 %collective-permute-done.5 = bf16[27,32,256]{2,1,0:T(8,128)(2,1)S(1)} collective-permute-done((bf16[27,32,256]{2,1,0:T(8,128)(2,1)S(1)}, bf16[27,32,256]{2,1,0:T(8,128)(2,1)S(1)}, u32[]{:S(2)}, u32[]{:S(2)}) %collective-permute-start.5) | collective-permute-done | bytes 442400 | tf_op jit(solution)/shard_map/ppermute | solution.py:348
  42.7 1.6 %collective-permute-start.10 = (bf16[31,32,256]{2,1,0:T(8,128)(2,1)S(1)}, bf16[31,32,256]{2,1,0:T(8,128)(2,1)S(1)}, u32[]{:S(2)}, u32[]{:S(2)}) collective-permute-start(bf16[31,32,256]{2,1,0:T(8,128)(2,1)S(1)} %join.4), channel_id=1, source_target_pairs={{0,2},{1,3},{2,0},{3,1},{4,6},{5,7},{6,4},{7,5},{8,10},{9,11},{10,... | collective-permute-start | bytes 1523720 | tf_op jit(solution)/shard_map/ppermute | solution.py:348
  44.3 1.9 %collective-permute-start.12 = (bf16[9,32,256]{2,1,0:T(8,128)(2,1)S(1)}, bf16[9,32,256]{2,1,0:T(8,128)(2,1)S(1)}, u32[]{:S(2)}, u32[]{:S(2)}) collective-permute-start(bf16[9,32,256]{2,1,0:T(8,128)(2,1)S(1)} %get-tuple-element.63), channel_id=1, source_target_pairs={{0,28},{4,24},{8,20},{12,16},{16,12},{20,8},{24,4},{28,0},{1,29},{... | collective-permute-start | bytes 442376 | tf_op jit(solution)/shard_map/ppermute | solution.py:348
  46.1 2.3 %mask.1 = bf16[72,64,256]{2,1,0:T(8,128)(2,1)S(1)} custom-call(s32[3]{0:T(128)S(1)} %pad_add_fusion.info_ref, bf16[72,256,256]{2,1,0:T(8,128)(2,1)} %mask_hbm.1), custom_call_target="tpu_custom_call" | custom-call | flops 1000000000 | tf_op jit(solution)/shard_map/mask/pallas_call | solution.py:484
  48.5 3.3 %collective-permute-done.10.arrived_ref = bf16[31,32,256]{2,1,0:T(8,128)(2,1)S(1)} collective-permute-done((bf16[31,32,256]{2,1,0:T(8,128)(2,1)S(1)}, bf16[31,32,256]{2,1,0:T(8,128)(2,1)S(1)}, u32[]{:S(2)}, u32[]{:S(2)}) %collective-permute-start.10) | collective-permute-done | bytes 507936 | tf_op jit(solution)/shard_map/ppermute | solution.py:348
  52.2 3.1 %collective-permute-done.13.refs_1_ = bf16[9,32,256]{2,1,0:T(8,128)(2,1)S(1)} collective-permute-done((bf16[9,32,256]{2,1,0:T(8,128)(2,1)S(1)}, bf16[9,32,256]{2,1,0:T(8,128)(2,1)S(1)}, u32[]{:S(2)}, u32[]{:S(2)}) %collective-permute-start.13) | collective-permute-done | bytes 147488 | tf_op jit(solution)/shard_map/ppermute | solution.py:348
  56.7 5.8 %collective-permute-done.14 = bf16[18,32,256]{2,1,0:T(8,128)(2,1)S(1)} collective-permute-done((bf16[18,32,256]{2,1,0:T(8,128)(2,1)S(1)}, bf16[18,32,256]{2,1,0:T(8,128)(2,1)S(1)}, u32[]{:S(2)}, u32[]{:S(2)}) %collective-permute-start.14) | collective-permute-done | bytes 294944 | tf_op jit(solution)/shard_map/ppermute | solution.py:348
  62.8 4.4 %collective-permute-done.17.arrived_ref = bf16[4,32,256]{2,1,0:T(8,128)(2,1)S(1)} collective-permute-done((bf16[4,32,256]{2,1,0:T(8,128)(2,1)S(1)}, bf16[4,32,256]{2,1,0:T(8,128)(2,1)S(1)}, u32[]{:S(2)}, u32[]{:S(2)}) %collective-permute-start.17) | collective-permute-done | bytes 65568 | tf_op jit(solution)/shard_map/ppermute | solution.py:348
  67.6 5.7 %start.1 = (f32[512,128]{1,0:T(8,128)S(1)}, bf16[72,128,256]{2,1,0:T(8,128)(2,1)S(1)}) custom-call(s32[72]{0:T(128)S(1)} %get-tuple-element.97.slot_ref, s32[72]{0:T(128)S(1)} %get-tuple-element.96.user_ref, s32[3]{0:T(128)S(1)} %pad_add_fusion.info_ref, f32[128,512]{1,0:T(8,128)S(1)} %get-tuple-element.51.x_ref, bf16[72,64,256]{2,1,0:T(8,128)(2,1)S(1)} %mask.1, ...), custom_call_target="tpu_custom_call" | custom-call | flops 8000000000 | tf_op jit(solution)/shard_map/start/pallas_call | solution.py:545
  73.9 5.4 %first.1 = (f32[4,64,512]{2,1,0:T(8,128)S(1)}, f32[512,128]{1,0:T(8,128)S(1)}, f32[512,128]{1,0:T(8,128)S(1)}) custom-call(s32[72]{0:T(128)S(1)} %get-tuple-element.97.slot_ref, s32[72]{0:T(128)S(1)} %get-tuple-element.96.user_ref, s32[3]{0:T(128)S(1)} %pad_add_fusion.info_ref, f32[128,512]{1,0:T(8,128)S(1)} %get-tuple-element.51.x_ref, ...), custom_call_target="tpu_custom_call" | custom-call | flops 8000000000 | tf_op jit(solution)/shard_map/first/pallas_call | solution.py:556
  81.3 5.8 %second.1 = (f32[4,32,512]{2,1,0:T(8,128)S(1)}, f32[32,128]{1,0:T(8,128)}) custom-call(s32[72]{0:T(128)S(1)} %get-tuple-element.97.slot_ref, s32[72]{0:T(128)S(1)} %get-tuple-element.96.user_ref, s32[3]{0:T(128)S(1)} %pad_add_fusion.info_ref, f32[512,128]{1,0:T(8,128)S(1)} %get-tuple-element.78.field_ref, f32[512,128]{1,0:T(8,128)S(1)} %get-tuple-element.79.first_ref, ...), custom_call_target="tpu_custom_call" | custom-call | flops 8000000000 | tf_op jit(solution)/shard_map/second/pallas_call | solution.py:564
  89.1 5.0 %all-to-all-start.1 = ((f32[32,1,128]{2,1,0:T(1,128)}), f32[32,1,128]{2,1,0:T(1,128)S(1)}, u32[]{:S(2)}, u32[]{:S(2)}) async-start(f32[32,1,128]{2,1,0:T(1,128)} %bitcast.12), calls=%async_computation.1 | async-start | bytes 32768 | tf_op jit(solution)/shard_map/all_to_all | solution.py:579
  94.2 7.0 %all-to-all-done.1 = f32[32,1,128]{2,1,0:T(1,128)S(1)} async-done(((f32[32,1,128]{2,1,0:T(1,128)}), f32[32,1,128]{2,1,0:T(1,128)S(1)}, u32[]{:S(2)}, u32[]{:S(2)}) %all-to-all-start.1) | async-done | bytes 16416 | tf_op jit(solution)/shard_map/all_to_all | solution.py:579
  101.2 2.0 %finish.1 = (f32[32,2048]{1,0:T(8,128)}, f32[32,2048]{1,0:T(8,128)}) custom-call(s32[3]{0:T(128)S(1)} %pad_add_fusion.info_ref, f32[32,128]{1,0:T(8,128)S(1)} %bitcast.31, f32[32,2048]{1,0:T(8,128)S(1)} %copy-done.1, f32[64,512]{1,0:T(8,128)S(1)} %get-tuple-element.87.refs_0_, f32[64,512]{1,0:T(8,128)S(1)} %collective-permute-done.19.refs_1_, ...), custom_call_target="tpu_custom_call" | custom-call | flops 1000000000 | tf_op jit(solution)/shard_map/finish/pallas_call | solution.py:582
  (68 shorter events, 16.5 us)
Async XLA Ops:
  3.1 10.9 %collective-permute-start = (bf16[32,3072]{1,0:T(8,128)(2,1)S(1)}, bf16[32,3072]{1,0:T(8,128)(2,1)S(1)}, u32[]{:S(2)}, u32[]{:S(2)}) collective-permute-start(bf16[32,3072]{1,0:T(8,128)(2,1)S(1)} %get-tuple-element.45), channel_id=1, source_target_pairs={{0,1},{1,0},{2,3},{3,2},{4,5},{5,4},{6,7},{7,6},{8,9},{9,8},{10,11... | collective-permute-start | bytes 589832 | tf_op jit(solution)/shard_map/ppermute | solution.py:348
  3.6 10.4 %collective-permute-start.1 = (bf16[32,3072]{1,0:T(8,128)(2,1)S(1)}, bf16[32,3072]{1,0:T(8,128)(2,1)S(1)}, u32[]{:S(2)}, u32[]{:S(2)}) collective-permute-start(bf16[32,3072]{1,0:T(8,128)(2,1)S(1)} %get-tuple-element.46), channel_id=1, source_target_pairs={{0,2},{1,3},{2,0},{3,1},{4,6},{5,7},{6,4},{7,5},{8,10},{9,11},{10,... | collective-permute-start | bytes 589832 | tf_op jit(solution)/shard_map/ppermute | solution.py:348
  6.2 9.4 %collective-permute-start.2 = (bf16[32,3072]{1,0:T(8,128)(2,1)S(1)}, bf16[32,3072]{1,0:T(8,128)(2,1)S(1)}, u32[]{:S(2)}, u32[]{:S(2)}) collective-permute-start(bf16[32,3072]{1,0:T(8,128)(2,1)S(1)} %get-tuple-element.47), channel_id=1, source_target_pairs={{0,3},{1,2},{2,1},{3,0},{4,7},{5,6},{6,5},{7,4},{8,11},{9,10},{10,... | collective-permute-start | bytes 589832 | tf_op jit(solution)/shard_map/ppermute | solution.py:348
  7.9 12.5 %all-to-all-start = ((s32[8,1,9]{2,1,0:T(1,128)}), s32[8,1,9]{2,1,0:T(1,128)S(1)}, u32[]{:S(2)}, u32[]{:S(2)}) async-start(s32[8,1,9]{2,1,0:T(1,128)} %bitcast.5), calls=%async_computation | async-start | bytes 8192 | tf_op jit(solution)/shard_map/all_to_all | solution.py:439
  22.2 9.6 %collective-permute-start.3 = (bf16[9,32,256]{2,1,0:T(8,128)(2,1)S(1)}, bf16[9,32,256]{2,1,0:T(8,128)(2,1)S(1)}, u32[]{:S(2)}, u32[]{:S(2)}) collective-permute-start(bf16[9,32,256]{2,1,0:T(8,128)(2,1)S(1)} %get-tuple-element.49), channel_id=1, source_target_pairs={{0,4},{4,0},{8,12},{12,8},{16,20},{20,16},{24,28},{28,24},{1,5},{5... | collective-permute-start | bytes 442376 | tf_op jit(solution)/shard_map/ppermute | solution.py:348
  22.8 9.0 %collective-permute-start.4 = (bf16[9,32,256]{2,1,0:T(8,128)(2,1)S(1)}, bf16[9,32,256]{2,1,0:T(8,128)(2,1)S(1)}, u32[]{:S(2)}, u32[]{:S(2)}) collective-permute-start(bf16[9,32,256]{2,1,0:T(8,128)(2,1)S(1)} %get-tuple-element.53), channel_id=1, source_target_pairs={{0,12},{4,8},{8,4},{12,0},{16,28},{20,24},{24,20},{28,16},{1,13},{... | collective-permute-start | bytes 442376 | tf_op jit(solution)/shard_map/ppermute | solution.py:348
  24.3 11.1 %collective-permute-start.7 = (bf16[9,32,256]{2,1,0:T(8,128)(2,1)S(1)}, bf16[9,32,256]{2,1,0:T(8,128)(2,1)S(1)}, u32[]{:S(2)}, u32[]{:S(2)}) collective-permute-start(bf16[9,32,256]{2,1,0:T(8,128)(2,1)S(1)} %get-tuple-element.54), channel_id=1, source_target_pairs={{0,8},{4,12},{8,0},{12,4},{16,24},{20,28},{24,16},{28,20},{1,9},{5... | collective-permute-start | bytes 442376 | tf_op jit(solution)/shard_map/ppermute | solution.py:348
  25.8 13.5 %collective-permute-start.8 = (bf16[9,32,256]{2,1,0:T(8,128)(2,1)S(1)}, bf16[9,32,256]{2,1,0:T(8,128)(2,1)S(1)}, u32[]{:S(2)}, u32[]{:S(2)}) collective-permute-start(bf16[9,32,256]{2,1,0:T(8,128)(2,1)S(1)} %get-tuple-element.55), channel_id=1, source_target_pairs={{0,20},{4,16},{8,28},{12,24},{16,4},{20,0},{24,12},{28,8},{1,21},{... | collective-permute-start | bytes 442376 | tf_op jit(solution)/shard_map/ppermute | solution.py:348
  26.3 13.0 %collective-permute-start.9 = (bf16[9,32,256]{2,1,0:T(8,128)(2,1)S(1)}, bf16[9,32,256]{2,1,0:T(8,128)(2,1)S(1)}, u32[]{:S(2)}, u32[]{:S(2)}) collective-permute-start(bf16[9,32,256]{2,1,0:T(8,128)(2,1)S(1)} %get-tuple-element.56), channel_id=1, source_target_pairs={{0,24},{4,28},{8,16},{12,20},{16,8},{20,12},{24,0},{28,4},{1,25},{... | collective-permute-start | bytes 442376 | tf_op jit(solution)/shard_map/ppermute | solution.py:348
  32.4 10.2 %collective-permute-start.5 = (bf16[27,32,256]{2,1,0:T(8,128)(2,1)S(1)}, bf16[27,32,256]{2,1,0:T(8,128)(2,1)S(1)}, u32[]{:S(2)}, u32[]{:S(2)}) collective-permute-start(bf16[27,32,256]{2,1,0:T(8,128)(2,1)S(1)} %join.3), channel_id=1, source_target_pairs={{0,2},{1,3},{2,0},{3,1},{4,6},{5,7},{6,4},{7,5},{8,10},{9,11},{10,... | collective-permute-start | bytes 1327112 | tf_op jit(solution)/shard_map/ppermute | solution.py:348
  42.7 9.1 %collective-permute-start.10 = (bf16[31,32,256]{2,1,0:T(8,128)(2,1)S(1)}, bf16[31,32,256]{2,1,0:T(8,128)(2,1)S(1)}, u32[]{:S(2)}, u32[]{:S(2)}) collective-permute-start(bf16[31,32,256]{2,1,0:T(8,128)(2,1)S(1)} %join.4), channel_id=1, source_target_pairs={{0,2},{1,3},{2,0},{3,1},{4,6},{5,7},{6,4},{7,5},{8,10},{9,11},{10,... | collective-permute-start | bytes 1523720 | tf_op jit(solution)/shard_map/ppermute | solution.py:348
  44.3 7.9 %collective-permute-start.12 = (bf16[9,32,256]{2,1,0:T(8,128)(2,1)S(1)}, bf16[9,32,256]{2,1,0:T(8,128)(2,1)S(1)}, u32[]{:S(2)}, u32[]{:S(2)}) collective-permute-start(bf16[9,32,256]{2,1,0:T(8,128)(2,1)S(1)} %get-tuple-element.63), channel_id=1, source_target_pairs={{0,28},{4,24},{8,20},{12,16},{16,12},{20,8},{24,4},{28,0},{1,29},{... | collective-permute-start | bytes 442376 | tf_op jit(solution)/shard_map/ppermute | solution.py:348
  46.1 9.2 %collective-permute-start.13 = (bf16[9,32,256]{2,1,0:T(8,128)(2,1)S(1)}, bf16[9,32,256]{2,1,0:T(8,128)(2,1)S(1)}, u32[]{:S(2)}, u32[]{:S(2)}) collective-permute-start(bf16[9,32,256]{2,1,0:T(8,128)(2,1)S(1)} %get-tuple-element.65), channel_id=1, source_target_pairs={{0,16},{4,20},{8,24},{12,28},{16,0},{20,4},{24,8},{28,12},{1,17},{... | collective-permute-start | bytes 442376 | tf_op jit(solution)/shard_map/ppermute | solution.py:348
  55.7 6.8 %collective-permute-start.14 = (bf16[18,32,256]{2,1,0:T(8,128)(2,1)S(1)}, bf16[18,32,256]{2,1,0:T(8,128)(2,1)S(1)}, u32[]{:S(2)}, u32[]{:S(2)}) collective-permute-start(bf16[18,32,256]{2,1,0:T(8,128)(2,1)S(1)} %join.5), channel_id=1, source_target_pairs={{0,2},{1,3},{2,0},{3,1},{4,6},{5,7},{6,4},{7,5},{8,10},{9,11},{10,... | collective-permute-start | bytes 884744 | tf_op jit(solution)/shard_map/ppermute | solution.py:348
  56.3 11.2 %collective-permute-start.6 = (bf16[54,32,256]{2,1,0:T(8,128)(2,1)S(1)}, bf16[54,32,256]{2,1,0:T(8,128)(2,1)S(1)}, u32[]{:S(2)}, u32[]{:S(2)}) collective-permute-start(bf16[54,32,256]{2,1,0:T(8,128)(2,1)S(1)} %pad_maximum_fusion.1.refs_0_), channel_id=1, source_target_pairs={{0,1},{1,0},{2,3},{3,2},{4,5},{5,4},{6,7},{7,6},{8,9},{9,8},{10,11... | collective-permute-start | bytes 2654216 | tf_op jit(solution)/shard_map/ppermute | solution.py:348
  56.4 6.2 %collective-permute-start.15 = (bf16[4,32,256]{2,1,0:T(8,128)(2,1)S(1)}, bf16[4,32,256]{2,1,0:T(8,128)(2,1)S(1)}, u32[]{:S(2)}, u32[]{:S(2)}) collective-permute-start(bf16[4,32,256]{2,1,0:T(8,128)(2,1)S(1)} %get-tuple-element.68), channel_id=1, source_target_pairs={{0,4},{4,0},{8,12},{12,8},{16,20},{20,16},{24,28},{28,24},{1,5},{5... | collective-permute-start | bytes 196616 | tf_op jit(solution)/shard_map/ppermute | solution.py:348
  67.2 6.1 %collective-permute-start.18 = (bf16[4,32,256]{2,1,0:T(8,128)(2,1)S(1)}, bf16[4,32,256]{2,1,0:T(8,128)(2,1)S(1)}, u32[]{:S(2)}, u32[]{:S(2)}) collective-permute-start(bf16[4,32,256]{2,1,0:T(8,128)(2,1)S(1)} %get-tuple-element.74), channel_id=1, source_target_pairs={{0,16},{4,20},{8,24},{12,28},{16,0},{20,4},{24,8},{28,12},{1,17},{... | collective-permute-start | bytes 196616 | tf_op jit(solution)/shard_map/ppermute | solution.py:348
  79.4 9.5 %collective-permute-start.21 = (f32[64,512]{1,0:T(8,128)S(1)}, f32[64,512]{1,0:T(8,128)S(1)}, u32[]{:S(2)}, u32[]{:S(2)}) collective-permute-start(f32[64,512]{1,0:T(8,128)S(1)} %get-tuple-element.84), channel_id=1, source_target_pairs={{0,3},{1,2},{2,1},{3,0},{4,7},{5,6},{6,5},{7,4},{8,11},{9,10},{10,... | collective-permute-start | bytes 393224 | tf_op jit(solution)/shard_map/ppermute | solution.py:348
  79.5 9.6 %collective-permute-start.20 = (f32[64,512]{1,0:T(8,128)S(1)}, f32[64,512]{1,0:T(8,128)S(1)}, u32[]{:S(2)}, u32[]{:S(2)}) collective-permute-start(f32[64,512]{1,0:T(8,128)S(1)} %get-tuple-element.85), channel_id=1, source_target_pairs={{0,2},{1,3},{2,0},{3,1},{4,6},{5,7},{6,4},{7,5},{8,10},{9,11},{10,... | collective-permute-start | bytes 393224 | tf_op jit(solution)/shard_map/ppermute | solution.py:348
  80.6 8.5 %collective-permute-start.19 = (f32[64,512]{1,0:T(8,128)S(1)}, f32[64,512]{1,0:T(8,128)S(1)}, u32[]{:S(2)}, u32[]{:S(2)}) collective-permute-start(f32[64,512]{1,0:T(8,128)S(1)} %get-tuple-element.86), channel_id=1, source_target_pairs={{0,1},{1,0},{2,3},{3,2},{4,5},{5,4},{6,7},{7,6},{8,9},{9,8},{10,11... | collective-permute-start | bytes 393224 | tf_op jit(solution)/shard_map/ppermute | solution.py:348
  87.2 7.0 %collective-permute-start.24 = (f32[32,512]{1,0:T(8,128)S(1)}, f32[32,512]{1,0:T(8,128)S(1)}, u32[]{:S(2)}, u32[]{:S(2)}) collective-permute-start(f32[32,512]{1,0:T(8,128)S(1)} %get-tuple-element.88), channel_id=1, source_target_pairs={{0,3},{1,2},{2,1},{3,0},{4,7},{5,6},{6,5},{7,4},{8,11},{9,10},{10,... | collective-permute-start | bytes 196616 | tf_op jit(solution)/shard_map/ppermute | solution.py:348
  87.6 6.5 %collective-permute-start.23 = (f32[32,512]{1,0:T(8,128)S(1)}, f32[32,512]{1,0:T(8,128)S(1)}, u32[]{:S(2)}, u32[]{:S(2)}) collective-permute-start(f32[32,512]{1,0:T(8,128)S(1)} %get-tuple-element.89), channel_id=1, source_target_pairs={{0,2},{1,3},{2,0},{3,1},{4,6},{5,7},{6,4},{7,5},{8,10},{9,11},{10,... | collective-permute-start | bytes 196616 | tf_op jit(solution)/shard_map/ppermute | solution.py:348
  88.9 5.3 %collective-permute-start.22 = (f32[32,512]{1,0:T(8,128)S(1)}, f32[32,512]{1,0:T(8,128)S(1)}, u32[]{:S(2)}, u32[]{:S(2)}) collective-permute-start(f32[32,512]{1,0:T(8,128)S(1)} %get-tuple-element.90), channel_id=1, source_target_pairs={{0,1},{1,0},{2,3},{3,2},{4,5},{5,4},{6,7},{7,6},{8,9},{9,8},{10,11... | collective-permute-start | bytes 196616 | tf_op jit(solution)/shard_map/ppermute | solution.py:348
  89.1 12.1 %all-to-all-start.1 = ((f32[32,1,128]{2,1,0:T(1,128)}), f32[32,1,128]{2,1,0:T(1,128)S(1)}, u32[]{:S(2)}, u32[]{:S(2)}) async-start(f32[32,1,128]{2,1,0:T(1,128)} %bitcast.12), calls=%async_computation.1 | async-start | bytes 32768 | tf_op jit(solution)/shard_map/all_to_all | solution.py:579
  (6 other events, 45.6 us)

commit v6 on v5

--- a/solution.py
+++ b/solution.py
@@ -9,7 +9,6 @@
 
 ridge = 0.5
 confidence = 40.0
-UNROLL = 8
 LIMIT = 24 * 1024 * 1024
 f32 = jnp.float32
 bf16 = jnp.bfloat16
@@ -58,19 +57,23 @@
         copy.wait()
 
 
-def mask_kernel(info_ref, mask_hbm, mask, sem):
-    tiles, share, side = mask.shape
-    copy = pltpu.make_async_copy(
-        mask_hbm.at[:, pl.ds(pl.multiple_of(info_ref[1] * share, share), share), :], mask, sem
-    )
-    copy.start()
-    copy.wait()
-
-    def clear(t, carry):
-        mask[t] = jnp.zeros((share, side), bf16)
+def mask_kernel(tile_ref, info_ref, mask_hbm, mask, sem):
+    slots, share, side = mask.shape
+    place = pl.multiple_of(info_ref[1] * share, share)
+    for s in range(slots):
+        pltpu.make_async_copy(
+            mask_hbm.at[jnp.maximum(tile_ref[s], 0), pl.ds(place, share), :], mask.at[s], sem
+        ).start()
+    pltpu.make_async_copy(mask, mask, sem).wait()
+
+    def clear(s, carry):
+        @pl.when(tile_ref[s] < 0)
+        def _():
+            mask[s] = jnp.zeros((share, side), bf16)
+
         return carry
 
-    lax.fori_loop(info_ref[0], tiles, clear, 0)
+    lax.fori_loop(0, slots, clear, 0)
 
 
 def pick_kernel(direct, info_ref, wanted_ref, items_ref, *out_refs):
@@ -169,29 +172,28 @@
     return product[:, :width] + product[:, width:] + ridge * vector
 
 
-def sparse(starting, slot_ref, user_ref, y, mask, p_hl, acc, held):
-    tiles, share, side = mask.shape
-    groups = tiles // UNROLL
-    acc[...] = jnp.zeros_like(acc)
+def sparse(starting, first_slot, slots, user_ref, y, mask, p_hl, acc, held):
+    share = mask.shape[1]
+    unroll = held.shape[1]
+    groups = slots // unroll
 
     def score(group):
-        for j in range(UNROLL):
-            t = group * UNROLL + j
-            tile = y[slot_ref[t]]
-            scores = matmul(p_hl[user_ref[t]], jnp.concatenate([tile, tile], axis=0))
+        for j in range(unroll):
+            s = first_slot + group * unroll + j
+            tile = y[s]
+            scores = matmul(p_hl[user_ref[s]], jnp.concatenate([tile, tile], axis=0))
             if starting:
                 scores = (1.0 + confidence) - confidence * scores
-            high, low = split(mask[t].astype(f32) * scores)
+            high, low = split(mask[s].astype(f32) * scores)
             held[group % 2, j, :share] = high
             held[group % 2, j, share:] = low
 
     def collect(group):
         terms = []
-        for j in range(UNROLL):
-            t = group * UNROLL + j
+        for j in range(unroll):
             term = lax.dot_general(
                 held[group % 2, j],
-                y[slot_ref[t]],
+                y[first_slot + group * unroll + j],
                 (((1,), (1,)), ((), ())),
                 preferred_element_type=f32,
             )
@@ -200,7 +202,7 @@
 
     def add(group, terms):
         for j, term in enumerate(terms):
-            acc[user_ref[group * UNROLL + j]] += term
+            acc[user_ref[first_slot + group * unroll + j]] += term
 
     score(0)
 
@@ -222,57 +224,56 @@
         ref[column ^ m, part * width : (part + 1) * width] = turned[m * width : (m + 1) * width]
 
 
-def start_kernel(n_cols, slots, slot_ref, user_ref, info_ref, x_ref, mask, *refs):
-    pieces = refs[: 2 * len(slots)]
-    part_ref, y, p_hl, acc, held, sems = refs[2 * len(slots) :]
+def start_kernel(n_cols, first_slot, slots, user_ref, info_ref, x_ref, mask, own, other, *refs):
+    part_ref, y, p_hl, held, sems = refs[-5:]
     piece_width = y.shape[1] // n_cols
     column = info_ref[1]
     copies = []
-    base = 0
-    for k, count in enumerate(slots):
-        for m in range(n_cols):
-            place = pl.multiple_of((column ^ m) * piece_width, piece_width)
-            source = pieces[2 * k + m % 2].at[pl.ds(m // 2 * count, count)]
-            copies.append(
-                pltpu.make_async_copy(
-                    source,
-                    y.at[pl.ds(base, count), pl.ds(place, piece_width), :],
-                    sems.at[len(copies)],
-                )
+    for m in range(n_cols):
+        place = pl.multiple_of((column ^ m) * piece_width, piece_width)
+        copies.append(
+            pltpu.make_async_copy(
+                (other if m % 2 else own).at[pl.ds(m // 2 * slots, slots)],
+                y.at[pl.ds(first_slot, slots), pl.ds(place, piece_width), :],
+                sems.at[m],
             )
-        base += count
-    for copy in copies:
-        copy.start()
+        )
+        copies[-1].start()
     load(p_hl, x_ref[...].T)
+    if first_slot:
+        part_ref[...] = refs[0][...]
+    else:
+        part_ref[...] = jnp.zeros_like(part_ref)
     for copy in copies:
         copy.wait()
-    sparse(True, slot_ref, user_ref, y, mask, p_hl, acc, held)
-    part_ref[...] = acc[...].reshape(part_ref.shape)
+    sparse(True, first_slot, slots, user_ref, y, mask, p_hl, part_ref, held)
 
 
 def first_kernel(
-    slot_ref, user_ref, info_ref, x_ref, part_ref, gram_ref, y, mask,
+    user_ref, info_ref, x_ref, part_ref, gram_ref, y, mask,
     sent_ref, field_ref, first_ref, p_hl, acc, held,
 ):
     start = x_ref[...].T
     load(p_hl, start)
-    field = part_ref[...] - dense(p_hl, gram_ref, start)
+    field = part_ref[...].reshape(start.shape) - dense(p_hl, gram_ref, start)
     field_ref[...] = field
     put(info_ref[1], sent_ref, field)
     load(p_hl, field)
-    sparse(False, slot_ref, user_ref, y, mask, p_hl, acc, held)
+    acc[...] = jnp.zeros_like(acc)
+    sparse(False, 0, y.shape[0], user_ref, y, mask, p_hl, acc, held)
     first = confidence * acc[...].reshape(field.shape) + dense(p_hl, gram_ref, field)
     first_ref[...] = first
     put(info_ref[1], sent_ref, first, 1)
 
 
 def second_kernel(
-    slot_ref, user_ref, info_ref, field_ref, first_ref, gram_ref, y, mask, sent_ref, dots_ref, p_hl, acc, held
+    user_ref, info_ref, field_ref, first_ref, gram_ref, y, mask, sent_ref, dots_ref, p_hl, acc, held
 ):
     field = field_ref[...]
     first = first_ref[...]
     load(p_hl, first)
-    sparse(False, slot_ref, user_ref, y, mask, p_hl, acc, held)
+    acc[...] = jnp.zeros_like(acc)
+    sparse(False, 0, y.shape[0], user_ref, y, mask, p_hl, acc, held)
     second = confidence * acc[...].reshape(field.shape) + dense(p_hl, gram_ref, first)
     put(info_ref[1], sent_ref, second)
 
@@ -387,7 +388,7 @@
     anywhere = pl.BlockSpec(memory_space=pl.ANY)
     params = pltpu.CompilerParams(vmem_limit_bytes=LIMIT)
 
-    def call(kernel, out_shape, in_specs, name, scratch=(), flops=0):
+    def call(kernel, out_shape, in_specs, name, scratch=(), flops=0, aliases={}):
         return pl.pallas_call(
             kernel,
             out_shape=out_shape,
@@ -395,6 +396,7 @@
             out_specs=jax.tree.map(lambda _: vmem, out_shape),
             scratch_shapes=scratch,
             compiler_params=params,
+            input_output_aliases=aliases,
             cost_estimate=pl.CostEstimate(
                 flops=flops, bytes_accessed=0, transcendentals=0
             ),
@@ -444,8 +446,9 @@
         for j, spot in ((1, 1), (3, 2), (2, 3), (5, 4), (6, 5), (7, 6), (4, 7)):
             block = jnp.where(step == j, spot, block)
     places = block * capacity + jnp.minimum(rank, capacity - 1)
-    places = jnp.where(live > 0, places, places[0])
-    tile_users = jnp.where(live > 0, tile_user, tile_user[0])
+    hits = (places[None, :] == slot_range[:, None]) & (live[None, :] > 0)
+    slot_tiles = jnp.sum(hits.astype(jnp.int32) * (order + 1)[None, :], axis=1) - 1
+    slot_users = jnp.sum(hits.astype(jnp.int32) * tile_user[None, :], axis=1)
 
     picked = call(
         functools.partial(pick_kernel, direct),
@@ -456,6 +459,9 @@
         "pick",
         flops=10**9,
     )(after(info, *shared), wanted, item_factors)
+
+    def add(gram, arrived):
+        return call(add_kernel, [square, packed], [vmem] * 2, "add")(gram, arrived)
 
     def join(*arrays):
         return jnp.concatenate(arrays, axis=0)
@@ -471,27 +477,15 @@
             2 * 10**10,
         )(*arrays)[0]
 
-    def add(gram, arrived):
-        return call(add_kernel, [square, packed], [vmem] * 2, "add")(gram, arrived)
-
     got = {0: picked[0]}
     if direct:
-        for j in (1, 3, 5, 6, 2, 7, 4):
-            message = picked[j] if j not in (4, 7) else after(picked[j], got[5], got[6])
-            got[j] = flip(message, "rows", j)
-
-    strengths = jax.ShapeDtypeStruct((tile_total, share, side), bf16)
-    (mask,) = call(
-        mask_kernel,
-        [strengths],
-        [smem, anywhere],
-        "mask",
-        [pltpu.SemaphoreType.DMA],
-        10**9,
-    )(
-        after(info, got[1] if direct else picked[0]),
-        pltpu.with_memory_space_constraint(tile_mask, pltpu.HBM),
-    )
+        for j in (1, 3, 5, 6, 2):
+            got[j] = flip(picked[j], "rows", j)
+        across = flip(got[0], "cols", 2)
+        near = after(gather(got[1], got[3]), across)
+        for j in (7, 4):
+            got[j] = flip(after(picked[j], got[5], got[6], near), "rows", j)
+
     square = jax.ShapeDtypeStruct((width, width), f32)
     extra = width // col_width
     packed = jax.ShapeDtypeStruct((extra, col_width, 2 * width), bf16)
@@ -507,56 +501,81 @@
         ],
         10**9,
     )(after(info, got[1] if direct else picked[0]), *shared)
-    if direct:
-        slots = (3 * capacity, 3 * capacity, 2 * capacity)
-        own = gather(got[0], got[1], got[3])
-        early = join(own, flip(own, "cols", 2))
-        pieces = [early, flip(early, "cols", 1)]
-
-        own = after(gather(got[2], got[5], got[6], carried), early)
-        arrived = flip(own, "cols", 2)
-        gram, carried = add(gram, arrived)
-        own = join(own[: 3 * capacity], arrived[: 3 * capacity], carried)
-        arrived = flip(after(own, mask), "cols", 1)
-        gram, carried = add(gram, arrived)
-        pieces += [own, arrived]
-
-        own = gather(got[7], got[4])
-        own = join(own, flip(own, "cols", 2))
-        gram, carried = add(gram, flip(carried, "rows", 1))
-        pieces += [own, flip(after(own, carried), "cols", 1)]
-        gram, carried = add(gram, flip(carried, "rows", 2))
-        arrived = flip(carried, "rows", 4)
-    else:
-        slots = (row_devs * capacity,)
-        gram = add_all(gram)
-        own = lax.all_to_all(picked[0], "rows", split_axis=0, concat_axis=0, tiled=True)
-        own = join(own, flip(own, "cols", 2))
-        pieces = [own, flip(own, "cols", 1)]
-
+    strengths = jax.ShapeDtypeStruct((row_devs * capacity, share, side), bf16)
+    unroll = capacity if direct else 8
     vector = jax.ShapeDtypeStruct((own_users, width), f32)
     held = jax.ShapeDtypeStruct((row_devs * capacity, width, side), bf16)
     work = [
         pltpu.VMEM((user_blocks, share, 2 * width), bf16),
         pltpu.VMEM((user_blocks, share, width), f32),
-        pltpu.VMEM((2, UNROLL, 2 * share, side), bf16),
+        pltpu.VMEM((2, unroll, 2 * share, side), bf16),
     ]
-    lists = (places, tile_users, info)
-    part, y = call(
-        functools.partial(start_kernel, n_cols, slots),
-        [vector, held],
-        [smem] * 3 + [vmem] * 2 + [anywhere] * len(pieces),
-        "start",
-        work + [pltpu.SemaphoreType.DMA((n_cols * len(slots),))],
-        8 * 10**9,
-    )(*lists, start, mask, *pieces)
+    lists = (slot_users, info)
+
+    def slice_mask(ready):
+        return call(
+            mask_kernel,
+            [strengths],
+            [smem, smem, anywhere],
+            "mask",
+            [pltpu.SemaphoreType.DMA],
+            10**9,
+        )(
+            slot_tiles,
+            after(info, ready),
+            pltpu.with_memory_space_constraint(tile_mask, pltpu.HBM),
+        )[0]
+
+    def begin(first_slot, slots, own, other, *earlier, flops=3 * 10**9):
+        return call(
+            functools.partial(start_kernel, n_cols, first_slot, slots),
+            [jax.ShapeDtypeStruct((user_blocks, share, width), f32), held],
+            [smem] * 2 + [vmem] * 2 + [anywhere] * 2 + [vmem] * len(earlier),
+            "start",
+            [work[0], work[2], pltpu.SemaphoreType.DMA((n_cols,))],
+            flops,
+            {7: 1} if earlier else {},
+        )(*lists, start, mask, own, other, *earlier)
+
+    if direct:
+        early = join(got[0], near, across, flip(near, "cols", 2))
+        own = gather(got[2], got[5], got[6], carried)
+        early_other = flip(after(early, own), "cols", 1)
+        own = after(own, early)
+        mask = slice_mask(own)
+        arrived = flip(own, "cols", 2)
+        state = begin(0, 3 * capacity, early, early_other, flops=2 * 10**10)
+        last = gather(got[7], got[4])
+        arrived = after(arrived, state[0], got[7], got[4])
+        gram, carried = add(gram, arrived)
+        middle = join(own[: 3 * capacity], arrived[: 3 * capacity], carried)
+        middle_other = flip(middle, "cols", 1)
+        gram, carried = add(gram, middle_other)
+
+        late = flip(last, "cols", 2)
+        state = begin(
+            3 * capacity, 3 * capacity, middle, middle_other, *state, flops=2 * 10**10
+        )
+        gram, carried = add(gram, flip(after(carried, state[0]), "rows", 1))
+        late = join(last, after(late, carried))
+        late_other = flip(late, "cols", 1)
+        gram, carried = add(gram, flip(carried, "rows", 2))
+        state = after(state, carried)
+        arrived = flip(carried, "rows", 4)
+        part, y = begin(6 * capacity, 2 * capacity, late, late_other, *state)
+    else:
+        mask = slice_mask(gram)
+        gram = add_all(gram)
+        own = lax.all_to_all(picked[0], "rows", split_axis=0, concat_axis=0, tiled=True)
+        own = join(own, flip(own, "cols", 2))
+        part, y = begin(0, row_devs * capacity, own, flip(own, "cols", 1))
     if direct:
         gram, _ = add(gram, after(arrived, part))
     pair = jax.ShapeDtypeStruct((n_cols, 2 * col_width, own_users), f32)
     pair_sent, field, first = call(
         first_kernel,
         [pair, vector, vector],
-        [smem] * 3 + [vmem] * 5,
+        [smem] * 2 + [vmem] * 5,
         "first",
         work,
         8 * 10**9,
@@ -567,7 +586,7 @@
             jax.ShapeDtypeStruct((n_cols, col_width, own_users), f32),
             jax.ShapeDtypeStruct((devices, 128), f32),
         ],
-        [smem] * 3 + [vmem] * 5,
+        [smem] * 2 + [vmem] * 5,
         "second",
         work,
         8 * 10**9,

time: 104 us -> 109 us (1.048)
  waiting for transfers between devices: 40 us -> 42.2 us
  Pallas kernels: 27.4 us -> 29.5 us
    pallas_call x3 -> x5, Pallas kernels: 13.4 us -> 15.7 us  [the longest x3 6.95 us: begin(): call(functools.partial(start_kernel, n_cols, first_slot, slots), [jax.Sha...]
    all_to_all x1, starting transfers between devices: 5.01 us -> 2.7 us  [on_device(): lax.all_to_all(dots, ('rows', 'cols'), split_axis=0, concat_axis=0, tiled...]
    ppermute x25 -> x26, starting transfers between devices: 20 us -> 22.3 us  [flip(): return lax.ppermute(value, axis, [(i, i ^ bit) for i in range(size)])]
    ppermute x25 -> x26, waiting for transfers between devices: 28.2 us -> 30.4 us  [flip(): return lax.ppermute(value, axis, [(i, i ^ bit) for i in range(size)])]
  transfers between devices with their start and end apart: 27 -> 28, of which waited for: 12 -> 13; matrix products, arithmetic and copies ran while one was open for 2% -> 2% of each run, Pallas kernels for 16% -> 18%
where the time goes in v6:
time: 109 us; the launch traced here: 108 us
  waiting for transfers between devices  42.2 us (39%)
  starting transfers between devices  31 us (28%)
  Pallas kernels  29.5 us (27%)
  other arithmetic  1.94 us (2%)
  local copies, waits for them, and re-layouts  1.91 us (2%)
  between operations  1.6 us (1%)
    ppermute x26, waiting for transfers between devices, flip(): return lax.ppermute(value, axis, [(i, i ^ bit) for i in range(size)])  30.4 us
    ppermute x26, starting transfers between devices, flip(): return lax.ppermute(value, axis, [(i, i ^ bit) for i in range(size)])  22.3 us
    pallas_call x3, Pallas kernels, begin(): call(functools.partial(start_kernel, n_cols, first_slot, slots), [jax.Sha...  6.95 us
    all_to_all x1, waiting for transfers between devices, on_device(): lax.all_to_all(dots, ('rows', 'cols'), split_axis=0, concat_axis=0, tiled...  6.37 us
    all_to_all x1, starting transfers between devices, on_device(): lax.all_to_all(requests, 'rows', split_axis=0, concat_axis=0, tiled=True)  6.07 us
    pallas_call x1, Pallas kernels, on_device(): call(second_kernel, [jax.ShapeDtypeStruct((n_cols, col_width, own_users),...  5.75 us
    all_to_all x1, waiting for transfers between devices, on_device(): lax.all_to_all(requests, 'rows', split_axis=0, concat_axis=0, tiled=True)  5.47 us
    pallas_call x1, Pallas kernels, on_device(): call(first_kernel, [pair, vector, vector], [smem] * 2 + [vmem] * 5, 'firs...  5.28 us
  transfers between devices with their start and end apart: 28, of which 13 were waited for; matrix products, arithmetic and copies ran while one was open for 2% of the time, Pallas kernels for 18%

profile of v6, /device:TPU:0, one launch (start us, length us, event | category | flops | bytes accessed | tf_op | source)
XLA Modules:
  0.0 108.2 jit_solution(9083737067879976349)
XLA Ops:
  1.4 1.7 %prepare.1 = (bf16[32,3072]{1,0:T(8,128)(2,1)S(1)}, bf16[32,3072]{1,0:T(8,128)(2,1)S(1)}, bf16[32,3072]{1,0:T(8,128)(2,1)S(1)}, bf16[32,3072]{1,0:T(8,128)(2,1)S(1)}) custom-call(s32[3]{0:T(128)S(1)} %pad_add_fusion.info_ref, f32[32,2048]{1,0:T(8,128)} %x_ref.1, bf16[32,8192]{1,0:T(8,128)(2,1)} %items_ref.1), custom_call_target="tpu_custom_call" | custom-call | flops 1000000000 | tf_op jit(solution)/shard_map/prepare/pallas_call | solution.py:408
  3.6 2.6 %collective-permute-start.1 = (bf16[32,3072]{1,0:T(8,128)(2,1)S(1)}, bf16[32,3072]{1,0:T(8,128)(2,1)S(1)}, u32[]{:S(2)}, u32[]{:S(2)}) collective-permute-start(bf16[32,3072]{1,0:T(8,128)(2,1)S(1)} %get-tuple-element.56), channel_id=1, source_target_pairs={{0,2},{1,3},{2,0},{3,1},{4,6},{5,7},{6,4},{7,5},{8,10},{9,11},{10,... | collective-permute-start | bytes 589832 | tf_op jit(solution)/shard_map/ppermute | solution.py:349
  8.6 6.1 %all-to-all-start = ((s32[8,1,9]{2,1,0:T(1,128)}), s32[8,1,9]{2,1,0:T(1,128)S(1)}, u32[]{:S(2)}, u32[]{:S(2)}) async-start(s32[8,1,9]{2,1,0:T(1,128)} %bitcast.3), calls=%async_computation | async-start | bytes 8192 | tf_op jit(solution)/shard_map/all_to_all | solution.py:441
  15.6 5.5 %all-to-all-done = s32[8,1,9]{2,1,0:T(1,128)S(1)} async-done(((s32[8,1,9]{2,1,0:T(1,128)}), s32[8,1,9]{2,1,0:T(1,128)S(1)}, u32[]{:S(2)}, u32[]{:S(2)}) %all-to-all-start) | async-done | bytes 320 | tf_op jit(solution)/shard_map/all_to_all | solution.py:441
  25.0 1.5 %collective-permute-start.8 = (bf16[9,32,256]{2,1,0:T(8,128)(2,1)S(1)}, bf16[9,32,256]{2,1,0:T(8,128)(2,1)S(1)}, u32[]{:S(2)}, u32[]{:S(2)}) collective-permute-start(bf16[9,32,256]{2,1,0:T(8,128)(2,1)S(1)} %get-tuple-element.66), channel_id=1, source_target_pairs={{0,2},{1,3},{2,0},{3,1},{4,6},{5,7},{6,4},{7,5},{8,10},{9,11},{10,... | collective-permute-start | bytes 442376 | tf_op jit(solution)/shard_map/ppermute | solution.py:349
  28.5 3.0 %collective-permute-done.3.refs_0_ = bf16[9,32,256]{2,1,0:T(8,128)(2,1)S(1)} collective-permute-done((bf16[9,32,256]{2,1,0:T(8,128)(2,1)S(1)}, bf16[9,32,256]{2,1,0:T(8,128)(2,1)S(1)}, u32[]{:S(2)}, u32[]{:S(2)}) %collective-permute-start.3) | collective-permute-done | bytes 147488 | tf_op jit(solution)/shard_map/ppermute | solution.py:349
  33.0 1.9 %collective-permute-start.9 = (bf16[18,32,256]{2,1,0:T(8,128)(2,1)S(1)}, bf16[18,32,256]{2,1,0:T(8,128)(2,1)S(1)}, u32[]{:S(2)}, u32[]{:S(2)}) collective-permute-start(bf16[18,32,256]{2,1,0:T(8,128)(2,1)S(1)} %join.4), channel_id=1, source_target_pairs={{0,2},{1,3},{2,0},{3,1},{4,6},{5,7},{6,4},{7,5},{8,10},{9,11},{10,... | collective-permute-start | bytes 884744 | tf_op jit(solution)/shard_map/ppermute | solution.py:349
  36.2 5.0 %collective-permute-done.5.refs_1_ = bf16[9,32,256]{2,1,0:T(8,128)(2,1)S(1)} collective-permute-done((bf16[9,32,256]{2,1,0:T(8,128)(2,1)S(1)}, bf16[9,32,256]{2,1,0:T(8,128)(2,1)S(1)}, u32[]{:S(2)}, u32[]{:S(2)}) %collective-permute-start.5) | collective-permute-done | bytes 147488 | tf_op jit(solution)/shard_map/ppermute | solution.py:349
  43.1 3.5 %collective-permute-start.10 = (bf16[9,32,256]{2,1,0:T(8,128)(2,1)S(1)}, bf16[9,32,256]{2,1,0:T(8,128)(2,1)S(1)}, u32[]{:S(2)}, u32[]{:S(2)}) collective-permute-start(bf16[9,32,256]{2,1,0:T(8,128)(2,1)S(1)} %get-tuple-element.72), channel_id=1, source_target_pairs={{0,28},{4,24},{8,20},{12,16},{16,12},{20,8},{24,4},{28,0},{1,29},{... | collective-permute-start | bytes 442376 | tf_op jit(solution)/shard_map/ppermute | solution.py:349
  47.2 3.5 %mask.1 = bf16[72,64,256]{2,1,0:T(8,128)(2,1)S(1)} custom-call(s32[72]{0:T(128)S(1)} %broadcast_add_fusion.tile_ref, s32[3]{0:T(128)S(1)} %pad_add_fusion.info_ref, bf16[72,256,256]{2,1,0:T(8,128)(2,1)} %mask_hbm.1), custom_call_target="tpu_custom_call" | custom-call | flops 1000000000 | tf_op jit(solution)/shard_map/mask/pallas_call | solution.py:516
  50.7 2.6 %start.3 = (f32[8,64,128]{2,1,0:T(8,128)S(1)}, bf16[72,128,256]{2,1,0:T(8,128)(2,1)S(1)}) custom-call(s32[72]{0:T(128)S(1)} %get-tuple-element.105.user_ref, s32[3]{0:T(128)S(1)} %pad_add_fusion.info_ref, f32[128,512]{1,0:T(8,128)S(1)} %get-tuple-element.61.x_ref, bf16[72,64,256]{2,1,0:T(8,128)(2,1)S(1)} %mask.1, ...), custom_call_target="tpu_custom_call" | custom-call | flops 20000000000 | tf_op jit(solution)/shard_map/start/pallas_call | solution.py:530
  53.3 2.7 %collective-permute-done.11.refs_1_ = bf16[9,32,256]{2,1,0:T(8,128)(2,1)S(1)} collective-permute-done((bf16[9,32,256]{2,1,0:T(8,128)(2,1)S(1)}, bf16[9,32,256]{2,1,0:T(8,128)(2,1)S(1)}, u32[]{:S(2)}, u32[]{:S(2)}) %collective-permute-start.11) | collective-permute-done | bytes 147488 | tf_op jit(solution)/shard_map/ppermute | solution.py:349
  56.0 4.0 %collective-permute-done.13.arrived_ref = bf16[31,32,256]{2,1,0:T(8,128)(2,1)S(1)} collective-permute-done((bf16[31,32,256]{2,1,0:T(8,128)(2,1)S(1)}, bf16[31,32,256]{2,1,0:T(8,128)(2,1)S(1)}, u32[]{:S(2)}, u32[]{:S(2)}) %collective-permute-start.13) | collective-permute-done | bytes 507936 | tf_op jit(solution)/shard_map/ppermute | solution.py:349
  61.3 1.5 %collective-permute-done.15.arrived_ref.other = bf16[58,32,256]{2,1,0:T(8,128)(2,1)S(1)} collective-permute-done((bf16[58,32,256]{2,1,0:T(8,128)(2,1)S(1)}, bf16[58,32,256]{2,1,0:T(8,128)(2,1)S(1)}, u32[]{:S(2)}, u32[]{:S(2)}) %collective-permute-start.15) | collective-permute-done | bytes 950304 | tf_op jit(solution)/shard_map/ppermute | solution.py:349
  62.8 2.6 %start.4 = (f32[8,64,128]{2,1,0:T(8,128)S(1)}, bf16[72,128,256]{2,1,0:T(8,128)(2,1)S(1)}) custom-call(s32[72]{0:T(128)S(1)} %get-tuple-element.105.user_ref, s32[3]{0:T(128)S(1)} %pad_add_fusion.info_ref, f32[128,512]{1,0:T(8,128)S(1)} %get-tuple-element.61.x_ref, bf16[72,64,256]{2,1,0:T(8,128)(2,1)S(1)} %mask.1, ...), custom_call_target="tpu_custom_call", output_to_operand_aliasing={{1}: (7, {})} | custom-call | flops 20000000000 | tf_op jit(solution)/shard_map/start/pallas_call | solution.py:530
  66.0 3.7 %collective-permute-done.16.arrived_ref = bf16[4,32,256]{2,1,0:T(8,128)(2,1)S(1)} collective-permute-done((bf16[4,32,256]{2,1,0:T(8,128)(2,1)S(1)}, bf16[4,32,256]{2,1,0:T(8,128)(2,1)S(1)}, u32[]{:S(2)}, u32[]{:S(2)}) %collective-permute-start.16) | collective-permute-done | bytes 65568 | tf_op jit(solution)/shard_map/ppermute | solution.py:349
  70.3 4.4 %collective-permute-done.18.arrived_ref = bf16[4,32,256]{2,1,0:T(8,128)(2,1)S(1)} collective-permute-done((bf16[4,32,256]{2,1,0:T(8,128)(2,1)S(1)}, bf16[4,32,256]{2,1,0:T(8,128)(2,1)S(1)}, u32[]{:S(2)}, u32[]{:S(2)}) %collective-permute-start.18) | collective-permute-done | bytes 65568 | tf_op jit(solution)/shard_map/ppermute | solution.py:349
  74.9 1.8 %start.5 = (f32[8,64,128]{2,1,0:T(8,128)S(1)}, bf16[72,128,256]{2,1,0:T(8,128)(2,1)S(1)}) custom-call(s32[72]{0:T(128)S(1)} %get-tuple-element.105.user_ref, s32[3]{0:T(128)S(1)} %pad_add_fusion.info_ref, f32[128,512]{1,0:T(8,128)S(1)} %get-tuple-element.61.x_ref, bf16[72,64,256]{2,1,0:T(8,128)(2,1)S(1)} %mask.1, ...), custom_call_target="tpu_custom_call", output_to_operand_aliasing={{1}: (7, {})} | custom-call | flops 3000000000 | tf_op jit(solution)/shard_map/start/pallas_call | solution.py:530
  76.6 4.1 %collective-permute-done.19.arrived_ref = bf16[4,32,256]{2,1,0:T(8,128)(2,1)S(1)} collective-permute-done((bf16[4,32,256]{2,1,0:T(8,128)(2,1)S(1)}, bf16[4,32,256]{2,1,0:T(8,128)(2,1)S(1)}, u32[]{:S(2)}, u32[]{:S(2)}) %collective-permute-start.19) | collective-permute-done | bytes 65568 | tf_op jit(solution)/shard_map/ppermute | solution.py:349
  81.4 5.3 %first.1 = (f32[4,64,512]{2,1,0:T(8,128)S(1)}, f32[512,128]{1,0:T(8,128)S(1)}, f32[512,128]{1,0:T(8,128)S(1)}) custom-call(s32[72]{0:T(128)S(1)} %get-tuple-element.105.user_ref, s32[3]{0:T(128)S(1)} %pad_add_fusion.info_ref, f32[128,512]{1,0:T(8,128)S(1)} %get-tuple-element.61.x_ref, f32[8,64,128]{2,1,0:T(8,128)S(1)} %get-tuple-element.93.part_ref, ...), custom_call_target="tpu_custom_call" | custom-call | flops 8000000000 | tf_op jit(solution)/shard_map/first/pallas_call | solution.py:575
  88.6 5.7 %second.1 = (f32[4,32,512]{2,1,0:T(8,128)S(1)}, f32[32,128]{1,0:T(8,128)}) custom-call(s32[72]{0:T(128)S(1)} %get-tuple-element.105.user_ref, s32[3]{0:T(128)S(1)} %pad_add_fusion.info_ref, f32[512,128]{1,0:T(8,128)S(1)} %get-tuple-element.98.field_ref, f32[512,128]{1,0:T(8,128)S(1)} %get-tuple-element.99.first_ref, ...), custom_call_target="tpu_custom_call" | custom-call | flops 8000000000 | tf_op jit(solution)/shard_map/second/pallas_call | solution.py:583
  96.3 2.7 %all-to-all-start.1 = ((f32[32,1,128]{2,1,0:T(1,128)}), f32[32,1,128]{2,1,0:T(1,128)S(1)}, u32[]{:S(2)}, u32[]{:S(2)}) async-start(f32[32,1,128]{2,1,0:T(1,128)} %bitcast.10), calls=%async_computation.1 | async-start | bytes 32768 | tf_op jit(solution)/shard_map/all_to_all | solution.py:598
  99.8 6.4 %all-to-all-done.1 = f32[32,1,128]{2,1,0:T(1,128)S(1)} async-done(((f32[32,1,128]{2,1,0:T(1,128)}), f32[32,1,128]{2,1,0:T(1,128)S(1)}, u32[]{:S(2)}, u32[]{:S(2)}) %all-to-all-start.1) | async-done | bytes 16416 | tf_op jit(solution)/shard_map/all_to_all | solution.py:598
  106.1 2.0 %finish.1 = (f32[32,2048]{1,0:T(8,128)}, f32[32,2048]{1,0:T(8,128)}) custom-call(s32[3]{0:T(128)S(1)} %pad_add_fusion.info_ref, f32[32,128]{1,0:T(8,128)S(1)} %bitcast.26, f32[32,2048]{1,0:T(8,128)S(1)} %copy-done.1, f32[64,512]{1,0:T(8,128)S(1)} %get-tuple-element.110.refs_0_, f32[64,512]{1,0:T(8,128)S(1)} %collective-permute-done.20.refs_1_, ...), custom_call_target="tpu_custom_call" | custom-call | flops 1000000000 | tf_op jit(solution)/shard_map/finish/pallas_call | solution.py:601
  (73 shorter events, 22.8 us)
Async XLA Ops:
  3.1 11.6 %collective-permute-start = (bf16[32,3072]{1,0:T(8,128)(2,1)S(1)}, bf16[32,3072]{1,0:T(8,128)(2,1)S(1)}, u32[]{:S(2)}, u32[]{:S(2)}) collective-permute-start(bf16[32,3072]{1,0:T(8,128)(2,1)S(1)} %get-tuple-element.55), channel_id=1, source_target_pairs={{0,1},{1,0},{2,3},{3,2},{4,5},{5,4},{6,7},{7,6},{8,9},{9,8},{10,11... | collective-permute-start | bytes 589832 | tf_op jit(solution)/shard_map/ppermute | solution.py:349
  3.6 11.1 %collective-permute-start.1 = (bf16[32,3072]{1,0:T(8,128)(2,1)S(1)}, bf16[32,3072]{1,0:T(8,128)(2,1)S(1)}, u32[]{:S(2)}, u32[]{:S(2)}) collective-permute-start(bf16[32,3072]{1,0:T(8,128)(2,1)S(1)} %get-tuple-element.56), channel_id=1, source_target_pairs={{0,2},{1,3},{2,0},{3,1},{4,6},{5,7},{6,4},{7,5},{8,10},{9,11},{10,... | collective-permute-start | bytes 589832 | tf_op jit(solution)/shard_map/ppermute | solution.py:349
  6.2 9.4 %collective-permute-start.2 = (bf16[32,3072]{1,0:T(8,128)(2,1)S(1)}, bf16[32,3072]{1,0:T(8,128)(2,1)S(1)}, u32[]{:S(2)}, u32[]{:S(2)}) collective-permute-start(bf16[32,3072]{1,0:T(8,128)(2,1)S(1)} %get-tuple-element.57), channel_id=1, source_target_pairs={{0,3},{1,2},{2,1},{3,0},{4,7},{5,6},{6,5},{7,4},{8,11},{9,10},{10,... | collective-permute-start | bytes 589832 | tf_op jit(solution)/shard_map/ppermute | solution.py:349
  8.6 12.5 %all-to-all-start = ((s32[8,1,9]{2,1,0:T(1,128)}), s32[8,1,9]{2,1,0:T(1,128)S(1)}, u32[]{:S(2)}, u32[]{:S(2)}) async-start(s32[8,1,9]{2,1,0:T(1,128)} %bitcast.3), calls=%async_computation | async-start | bytes 8192 | tf_op jit(solution)/shard_map/all_to_all | solution.py:441
  22.9 8.6 %collective-permute-start.3 = (bf16[9,32,256]{2,1,0:T(8,128)(2,1)S(1)}, bf16[9,32,256]{2,1,0:T(8,128)(2,1)S(1)}, u32[]{:S(2)}, u32[]{:S(2)}) collective-permute-start(bf16[9,32,256]{2,1,0:T(8,128)(2,1)S(1)} %get-tuple-element.59), channel_id=1, source_target_pairs={{0,4},{4,0},{8,12},{12,8},{16,20},{20,16},{24,28},{28,24},{1,5},{5... | collective-permute-start | bytes 442376 | tf_op jit(solution)/shard_map/ppermute | solution.py:349
  23.5 9.1 %collective-permute-start.7 = (bf16[9,32,256]{2,1,0:T(8,128)(2,1)S(1)}, bf16[9,32,256]{2,1,0:T(8,128)(2,1)S(1)}, u32[]{:S(2)}, u32[]{:S(2)}) collective-permute-start(bf16[9,32,256]{2,1,0:T(8,128)(2,1)S(1)} %get-tuple-element.67), channel_id=1, source_target_pairs={{0,12},{4,8},{8,4},{12,0},{16,28},{20,24},{24,20},{28,16},{1,13},{... | collective-permute-start | bytes 442376 | tf_op jit(solution)/shard_map/ppermute | solution.py:349
  25.0 8.0 %collective-permute-start.8 = (bf16[9,32,256]{2,1,0:T(8,128)(2,1)S(1)}, bf16[9,32,256]{2,1,0:T(8,128)(2,1)S(1)}, u32[]{:S(2)}, u32[]{:S(2)}) collective-permute-start(bf16[9,32,256]{2,1,0:T(8,128)(2,1)S(1)} %get-tuple-element.66), channel_id=1, source_target_pairs={{0,2},{1,3},{2,0},{3,1},{4,6},{5,7},{6,4},{7,5},{8,10},{9,11},{10,... | collective-permute-start | bytes 442376 | tf_op jit(solution)/shard_map/ppermute | solution.py:349
  26.5 9.7 %collective-permute-start.4 = (bf16[9,32,256]{2,1,0:T(8,128)(2,1)S(1)}, bf16[9,32,256]{2,1,0:T(8,128)(2,1)S(1)}, u32[]{:S(2)}, u32[]{:S(2)}) collective-permute-start(bf16[9,32,256]{2,1,0:T(8,128)(2,1)S(1)} %get-tuple-element.62), channel_id=1, source_target_pairs={{0,8},{4,12},{8,0},{12,4},{16,24},{20,28},{24,16},{28,20},{1,9},{5... | collective-permute-start | bytes 442376 | tf_op jit(solution)/shard_map/ppermute | solution.py:349
  28.0 13.2 %collective-permute-start.5 = (bf16[9,32,256]{2,1,0:T(8,128)(2,1)S(1)}, bf16[9,32,256]{2,1,0:T(8,128)(2,1)S(1)}, u32[]{:S(2)}, u32[]{:S(2)}) collective-permute-start(bf16[9,32,256]{2,1,0:T(8,128)(2,1)S(1)} %get-tuple-element.63), channel_id=1, source_target_pairs={{0,20},{4,16},{8,28},{12,24},{16,4},{20,0},{24,12},{28,8},{1,21},{... | collective-permute-start | bytes 442376 | tf_op jit(solution)/shard_map/ppermute | solution.py:349
  31.5 9.7 %collective-permute-start.6 = (bf16[9,32,256]{2,1,0:T(8,128)(2,1)S(1)}, bf16[9,32,256]{2,1,0:T(8,128)(2,1)S(1)}, u32[]{:S(2)}, u32[]{:S(2)}) collective-permute-start(bf16[9,32,256]{2,1,0:T(8,128)(2,1)S(1)} %get-tuple-element.64), channel_id=1, source_target_pairs={{0,24},{4,28},{8,16},{12,20},{16,8},{20,12},{24,0},{28,4},{1,25},{... | collective-permute-start | bytes 442376 | tf_op jit(solution)/shard_map/ppermute | solution.py:349
  33.0 8.9 %collective-permute-start.9 = (bf16[18,32,256]{2,1,0:T(8,128)(2,1)S(1)}, bf16[18,32,256]{2,1,0:T(8,128)(2,1)S(1)}, u32[]{:S(2)}, u32[]{:S(2)}) collective-permute-start(bf16[18,32,256]{2,1,0:T(8,128)(2,1)S(1)} %join.4), channel_id=1, source_target_pairs={{0,2},{1,3},{2,0},{3,1},{4,6},{5,7},{6,4},{7,5},{8,10},{9,11},{10,... | collective-permute-start | bytes 884744 | tf_op jit(solution)/shard_map/ppermute | solution.py:349
  42.0 8.7 %collective-permute-start.14 = (bf16[54,32,256]{2,1,0:T(8,128)(2,1)S(1)}, bf16[54,32,256]{2,1,0:T(8,128)(2,1)S(1)}, u32[]{:S(2)}, u32[]{:S(2)}) collective-permute-start(bf16[54,32,256]{2,1,0:T(8,128)(2,1)S(1)} %constant_dynamic-update-slice_fusion.own), channel_id=1, source_target_pairs={{0,1},{1,0},{2,3},{3,2},{4,5},{5,4},{6,7},{7,6},{8,9},{9,8},{10,11... | collective-permute-start | bytes 2654216 | tf_op jit(solution)/shard_map/ppermute | solution.py:349
  42.1 13.9 %collective-permute-start.11 = (bf16[9,32,256]{2,1,0:T(8,128)(2,1)S(1)}, bf16[9,32,256]{2,1,0:T(8,128)(2,1)S(1)}, u32[]{:S(2)}, u32[]{:S(2)}) collective-permute-start(bf16[9,32,256]{2,1,0:T(8,128)(2,1)S(1)} %get-tuple-element.74), channel_id=1, source_target_pairs={{0,16},{4,20},{8,24},{12,28},{16,0},{20,4},{24,8},{28,12},{1,17},{... | collective-permute-start | bytes 442376 | tf_op jit(solution)/shard_map/ppermute | solution.py:349
  43.1 12.9 %collective-permute-start.10 = (bf16[9,32,256]{2,1,0:T(8,128)(2,1)S(1)}, bf16[9,32,256]{2,1,0:T(8,128)(2,1)S(1)}, u32[]{:S(2)}, u32[]{:S(2)}) collective-permute-start(bf16[9,32,256]{2,1,0:T(8,128)(2,1)S(1)} %get-tuple-element.72), channel_id=1, source_target_pairs={{0,28},{4,24},{8,20},{12,16},{16,12},{20,8},{24,4},{28,0},{1,29},{... | collective-permute-start | bytes 442376 | tf_op jit(solution)/shard_map/ppermute | solution.py:349
  46.6 13.4 %collective-permute-start.13 = (bf16[31,32,256]{2,1,0:T(8,128)(2,1)S(1)}, bf16[31,32,256]{2,1,0:T(8,128)(2,1)S(1)}, u32[]{:S(2)}, u32[]{:S(2)}) collective-permute-start(bf16[31,32,256]{2,1,0:T(8,128)(2,1)S(1)} %join.3), channel_id=1, source_target_pairs={{0,2},{1,3},{2,0},{3,1},{4,6},{5,7},{6,4},{7,5},{8,10},{9,11},{10,... | collective-permute-start | bytes 1523720 | tf_op jit(solution)/shard_map/ppermute | solution.py:349
  60.7 9.4 %collective-permute-start.12 = (bf16[18,32,256]{2,1,0:T(8,128)(2,1)S(1)}, bf16[18,32,256]{2,1,0:T(8,128)(2,1)S(1)}, u32[]{:S(2)}, u32[]{:S(2)}) collective-permute-start(bf16[18,32,256]{2,1,0:T(8,128)(2,1)S(1)} %join.5), channel_id=1, source_target_pairs={{0,2},{1,3},{2,0},{3,1},{4,6},{5,7},{6,4},{7,5},{8,10},{9,11},{10,... | collective-permute-start | bytes 884744 | tf_op jit(solution)/shard_map/ppermute | solution.py:349
  70.2 4.7 %collective-permute-start.17 = (bf16[36,32,256]{2,1,0:T(8,128)(2,1)S(1)}, bf16[36,32,256]{2,1,0:T(8,128)(2,1)S(1)}, u32[]{:S(2)}, u32[]{:S(2)}) collective-permute-start(bf16[36,32,256]{2,1,0:T(8,128)(2,1)S(1)} %pad_maximum_fusion.1.own), channel_id=1, source_target_pairs={{0,1},{1,0},{2,3},{3,2},{4,5},{5,4},{6,7},{7,6},{8,9},{9,8},{10,11... | collective-permute-start | bytes 1769480 | tf_op jit(solution)/shard_map/ppermute | solution.py:349
  74.8 5.9 %collective-permute-start.19 = (bf16[4,32,256]{2,1,0:T(8,128)(2,1)S(1)}, bf16[4,32,256]{2,1,0:T(8,128)(2,1)S(1)}, u32[]{:S(2)}, u32[]{:S(2)}) collective-permute-start(bf16[4,32,256]{2,1,0:T(8,128)(2,1)S(1)} %get-tuple-element.90), channel_id=1, source_target_pairs={{0,16},{4,20},{8,24},{12,28},{16,0},{20,4},{24,8},{28,12},{1,17},{... | collective-permute-start | bytes 196616 | tf_op jit(solution)/shard_map/ppermute | solution.py:349
  86.7 8.7 %collective-permute-start.20 = (f32[64,512]{1,0:T(8,128)S(1)}, f32[64,512]{1,0:T(8,128)S(1)}, u32[]{:S(2)}, u32[]{:S(2)}) collective-permute-start(f32[64,512]{1,0:T(8,128)S(1)} %get-tuple-element.109), channel_id=1, source_target_pairs={{0,1},{1,0},{2,3},{3,2},{4,5},{5,4},{6,7},{7,6},{8,9},{9,8},{10,11... | collective-permute-start | bytes 393224 | tf_op jit(solution)/shard_map/ppermute | solution.py:349
  86.8 9.6 %collective-permute-start.21 = (f32[64,512]{1,0:T(8,128)S(1)}, f32[64,512]{1,0:T(8,128)S(1)}, u32[]{:S(2)}, u32[]{:S(2)}) collective-permute-start(f32[64,512]{1,0:T(8,128)S(1)} %get-tuple-element.108), channel_id=1, source_target_pairs={{0,2},{1,3},{2,0},{3,1},{4,6},{5,7},{6,4},{7,5},{8,10},{9,11},{10,... | collective-permute-start | bytes 393224 | tf_op jit(solution)/shard_map/ppermute | solution.py:349
  87.4 9.0 %collective-permute-start.22 = (f32[64,512]{1,0:T(8,128)S(1)}, f32[64,512]{1,0:T(8,128)S(1)}, u32[]{:S(2)}, u32[]{:S(2)}) collective-permute-start(f32[64,512]{1,0:T(8,128)S(1)} %get-tuple-element.107), channel_id=1, source_target_pairs={{0,3},{1,2},{2,1},{3,0},{4,7},{5,6},{6,5},{7,4},{8,11},{9,10},{10,... | collective-permute-start | bytes 393224 | tf_op jit(solution)/shard_map/ppermute | solution.py:349
  94.4 4.6 %collective-permute-start.23 = (f32[32,512]{1,0:T(8,128)S(1)}, f32[32,512]{1,0:T(8,128)S(1)}, u32[]{:S(2)}, u32[]{:S(2)}) collective-permute-start(f32[32,512]{1,0:T(8,128)S(1)} %get-tuple-element.113), channel_id=1, source_target_pairs={{0,1},{1,0},{2,3},{3,2},{4,5},{5,4},{6,7},{7,6},{8,9},{9,8},{10,11... | collective-permute-start | bytes 196616 | tf_op jit(solution)/shard_map/ppermute | solution.py:349
  94.8 5.0 %collective-permute-start.24 = (f32[32,512]{1,0:T(8,128)S(1)}, f32[32,512]{1,0:T(8,128)S(1)}, u32[]{:S(2)}, u32[]{:S(2)}) collective-permute-start(f32[32,512]{1,0:T(8,128)S(1)} %get-tuple-element.112), channel_id=1, source_target_pairs={{0,2},{1,3},{2,0},{3,1},{4,6},{5,7},{6,4},{7,5},{8,10},{9,11},{10,... | collective-permute-start | bytes 196616 | tf_op jit(solution)/shard_map/ppermute | solution.py:349
  96.3 9.8 %all-to-all-start.1 = ((f32[32,1,128]{2,1,0:T(1,128)}), f32[32,1,128]{2,1,0:T(1,128)S(1)}, u32[]{:S(2)}, u32[]{:S(2)}) async-start(f32[32,1,128]{2,1,0:T(1,128)} %bitcast.10), calls=%async_computation.1 | async-start | bytes 32768 | tf_op jit(solution)/shard_map/all_to_all | solution.py:598
  (6 other events, 34.4 us)

commit v7 on v5

--- a/solution.py
+++ b/solution.py
@@ -441,7 +441,7 @@
     if direct:
         step = holder ^ row
         block = step
-        for j, spot in ((1, 1), (3, 2), (2, 3), (5, 4), (6, 5), (7, 6), (4, 7)):
+        for j, spot in ((2, 3), (3, 2), (5, 6), (6, 5)):
             block = jnp.where(step == j, spot, block)
     places = block * capacity + jnp.minimum(rank, capacity - 1)
     places = jnp.where(live > 0, places, places[0])
@@ -476,22 +476,13 @@
 
     got = {0: picked[0]}
     if direct:
-        for j in (1, 3, 5, 6, 2, 7, 4):
-            message = picked[j] if j not in (4, 7) else after(picked[j], got[5], got[6])
-            got[j] = flip(message, "rows", j)
-
-    strengths = jax.ShapeDtypeStruct((tile_total, share, side), bf16)
-    (mask,) = call(
-        mask_kernel,
-        [strengths],
-        [smem, anywhere],
-        "mask",
-        [pltpu.SemaphoreType.DMA],
-        10**9,
-    )(
-        after(info, got[1] if direct else picked[0]),
-        pltpu.with_memory_space_constraint(tile_mask, pltpu.HBM),
-    )
+        for j in (1, 3, 4, 6, 2):
+            got[j] = flip(picked[j], "rows", j)
+        across = flip(got[0], "cols", 2)
+        near = after(gather(got[1], got[3]), across)
+        for j in (5, 7):
+            got[j] = flip(after(picked[j], got[4], got[6], near), "rows", j)
+
     square = jax.ShapeDtypeStruct((width, width), f32)
     extra = width // col_width
     packed = jax.ShapeDtypeStruct((extra, col_width, 2 * width), bf16)
@@ -506,29 +497,43 @@
             pltpu.SemaphoreType.DMA((2 * n_cols,)),
         ],
         10**9,
-    )(after(info, got[1] if direct else picked[0]), *shared)
+    )(after(info, near if direct else picked[0]), *shared)
+    strengths = jax.ShapeDtypeStruct((tile_total, share, side), bf16)
+
+    def slice_mask(ready):
+        return call(
+            mask_kernel,
+            [strengths],
+            [smem, anywhere],
+            "mask",
+            [pltpu.SemaphoreType.DMA],
+            10**9,
+        )(after(info, ready), pltpu.with_memory_space_constraint(tile_mask, pltpu.HBM))[0]
+
     if direct:
         slots = (3 * capacity, 3 * capacity, 2 * capacity)
-        own = gather(got[0], got[1], got[3])
-        early = join(own, flip(own, "cols", 2))
+        early = join(got[0], near, across, flip(near, "cols", 2))
         pieces = [early, flip(early, "cols", 1)]
 
-        own = after(gather(got[2], got[5], got[6], carried), early)
+        arrived = flip(carried, "rows", 1)
+        gram, carried = add(gram, after(arrived, got[4], got[6]))
+        own = after(gather(got[2], got[4], got[6]), early)
+        mask = slice_mask(own)
+        arrived = flip(after(carried, own), "rows", 2)
+        gram, carried = add(gram, after(arrived, mask))
+        own = join(own, flip(own, "cols", 2))
+        pieces += [own, flip(after(own, mask), "cols", 1)]
+
+        gram, carried = add(gram, after(flip(carried, "rows", 4), own))
+        own = gather(got[5], got[7], carried)
         arrived = flip(own, "cols", 2)
         gram, carried = add(gram, arrived)
-        own = join(own[: 3 * capacity], arrived[: 3 * capacity], carried)
-        arrived = flip(after(own, mask), "cols", 1)
-        gram, carried = add(gram, arrived)
+        own = join(own[: 2 * capacity], arrived[: 2 * capacity], carried)
+        arrived = flip(own, "cols", 1)
         pieces += [own, arrived]
-
-        own = gather(got[7], got[4])
-        own = join(own, flip(own, "cols", 2))
-        gram, carried = add(gram, flip(carried, "rows", 1))
-        pieces += [own, flip(after(own, carried), "cols", 1)]
-        gram, carried = add(gram, flip(carried, "rows", 2))
-        arrived = flip(carried, "rows", 4)
     else:
         slots = (row_devs * capacity,)
+        mask = slice_mask(gram)
         gram = add_all(gram)
         own = lax.all_to_all(picked[0], "rows", split_axis=0, concat_axis=0, tiled=True)
         own = join(own, flip(own, "cols", 2))

time: 104 us -> 105 us (level)
  starting transfers between devices: 31.1 us -> 36 us
  waiting for transfers between devices: 40 us -> 37.2 us
    ppermute x25 -> x26, starting transfers between devices: 20 us -> 27.3 us  [flip(): return lax.ppermute(value, axis, [(i, i ^ bit) for i in range(size)])]
    all_to_all x1, starting transfers between devices: 5.01 us -> 2.56 us  [on_device(): lax.all_to_all(dots, ('rows', 'cols'), split_axis=0, concat_axis=0, tiled...]
    ppermute x25 -> x26, waiting for transfers between devices: 28.2 us -> 26.5 us  [flip(): return lax.ppermute(value, axis, [(i, i ^ bit) for i in range(size)])]
    all_to_all x1, waiting for transfers between devices: 7.04 us -> 5.93 us  [on_device(): lax.all_to_all(dots, ('rows', 'cols'), split_axis=0, concat_axis=0, tiled...]
  transfers between devices with their start and end apart: 27 -> 28, of which waited for: 12 -> 12; matrix products, arithmetic and copies ran while one was open for 2% -> 2% of each run, Pallas kernels for 16% -> 10%
where the time goes in v7:
time: 105 us
  waiting for transfers between devices  37.2 us (35%)
  starting transfers between devices  36 us (34%)
  Pallas kernels  27.2 us (26%)
  local copies, waits for them, and re-layouts  1.95 us (2%)
  between operations  1.61 us (2%)
  other arithmetic  1.17 us (1%)
    ppermute x26, starting transfers between devices, flip(): return lax.ppermute(value, axis, [(i, i ^ bit) for i in range(size)])  27.3 us
    ppermute x26, waiting for transfers between devices, flip(): return lax.ppermute(value, axis, [(i, i ^ bit) for i in range(size)])  26.5 us
    all_to_all x1, starting transfers between devices, on_device(): lax.all_to_all(requests, 'rows', split_axis=0, concat_axis=0, tiled=True)  6.07 us
    all_to_all x1, waiting for transfers between devices, on_device(): lax.all_to_all(dots, ('rows', 'cols'), split_axis=0, concat_axis=0, tiled...  5.93 us
    pallas_call x1, Pallas kernels, on_device(): call(second_kernel, [jax.ShapeDtypeStruct((n_cols, col_width, own_users),...  5.84 us
    pallas_call x1, Pallas kernels, on_device(): call(functools.partial(start_kernel, n_cols, slots), [vector, held], [sme...  5.7 us
    pallas_call x1, Pallas kernels, on_device(): call(first_kernel, [pair, vector, vector], [smem] * 3 + [vmem] * 5, 'firs...  5.38 us
    all_to_all x1, waiting for transfers between devices, on_device(): lax.all_to_all(requests, 'rows', split_axis=0, concat_axis=0, tiled=True)  4.76 us
  transfers between devices with their start and end apart: 28, of which 12 were waited for; matrix products, arithmetic and copies ran while one was open for 2% of the time, Pallas kernels for 10%

profile of v7, /device:TPU:0, one launch (start us, length us, event | category | flops | bytes accessed | tf_op | source)
XLA Modules:
  0.0 105.0 jit_solution(15710581487958725477)
XLA Ops:
  1.4 1.7 %prepare.1 = (bf16[32,3072]{1,0:T(8,128)(2,1)S(1)}, bf16[32,3072]{1,0:T(8,128)(2,1)S(1)}, bf16[32,3072]{1,0:T(8,128)(2,1)S(1)}, bf16[32,3072]{1,0:T(8,128)(2,1)S(1)}) custom-call(s32[3]{0:T(128)S(1)} %pad_add_fusion.info_ref, f32[32,2048]{1,0:T(8,128)} %x_ref.1, bf16[32,8192]{1,0:T(8,128)(2,1)} %items_ref.1), custom_call_target="tpu_custom_call" | custom-call | flops 1000000000 | tf_op jit(solution)/shard_map/prepare/pallas_call | solution.py:406
  3.6 2.6 %collective-permute-start.1 = (bf16[32,3072]{1,0:T(8,128)(2,1)S(1)}, bf16[32,3072]{1,0:T(8,128)(2,1)S(1)}, u32[]{:S(2)}, u32[]{:S(2)}) collective-permute-start(bf16[32,3072]{1,0:T(8,128)(2,1)S(1)} %get-tuple-element.51), channel_id=1, source_target_pairs={{0,2},{1,3},{2,0},{3,1},{4,6},{5,7},{6,4},{7,5},{8,10},{9,11},{10,... | collective-permute-start | bytes 589832 | tf_op jit(solution)/shard_map/ppermute | solution.py:348
  7.9 6.1 %all-to-all-start = ((s32[8,1,9]{2,1,0:T(1,128)}), s32[8,1,9]{2,1,0:T(1,128)S(1)}, u32[]{:S(2)}, u32[]{:S(2)}) async-start(s32[8,1,9]{2,1,0:T(1,128)} %bitcast.5), calls=%async_computation | async-start | bytes 8192 | tf_op jit(solution)/shard_map/all_to_all | solution.py:439
  14.0 1.6 %collective-permute-done.2.refs_3_ = bf16[32,3072]{1,0:T(8,128)(2,1)S(1)} collective-permute-done((bf16[32,3072]{1,0:T(8,128)(2,1)S(1)}, bf16[32,3072]{1,0:T(8,128)(2,1)S(1)}, u32[]{:S(2)}, u32[]{:S(2)}) %collective-permute-start.2) | collective-permute-done | bytes 196640 | tf_op jit(solution)/shard_map/ppermute | solution.py:348
  15.6 4.8 %all-to-all-done = s32[8,1,9]{2,1,0:T(1,128)S(1)} async-done(((s32[8,1,9]{2,1,0:T(1,128)}), s32[8,1,9]{2,1,0:T(1,128)S(1)}, u32[]{:S(2)}, u32[]{:S(2)}) %all-to-all-start) | async-done | bytes 320 | tf_op jit(solution)/shard_map/all_to_all | solution.py:439
  28.6 1.7 %collective-permute-start.8 = (bf16[9,32,256]{2,1,0:T(8,128)(2,1)S(1)}, bf16[9,32,256]{2,1,0:T(8,128)(2,1)S(1)}, u32[]{:S(2)}, u32[]{:S(2)}) collective-permute-start(bf16[9,32,256]{2,1,0:T(8,128)(2,1)S(1)} %get-tuple-element.62), channel_id=1, source_target_pairs={{0,24},{4,28},{8,16},{12,20},{16,8},{20,12},{24,0},{28,4},{1,25},{... | collective-permute-start | bytes 442376 | tf_op jit(solution)/shard_map/ppermute | solution.py:348
  33.6 1.8 %collective-permute-done.6.refs_0_ = bf16[9,32,256]{2,1,0:T(8,128)(2,1)S(1)} collective-permute-done((bf16[9,32,256]{2,1,0:T(8,128)(2,1)S(1)}, bf16[9,32,256]{2,1,0:T(8,128)(2,1)S(1)}, u32[]{:S(2)}, u32[]{:S(2)}) %collective-permute-start.6) | collective-permute-done | bytes 147488 | tf_op jit(solution)/shard_map/ppermute | solution.py:348
  35.4 3.5 %collective-permute-done.7.refs_1_ = bf16[9,32,256]{2,1,0:T(8,128)(2,1)S(1)} collective-permute-done((bf16[9,32,256]{2,1,0:T(8,128)(2,1)S(1)}, bf16[9,32,256]{2,1,0:T(8,128)(2,1)S(1)}, u32[]{:S(2)}, u32[]{:S(2)}) %collective-permute-start.7) | collective-permute-done | bytes 147488 | tf_op jit(solution)/shard_map/ppermute | solution.py:348
  42.4 2.0 %collective-permute-start.15 = (bf16[4,32,256]{2,1,0:T(8,128)(2,1)S(1)}, bf16[4,32,256]{2,1,0:T(8,128)(2,1)S(1)}, u32[]{:S(2)}, u32[]{:S(2)}) collective-permute-start(bf16[4,32,256]{2,1,0:T(8,128)(2,1)S(1)} %get-tuple-element.71), channel_id=1, source_target_pairs={{0,4},{4,0},{8,12},{12,8},{16,20},{20,16},{24,28},{28,24},{1,5},{5... | collective-permute-start | bytes 196616 | tf_op jit(solution)/shard_map/ppermute | solution.py:348
  45.9 2.0 %collective-permute-start.14 = (bf16[9,32,256]{2,1,0:T(8,128)(2,1)S(1)}, bf16[9,32,256]{2,1,0:T(8,128)(2,1)S(1)}, u32[]{:S(2)}, u32[]{:S(2)}) collective-permute-start(bf16[9,32,256]{2,1,0:T(8,128)(2,1)S(1)} %get-tuple-element.69), channel_id=1, source_target_pairs={{0,28},{4,24},{8,20},{12,16},{16,12},{20,8},{24,4},{28,0},{1,29},{... | collective-permute-start | bytes 442376 | tf_op jit(solution)/shard_map/ppermute | solution.py:348
  48.0 3.0 %collective-permute-start.16 = (bf16[4,32,256]{2,1,0:T(8,128)(2,1)S(1)}, bf16[4,32,256]{2,1,0:T(8,128)(2,1)S(1)}, u32[]{:S(2)}, u32[]{:S(2)}) collective-permute-start(bf16[4,32,256]{2,1,0:T(8,128)(2,1)S(1)} %get-tuple-element.75), channel_id=1, source_target_pairs={{0,8},{4,12},{8,0},{12,4},{16,24},{20,28},{24,16},{28,20},{1,9},{5... | collective-permute-start | bytes 196616 | tf_op jit(solution)/shard_map/ppermute | solution.py:348
  51.0 2.3 %mask.1 = bf16[72,64,256]{2,1,0:T(8,128)(2,1)S(1)} custom-call(s32[3]{0:T(128)S(1)} %pad_add_fusion.info_ref, bf16[72,256,256]{2,1,0:T(8,128)(2,1)} %mask_hbm.1), custom_call_target="tpu_custom_call" | custom-call | flops 1000000000 | tf_op jit(solution)/shard_map/mask/pallas_call | solution.py:504
  53.3 2.7 %collective-permute-done.16.arrived_ref = bf16[4,32,256]{2,1,0:T(8,128)(2,1)S(1)} collective-permute-done((bf16[4,32,256]{2,1,0:T(8,128)(2,1)S(1)}, bf16[4,32,256]{2,1,0:T(8,128)(2,1)S(1)}, u32[]{:S(2)}, u32[]{:S(2)}) %collective-permute-start.16) | collective-permute-done | bytes 65568 | tf_op jit(solution)/shard_map/ppermute | solution.py:348
  56.1 5.1 %collective-permute-done.17.arrived_ref = bf16[4,32,256]{2,1,0:T(8,128)(2,1)S(1)} collective-permute-done((bf16[4,32,256]{2,1,0:T(8,128)(2,1)S(1)}, bf16[4,32,256]{2,1,0:T(8,128)(2,1)S(1)}, u32[]{:S(2)}, u32[]{:S(2)}) %collective-permute-start.17) | collective-permute-done | bytes 65568 | tf_op jit(solution)/shard_map/ppermute | solution.py:348
  62.9 6.4 %collective-permute-done.18.arrived_ref = bf16[22,32,256]{2,1,0:T(8,128)(2,1)S(1)} collective-permute-done((bf16[22,32,256]{2,1,0:T(8,128)(2,1)S(1)}, bf16[22,32,256]{2,1,0:T(8,128)(2,1)S(1)}, u32[]{:S(2)}, u32[]{:S(2)}) %collective-permute-start.18) | collective-permute-done | bytes 360480 | tf_op jit(solution)/shard_map/ppermute | solution.py:348
  69.6 2.0 %collective-permute-done.19.refs_5_.arrived_ref = bf16[40,32,256]{2,1,0:T(8,128)(2,1)S(1)} collective-permute-done((bf16[40,32,256]{2,1,0:T(8,128)(2,1)S(1)}, bf16[40,32,256]{2,1,0:T(8,128)(2,1)S(1)}, u32[]{:S(2)}, u32[]{:S(2)}) %collective-permute-start.19) | collective-permute-done | bytes 655392 | tf_op jit(solution)/shard_map/ppermute | solution.py:348
  71.6 5.7 %start.1 = (f32[512,128]{1,0:T(8,128)S(1)}, bf16[72,128,256]{2,1,0:T(8,128)(2,1)S(1)}) custom-call(s32[72]{0:T(128)S(1)} %get-tuple-element.107.slot_ref, s32[72]{0:T(128)S(1)} %get-tuple-element.106.user_ref, s32[3]{0:T(128)S(1)} %pad_add_fusion.info_ref, f32[128,512]{1,0:T(8,128)S(1)} %get-tuple-element.59.x_ref, bf16[72,64,256]{2,1,0:T(8,128)(2,1)S(1)} %mask.1, ...), custom_call_target="tpu_custom_call" | custom-call | flops 8000000000 | tf_op jit(solution)/shard_map/start/pallas_call | solution.py:550
  78.0 5.4 %first.1 = (f32[4,64,512]{2,1,0:T(8,128)S(1)}, f32[512,128]{1,0:T(8,128)S(1)}, f32[512,128]{1,0:T(8,128)S(1)}) custom-call(s32[72]{0:T(128)S(1)} %get-tuple-element.107.slot_ref, s32[72]{0:T(128)S(1)} %get-tuple-element.106.user_ref, s32[3]{0:T(128)S(1)} %pad_add_fusion.info_ref, f32[128,512]{1,0:T(8,128)S(1)} %get-tuple-element.59.x_ref, ...), custom_call_target="tpu_custom_call" | custom-call | flops 8000000000 | tf_op jit(solution)/shard_map/first/pallas_call | solution.py:561
  83.7 1.6 %collective-permute-start.21 = (f32[64,512]{1,0:T(8,128)S(1)}, f32[64,512]{1,0:T(8,128)S(1)}, u32[]{:S(2)}, u32[]{:S(2)}) collective-permute-start(f32[64,512]{1,0:T(8,128)S(1)} %get-tuple-element.95), channel_id=1, source_target_pairs={{0,2},{1,3},{2,0},{3,1},{4,6},{5,7},{6,4},{7,5},{8,10},{9,11},{10,... | collective-permute-start | bytes 393224 | tf_op jit(solution)/shard_map/ppermute | solution.py:348
  85.3 5.8 %second.1 = (f32[4,32,512]{2,1,0:T(8,128)S(1)}, f32[32,128]{1,0:T(8,128)}) custom-call(s32[72]{0:T(128)S(1)} %get-tuple-element.107.slot_ref, s32[72]{0:T(128)S(1)} %get-tuple-element.106.user_ref, s32[3]{0:T(128)S(1)} %pad_add_fusion.info_ref, f32[512,128]{1,0:T(8,128)S(1)} %get-tuple-element.88.field_ref, f32[512,128]{1,0:T(8,128)S(1)} %get-tuple-element.89.first_ref, ...), custom_call_target="tpu_custom_call" | custom-call | flops 8000000000 | tf_op jit(solution)/shard_map/second/pallas_call | solution.py:569
  91.8 1.6 %collective-permute-start.24 = (f32[32,512]{1,0:T(8,128)S(1)}, f32[32,512]{1,0:T(8,128)S(1)}, u32[]{:S(2)}, u32[]{:S(2)}) collective-permute-start(f32[32,512]{1,0:T(8,128)S(1)} %get-tuple-element.99), channel_id=1, source_target_pairs={{0,2},{1,3},{2,0},{3,1},{4,6},{5,7},{6,4},{7,5},{8,10},{9,11},{10,... | collective-permute-start | bytes 196616 | tf_op jit(solution)/shard_map/ppermute | solution.py:348
  93.4 2.6 %all-to-all-start.1 = ((f32[32,1,128]{2,1,0:T(1,128)}), f32[32,1,128]{2,1,0:T(1,128)S(1)}, u32[]{:S(2)}, u32[]{:S(2)}) async-start(f32[32,1,128]{2,1,0:T(1,128)} %bitcast.12), calls=%async_computation.1 | async-start | bytes 32768 | tf_op jit(solution)/shard_map/all_to_all | solution.py:584
  97.1 5.9 %all-to-all-done.1 = f32[32,1,128]{2,1,0:T(1,128)S(1)} async-done(((f32[32,1,128]{2,1,0:T(1,128)}), f32[32,1,128]{2,1,0:T(1,128)S(1)}, u32[]{:S(2)}, u32[]{:S(2)}) %all-to-all-start.1) | async-done | bytes 16416 | tf_op jit(solution)/shard_map/all_to_all | solution.py:584
  103.0 2.0 %finish.1 = (f32[32,2048]{1,0:T(8,128)}, f32[32,2048]{1,0:T(8,128)}) custom-call(s32[3]{0:T(128)S(1)} %pad_add_fusion.info_ref, f32[32,128]{1,0:T(8,128)S(1)} %bitcast.31, f32[32,2048]{1,0:T(8,128)S(1)} %copy-done.1, f32[64,512]{1,0:T(8,128)S(1)} %get-tuple-element.97.refs_0_, f32[64,512]{1,0:T(8,128)S(1)} %collective-permute-done.20.refs_1_, ...), custom_call_target="tpu_custom_call" | custom-call | flops 1000000000 | tf_op jit(solution)/shard_map/finish/pallas_call | solution.py:587
  (74 shorter events, 23.5 us)
Async XLA Ops:
  3.1 10.9 %collective-permute-start = (bf16[32,3072]{1,0:T(8,128)(2,1)S(1)}, bf16[32,3072]{1,0:T(8,128)(2,1)S(1)}, u32[]{:S(2)}, u32[]{:S(2)}) collective-permute-start(bf16[32,3072]{1,0:T(8,128)(2,1)S(1)} %get-tuple-element.50), channel_id=1, source_target_pairs={{0,1},{1,0},{2,3},{3,2},{4,5},{5,4},{6,7},{7,6},{8,9},{9,8},{10,11... | collective-permute-start | bytes 589832 | tf_op jit(solution)/shard_map/ppermute | solution.py:348
  3.6 10.4 %collective-permute-start.1 = (bf16[32,3072]{1,0:T(8,128)(2,1)S(1)}, bf16[32,3072]{1,0:T(8,128)(2,1)S(1)}, u32[]{:S(2)}, u32[]{:S(2)}) collective-permute-start(bf16[32,3072]{1,0:T(8,128)(2,1)S(1)} %get-tuple-element.51), channel_id=1, source_target_pairs={{0,2},{1,3},{2,0},{3,1},{4,6},{5,7},{6,4},{7,5},{8,10},{9,11},{10,... | collective-permute-start | bytes 589832 | tf_op jit(solution)/shard_map/ppermute | solution.py:348
  6.2 9.4 %collective-permute-start.2 = (bf16[32,3072]{1,0:T(8,128)(2,1)S(1)}, bf16[32,3072]{1,0:T(8,128)(2,1)S(1)}, u32[]{:S(2)}, u32[]{:S(2)}) collective-permute-start(bf16[32,3072]{1,0:T(8,128)(2,1)S(1)} %get-tuple-element.52), channel_id=1, source_target_pairs={{0,3},{1,2},{2,1},{3,0},{4,7},{5,6},{6,5},{7,4},{8,11},{9,10},{10,... | collective-permute-start | bytes 589832 | tf_op jit(solution)/shard_map/ppermute | solution.py:348
  7.9 12.5 %all-to-all-start = ((s32[8,1,9]{2,1,0:T(1,128)}), s32[8,1,9]{2,1,0:T(1,128)S(1)}, u32[]{:S(2)}, u32[]{:S(2)}) async-start(s32[8,1,9]{2,1,0:T(1,128)} %bitcast.5), calls=%async_computation | async-start | bytes 8192 | tf_op jit(solution)/shard_map/all_to_all | solution.py:439
  22.2 6.3 %collective-permute-start.3 = (bf16[9,32,256]{2,1,0:T(8,128)(2,1)S(1)}, bf16[9,32,256]{2,1,0:T(8,128)(2,1)S(1)}, u32[]{:S(2)}, u32[]{:S(2)}) collective-permute-start(bf16[9,32,256]{2,1,0:T(8,128)(2,1)S(1)} %get-tuple-element.54), channel_id=1, source_target_pairs={{0,4},{4,0},{8,12},{12,8},{16,20},{20,16},{24,28},{28,24},{1,5},{5... | collective-permute-start | bytes 442376 | tf_op jit(solution)/shard_map/ppermute | solution.py:348
  22.8 8.8 %collective-permute-start.4 = (bf16[9,32,256]{2,1,0:T(8,128)(2,1)S(1)}, bf16[9,32,256]{2,1,0:T(8,128)(2,1)S(1)}, u32[]{:S(2)}, u32[]{:S(2)}) collective-permute-start(bf16[9,32,256]{2,1,0:T(8,128)(2,1)S(1)} %get-tuple-element.55), channel_id=1, source_target_pairs={{0,12},{4,8},{8,4},{12,0},{16,28},{20,24},{24,20},{28,16},{1,13},{... | collective-permute-start | bytes 442376 | tf_op jit(solution)/shard_map/ppermute | solution.py:348
  24.3 11.1 %collective-permute-start.6 = (bf16[9,32,256]{2,1,0:T(8,128)(2,1)S(1)}, bf16[9,32,256]{2,1,0:T(8,128)(2,1)S(1)}, u32[]{:S(2)}, u32[]{:S(2)}) collective-permute-start(bf16[9,32,256]{2,1,0:T(8,128)(2,1)S(1)} %get-tuple-element.60), channel_id=1, source_target_pairs={{0,8},{4,12},{8,0},{12,4},{16,24},{20,28},{24,16},{28,20},{1,9},{5... | collective-permute-start | bytes 442376 | tf_op jit(solution)/shard_map/ppermute | solution.py:348
  25.8 13.1 %collective-permute-start.7 = (bf16[9,32,256]{2,1,0:T(8,128)(2,1)S(1)}, bf16[9,32,256]{2,1,0:T(8,128)(2,1)S(1)}, u32[]{:S(2)}, u32[]{:S(2)}) collective-permute-start(bf16[9,32,256]{2,1,0:T(8,128)(2,1)S(1)} %get-tuple-element.61), channel_id=1, source_target_pairs={{0,16},{4,20},{8,24},{12,28},{16,0},{20,4},{24,8},{28,12},{1,17},{... | collective-permute-start | bytes 442376 | tf_op jit(solution)/shard_map/ppermute | solution.py:348
  26.3 5.7 %collective-permute-start.5 = (bf16[9,32,256]{2,1,0:T(8,128)(2,1)S(1)}, bf16[9,32,256]{2,1,0:T(8,128)(2,1)S(1)}, u32[]{:S(2)}, u32[]{:S(2)}) collective-permute-start(bf16[9,32,256]{2,1,0:T(8,128)(2,1)S(1)} %get-tuple-element.56), channel_id=1, source_target_pairs={{0,2},{1,3},{2,0},{3,1},{4,6},{5,7},{6,4},{7,5},{8,10},{9,11},{10,... | collective-permute-start | bytes 442376 | tf_op jit(solution)/shard_map/ppermute | solution.py:348
  28.6 10.3 %collective-permute-start.8 = (bf16[9,32,256]{2,1,0:T(8,128)(2,1)S(1)}, bf16[9,32,256]{2,1,0:T(8,128)(2,1)S(1)}, u32[]{:S(2)}, u32[]{:S(2)}) collective-permute-start(bf16[9,32,256]{2,1,0:T(8,128)(2,1)S(1)} %get-tuple-element.62), channel_id=1, source_target_pairs={{0,24},{4,28},{8,16},{12,20},{16,8},{20,12},{24,0},{28,4},{1,25},{... | collective-permute-start | bytes 442376 | tf_op jit(solution)/shard_map/ppermute | solution.py:348
  32.1 7.5 %collective-permute-start.9 = (bf16[18,32,256]{2,1,0:T(8,128)(2,1)S(1)}, bf16[18,32,256]{2,1,0:T(8,128)(2,1)S(1)}, u32[]{:S(2)}, u32[]{:S(2)}) collective-permute-start(bf16[18,32,256]{2,1,0:T(8,128)(2,1)S(1)} %join.3), channel_id=1, source_target_pairs={{0,2},{1,3},{2,0},{3,1},{4,6},{5,7},{6,4},{7,5},{8,10},{9,11},{10,... | collective-permute-start | bytes 884744 | tf_op jit(solution)/shard_map/ppermute | solution.py:348
  39.6 16.5 %collective-permute-start.11 = (bf16[27,32,256]{2,1,0:T(8,128)(2,1)S(1)}, bf16[27,32,256]{2,1,0:T(8,128)(2,1)S(1)}, u32[]{:S(2)}, u32[]{:S(2)}) collective-permute-start(bf16[27,32,256]{2,1,0:T(8,128)(2,1)S(1)} %join.4), channel_id=1, source_target_pairs={{0,2},{1,3},{2,0},{3,1},{4,6},{5,7},{6,4},{7,5},{8,10},{9,11},{10,... | collective-permute-start | bytes 1327112 | tf_op jit(solution)/shard_map/ppermute | solution.py:348
  42.4 5.6 %collective-permute-start.15 = (bf16[4,32,256]{2,1,0:T(8,128)(2,1)S(1)}, bf16[4,32,256]{2,1,0:T(8,128)(2,1)S(1)}, u32[]{:S(2)}, u32[]{:S(2)}) collective-permute-start(bf16[4,32,256]{2,1,0:T(8,128)(2,1)S(1)} %get-tuple-element.71), channel_id=1, source_target_pairs={{0,4},{4,0},{8,12},{12,8},{16,20},{20,16},{24,28},{28,24},{1,5},{5... | collective-permute-start | bytes 196616 | tf_op jit(solution)/shard_map/ppermute | solution.py:348
  44.4 16.9 %collective-permute-start.13 = (bf16[9,32,256]{2,1,0:T(8,128)(2,1)S(1)}, bf16[9,32,256]{2,1,0:T(8,128)(2,1)S(1)}, u32[]{:S(2)}, u32[]{:S(2)}) collective-permute-start(bf16[9,32,256]{2,1,0:T(8,128)(2,1)S(1)} %get-tuple-element.67), channel_id=1, source_target_pairs={{0,20},{4,16},{8,28},{12,24},{16,4},{20,0},{24,12},{28,8},{1,21},{... | collective-permute-start | bytes 442376 | tf_op jit(solution)/shard_map/ppermute | solution.py:348
  45.9 15.4 %collective-permute-start.14 = (bf16[9,32,256]{2,1,0:T(8,128)(2,1)S(1)}, bf16[9,32,256]{2,1,0:T(8,128)(2,1)S(1)}, u32[]{:S(2)}, u32[]{:S(2)}) collective-permute-start(bf16[9,32,256]{2,1,0:T(8,128)(2,1)S(1)} %get-tuple-element.69), channel_id=1, source_target_pairs={{0,28},{4,24},{8,20},{12,16},{16,12},{20,8},{24,4},{28,0},{1,29},{... | collective-permute-start | bytes 442376 | tf_op jit(solution)/shard_map/ppermute | solution.py:348
  48.0 8.0 %collective-permute-start.16 = (bf16[4,32,256]{2,1,0:T(8,128)(2,1)S(1)}, bf16[4,32,256]{2,1,0:T(8,128)(2,1)S(1)}, u32[]{:S(2)}, u32[]{:S(2)}) collective-permute-start(bf16[4,32,256]{2,1,0:T(8,128)(2,1)S(1)} %get-tuple-element.75), channel_id=1, source_target_pairs={{0,8},{4,12},{8,0},{12,4},{16,24},{20,28},{24,16},{28,20},{1,9},{5... | collective-permute-start | bytes 196616 | tf_op jit(solution)/shard_map/ppermute | solution.py:348
  61.8 7.5 %collective-permute-start.18 = (bf16[22,32,256]{2,1,0:T(8,128)(2,1)S(1)}, bf16[22,32,256]{2,1,0:T(8,128)(2,1)S(1)}, u32[]{:S(2)}, u32[]{:S(2)}) collective-permute-start(bf16[22,32,256]{2,1,0:T(8,128)(2,1)S(1)} %join.5), channel_id=1, source_target_pairs={{0,2},{1,3},{2,0},{3,1},{4,6},{5,7},{6,4},{7,5},{8,10},{9,11},{10,... | collective-permute-start | bytes 1081352 | tf_op jit(solution)/shard_map/ppermute | solution.py:348
  62.3 7.3 %collective-permute-start.10 = (bf16[54,32,256]{2,1,0:T(8,128)(2,1)S(1)}, bf16[54,32,256]{2,1,0:T(8,128)(2,1)S(1)}, u32[]{:S(2)}, u32[]{:S(2)}) collective-permute-start(bf16[54,32,256]{2,1,0:T(8,128)(2,1)S(1)} %constant_dynamic-update-slice_fusion.refs_0_), channel_id=1, source_target_pairs={{0,1},{1,0},{2,3},{3,2},{4,5},{5,4},{6,7},{7,6},{8,9},{9,8},{10,11... | collective-permute-start | bytes 2654216 | tf_op jit(solution)/shard_map/ppermute | solution.py:348
  62.3 7.3 %collective-permute-start.12 = (bf16[54,32,256]{2,1,0:T(8,128)(2,1)S(1)}, bf16[54,32,256]{2,1,0:T(8,128)(2,1)S(1)}, u32[]{:S(2)}, u32[]{:S(2)}) collective-permute-start(bf16[54,32,256]{2,1,0:T(8,128)(2,1)S(1)} %constant_dynamic-update-slice_fusion.4.refs_2_), channel_id=1, source_target_pairs={{0,1},{1,0},{2,3},{3,2},{4,5},{5,4},{6,7},{7,6},{8,9},{9,8},{10,11... | collective-permute-start | bytes 2654216 | tf_op jit(solution)/shard_map/ppermute | solution.py:348
  83.4 9.9 %collective-permute-start.22 = (f32[64,512]{1,0:T(8,128)S(1)}, f32[64,512]{1,0:T(8,128)S(1)}, u32[]{:S(2)}, u32[]{:S(2)}) collective-permute-start(f32[64,512]{1,0:T(8,128)S(1)} %get-tuple-element.94), channel_id=1, source_target_pairs={{0,3},{1,2},{2,1},{3,0},{4,7},{5,6},{6,5},{7,4},{8,11},{9,10},{10,... | collective-permute-start | bytes 393224 | tf_op jit(solution)/shard_map/ppermute | solution.py:348
  83.7 9.7 %collective-permute-start.21 = (f32[64,512]{1,0:T(8,128)S(1)}, f32[64,512]{1,0:T(8,128)S(1)}, u32[]{:S(2)}, u32[]{:S(2)}) collective-permute-start(f32[64,512]{1,0:T(8,128)S(1)} %get-tuple-element.95), channel_id=1, source_target_pairs={{0,2},{1,3},{2,0},{3,1},{4,6},{5,7},{6,4},{7,5},{8,10},{9,11},{10,... | collective-permute-start | bytes 393224 | tf_op jit(solution)/shard_map/ppermute | solution.py:348
  85.3 8.1 %collective-permute-start.20 = (f32[64,512]{1,0:T(8,128)S(1)}, f32[64,512]{1,0:T(8,128)S(1)}, u32[]{:S(2)}, u32[]{:S(2)}) collective-permute-start(f32[64,512]{1,0:T(8,128)S(1)} %get-tuple-element.96), channel_id=1, source_target_pairs={{0,1},{1,0},{2,3},{3,2},{4,5},{5,4},{6,7},{7,6},{8,9},{9,8},{10,11... | collective-permute-start | bytes 393224 | tf_op jit(solution)/shard_map/ppermute | solution.py:348
  91.8 5.3 %collective-permute-start.24 = (f32[32,512]{1,0:T(8,128)S(1)}, f32[32,512]{1,0:T(8,128)S(1)}, u32[]{:S(2)}, u32[]{:S(2)}) collective-permute-start(f32[32,512]{1,0:T(8,128)S(1)} %get-tuple-element.99), channel_id=1, source_target_pairs={{0,2},{1,3},{2,0},{3,1},{4,6},{5,7},{6,4},{7,5},{8,10},{9,11},{10,... | collective-permute-start | bytes 196616 | tf_op jit(solution)/shard_map/ppermute | solution.py:348
  93.4 9.6 %all-to-all-start.1 = ((f32[32,1,128]{2,1,0:T(1,128)}), f32[32,1,128]{2,1,0:T(1,128)S(1)}, u32[]{:S(2)}, u32[]{:S(2)}) async-start(f32[32,1,128]{2,1,0:T(1,128)} %bitcast.12), calls=%async_computation.1 | async-start | bytes 32768 | tf_op jit(solution)/shard_map/all_to_all | solution.py:584
  (7 other events, 42.8 us)

commit v8 on v7

--- a/solution.py
+++ b/solution.py
@@ -124,9 +124,12 @@
     pack(pack_ref, gram)
 
 
-def add_kernel(gram_ref, arrived_ref, out_ref, pack_ref):
+def add_kernel(gram_ref, *refs):
+    out_ref, pack_ref = refs[-2:]
     extra = pack_ref.shape[0]
-    total = gram_ref[...] + unpack(arrived_ref[arrived_ref.shape[0] - extra :])
+    total = gram_ref[...]
+    for arrived_ref in refs[:-2]:
+        total = total + unpack(arrived_ref[arrived_ref.shape[0] - extra :])
     out_ref[...] = total
     pack(pack_ref, total)
 
@@ -471,8 +474,10 @@
             2 * 10**10,
         )(*arrays)[0]
 
-    def add(gram, arrived):
-        return call(add_kernel, [square, packed], [vmem] * 2, "add")(gram, arrived)
+    def add(gram, *arrived):
+        return call(add_kernel, [square, packed], [vmem] * (1 + len(arrived)), "add")(
+            gram, *arrived
+        )
 
     got = {0: picked[0]}
     if direct:
@@ -515,22 +520,20 @@
         early = join(got[0], near, across, flip(near, "cols", 2))
         pieces = [early, flip(early, "cols", 1)]
 
-        arrived = flip(carried, "rows", 1)
-        gram, carried = add(gram, after(arrived, got[4], got[6]))
-        own = after(gather(got[2], got[4], got[6]), early)
+        own = after(gather(got[2], got[4], got[6], carried), early)
         mask = slice_mask(own)
-        arrived = flip(after(carried, own), "rows", 2)
-        gram, carried = add(gram, after(arrived, mask))
-        own = join(own, flip(own, "cols", 2))
-        pieces += [own, flip(after(own, mask), "cols", 1)]
-
-        gram, carried = add(gram, after(flip(carried, "rows", 4), own))
-        own = gather(got[5], got[7], carried)
         arrived = flip(own, "cols", 2)
         gram, carried = add(gram, arrived)
-        own = join(own[: 2 * capacity], arrived[: 2 * capacity], carried)
-        arrived = flip(own, "cols", 1)
+        own = join(own[: 3 * capacity], arrived[: 3 * capacity], carried)
+        arrived = flip(after(own, mask), "cols", 1)
+        gram, carried = add(gram, arrived)
         pieces += [own, arrived]
+
+        own = gather(got[5], got[7])
+        own = join(own, flip(own, "cols", 2))
+        gram, carried = add(gram, *[flip(carried, "rows", j) for j in (1, 2, 3)])
+        pieces += [own, flip(after(own, carried), "cols", 1)]
+        arrived = flip(carried, "rows", 4)
     else:
         slots = (row_devs * capacity,)
         mask = slice_mask(gram)

time: 105 us -> 99.7 us (0.950)
  waiting for transfers between devices: 37.2 us -> 27.7 us
  starting transfers between devices: 36 us -> 39.8 us
    ppermute x26 -> x27, waiting for transfers between devices: 26.5 us -> 15.9 us  [flip(): return lax.ppermute(value, axis, [(i, i ^ bit) for i in range(size)])]
    ppermute x26 -> x27, starting transfers between devices: 27.3 us -> 30 us  [flip(): return lax.ppermute(value, axis, [(i, i ^ bit) for i in range(size)])]
    all_to_all x1, starting transfers between devices: 2.56 us -> 3.71 us  [on_device(): lax.all_to_all(dots, ('rows', 'cols'), split_axis=0, concat_axis=0, tiled...]
    all_to_all x1, waiting for transfers between devices: 5.93 us -> 7.04 us  [on_device(): lax.all_to_all(dots, ('rows', 'cols'), split_axis=0, concat_axis=0, tiled...]
  transfers between devices with their start and end apart: 28 -> 29, of which waited for: 12 -> 11; matrix products, arithmetic and copies ran while one was open for 2% -> 2% of each run, Pallas kernels for 10% -> 17%
where the time goes in v8:
time: 99.7 us; the launch traced here: 99.4 us
  starting transfers between devices  39.8 us (40%)
  waiting for transfers between devices  27.7 us (28%)
  Pallas kernels  27.2 us (27%)
  local copies, waits for them, and re-layouts  1.91 us (2%)
  between operations  1.6 us (2%)
  other arithmetic  1.26 us (1%)
    ppermute x27, starting transfers between devices, flip(): return lax.ppermute(value, axis, [(i, i ^ bit) for i in range(size)])  30 us
    ppermute x27, waiting for transfers between devices, flip(): return lax.ppermute(value, axis, [(i, i ^ bit) for i in range(size)])  15.9 us
    all_to_all x1, waiting for transfers between devices, on_device(): lax.all_to_all(dots, ('rows', 'cols'), split_axis=0, concat_axis=0, tiled...  7.04 us
    all_to_all x1, starting transfers between devices, on_device(): lax.all_to_all(requests, 'rows', split_axis=0, concat_axis=0, tiled=True)  6.07 us
    pallas_call x1, Pallas kernels, on_device(): call(second_kernel, [jax.ShapeDtypeStruct((n_cols, col_width, own_users),...  5.84 us
    pallas_call x1, Pallas kernels, on_device(): call(functools.partial(start_kernel, n_cols, slots), [vector, held], [sme...  5.7 us
    pallas_call x1, Pallas kernels, on_device(): call(first_kernel, [pair, vector, vector], [smem] * 3 + [vmem] * 5, 'firs...  5.38 us
    all_to_all x1, waiting for transfers between devices, on_device(): lax.all_to_all(requests, 'rows', split_axis=0, concat_axis=0, tiled=True)  4.76 us
  transfers between devices with their start and end apart: 29, of which 11 were waited for; matrix products, arithmetic and copies ran while one was open for 2% of the time, Pallas kernels for 17%

profile of v8, /device:TPU:0, one launch (start us, length us, event | category | flops | bytes accessed | tf_op | source)
XLA Modules:
  0.0 99.4 jit_solution(6978684123972129073)
XLA Ops:
  1.4 1.7 %prepare.1 = (bf16[32,3072]{1,0:T(8,128)(2,1)S(1)}, bf16[32,3072]{1,0:T(8,128)(2,1)S(1)}, bf16[32,3072]{1,0:T(8,128)(2,1)S(1)}, bf16[32,3072]{1,0:T(8,128)(2,1)S(1)}) custom-call(s32[3]{0:T(128)S(1)} %pad_add_fusion.info_ref, f32[32,2048]{1,0:T(8,128)} %x_ref.1, bf16[32,8192]{1,0:T(8,128)(2,1)} %items_ref.1), custom_call_target="tpu_custom_call" | custom-call | flops 1000000000 | tf_op jit(solution)/shard_map/prepare/pallas_call | solution.py:409
  3.6 2.6 %collective-permute-start.1 = (bf16[32,3072]{1,0:T(8,128)(2,1)S(1)}, bf16[32,3072]{1,0:T(8,128)(2,1)S(1)}, u32[]{:S(2)}, u32[]{:S(2)}) collective-permute-start(bf16[32,3072]{1,0:T(8,128)(2,1)S(1)} %get-tuple-element.46), channel_id=1, source_target_pairs={{0,2},{1,3},{2,0},{3,1},{4,6},{5,7},{6,4},{7,5},{8,10},{9,11},{10,... | collective-permute-start | bytes 589832 | tf_op jit(solution)/shard_map/ppermute | solution.py:351
  7.9 6.1 %all-to-all-start = ((s32[8,1,9]{2,1,0:T(1,128)}), s32[8,1,9]{2,1,0:T(1,128)S(1)}, u32[]{:S(2)}, u32[]{:S(2)}) async-start(s32[8,1,9]{2,1,0:T(1,128)} %bitcast.5), calls=%async_computation | async-start | bytes 8192 | tf_op jit(solution)/shard_map/all_to_all | solution.py:442
  14.0 1.6 %collective-permute-done.2.refs_3_ = bf16[32,3072]{1,0:T(8,128)(2,1)S(1)} collective-permute-done((bf16[32,3072]{1,0:T(8,128)(2,1)S(1)}, bf16[32,3072]{1,0:T(8,128)(2,1)S(1)}, u32[]{:S(2)}, u32[]{:S(2)}) %collective-permute-start.2) | collective-permute-done | bytes 196640 | tf_op jit(solution)/shard_map/ppermute | solution.py:351
  15.6 4.8 %all-to-all-done = s32[8,1,9]{2,1,0:T(1,128)S(1)} async-done(((s32[8,1,9]{2,1,0:T(1,128)}), s32[8,1,9]{2,1,0:T(1,128)S(1)}, u32[]{:S(2)}, u32[]{:S(2)}) %all-to-all-start) | async-done | bytes 320 | tf_op jit(solution)/shard_map/all_to_all | solution.py:442
  26.3 1.5 %collective-permute-start.5 = (bf16[9,32,256]{2,1,0:T(8,128)(2,1)S(1)}, bf16[9,32,256]{2,1,0:T(8,128)(2,1)S(1)}, u32[]{:S(2)}, u32[]{:S(2)}) collective-permute-start(bf16[9,32,256]{2,1,0:T(8,128)(2,1)S(1)} %get-tuple-element.51), channel_id=1, source_target_pairs={{0,2},{1,3},{2,0},{3,1},{4,6},{5,7},{6,4},{7,5},{8,10},{9,11},{10,... | collective-permute-start | bytes 442376 | tf_op jit(solution)/shard_map/ppermute | solution.py:351
  28.6 1.7 %collective-permute-start.8 = (bf16[9,32,256]{2,1,0:T(8,128)(2,1)S(1)}, bf16[9,32,256]{2,1,0:T(8,128)(2,1)S(1)}, u32[]{:S(2)}, u32[]{:S(2)}) collective-permute-start(bf16[9,32,256]{2,1,0:T(8,128)(2,1)S(1)} %get-tuple-element.57), channel_id=1, source_target_pairs={{0,24},{4,28},{8,16},{12,20},{16,8},{20,12},{24,0},{28,4},{1,25},{... | collective-permute-start | bytes 442376 | tf_op jit(solution)/shard_map/ppermute | solution.py:351
  32.1 1.5 %collective-permute-start.9 = (bf16[18,32,256]{2,1,0:T(8,128)(2,1)S(1)}, bf16[18,32,256]{2,1,0:T(8,128)(2,1)S(1)}, u32[]{:S(2)}, u32[]{:S(2)}) collective-permute-start(bf16[18,32,256]{2,1,0:T(8,128)(2,1)S(1)} %join.3), channel_id=1, source_target_pairs={{0,2},{1,3},{2,0},{3,1},{4,6},{5,7},{6,4},{7,5},{8,10},{9,11},{10,... | collective-permute-start | bytes 884744 | tf_op jit(solution)/shard_map/ppermute | solution.py:351
  35.4 3.5 %collective-permute-done.7.refs_1_ = bf16[9,32,256]{2,1,0:T(8,128)(2,1)S(1)} collective-permute-done((bf16[9,32,256]{2,1,0:T(8,128)(2,1)S(1)}, bf16[9,32,256]{2,1,0:T(8,128)(2,1)S(1)}, u32[]{:S(2)}, u32[]{:S(2)}) %collective-permute-start.7) | collective-permute-done | bytes 147488 | tf_op jit(solution)/shard_map/ppermute | solution.py:351
  39.7 1.6 %collective-permute-start.11 = (bf16[31,32,256]{2,1,0:T(8,128)(2,1)S(1)}, bf16[31,32,256]{2,1,0:T(8,128)(2,1)S(1)}, u32[]{:S(2)}, u32[]{:S(2)}) collective-permute-start(bf16[31,32,256]{2,1,0:T(8,128)(2,1)S(1)} %join.4), channel_id=1, source_target_pairs={{0,2},{1,3},{2,0},{3,1},{4,6},{5,7},{6,4},{7,5},{8,10},{9,11},{10,... | collective-permute-start | bytes 1523720 | tf_op jit(solution)/shard_map/ppermute | solution.py:351
  41.2 1.8 %collective-permute-start.13 = (bf16[9,32,256]{2,1,0:T(8,128)(2,1)S(1)}, bf16[9,32,256]{2,1,0:T(8,128)(2,1)S(1)}, u32[]{:S(2)}, u32[]{:S(2)}) collective-permute-start(bf16[9,32,256]{2,1,0:T(8,128)(2,1)S(1)} %get-tuple-element.65), channel_id=1, source_target_pairs={{0,20},{4,16},{8,28},{12,24},{16,4},{20,0},{24,12},{28,8},{1,21},{... | collective-permute-start | bytes 442376 | tf_op jit(solution)/shard_map/ppermute | solution.py:351
  43.0 3.6 %collective-permute-start.14 = (bf16[9,32,256]{2,1,0:T(8,128)(2,1)S(1)}, bf16[9,32,256]{2,1,0:T(8,128)(2,1)S(1)}, u32[]{:S(2)}, u32[]{:S(2)}) collective-permute-start(bf16[9,32,256]{2,1,0:T(8,128)(2,1)S(1)} %get-tuple-element.67), channel_id=1, source_target_pairs={{0,28},{4,24},{8,20},{12,16},{16,12},{20,8},{24,4},{28,0},{1,29},{... | collective-permute-start | bytes 442376 | tf_op jit(solution)/shard_map/ppermute | solution.py:351
  46.6 2.3 %mask.1 = bf16[72,64,256]{2,1,0:T(8,128)(2,1)S(1)} custom-call(s32[3]{0:T(128)S(1)} %pad_add_fusion.info_ref, bf16[72,256,256]{2,1,0:T(8,128)(2,1)} %mask_hbm.1), custom_call_target="tpu_custom_call" | custom-call | flops 1000000000 | tf_op jit(solution)/shard_map/mask/pallas_call | solution.py:509
  50.0 3.7 %collective-permute-done.13.refs_0_ = bf16[9,32,256]{2,1,0:T(8,128)(2,1)S(1)} collective-permute-done((bf16[9,32,256]{2,1,0:T(8,128)(2,1)S(1)}, bf16[9,32,256]{2,1,0:T(8,128)(2,1)S(1)}, u32[]{:S(2)}, u32[]{:S(2)}) %collective-permute-start.13) | collective-permute-done | bytes 147488 | tf_op jit(solution)/shard_map/ppermute | solution.py:351
  54.9 3.1 %collective-permute-start.18 = (bf16[4,32,256]{2,1,0:T(8,128)(2,1)S(1)}, bf16[4,32,256]{2,1,0:T(8,128)(2,1)S(1)}, u32[]{:S(2)}, u32[]{:S(2)}) collective-permute-start(bf16[4,32,256]{2,1,0:T(8,128)(2,1)S(1)} %get-tuple-element.70), channel_id=1, source_target_pairs={{0,12},{4,8},{8,4},{12,0},{16,28},{20,24},{24,20},{28,16},{1,13},{... | collective-permute-start | bytes 196616 | tf_op jit(solution)/shard_map/ppermute | solution.py:351
  58.6 2.3 %collective-permute-done.15 = bf16[18,32,256]{2,1,0:T(8,128)(2,1)S(1)} collective-permute-done((bf16[18,32,256]{2,1,0:T(8,128)(2,1)S(1)}, bf16[18,32,256]{2,1,0:T(8,128)(2,1)S(1)}, u32[]{:S(2)}, u32[]{:S(2)}) %collective-permute-start.15) | collective-permute-done | bytes 294944 | tf_op jit(solution)/shard_map/ppermute | solution.py:351
  62.4 2.4 %collective-permute-start.20 = (bf16[4,32,256]{2,1,0:T(8,128)(2,1)S(1)}, bf16[4,32,256]{2,1,0:T(8,128)(2,1)S(1)}, u32[]{:S(2)}, u32[]{:S(2)}) collective-permute-start(bf16[4,32,256]{2,1,0:T(8,128)(2,1)S(1)} %get-tuple-element.71), channel_id=1, source_target_pairs={{0,16},{4,20},{8,24},{12,28},{16,0},{20,4},{24,8},{28,12},{1,17},{... | collective-permute-start | bytes 196616 | tf_op jit(solution)/shard_map/ppermute | solution.py:351
  64.8 5.7 %start.1 = (f32[512,128]{1,0:T(8,128)S(1)}, bf16[72,128,256]{2,1,0:T(8,128)(2,1)S(1)}) custom-call(s32[72]{0:T(128)S(1)} %get-tuple-element.97.slot_ref, s32[72]{0:T(128)S(1)} %get-tuple-element.96.user_ref, s32[3]{0:T(128)S(1)} %pad_add_fusion.info_ref, f32[128,512]{1,0:T(8,128)S(1)} %get-tuple-element.54.x_ref, bf16[72,64,256]{2,1,0:T(8,128)(2,1)S(1)} %mask.1, ...), custom_call_target="tpu_custom_call" | custom-call | flops 8000000000 | tf_op jit(solution)/shard_map/start/pallas_call | solution.py:553
  71.2 5.4 %first.1 = (f32[4,64,512]{2,1,0:T(8,128)S(1)}, f32[512,128]{1,0:T(8,128)S(1)}, f32[512,128]{1,0:T(8,128)S(1)}) custom-call(s32[72]{0:T(128)S(1)} %get-tuple-element.97.slot_ref, s32[72]{0:T(128)S(1)} %get-tuple-element.96.user_ref, s32[3]{0:T(128)S(1)} %pad_add_fusion.info_ref, f32[128,512]{1,0:T(8,128)S(1)} %get-tuple-element.54.x_ref, ...), custom_call_target="tpu_custom_call" | custom-call | flops 8000000000 | tf_op jit(solution)/shard_map/first/pallas_call | solution.py:564
  78.5 5.8 %second.1 = (f32[4,32,512]{2,1,0:T(8,128)S(1)}, f32[32,128]{1,0:T(8,128)}) custom-call(s32[72]{0:T(128)S(1)} %get-tuple-element.97.slot_ref, s32[72]{0:T(128)S(1)} %get-tuple-element.96.user_ref, s32[3]{0:T(128)S(1)} %pad_add_fusion.info_ref, f32[512,128]{1,0:T(8,128)S(1)} %get-tuple-element.78.field_ref, f32[512,128]{1,0:T(8,128)S(1)} %get-tuple-element.79.first_ref, ...), custom_call_target="tpu_custom_call" | custom-call | flops 8000000000 | tf_op jit(solution)/shard_map/second/pallas_call | solution.py:572
  84.4 1.6 %collective-permute-start.26 = (f32[32,512]{1,0:T(8,128)S(1)}, f32[32,512]{1,0:T(8,128)S(1)}, u32[]{:S(2)}, u32[]{:S(2)}) collective-permute-start(f32[32,512]{1,0:T(8,128)S(1)} %get-tuple-element.88), channel_id=1, source_target_pairs={{0,3},{1,2},{2,1},{3,0},{4,7},{5,6},{6,5},{7,4},{8,11},{9,10},{10,... | collective-permute-start | bytes 196616 | tf_op jit(solution)/shard_map/ppermute | solution.py:351
  86.6 3.7 %all-to-all-start.1 = ((f32[32,1,128]{2,1,0:T(1,128)}), f32[32,1,128]{2,1,0:T(1,128)S(1)}, u32[]{:S(2)}, u32[]{:S(2)}) async-start(f32[32,1,128]{2,1,0:T(1,128)} %bitcast.12), calls=%async_computation.1 | async-start | bytes 32768 | tf_op jit(solution)/shard_map/all_to_all | solution.py:587
  90.3 7.0 %all-to-all-done.1 = f32[32,1,128]{2,1,0:T(1,128)S(1)} async-done(((f32[32,1,128]{2,1,0:T(1,128)}), f32[32,1,128]{2,1,0:T(1,128)S(1)}, u32[]{:S(2)}, u32[]{:S(2)}) %all-to-all-start.1) | async-done | bytes 16416 | tf_op jit(solution)/shard_map/all_to_all | solution.py:587
  97.4 2.0 %finish.1 = (f32[32,2048]{1,0:T(8,128)}, f32[32,2048]{1,0:T(8,128)}) custom-call(s32[3]{0:T(128)S(1)} %pad_add_fusion.info_ref, f32[32,128]{1,0:T(8,128)S(1)} %bitcast.31, f32[32,2048]{1,0:T(8,128)S(1)} %copy-done.1, f32[64,512]{1,0:T(8,128)S(1)} %get-tuple-element.87.refs_0_, f32[64,512]{1,0:T(8,128)S(1)} %collective-permute-done.21.refs_1_, ...), custom_call_target="tpu_custom_call" | custom-call | flops 1000000000 | tf_op jit(solution)/shard_map/finish/pallas_call | solution.py:590
  (74 shorter events, 20.7 us)
Async XLA Ops:
  3.1 10.9 %collective-permute-start = (bf16[32,3072]{1,0:T(8,128)(2,1)S(1)}, bf16[32,3072]{1,0:T(8,128)(2,1)S(1)}, u32[]{:S(2)}, u32[]{:S(2)}) collective-permute-start(bf16[32,3072]{1,0:T(8,128)(2,1)S(1)} %get-tuple-element.45), channel_id=1, source_target_pairs={{0,1},{1,0},{2,3},{3,2},{4,5},{5,4},{6,7},{7,6},{8,9},{9,8},{10,11... | collective-permute-start | bytes 589832 | tf_op jit(solution)/shard_map/ppermute | solution.py:351
  3.6 10.4 %collective-permute-start.1 = (bf16[32,3072]{1,0:T(8,128)(2,1)S(1)}, bf16[32,3072]{1,0:T(8,128)(2,1)S(1)}, u32[]{:S(2)}, u32[]{:S(2)}) collective-permute-start(bf16[32,3072]{1,0:T(8,128)(2,1)S(1)} %get-tuple-element.46), channel_id=1, source_target_pairs={{0,2},{1,3},{2,0},{3,1},{4,6},{5,7},{6,4},{7,5},{8,10},{9,11},{10,... | collective-permute-start | bytes 589832 | tf_op jit(solution)/shard_map/ppermute | solution.py:351
  6.2 9.4 %collective-permute-start.2 = (bf16[32,3072]{1,0:T(8,128)(2,1)S(1)}, bf16[32,3072]{1,0:T(8,128)(2,1)S(1)}, u32[]{:S(2)}, u32[]{:S(2)}) collective-permute-start(bf16[32,3072]{1,0:T(8,128)(2,1)S(1)} %get-tuple-element.47), channel_id=1, source_target_pairs={{0,3},{1,2},{2,1},{3,0},{4,7},{5,6},{6,5},{7,4},{8,11},{9,10},{10,... | collective-permute-start | bytes 589832 | tf_op jit(solution)/shard_map/ppermute | solution.py:351
  7.9 12.5 %all-to-all-start = ((s32[8,1,9]{2,1,0:T(1,128)}), s32[8,1,9]{2,1,0:T(1,128)S(1)}, u32[]{:S(2)}, u32[]{:S(2)}) async-start(s32[8,1,9]{2,1,0:T(1,128)} %bitcast.5), calls=%async_computation | async-start | bytes 8192 | tf_op jit(solution)/shard_map/all_to_all | solution.py:442
  22.2 6.3 %collective-permute-start.3 = (bf16[9,32,256]{2,1,0:T(8,128)(2,1)S(1)}, bf16[9,32,256]{2,1,0:T(8,128)(2,1)S(1)}, u32[]{:S(2)}, u32[]{:S(2)}) collective-permute-start(bf16[9,32,256]{2,1,0:T(8,128)(2,1)S(1)} %get-tuple-element.49), channel_id=1, source_target_pairs={{0,4},{4,0},{8,12},{12,8},{16,20},{20,16},{24,28},{28,24},{1,5},{5... | collective-permute-start | bytes 442376 | tf_op jit(solution)/shard_map/ppermute | solution.py:351
  22.8 8.8 %collective-permute-start.4 = (bf16[9,32,256]{2,1,0:T(8,128)(2,1)S(1)}, bf16[9,32,256]{2,1,0:T(8,128)(2,1)S(1)}, u32[]{:S(2)}, u32[]{:S(2)}) collective-permute-start(bf16[9,32,256]{2,1,0:T(8,128)(2,1)S(1)} %get-tuple-element.50), channel_id=1, source_target_pairs={{0,12},{4,8},{8,4},{12,0},{16,28},{20,24},{24,20},{28,16},{1,13},{... | collective-permute-start | bytes 442376 | tf_op jit(solution)/shard_map/ppermute | solution.py:351
  24.3 11.1 %collective-permute-start.6 = (bf16[9,32,256]{2,1,0:T(8,128)(2,1)S(1)}, bf16[9,32,256]{2,1,0:T(8,128)(2,1)S(1)}, u32[]{:S(2)}, u32[]{:S(2)}) collective-permute-start(bf16[9,32,256]{2,1,0:T(8,128)(2,1)S(1)} %get-tuple-element.55), channel_id=1, source_target_pairs={{0,8},{4,12},{8,0},{12,4},{16,24},{20,28},{24,16},{28,20},{1,9},{5... | collective-permute-start | bytes 442376 | tf_op jit(solution)/shard_map/ppermute | solution.py:351
  25.8 13.1 %collective-permute-start.7 = (bf16[9,32,256]{2,1,0:T(8,128)(2,1)S(1)}, bf16[9,32,256]{2,1,0:T(8,128)(2,1)S(1)}, u32[]{:S(2)}, u32[]{:S(2)}) collective-permute-start(bf16[9,32,256]{2,1,0:T(8,128)(2,1)S(1)} %get-tuple-element.56), channel_id=1, source_target_pairs={{0,16},{4,20},{8,24},{12,28},{16,0},{20,4},{24,8},{28,12},{1,17},{... | collective-permute-start | bytes 442376 | tf_op jit(solution)/shard_map/ppermute | solution.py:351
  26.3 5.7 %collective-permute-start.5 = (bf16[9,32,256]{2,1,0:T(8,128)(2,1)S(1)}, bf16[9,32,256]{2,1,0:T(8,128)(2,1)S(1)}, u32[]{:S(2)}, u32[]{:S(2)}) collective-permute-start(bf16[9,32,256]{2,1,0:T(8,128)(2,1)S(1)} %get-tuple-element.51), channel_id=1, source_target_pairs={{0,2},{1,3},{2,0},{3,1},{4,6},{5,7},{6,4},{7,5},{8,10},{9,11},{10,... | collective-permute-start | bytes 442376 | tf_op jit(solution)/shard_map/ppermute | solution.py:351
  28.6 10.3 %collective-permute-start.8 = (bf16[9,32,256]{2,1,0:T(8,128)(2,1)S(1)}, bf16[9,32,256]{2,1,0:T(8,128)(2,1)S(1)}, u32[]{:S(2)}, u32[]{:S(2)}) collective-permute-start(bf16[9,32,256]{2,1,0:T(8,128)(2,1)S(1)} %get-tuple-element.57), channel_id=1, source_target_pairs={{0,24},{4,28},{8,16},{12,20},{16,8},{20,12},{24,0},{28,4},{1,25},{... | collective-permute-start | bytes 442376 | tf_op jit(solution)/shard_map/ppermute | solution.py:351
  32.1 7.6 %collective-permute-start.9 = (bf16[18,32,256]{2,1,0:T(8,128)(2,1)S(1)}, bf16[18,32,256]{2,1,0:T(8,128)(2,1)S(1)}, u32[]{:S(2)}, u32[]{:S(2)}) collective-permute-start(bf16[18,32,256]{2,1,0:T(8,128)(2,1)S(1)} %join.3), channel_id=1, source_target_pairs={{0,2},{1,3},{2,0},{3,1},{4,6},{5,7},{6,4},{7,5},{8,10},{9,11},{10,... | collective-permute-start | bytes 884744 | tf_op jit(solution)/shard_map/ppermute | solution.py:351
  39.7 10.1 %collective-permute-start.11 = (bf16[31,32,256]{2,1,0:T(8,128)(2,1)S(1)}, bf16[31,32,256]{2,1,0:T(8,128)(2,1)S(1)}, u32[]{:S(2)}, u32[]{:S(2)}) collective-permute-start(bf16[31,32,256]{2,1,0:T(8,128)(2,1)S(1)} %join.4), channel_id=1, source_target_pairs={{0,2},{1,3},{2,0},{3,1},{4,6},{5,7},{6,4},{7,5},{8,10},{9,11},{10,... | collective-permute-start | bytes 1523720 | tf_op jit(solution)/shard_map/ppermute | solution.py:351
  41.2 12.5 %collective-permute-start.13 = (bf16[9,32,256]{2,1,0:T(8,128)(2,1)S(1)}, bf16[9,32,256]{2,1,0:T(8,128)(2,1)S(1)}, u32[]{:S(2)}, u32[]{:S(2)}) collective-permute-start(bf16[9,32,256]{2,1,0:T(8,128)(2,1)S(1)} %get-tuple-element.65), channel_id=1, source_target_pairs={{0,20},{4,16},{8,28},{12,24},{16,4},{20,0},{24,12},{28,8},{1,21},{... | collective-permute-start | bytes 442376 | tf_op jit(solution)/shard_map/ppermute | solution.py:351
  43.0 10.8 %collective-permute-start.14 = (bf16[9,32,256]{2,1,0:T(8,128)(2,1)S(1)}, bf16[9,32,256]{2,1,0:T(8,128)(2,1)S(1)}, u32[]{:S(2)}, u32[]{:S(2)}) collective-permute-start(bf16[9,32,256]{2,1,0:T(8,128)(2,1)S(1)} %get-tuple-element.67), channel_id=1, source_target_pairs={{0,28},{4,24},{8,20},{12,16},{16,12},{20,8},{24,4},{28,0},{1,29},{... | collective-permute-start | bytes 442376 | tf_op jit(solution)/shard_map/ppermute | solution.py:351
  49.9 4.9 %collective-permute-start.12 = (bf16[58,32,256]{2,1,0:T(8,128)(2,1)S(1)}, bf16[58,32,256]{2,1,0:T(8,128)(2,1)S(1)}, u32[]{:S(2)}, u32[]{:S(2)}) collective-permute-start(bf16[58,32,256]{2,1,0:T(8,128)(2,1)S(1)} %pad_maximum_fusion.refs_2_), channel_id=1, source_target_pairs={{0,1},{1,0},{2,3},{3,2},{4,5},{5,4},{6,7},{7,6},{8,9},{9,8},{10,11... | collective-permute-start | bytes 2850824 | tf_op jit(solution)/shard_map/ppermute | solution.py:351
  54.1 6.8 %collective-permute-start.15 = (bf16[18,32,256]{2,1,0:T(8,128)(2,1)S(1)}, bf16[18,32,256]{2,1,0:T(8,128)(2,1)S(1)}, u32[]{:S(2)}, u32[]{:S(2)}) collective-permute-start(bf16[18,32,256]{2,1,0:T(8,128)(2,1)S(1)} %join.5), channel_id=1, source_target_pairs={{0,2},{1,3},{2,0},{3,1},{4,6},{5,7},{6,4},{7,5},{8,10},{9,11},{10,... | collective-permute-start | bytes 884744 | tf_op jit(solution)/shard_map/ppermute | solution.py:351
  54.8 10.0 %collective-permute-start.10 = (bf16[54,32,256]{2,1,0:T(8,128)(2,1)S(1)}, bf16[54,32,256]{2,1,0:T(8,128)(2,1)S(1)}, u32[]{:S(2)}, u32[]{:S(2)}) collective-permute-start(bf16[54,32,256]{2,1,0:T(8,128)(2,1)S(1)} %constant_dynamic-update-slice_fusion.refs_0_), channel_id=1, source_target_pairs={{0,1},{1,0},{2,3},{3,2},{4,5},{5,4},{6,7},{7,6},{8,9},{9,8},{10,11... | collective-permute-start | bytes 2654216 | tf_op jit(solution)/shard_map/ppermute | solution.py:351
  54.9 6.1 %collective-permute-start.18 = (bf16[4,32,256]{2,1,0:T(8,128)(2,1)S(1)}, bf16[4,32,256]{2,1,0:T(8,128)(2,1)S(1)}, u32[]{:S(2)}, u32[]{:S(2)}) collective-permute-start(bf16[4,32,256]{2,1,0:T(8,128)(2,1)S(1)} %get-tuple-element.70), channel_id=1, source_target_pairs={{0,12},{4,8},{8,4},{12,0},{16,28},{20,24},{24,20},{28,16},{1,13},{... | collective-permute-start | bytes 196616 | tf_op jit(solution)/shard_map/ppermute | solution.py:351
  62.4 8.1 %collective-permute-start.20 = (bf16[4,32,256]{2,1,0:T(8,128)(2,1)S(1)}, bf16[4,32,256]{2,1,0:T(8,128)(2,1)S(1)}, u32[]{:S(2)}, u32[]{:S(2)}) collective-permute-start(bf16[4,32,256]{2,1,0:T(8,128)(2,1)S(1)} %get-tuple-element.71), channel_id=1, source_target_pairs={{0,16},{4,20},{8,24},{12,28},{16,0},{20,4},{24,8},{28,12},{1,17},{... | collective-permute-start | bytes 196616 | tf_op jit(solution)/shard_map/ppermute | solution.py:351
  76.6 10.0 %collective-permute-start.23 = (f32[64,512]{1,0:T(8,128)S(1)}, f32[64,512]{1,0:T(8,128)S(1)}, u32[]{:S(2)}, u32[]{:S(2)}) collective-permute-start(f32[64,512]{1,0:T(8,128)S(1)} %get-tuple-element.84), channel_id=1, source_target_pairs={{0,3},{1,2},{2,1},{3,0},{4,7},{5,6},{6,5},{7,4},{8,11},{9,10},{10,... | collective-permute-start | bytes 393224 | tf_op jit(solution)/shard_map/ppermute | solution.py:351
  78.0 8.6 %collective-permute-start.22 = (f32[64,512]{1,0:T(8,128)S(1)}, f32[64,512]{1,0:T(8,128)S(1)}, u32[]{:S(2)}, u32[]{:S(2)}) collective-permute-start(f32[64,512]{1,0:T(8,128)S(1)} %get-tuple-element.85), channel_id=1, source_target_pairs={{0,2},{1,3},{2,0},{3,1},{4,6},{5,7},{6,4},{7,5},{8,10},{9,11},{10,... | collective-permute-start | bytes 393224 | tf_op jit(solution)/shard_map/ppermute | solution.py:351
  78.5 8.1 %collective-permute-start.21 = (f32[64,512]{1,0:T(8,128)S(1)}, f32[64,512]{1,0:T(8,128)S(1)}, u32[]{:S(2)}, u32[]{:S(2)}) collective-permute-start(f32[64,512]{1,0:T(8,128)S(1)} %get-tuple-element.86), channel_id=1, source_target_pairs={{0,1},{1,0},{2,3},{3,2},{4,5},{5,4},{6,7},{7,6},{8,9},{9,8},{10,11... | collective-permute-start | bytes 393224 | tf_op jit(solution)/shard_map/ppermute | solution.py:351
  84.4 5.9 %collective-permute-start.26 = (f32[32,512]{1,0:T(8,128)S(1)}, f32[32,512]{1,0:T(8,128)S(1)}, u32[]{:S(2)}, u32[]{:S(2)}) collective-permute-start(f32[32,512]{1,0:T(8,128)S(1)} %get-tuple-element.88), channel_id=1, source_target_pairs={{0,3},{1,2},{2,1},{3,0},{4,7},{5,6},{6,5},{7,4},{8,11},{9,10},{10,... | collective-permute-start | bytes 196616 | tf_op jit(solution)/shard_map/ppermute | solution.py:351
  86.6 10.8 %all-to-all-start.1 = ((f32[32,1,128]{2,1,0:T(1,128)}), f32[32,1,128]{2,1,0:T(1,128)S(1)}, u32[]{:S(2)}, u32[]{:S(2)}) async-start(f32[32,1,128]{2,1,0:T(1,128)} %bitcast.12), calls=%async_computation.1 | async-start | bytes 32768 | tf_op jit(solution)/shard_map/all_to_all | solution.py:587
  (8 other events, 51.4 us)

commit v9 on v8

--- a/solution.py
+++ b/solution.py
@@ -172,7 +172,7 @@
     return product[:, :width] + product[:, width:] + ridge * vector
 
 
-def sparse(starting, slot_ref, user_ref, y, mask, p_hl, acc, held):
+def sparse(starting, slot_ref, user_ref, y, turned, mask, p_hl, acc, held):
     tiles, share, side = mask.shape
     groups = tiles // UNROLL
     acc[...] = jnp.zeros_like(acc)
@@ -192,12 +192,7 @@
         terms = []
         for j in range(UNROLL):
             t = group * UNROLL + j
-            term = lax.dot_general(
-                held[group % 2, j],
-                y[slot_ref[t]],
-                (((1,), (1,)), ((), ())),
-                preferred_element_type=f32,
-            )
+            term = matmul(held[group % 2, j], turned[slot_ref[t]])
             terms.append(term[:share] + term[share:])
         return terms
 
@@ -227,7 +222,7 @@
 
 def start_kernel(n_cols, slots, slot_ref, user_ref, info_ref, x_ref, mask, *refs):
     pieces = refs[: 2 * len(slots)]
-    part_ref, y, p_hl, acc, held, sems = refs[2 * len(slots) :]
+    part_ref, y, turned, p_hl, acc, held, sems = refs[2 * len(slots) :]
     piece_width = y.shape[1] // n_cols
     column = info_ref[1]
     copies = []
@@ -249,12 +244,17 @@
     load(p_hl, x_ref[...].T)
     for copy in copies:
         copy.wait()
-    sparse(True, slot_ref, user_ref, y, mask, p_hl, acc, held)
+    def turn(s, carry):
+        turned[s] = y[s].T
+        return carry
+
+    lax.fori_loop(0, y.shape[0], turn, 0, unroll=8)
+    sparse(True, slot_ref, user_ref, y, turned, mask, p_hl, acc, held)
     part_ref[...] = acc[...].reshape(part_ref.shape)
 
 
 def first_kernel(
-    slot_ref, user_ref, info_ref, x_ref, part_ref, gram_ref, y, mask,
+    slot_ref, user_ref, info_ref, x_ref, part_ref, gram_ref, y, turned, mask,
     sent_ref, field_ref, first_ref, p_hl, acc, held,
 ):
     start = x_ref[...].T
@@ -263,19 +263,19 @@
     field_ref[...] = field
     put(info_ref[1], sent_ref, field)
     load(p_hl, field)
-    sparse(False, slot_ref, user_ref, y, mask, p_hl, acc, held)
+    sparse(False, slot_ref, user_ref, y, turned, mask, p_hl, acc, held)
     first = confidence * acc[...].reshape(field.shape) + dense(p_hl, gram_ref, field)
     first_ref[...] = first
     put(info_ref[1], sent_ref, first, 1)
 
 
 def second_kernel(
-    slot_ref, user_ref, info_ref, field_ref, first_ref, gram_ref, y, mask, sent_ref, dots_ref, p_hl, acc, held
+    slot_ref, user_ref, info_ref, field_ref, first_ref, gram_ref, y, turned, mask, sent_ref, dots_ref, p_hl, acc, held
 ):
     field = field_ref[...]
     first = first_ref[...]
     load(p_hl, first)
-    sparse(False, slot_ref, user_ref, y, mask, p_hl, acc, held)
+    sparse(False, slot_ref, user_ref, y, turned, mask, p_hl, acc, held)
     second = confidence * acc[...].reshape(field.shape) + dense(p_hl, gram_ref, first)
     put(info_ref[1], sent_ref, second)
 
@@ -550,9 +550,9 @@
         pltpu.VMEM((2, UNROLL, 2 * share, side), bf16),
     ]
     lists = (places, tile_users, info)
-    part, y = call(
+    part, y, turned_y = call(
         functools.partial(start_kernel, n_cols, slots),
-        [vector, held],
+        [vector, held, jax.ShapeDtypeStruct((row_devs * capacity, side, width), bf16)],
         [smem] * 3 + [vmem] * 2 + [anywhere] * len(pieces),
         "start",
         work + [pltpu.SemaphoreType.DMA((n_cols * len(slots),))],
@@ -564,22 +564,22 @@
     pair_sent, field, first = call(
         first_kernel,
         [pair, vector, vector],
-        [smem] * 3 + [vmem] * 5,
+        [smem] * 3 + [vmem] * 6,
         "first",
         work,
         8 * 10**9,
-    )(*lists, start, part, gram, y, mask)
+    )(*lists, start, part, gram, y, turned_y, mask)
     second_sent, dots = call(
         second_kernel,
         [
             jax.ShapeDtypeStruct((n_cols, col_width, own_users), f32),
             jax.ShapeDtypeStruct((devices, 128), f32),
         ],
-        [smem] * 3 + [vmem] * 5,
+        [smem] * 3 + [vmem] * 6,
         "second",
         work,
         8 * 10**9,
-    )(*lists, field, first, gram, y, mask)
+    )(*lists, field, first, gram, y, turned_y, mask)
 
     turned = swap(pair_sent)
     dots = after(dots, *turned)

time: 99.7 us -> 101 us (1.013)
  Pallas kernels: 27.2 us -> 28.7 us
    pallas_call x2, Pallas kernels: 11.1 us -> 12.6 us  [the longest x1 7.32 us: on_device(): call(functools.partial(start_kernel, n_cols, slots), [vector, held, jax.S...]
  transfers between devices with their start and end apart: 29 -> 29, of which waited for: 11 -> 11; matrix products, arithmetic and copies ran while one was open for 2% -> 2% of each run, Pallas kernels for 17% -> 18%
where the time goes in v9:
time: 101 us
  starting transfers between devices  39.8 us (39%)
  Pallas kernels  28.7 us (28%)
  waiting for transfers between devices  27.6 us (27%)
  local copies, waits for them, and re-layouts  1.91 us (2%)
  between operations  1.6 us (2%)
  other arithmetic  1.26 us (1%)
    ppermute x27, starting transfers between devices, flip(): return lax.ppermute(value, axis, [(i, i ^ bit) for i in range(size)])  30 us
    ppermute x27, waiting for transfers between devices, flip(): return lax.ppermute(value, axis, [(i, i ^ bit) for i in range(size)])  15.8 us
    pallas_call x1, Pallas kernels, on_device(): call(functools.partial(start_kernel, n_cols, slots), [vector, held, jax.S...  7.32 us
    all_to_all x1, waiting for transfers between devices, on_device(): lax.all_to_all(dots, ('rows', 'cols'), split_axis=0, concat_axis=0, tiled...  7.04 us
    all_to_all x1, starting transfers between devices, on_device(): lax.all_to_all(requests, 'rows', split_axis=0, concat_axis=0, tiled=True)  6.07 us
    pallas_call x1, Pallas kernels, on_device(): call(second_kernel, [jax.ShapeDtypeStruct((n_cols, col_width, own_users),...  5.76 us
    pallas_call x1, Pallas kernels, on_device(): call(first_kernel, [pair, vector, vector], [smem] * 3 + [vmem] * 6, 'firs...  5.32 us
    all_to_all x1, waiting for transfers between devices, on_device(): lax.all_to_all(requests, 'rows', split_axis=0, concat_axis=0, tiled=True)  4.76 us
  transfers between devices with their start and end apart: 29, of which 11 were waited for; matrix products, arithmetic and copies ran while one was open for 2% of the time, Pallas kernels for 18%

profile of v9, /device:TPU:0, one launch (start us, length us, event | category | flops | bytes accessed | tf_op | source)
XLA Modules:
  0.0 100.9 jit_solution(1341312695083372027)
XLA Ops:
  1.4 1.7 %prepare.1 = (bf16[32,3072]{1,0:T(8,128)(2,1)S(1)}, bf16[32,3072]{1,0:T(8,128)(2,1)S(1)}, bf16[32,3072]{1,0:T(8,128)(2,1)S(1)}, bf16[32,3072]{1,0:T(8,128)(2,1)S(1)}) custom-call(s32[3]{0:T(128)S(1)} %pad_add_fusion.info_ref, f32[32,2048]{1,0:T(8,128)} %x_ref.1, bf16[32,8192]{1,0:T(8,128)(2,1)} %items_ref.1), custom_call_target="tpu_custom_call" | custom-call | flops 1000000000 | tf_op jit(solution)/shard_map/prepare/pallas_call | solution.py:409
  3.6 2.6 %collective-permute-start.1 = (bf16[32,3072]{1,0:T(8,128)(2,1)S(1)}, bf16[32,3072]{1,0:T(8,128)(2,1)S(1)}, u32[]{:S(2)}, u32[]{:S(2)}) collective-permute-start(bf16[32,3072]{1,0:T(8,128)(2,1)S(1)} %get-tuple-element.47), channel_id=1, source_target_pairs={{0,2},{1,3},{2,0},{3,1},{4,6},{5,7},{6,4},{7,5},{8,10},{9,11},{10,... | collective-permute-start | bytes 589832 | tf_op jit(solution)/shard_map/ppermute | solution.py:351
  7.9 6.1 %all-to-all-start = ((s32[8,1,9]{2,1,0:T(1,128)}), s32[8,1,9]{2,1,0:T(1,128)S(1)}, u32[]{:S(2)}, u32[]{:S(2)}) async-start(s32[8,1,9]{2,1,0:T(1,128)} %bitcast.5), calls=%async_computation | async-start | bytes 8192 | tf_op jit(solution)/shard_map/all_to_all | solution.py:442
  14.0 1.6 %collective-permute-done.2.refs_3_ = bf16[32,3072]{1,0:T(8,128)(2,1)S(1)} collective-permute-done((bf16[32,3072]{1,0:T(8,128)(2,1)S(1)}, bf16[32,3072]{1,0:T(8,128)(2,1)S(1)}, u32[]{:S(2)}, u32[]{:S(2)}) %collective-permute-start.2) | collective-permute-done | bytes 196640 | tf_op jit(solution)/shard_map/ppermute | solution.py:351
  15.6 4.8 %all-to-all-done = s32[8,1,9]{2,1,0:T(1,128)S(1)} async-done(((s32[8,1,9]{2,1,0:T(1,128)}), s32[8,1,9]{2,1,0:T(1,128)S(1)}, u32[]{:S(2)}, u32[]{:S(2)}) %all-to-all-start) | async-done | bytes 320 | tf_op jit(solution)/shard_map/all_to_all | solution.py:442
  26.3 1.5 %collective-permute-start.5 = (bf16[9,32,256]{2,1,0:T(8,128)(2,1)S(1)}, bf16[9,32,256]{2,1,0:T(8,128)(2,1)S(1)}, u32[]{:S(2)}, u32[]{:S(2)}) collective-permute-start(bf16[9,32,256]{2,1,0:T(8,128)(2,1)S(1)} %get-tuple-element.52), channel_id=1, source_target_pairs={{0,2},{1,3},{2,0},{3,1},{4,6},{5,7},{6,4},{7,5},{8,10},{9,11},{10,... | collective-permute-start | bytes 442376 | tf_op jit(solution)/shard_map/ppermute | solution.py:351
  28.6 1.7 %collective-permute-start.8 = (bf16[9,32,256]{2,1,0:T(8,128)(2,1)S(1)}, bf16[9,32,256]{2,1,0:T(8,128)(2,1)S(1)}, u32[]{:S(2)}, u32[]{:S(2)}) collective-permute-start(bf16[9,32,256]{2,1,0:T(8,128)(2,1)S(1)} %get-tuple-element.58), channel_id=1, source_target_pairs={{0,24},{4,28},{8,16},{12,20},{16,8},{20,12},{24,0},{28,4},{1,25},{... | collective-permute-start | bytes 442376 | tf_op jit(solution)/shard_map/ppermute | solution.py:351
  32.1 1.5 %collective-permute-start.9 = (bf16[18,32,256]{2,1,0:T(8,128)(2,1)S(1)}, bf16[18,32,256]{2,1,0:T(8,128)(2,1)S(1)}, u32[]{:S(2)}, u32[]{:S(2)}) collective-permute-start(bf16[18,32,256]{2,1,0:T(8,128)(2,1)S(1)} %join.3), channel_id=1, source_target_pairs={{0,2},{1,3},{2,0},{3,1},{4,6},{5,7},{6,4},{7,5},{8,10},{9,11},{10,... | collective-permute-start | bytes 884744 | tf_op jit(solution)/shard_map/ppermute | solution.py:351
  35.4 3.5 %collective-permute-done.7.refs_1_ = bf16[9,32,256]{2,1,0:T(8,128)(2,1)S(1)} collective-permute-done((bf16[9,32,256]{2,1,0:T(8,128)(2,1)S(1)}, bf16[9,32,256]{2,1,0:T(8,128)(2,1)S(1)}, u32[]{:S(2)}, u32[]{:S(2)}) %collective-permute-start.7) | collective-permute-done | bytes 147488 | tf_op jit(solution)/shard_map/ppermute | solution.py:351
  39.7 1.6 %collective-permute-start.11 = (bf16[31,32,256]{2,1,0:T(8,128)(2,1)S(1)}, bf16[31,32,256]{2,1,0:T(8,128)(2,1)S(1)}, u32[]{:S(2)}, u32[]{:S(2)}) collective-permute-start(bf16[31,32,256]{2,1,0:T(8,128)(2,1)S(1)} %join.4), channel_id=1, source_target_pairs={{0,2},{1,3},{2,0},{3,1},{4,6},{5,7},{6,4},{7,5},{8,10},{9,11},{10,... | collective-permute-start | bytes 1523720 | tf_op jit(solution)/shard_map/ppermute | solution.py:351
  41.2 1.8 %collective-permute-start.13 = (bf16[9,32,256]{2,1,0:T(8,128)(2,1)S(1)}, bf16[9,32,256]{2,1,0:T(8,128)(2,1)S(1)}, u32[]{:S(2)}, u32[]{:S(2)}) collective-permute-start(bf16[9,32,256]{2,1,0:T(8,128)(2,1)S(1)} %get-tuple-element.66), channel_id=1, source_target_pairs={{0,20},{4,16},{8,28},{12,24},{16,4},{20,0},{24,12},{28,8},{1,21},{... | collective-permute-start | bytes 442376 | tf_op jit(solution)/shard_map/ppermute | solution.py:351
  43.0 3.6 %collective-permute-start.14 = (bf16[9,32,256]{2,1,0:T(8,128)(2,1)S(1)}, bf16[9,32,256]{2,1,0:T(8,128)(2,1)S(1)}, u32[]{:S(2)}, u32[]{:S(2)}) collective-permute-start(bf16[9,32,256]{2,1,0:T(8,128)(2,1)S(1)} %get-tuple-element.68), channel_id=1, source_target_pairs={{0,28},{4,24},{8,20},{12,16},{16,12},{20,8},{24,4},{28,0},{1,29},{... | collective-permute-start | bytes 442376 | tf_op jit(solution)/shard_map/ppermute | solution.py:351
  46.6 2.4 %mask.1 = bf16[72,64,256]{2,1,0:T(8,128)(2,1)S(1)} custom-call(s32[3]{0:T(128)S(1)} %pad_add_fusion.info_ref, bf16[72,256,256]{2,1,0:T(8,128)(2,1)} %mask_hbm.1), custom_call_target="tpu_custom_call" | custom-call | flops 1000000000 | tf_op jit(solution)/shard_map/mask/pallas_call | solution.py:509
  50.0 3.7 %collective-permute-done.13.refs_0_ = bf16[9,32,256]{2,1,0:T(8,128)(2,1)S(1)} collective-permute-done((bf16[9,32,256]{2,1,0:T(8,128)(2,1)S(1)}, bf16[9,32,256]{2,1,0:T(8,128)(2,1)S(1)}, u32[]{:S(2)}, u32[]{:S(2)}) %collective-permute-start.13) | collective-permute-done | bytes 147488 | tf_op jit(solution)/shard_map/ppermute | solution.py:351
  54.9 3.1 %collective-permute-start.18 = (bf16[4,32,256]{2,1,0:T(8,128)(2,1)S(1)}, bf16[4,32,256]{2,1,0:T(8,128)(2,1)S(1)}, u32[]{:S(2)}, u32[]{:S(2)}) collective-permute-start(bf16[4,32,256]{2,1,0:T(8,128)(2,1)S(1)} %get-tuple-element.71), channel_id=1, source_target_pairs={{0,12},{4,8},{8,4},{12,0},{16,28},{20,24},{24,20},{28,16},{1,13},{... | collective-permute-start | bytes 196616 | tf_op jit(solution)/shard_map/ppermute | solution.py:351
  58.6 2.3 %collective-permute-done.15 = bf16[18,32,256]{2,1,0:T(8,128)(2,1)S(1)} collective-permute-done((bf16[18,32,256]{2,1,0:T(8,128)(2,1)S(1)}, bf16[18,32,256]{2,1,0:T(8,128)(2,1)S(1)}, u32[]{:S(2)}, u32[]{:S(2)}) %collective-permute-start.15) | collective-permute-done | bytes 294944 | tf_op jit(solution)/shard_map/ppermute | solution.py:351
  62.4 2.4 %collective-permute-start.20 = (bf16[4,32,256]{2,1,0:T(8,128)(2,1)S(1)}, bf16[4,32,256]{2,1,0:T(8,128)(2,1)S(1)}, u32[]{:S(2)}, u32[]{:S(2)}) collective-permute-start(bf16[4,32,256]{2,1,0:T(8,128)(2,1)S(1)} %get-tuple-element.72), channel_id=1, source_target_pairs={{0,16},{4,20},{8,24},{12,28},{16,0},{20,4},{24,8},{28,12},{1,17},{... | collective-permute-start | bytes 196616 | tf_op jit(solution)/shard_map/ppermute | solution.py:351
  64.8 7.3 %start.1 = (f32[512,128]{1,0:T(8,128)S(1)}, bf16[72,128,256]{2,1,0:T(8,128)(2,1)S(1)}, bf16[72,256,128]{2,1,0:T(8,128)(2,1)S(1)}) custom-call(s32[72]{0:T(128)S(1)} %get-tuple-element.99.slot_ref, s32[72]{0:T(128)S(1)} %get-tuple-element.98.user_ref, s32[3]{0:T(128)S(1)} %pad_add_fusion.info_ref, f32[128,512]{1,0:T(8,128)S(1)} %get-tuple-element.55.x_ref, ...), custom_call_target="tpu_custom_call" | custom-call | flops 8000000000 | tf_op jit(solution)/shard_map/start/pallas_call | solution.py:553
  72.8 5.3 %first.1 = (f32[4,64,512]{2,1,0:T(8,128)S(1)}, f32[512,128]{1,0:T(8,128)S(1)}, f32[512,128]{1,0:T(8,128)S(1)}) custom-call(s32[72]{0:T(128)S(1)} %get-tuple-element.99.slot_ref, s32[72]{0:T(128)S(1)} %get-tuple-element.98.user_ref, s32[3]{0:T(128)S(1)} %pad_add_fusion.info_ref, f32[128,512]{1,0:T(8,128)S(1)} %get-tuple-element.55.x_ref, ...), custom_call_target="tpu_custom_call" | custom-call | flops 8000000000 | tf_op jit(solution)/shard_map/first/pallas_call | solution.py:564
  80.1 5.8 %second.1 = (f32[4,32,512]{2,1,0:T(8,128)S(1)}, f32[32,128]{1,0:T(8,128)}) custom-call(s32[72]{0:T(128)S(1)} %get-tuple-element.99.slot_ref, s32[72]{0:T(128)S(1)} %get-tuple-element.98.user_ref, s32[3]{0:T(128)S(1)} %pad_add_fusion.info_ref, f32[512,128]{1,0:T(8,128)S(1)} %get-tuple-element.80.field_ref, f32[512,128]{1,0:T(8,128)S(1)} %get-tuple-element.81.first_ref, ...), custom_call_target="tpu_custom_call" | custom-call | flops 8000000000 | tf_op jit(solution)/shard_map/second/pallas_call | solution.py:572
  85.9 1.7 %collective-permute-start.26 = (f32[32,512]{1,0:T(8,128)S(1)}, f32[32,512]{1,0:T(8,128)S(1)}, u32[]{:S(2)}, u32[]{:S(2)}) collective-permute-start(f32[32,512]{1,0:T(8,128)S(1)} %get-tuple-element.90), channel_id=1, source_target_pairs={{0,3},{1,2},{2,1},{3,0},{4,7},{5,6},{6,5},{7,4},{8,11},{9,10},{10,... | collective-permute-start | bytes 196616 | tf_op jit(solution)/shard_map/ppermute | solution.py:351
  88.1 3.7 %all-to-all-start.1 = ((f32[32,1,128]{2,1,0:T(1,128)}), f32[32,1,128]{2,1,0:T(1,128)S(1)}, u32[]{:S(2)}, u32[]{:S(2)}) async-start(f32[32,1,128]{2,1,0:T(1,128)} %bitcast.12), calls=%async_computation.1 | async-start | bytes 32768 | tf_op jit(solution)/shard_map/all_to_all | solution.py:587
  91.8 7.0 %all-to-all-done.1 = f32[32,1,128]{2,1,0:T(1,128)S(1)} async-done(((f32[32,1,128]{2,1,0:T(1,128)}), f32[32,1,128]{2,1,0:T(1,128)S(1)}, u32[]{:S(2)}, u32[]{:S(2)}) %all-to-all-start.1) | async-done | bytes 16416 | tf_op jit(solution)/shard_map/all_to_all | solution.py:587
  98.9 2.0 %finish.1 = (f32[32,2048]{1,0:T(8,128)}, f32[32,2048]{1,0:T(8,128)}) custom-call(s32[3]{0:T(128)S(1)} %pad_add_fusion.info_ref, f32[32,128]{1,0:T(8,128)S(1)} %bitcast.31, f32[32,2048]{1,0:T(8,128)S(1)} %copy-done.1, f32[64,512]{1,0:T(8,128)S(1)} %get-tuple-element.89.refs_0_, f32[64,512]{1,0:T(8,128)S(1)} %collective-permute-done.21.refs_1_, ...), custom_call_target="tpu_custom_call" | custom-call | flops 1000000000 | tf_op jit(solution)/shard_map/finish/pallas_call | solution.py:590
  (74 shorter events, 20.7 us)
Async XLA Ops:
  3.1 10.9 %collective-permute-start = (bf16[32,3072]{1,0:T(8,128)(2,1)S(1)}, bf16[32,3072]{1,0:T(8,128)(2,1)S(1)}, u32[]{:S(2)}, u32[]{:S(2)}) collective-permute-start(bf16[32,3072]{1,0:T(8,128)(2,1)S(1)} %get-tuple-element.46), channel_id=1, source_target_pairs={{0,1},{1,0},{2,3},{3,2},{4,5},{5,4},{6,7},{7,6},{8,9},{9,8},{10,11... | collective-permute-start | bytes 589832 | tf_op jit(solution)/shard_map/ppermute | solution.py:351
  3.6 10.4 %collective-permute-start.1 = (bf16[32,3072]{1,0:T(8,128)(2,1)S(1)}, bf16[32,3072]{1,0:T(8,128)(2,1)S(1)}, u32[]{:S(2)}, u32[]{:S(2)}) collective-permute-start(bf16[32,3072]{1,0:T(8,128)(2,1)S(1)} %get-tuple-element.47), channel_id=1, source_target_pairs={{0,2},{1,3},{2,0},{3,1},{4,6},{5,7},{6,4},{7,5},{8,10},{9,11},{10,... | collective-permute-start | bytes 589832 | tf_op jit(solution)/shard_map/ppermute | solution.py:351
  6.2 9.4 %collective-permute-start.2 = (bf16[32,3072]{1,0:T(8,128)(2,1)S(1)}, bf16[32,3072]{1,0:T(8,128)(2,1)S(1)}, u32[]{:S(2)}, u32[]{:S(2)}) collective-permute-start(bf16[32,3072]{1,0:T(8,128)(2,1)S(1)} %get-tuple-element.48), channel_id=1, source_target_pairs={{0,3},{1,2},{2,1},{3,0},{4,7},{5,6},{6,5},{7,4},{8,11},{9,10},{10,... | collective-permute-start | bytes 589832 | tf_op jit(solution)/shard_map/ppermute | solution.py:351
  7.9 12.5 %all-to-all-start = ((s32[8,1,9]{2,1,0:T(1,128)}), s32[8,1,9]{2,1,0:T(1,128)S(1)}, u32[]{:S(2)}, u32[]{:S(2)}) async-start(s32[8,1,9]{2,1,0:T(1,128)} %bitcast.5), calls=%async_computation | async-start | bytes 8192 | tf_op jit(solution)/shard_map/all_to_all | solution.py:442
  22.2 6.3 %collective-permute-start.3 = (bf16[9,32,256]{2,1,0:T(8,128)(2,1)S(1)}, bf16[9,32,256]{2,1,0:T(8,128)(2,1)S(1)}, u32[]{:S(2)}, u32[]{:S(2)}) collective-permute-start(bf16[9,32,256]{2,1,0:T(8,128)(2,1)S(1)} %get-tuple-element.50), channel_id=1, source_target_pairs={{0,4},{4,0},{8,12},{12,8},{16,20},{20,16},{24,28},{28,24},{1,5},{5... | collective-permute-start | bytes 442376 | tf_op jit(solution)/shard_map/ppermute | solution.py:351
  22.8 8.8 %collective-permute-start.4 = (bf16[9,32,256]{2,1,0:T(8,128)(2,1)S(1)}, bf16[9,32,256]{2,1,0:T(8,128)(2,1)S(1)}, u32[]{:S(2)}, u32[]{:S(2)}) collective-permute-start(bf16[9,32,256]{2,1,0:T(8,128)(2,1)S(1)} %get-tuple-element.51), channel_id=1, source_target_pairs={{0,12},{4,8},{8,4},{12,0},{16,28},{20,24},{24,20},{28,16},{1,13},{... | collective-permute-start | bytes 442376 | tf_op jit(solution)/shard_map/ppermute | solution.py:351
  24.3 11.1 %collective-permute-start.6 = (bf16[9,32,256]{2,1,0:T(8,128)(2,1)S(1)}, bf16[9,32,256]{2,1,0:T(8,128)(2,1)S(1)}, u32[]{:S(2)}, u32[]{:S(2)}) collective-permute-start(bf16[9,32,256]{2,1,0:T(8,128)(2,1)S(1)} %get-tuple-element.56), channel_id=1, source_target_pairs={{0,8},{4,12},{8,0},{12,4},{16,24},{20,28},{24,16},{28,20},{1,9},{5... | collective-permute-start | bytes 442376 | tf_op jit(solution)/shard_map/ppermute | solution.py:351
  25.8 13.1 %collective-permute-start.7 = (bf16[9,32,256]{2,1,0:T(8,128)(2,1)S(1)}, bf16[9,32,256]{2,1,0:T(8,128)(2,1)S(1)}, u32[]{:S(2)}, u32[]{:S(2)}) collective-permute-start(bf16[9,32,256]{2,1,0:T(8,128)(2,1)S(1)} %get-tuple-element.57), channel_id=1, source_target_pairs={{0,16},{4,20},{8,24},{12,28},{16,0},{20,4},{24,8},{28,12},{1,17},{... | collective-permute-start | bytes 442376 | tf_op jit(solution)/shard_map/ppermute | solution.py:351
  26.3 5.7 %collective-permute-start.5 = (bf16[9,32,256]{2,1,0:T(8,128)(2,1)S(1)}, bf16[9,32,256]{2,1,0:T(8,128)(2,1)S(1)}, u32[]{:S(2)}, u32[]{:S(2)}) collective-permute-start(bf16[9,32,256]{2,1,0:T(8,128)(2,1)S(1)} %get-tuple-element.52), channel_id=1, source_target_pairs={{0,2},{1,3},{2,0},{3,1},{4,6},{5,7},{6,4},{7,5},{8,10},{9,11},{10,... | collective-permute-start | bytes 442376 | tf_op jit(solution)/shard_map/ppermute | solution.py:351
  28.6 10.3 %collective-permute-start.8 = (bf16[9,32,256]{2,1,0:T(8,128)(2,1)S(1)}, bf16[9,32,256]{2,1,0:T(8,128)(2,1)S(1)}, u32[]{:S(2)}, u32[]{:S(2)}) collective-permute-start(bf16[9,32,256]{2,1,0:T(8,128)(2,1)S(1)} %get-tuple-element.58), channel_id=1, source_target_pairs={{0,24},{4,28},{8,16},{12,20},{16,8},{20,12},{24,0},{28,4},{1,25},{... | collective-permute-start | bytes 442376 | tf_op jit(solution)/shard_map/ppermute | solution.py:351
  32.1 7.6 %collective-permute-start.9 = (bf16[18,32,256]{2,1,0:T(8,128)(2,1)S(1)}, bf16[18,32,256]{2,1,0:T(8,128)(2,1)S(1)}, u32[]{:S(2)}, u32[]{:S(2)}) collective-permute-start(bf16[18,32,256]{2,1,0:T(8,128)(2,1)S(1)} %join.3), channel_id=1, source_target_pairs={{0,2},{1,3},{2,0},{3,1},{4,6},{5,7},{6,4},{7,5},{8,10},{9,11},{10,... | collective-permute-start | bytes 884744 | tf_op jit(solution)/shard_map/ppermute | solution.py:351
  39.7 10.1 %collective-permute-start.11 = (bf16[31,32,256]{2,1,0:T(8,128)(2,1)S(1)}, bf16[31,32,256]{2,1,0:T(8,128)(2,1)S(1)}, u32[]{:S(2)}, u32[]{:S(2)}) collective-permute-start(bf16[31,32,256]{2,1,0:T(8,128)(2,1)S(1)} %join.4), channel_id=1, source_target_pairs={{0,2},{1,3},{2,0},{3,1},{4,6},{5,7},{6,4},{7,5},{8,10},{9,11},{10,... | collective-permute-start | bytes 1523720 | tf_op jit(solution)/shard_map/ppermute | solution.py:351
  41.2 12.5 %collective-permute-start.13 = (bf16[9,32,256]{2,1,0:T(8,128)(2,1)S(1)}, bf16[9,32,256]{2,1,0:T(8,128)(2,1)S(1)}, u32[]{:S(2)}, u32[]{:S(2)}) collective-permute-start(bf16[9,32,256]{2,1,0:T(8,128)(2,1)S(1)} %get-tuple-element.66), channel_id=1, source_target_pairs={{0,20},{4,16},{8,28},{12,24},{16,4},{20,0},{24,12},{28,8},{1,21},{... | collective-permute-start | bytes 442376 | tf_op jit(solution)/shard_map/ppermute | solution.py:351
  43.0 10.8 %collective-permute-start.14 = (bf16[9,32,256]{2,1,0:T(8,128)(2,1)S(1)}, bf16[9,32,256]{2,1,0:T(8,128)(2,1)S(1)}, u32[]{:S(2)}, u32[]{:S(2)}) collective-permute-start(bf16[9,32,256]{2,1,0:T(8,128)(2,1)S(1)} %get-tuple-element.68), channel_id=1, source_target_pairs={{0,28},{4,24},{8,20},{12,16},{16,12},{20,8},{24,4},{28,0},{1,29},{... | collective-permute-start | bytes 442376 | tf_op jit(solution)/shard_map/ppermute | solution.py:351
  49.9 4.9 %collective-permute-start.12 = (bf16[58,32,256]{2,1,0:T(8,128)(2,1)S(1)}, bf16[58,32,256]{2,1,0:T(8,128)(2,1)S(1)}, u32[]{:S(2)}, u32[]{:S(2)}) collective-permute-start(bf16[58,32,256]{2,1,0:T(8,128)(2,1)S(1)} %pad_maximum_fusion.refs_2_), channel_id=1, source_target_pairs={{0,1},{1,0},{2,3},{3,2},{4,5},{5,4},{6,7},{7,6},{8,9},{9,8},{10,11... | collective-permute-start | bytes 2850824 | tf_op jit(solution)/shard_map/ppermute | solution.py:351
  54.1 6.8 %collective-permute-start.15 = (bf16[18,32,256]{2,1,0:T(8,128)(2,1)S(1)}, bf16[18,32,256]{2,1,0:T(8,128)(2,1)S(1)}, u32[]{:S(2)}, u32[]{:S(2)}) collective-permute-start(bf16[18,32,256]{2,1,0:T(8,128)(2,1)S(1)} %join.5), channel_id=1, source_target_pairs={{0,2},{1,3},{2,0},{3,1},{4,6},{5,7},{6,4},{7,5},{8,10},{9,11},{10,... | collective-permute-start | bytes 884744 | tf_op jit(solution)/shard_map/ppermute | solution.py:351
  54.8 10.0 %collective-permute-start.10 = (bf16[54,32,256]{2,1,0:T(8,128)(2,1)S(1)}, bf16[54,32,256]{2,1,0:T(8,128)(2,1)S(1)}, u32[]{:S(2)}, u32[]{:S(2)}) collective-permute-start(bf16[54,32,256]{2,1,0:T(8,128)(2,1)S(1)} %constant_dynamic-update-slice_fusion.refs_0_), channel_id=1, source_target_pairs={{0,1},{1,0},{2,3},{3,2},{4,5},{5,4},{6,7},{7,6},{8,9},{9,8},{10,11... | collective-permute-start | bytes 2654216 | tf_op jit(solution)/shard_map/ppermute | solution.py:351
  54.9 6.1 %collective-permute-start.18 = (bf16[4,32,256]{2,1,0:T(8,128)(2,1)S(1)}, bf16[4,32,256]{2,1,0:T(8,128)(2,1)S(1)}, u32[]{:S(2)}, u32[]{:S(2)}) collective-permute-start(bf16[4,32,256]{2,1,0:T(8,128)(2,1)S(1)} %get-tuple-element.71), channel_id=1, source_target_pairs={{0,12},{4,8},{8,4},{12,0},{16,28},{20,24},{24,20},{28,16},{1,13},{... | collective-permute-start | bytes 196616 | tf_op jit(solution)/shard_map/ppermute | solution.py:351
  62.4 9.7 %collective-permute-start.20 = (bf16[4,32,256]{2,1,0:T(8,128)(2,1)S(1)}, bf16[4,32,256]{2,1,0:T(8,128)(2,1)S(1)}, u32[]{:S(2)}, u32[]{:S(2)}) collective-permute-start(bf16[4,32,256]{2,1,0:T(8,128)(2,1)S(1)} %get-tuple-element.72), channel_id=1, source_target_pairs={{0,16},{4,20},{8,24},{12,28},{16,0},{20,4},{24,8},{28,12},{1,17},{... | collective-permute-start | bytes 196616 | tf_op jit(solution)/shard_map/ppermute | solution.py:351
  78.2 9.9 %collective-permute-start.23 = (f32[64,512]{1,0:T(8,128)S(1)}, f32[64,512]{1,0:T(8,128)S(1)}, u32[]{:S(2)}, u32[]{:S(2)}) collective-permute-start(f32[64,512]{1,0:T(8,128)S(1)} %get-tuple-element.86), channel_id=1, source_target_pairs={{0,3},{1,2},{2,1},{3,0},{4,7},{5,6},{6,5},{7,4},{8,11},{9,10},{10,... | collective-permute-start | bytes 393224 | tf_op jit(solution)/shard_map/ppermute | solution.py:351
  79.5 8.5 %collective-permute-start.22 = (f32[64,512]{1,0:T(8,128)S(1)}, f32[64,512]{1,0:T(8,128)S(1)}, u32[]{:S(2)}, u32[]{:S(2)}) collective-permute-start(f32[64,512]{1,0:T(8,128)S(1)} %get-tuple-element.87), channel_id=1, source_target_pairs={{0,2},{1,3},{2,0},{3,1},{4,6},{5,7},{6,4},{7,5},{8,10},{9,11},{10,... | collective-permute-start | bytes 393224 | tf_op jit(solution)/shard_map/ppermute | solution.py:351
  80.1 8.0 %collective-permute-start.21 = (f32[64,512]{1,0:T(8,128)S(1)}, f32[64,512]{1,0:T(8,128)S(1)}, u32[]{:S(2)}, u32[]{:S(2)}) collective-permute-start(f32[64,512]{1,0:T(8,128)S(1)} %get-tuple-element.88), channel_id=1, source_target_pairs={{0,1},{1,0},{2,3},{3,2},{4,5},{5,4},{6,7},{7,6},{8,9},{9,8},{10,11... | collective-permute-start | bytes 393224 | tf_op jit(solution)/shard_map/ppermute | solution.py:351
  85.9 5.9 %collective-permute-start.26 = (f32[32,512]{1,0:T(8,128)S(1)}, f32[32,512]{1,0:T(8,128)S(1)}, u32[]{:S(2)}, u32[]{:S(2)}) collective-permute-start(f32[32,512]{1,0:T(8,128)S(1)} %get-tuple-element.90), channel_id=1, source_target_pairs={{0,3},{1,2},{2,1},{3,0},{4,7},{5,6},{6,5},{7,4},{8,11},{9,10},{10,... | collective-permute-start | bytes 196616 | tf_op jit(solution)/shard_map/ppermute | solution.py:351
  88.1 10.8 %all-to-all-start.1 = ((f32[32,1,128]{2,1,0:T(1,128)}), f32[32,1,128]{2,1,0:T(1,128)S(1)}, u32[]{:S(2)}, u32[]{:S(2)}) async-start(f32[32,1,128]{2,1,0:T(1,128)} %bitcast.12), calls=%async_computation.1 | async-start | bytes 32768 | tf_op jit(solution)/shard_map/all_to_all | solution.py:587
  (8 other events, 51.3 us)

commit v10 on v8

--- a/solution.py
+++ b/solution.py
@@ -9,7 +9,7 @@
 
 ridge = 0.5
 confidence = 40.0
-UNROLL = 8
+UNROLL = 18
 LIMIT = 24 * 1024 * 1024
 f32 = jnp.float32
 bf16 = jnp.bfloat16
@@ -254,17 +254,21 @@
 
 
 def first_kernel(
-    slot_ref, user_ref, info_ref, x_ref, part_ref, gram_ref, y, mask,
-    sent_ref, field_ref, first_ref, p_hl, acc, held,
+    slot_ref, user_ref, info_ref, x_ref, part_ref, gram_ref, y, mask, *refs
 ):
+    sent_ref, field_ref, first_ref, gram_out, p_hl, acc, held = refs[-7:]
+    gram = gram_ref[...]
+    for arrived_ref in refs[:-7]:
+        gram = gram + unpack(arrived_ref)
+    gram_out[...] = gram
     start = x_ref[...].T
     load(p_hl, start)
-    field = part_ref[...] - dense(p_hl, gram_ref, start)
+    field = part_ref[...] - dense(p_hl, gram_out, start)
     field_ref[...] = field
     put(info_ref[1], sent_ref, field)
     load(p_hl, field)
     sparse(False, slot_ref, user_ref, y, mask, p_hl, acc, held)
-    first = confidence * acc[...].reshape(field.shape) + dense(p_hl, gram_ref, field)
+    first = confidence * acc[...].reshape(field.shape) + dense(p_hl, gram_out, field)
     first_ref[...] = first
     put(info_ref[1], sent_ref, first, 1)
 
@@ -558,17 +562,16 @@
         work + [pltpu.SemaphoreType.DMA((n_cols * len(slots),))],
         8 * 10**9,
     )(*lists, start, mask, *pieces)
-    if direct:
-        gram, _ = add(gram, after(arrived, part))
+    rest = [after(arrived, part)] if direct else []
     pair = jax.ShapeDtypeStruct((n_cols, 2 * col_width, own_users), f32)
-    pair_sent, field, first = call(
+    pair_sent, field, first, gram = call(
         first_kernel,
-        [pair, vector, vector],
-        [smem] * 3 + [vmem] * 5,
+        [pair, vector, vector, square],
+        [smem] * 3 + [vmem] * (5 + len(rest)),
         "first",
         work,
         8 * 10**9,
-    )(*lists, start, part, gram, y, mask)
+    )(*lists, start, part, gram, y, mask, *rest)
     second_sent, dots = call(
         second_kernel,
         [

time: 99.7 us -> 97.2 us (0.975)
  Pallas kernels: 27.2 us -> 24.6 us
  transfers between devices with their start and end apart: 29 -> 29, of which waited for: 11 -> 11; matrix products, arithmetic and copies ran while one was open for 2% -> 2% of each run, Pallas kernels for 17% -> 16%
where the time goes in v10:
time: 97.2 us; the launch traced here: 96.9 us
  starting transfers between devices  39.8 us (41%)
  waiting for transfers between devices  27.7 us (28%)
  Pallas kernels  24.6 us (25%)
  local copies, waits for them, and re-layouts  1.91 us (2%)
  between operations  1.6 us (2%)
  other arithmetic  1.26 us (1%)
    ppermute x27, starting transfers between devices, flip(): return lax.ppermute(value, axis, [(i, i ^ bit) for i in range(size)])  30 us
    ppermute x27, waiting for transfers between devices, flip(): return lax.ppermute(value, axis, [(i, i ^ bit) for i in range(size)])  15.9 us
    all_to_all x1, waiting for transfers between devices, on_device(): lax.all_to_all(dots, ('rows', 'cols'), split_axis=0, concat_axis=0, tiled...  7.04 us
    all_to_all x1, starting transfers between devices, on_device(): lax.all_to_all(requests, 'rows', split_axis=0, concat_axis=0, tiled=True)  6.07 us
    pallas_call x1, Pallas kernels, on_device(): call(second_kernel, [jax.ShapeDtypeStruct((n_cols, col_width, own_users),...  5.25 us
    pallas_call x1, Pallas kernels, on_device(): call(functools.partial(start_kernel, n_cols, slots), [vector, held], [sme...  4.97 us
    pallas_call x1, Pallas kernels, on_device(): call(first_kernel, [pair, vector, vector, square], [smem] * 3 + [vmem] *...  4.79 us
    all_to_all x1, waiting for transfers between devices, on_device(): lax.all_to_all(requests, 'rows', split_axis=0, concat_axis=0, tiled=True)  4.76 us
  transfers between devices with their start and end apart: 29, of which 11 were waited for; matrix products, arithmetic and copies ran while one was open for 2% of the time, Pallas kernels for 16%

profile of v10, /device:TPU:0, one launch (start us, length us, event | category | flops | bytes accessed | tf_op | source)
XLA Modules:
  0.0 96.9 jit_solution(8442459503425008107)
XLA Ops:
  1.4 1.7 %prepare.1 = (bf16[32,3072]{1,0:T(8,128)(2,1)S(1)}, bf16[32,3072]{1,0:T(8,128)(2,1)S(1)}, bf16[32,3072]{1,0:T(8,128)(2,1)S(1)}, bf16[32,3072]{1,0:T(8,128)(2,1)S(1)}) custom-call(s32[3]{0:T(128)S(1)} %pad_add_fusion.info_ref, f32[32,2048]{1,0:T(8,128)} %x_ref.1, bf16[32,8192]{1,0:T(8,128)(2,1)} %items_ref.1), custom_call_target="tpu_custom_call" | custom-call | flops 1000000000 | tf_op jit(solution)/shard_map/prepare/pallas_call | solution.py:413
  3.6 2.6 %collective-permute-start.1 = (bf16[32,3072]{1,0:T(8,128)(2,1)S(1)}, bf16[32,3072]{1,0:T(8,128)(2,1)S(1)}, u32[]{:S(2)}, u32[]{:S(2)}) collective-permute-start(bf16[32,3072]{1,0:T(8,128)(2,1)S(1)} %get-tuple-element.46), channel_id=1, source_target_pairs={{0,2},{1,3},{2,0},{3,1},{4,6},{5,7},{6,4},{7,5},{8,10},{9,11},{10,... | collective-permute-start | bytes 589832 | tf_op jit(solution)/shard_map/ppermute | solution.py:355
  7.9 6.1 %all-to-all-start = ((s32[8,1,9]{2,1,0:T(1,128)}), s32[8,1,9]{2,1,0:T(1,128)S(1)}, u32[]{:S(2)}, u32[]{:S(2)}) async-start(s32[8,1,9]{2,1,0:T(1,128)} %bitcast.5), calls=%async_computation | async-start | bytes 8192 | tf_op jit(solution)/shard_map/all_to_all | solution.py:446
  14.0 1.6 %collective-permute-done.2.refs_3_ = bf16[32,3072]{1,0:T(8,128)(2,1)S(1)} collective-permute-done((bf16[32,3072]{1,0:T(8,128)(2,1)S(1)}, bf16[32,3072]{1,0:T(8,128)(2,1)S(1)}, u32[]{:S(2)}, u32[]{:S(2)}) %collective-permute-start.2) | collective-permute-done | bytes 196640 | tf_op jit(solution)/shard_map/ppermute | solution.py:355
  15.6 4.8 %all-to-all-done = s32[8,1,9]{2,1,0:T(1,128)S(1)} async-done(((s32[8,1,9]{2,1,0:T(1,128)}), s32[8,1,9]{2,1,0:T(1,128)S(1)}, u32[]{:S(2)}, u32[]{:S(2)}) %all-to-all-start) | async-done | bytes 320 | tf_op jit(solution)/shard_map/all_to_all | solution.py:446
  26.3 1.5 %collective-permute-start.5 = (bf16[9,32,256]{2,1,0:T(8,128)(2,1)S(1)}, bf16[9,32,256]{2,1,0:T(8,128)(2,1)S(1)}, u32[]{:S(2)}, u32[]{:S(2)}) collective-permute-start(bf16[9,32,256]{2,1,0:T(8,128)(2,1)S(1)} %get-tuple-element.51), channel_id=1, source_target_pairs={{0,2},{1,3},{2,0},{3,1},{4,6},{5,7},{6,4},{7,5},{8,10},{9,11},{10,... | collective-permute-start | bytes 442376 | tf_op jit(solution)/shard_map/ppermute | solution.py:355
  28.6 1.7 %collective-permute-start.8 = (bf16[9,32,256]{2,1,0:T(8,128)(2,1)S(1)}, bf16[9,32,256]{2,1,0:T(8,128)(2,1)S(1)}, u32[]{:S(2)}, u32[]{:S(2)}) collective-permute-start(bf16[9,32,256]{2,1,0:T(8,128)(2,1)S(1)} %get-tuple-element.57), channel_id=1, source_target_pairs={{0,24},{4,28},{8,16},{12,20},{16,8},{20,12},{24,0},{28,4},{1,25},{... | collective-permute-start | bytes 442376 | tf_op jit(solution)/shard_map/ppermute | solution.py:355
  32.1 1.5 %collective-permute-start.9 = (bf16[18,32,256]{2,1,0:T(8,128)(2,1)S(1)}, bf16[18,32,256]{2,1,0:T(8,128)(2,1)S(1)}, u32[]{:S(2)}, u32[]{:S(2)}) collective-permute-start(bf16[18,32,256]{2,1,0:T(8,128)(2,1)S(1)} %join.3), channel_id=1, source_target_pairs={{0,2},{1,3},{2,0},{3,1},{4,6},{5,7},{6,4},{7,5},{8,10},{9,11},{10,... | collective-permute-start | bytes 884744 | tf_op jit(solution)/shard_map/ppermute | solution.py:355
  35.4 3.5 %collective-permute-done.7.refs_1_ = bf16[9,32,256]{2,1,0:T(8,128)(2,1)S(1)} collective-permute-done((bf16[9,32,256]{2,1,0:T(8,128)(2,1)S(1)}, bf16[9,32,256]{2,1,0:T(8,128)(2,1)S(1)}, u32[]{:S(2)}, u32[]{:S(2)}) %collective-permute-start.7) | collective-permute-done | bytes 147488 | tf_op jit(solution)/shard_map/ppermute | solution.py:355
  39.7 1.6 %collective-permute-start.11 = (bf16[31,32,256]{2,1,0:T(8,128)(2,1)S(1)}, bf16[31,32,256]{2,1,0:T(8,128)(2,1)S(1)}, u32[]{:S(2)}, u32[]{:S(2)}) collective-permute-start(bf16[31,32,256]{2,1,0:T(8,128)(2,1)S(1)} %join.4), channel_id=1, source_target_pairs={{0,2},{1,3},{2,0},{3,1},{4,6},{5,7},{6,4},{7,5},{8,10},{9,11},{10,... | collective-permute-start | bytes 1523720 | tf_op jit(solution)/shard_map/ppermute | solution.py:355
  41.2 1.8 %collective-permute-start.13 = (bf16[9,32,256]{2,1,0:T(8,128)(2,1)S(1)}, bf16[9,32,256]{2,1,0:T(8,128)(2,1)S(1)}, u32[]{:S(2)}, u32[]{:S(2)}) collective-permute-start(bf16[9,32,256]{2,1,0:T(8,128)(2,1)S(1)} %get-tuple-element.65), channel_id=1, source_target_pairs={{0,20},{4,16},{8,28},{12,24},{16,4},{20,0},{24,12},{28,8},{1,21},{... | collective-permute-start | bytes 442376 | tf_op jit(solution)/shard_map/ppermute | solution.py:355
  43.0 3.6 %collective-permute-start.14 = (bf16[9,32,256]{2,1,0:T(8,128)(2,1)S(1)}, bf16[9,32,256]{2,1,0:T(8,128)(2,1)S(1)}, u32[]{:S(2)}, u32[]{:S(2)}) collective-permute-start(bf16[9,32,256]{2,1,0:T(8,128)(2,1)S(1)} %get-tuple-element.67), channel_id=1, source_target_pairs={{0,28},{4,24},{8,20},{12,16},{16,12},{20,8},{24,4},{28,0},{1,29},{... | collective-permute-start | bytes 442376 | tf_op jit(solution)/shard_map/ppermute | solution.py:355
  46.6 2.3 %mask.1 = bf16[72,64,256]{2,1,0:T(8,128)(2,1)S(1)} custom-call(s32[3]{0:T(128)S(1)} %pad_add_fusion.info_ref, bf16[72,256,256]{2,1,0:T(8,128)(2,1)} %mask_hbm.1), custom_call_target="tpu_custom_call" | custom-call | flops 1000000000 | tf_op jit(solution)/shard_map/mask/pallas_call | solution.py:513
  50.0 3.7 %collective-permute-done.13.refs_0_ = bf16[9,32,256]{2,1,0:T(8,128)(2,1)S(1)} collective-permute-done((bf16[9,32,256]{2,1,0:T(8,128)(2,1)S(1)}, bf16[9,32,256]{2,1,0:T(8,128)(2,1)S(1)}, u32[]{:S(2)}, u32[]{:S(2)}) %collective-permute-start.13) | collective-permute-done | bytes 147488 | tf_op jit(solution)/shard_map/ppermute | solution.py:355
  54.9 3.1 %collective-permute-start.18 = (bf16[4,32,256]{2,1,0:T(8,128)(2,1)S(1)}, bf16[4,32,256]{2,1,0:T(8,128)(2,1)S(1)}, u32[]{:S(2)}, u32[]{:S(2)}) collective-permute-start(bf16[4,32,256]{2,1,0:T(8,128)(2,1)S(1)} %get-tuple-element.70), channel_id=1, source_target_pairs={{0,12},{4,8},{8,4},{12,0},{16,28},{20,24},{24,20},{28,16},{1,13},{... | collective-permute-start | bytes 196616 | tf_op jit(solution)/shard_map/ppermute | solution.py:355
  58.6 2.3 %collective-permute-done.15 = bf16[18,32,256]{2,1,0:T(8,128)(2,1)S(1)} collective-permute-done((bf16[18,32,256]{2,1,0:T(8,128)(2,1)S(1)}, bf16[18,32,256]{2,1,0:T(8,128)(2,1)S(1)}, u32[]{:S(2)}, u32[]{:S(2)}) %collective-permute-start.15) | collective-permute-done | bytes 294944 | tf_op jit(solution)/shard_map/ppermute | solution.py:355
  62.4 2.4 %collective-permute-start.20 = (bf16[4,32,256]{2,1,0:T(8,128)(2,1)S(1)}, bf16[4,32,256]{2,1,0:T(8,128)(2,1)S(1)}, u32[]{:S(2)}, u32[]{:S(2)}) collective-permute-start(bf16[4,32,256]{2,1,0:T(8,128)(2,1)S(1)} %get-tuple-element.71), channel_id=1, source_target_pairs={{0,16},{4,20},{8,24},{12,28},{16,0},{20,4},{24,8},{28,12},{1,17},{... | collective-permute-start | bytes 196616 | tf_op jit(solution)/shard_map/ppermute | solution.py:355
  64.8 5.0 %start.1 = (f32[512,128]{1,0:T(8,128)S(1)}, bf16[72,128,256]{2,1,0:T(8,128)(2,1)S(1)}) custom-call(s32[72]{0:T(128)S(1)} %get-tuple-element.97.slot_ref, s32[72]{0:T(128)S(1)} %get-tuple-element.96.user_ref, s32[3]{0:T(128)S(1)} %pad_add_fusion.info_ref, f32[128,512]{1,0:T(8,128)S(1)} %get-tuple-element.54.x_ref, bf16[72,64,256]{2,1,0:T(8,128)(2,1)S(1)} %mask.1, ...), custom_call_target="tpu_custom_call" | custom-call | flops 8000000000 | tf_op jit(solution)/shard_map/start/pallas_call | solution.py:557
  69.8 4.8 %first.1 = (f32[4,64,512]{2,1,0:T(8,128)S(1)}, f32[512,128]{1,0:T(8,128)S(1)}, f32[512,128]{1,0:T(8,128)S(1)}, f32[128,128]{1,0:T(8,128)S(1)}) custom-call(s32[72]{0:T(128)S(1)} %get-tuple-element.97.slot_ref, s32[72]{0:T(128)S(1)} %get-tuple-element.96.user_ref, s32[3]{0:T(128)S(1)} %pad_add_fusion.info_ref, f32[128,512]{1,0:T(8,128)S(1)} %get-tuple-element.54.x_ref, ...), custom_call_target="tpu_custom_call" | custom-call | flops 8000000000 | tf_op jit(solution)/shard_map/first/pallas_call | solution.py:567
  76.6 5.3 %second.1 = (f32[4,32,512]{2,1,0:T(8,128)S(1)}, f32[32,128]{1,0:T(8,128)}) custom-call(s32[72]{0:T(128)S(1)} %get-tuple-element.97.slot_ref, s32[72]{0:T(128)S(1)} %get-tuple-element.96.user_ref, s32[3]{0:T(128)S(1)} %pad_add_fusion.info_ref, f32[512,128]{1,0:T(8,128)S(1)} %get-tuple-element.77.field_ref, f32[512,128]{1,0:T(8,128)S(1)} %get-tuple-element.78.first_ref, ...), custom_call_target="tpu_custom_call" | custom-call | flops 8000000000 | tf_op jit(solution)/shard_map/second/pallas_call | solution.py:575
  81.8 1.7 %collective-permute-start.26 = (f32[32,512]{1,0:T(8,128)S(1)}, f32[32,512]{1,0:T(8,128)S(1)}, u32[]{:S(2)}, u32[]{:S(2)}) collective-permute-start(f32[32,512]{1,0:T(8,128)S(1)} %get-tuple-element.88), channel_id=1, source_target_pairs={{0,3},{1,2},{2,1},{3,0},{4,7},{5,6},{6,5},{7,4},{8,11},{9,10},{10,... | collective-permute-start | bytes 196616 | tf_op jit(solution)/shard_map/ppermute | solution.py:355
  84.1 3.7 %all-to-all-start.1 = ((f32[32,1,128]{2,1,0:T(1,128)}), f32[32,1,128]{2,1,0:T(1,128)S(1)}, u32[]{:S(2)}, u32[]{:S(2)}) async-start(f32[32,1,128]{2,1,0:T(1,128)} %bitcast.12), calls=%async_computation.1 | async-start | bytes 32768 | tf_op jit(solution)/shard_map/all_to_all | solution.py:590
  87.8 7.0 %all-to-all-done.1 = f32[32,1,128]{2,1,0:T(1,128)S(1)} async-done(((f32[32,1,128]{2,1,0:T(1,128)}), f32[32,1,128]{2,1,0:T(1,128)S(1)}, u32[]{:S(2)}, u32[]{:S(2)}) %all-to-all-start.1) | async-done | bytes 16416 | tf_op jit(solution)/shard_map/all_to_all | solution.py:590
  94.9 2.0 %finish.1 = (f32[32,2048]{1,0:T(8,128)}, f32[32,2048]{1,0:T(8,128)}) custom-call(s32[3]{0:T(128)S(1)} %pad_add_fusion.info_ref, f32[32,128]{1,0:T(8,128)S(1)} %bitcast.31, f32[32,2048]{1,0:T(8,128)S(1)} %copy-done.1, f32[64,512]{1,0:T(8,128)S(1)} %get-tuple-element.87.refs_0_, f32[64,512]{1,0:T(8,128)S(1)} %collective-permute-done.21.refs_1_, ...), custom_call_target="tpu_custom_call" | custom-call | flops 1000000000 | tf_op jit(solution)/shard_map/finish/pallas_call | solution.py:593
  (73 shorter events, 20.1 us)
Async XLA Ops:
  3.1 10.9 %collective-permute-start = (bf16[32,3072]{1,0:T(8,128)(2,1)S(1)}, bf16[32,3072]{1,0:T(8,128)(2,1)S(1)}, u32[]{:S(2)}, u32[]{:S(2)}) collective-permute-start(bf16[32,3072]{1,0:T(8,128)(2,1)S(1)} %get-tuple-element.45), channel_id=1, source_target_pairs={{0,1},{1,0},{2,3},{3,2},{4,5},{5,4},{6,7},{7,6},{8,9},{9,8},{10,11... | collective-permute-start | bytes 589832 | tf_op jit(solution)/shard_map/ppermute | solution.py:355
  3.6 10.4 %collective-permute-start.1 = (bf16[32,3072]{1,0:T(8,128)(2,1)S(1)}, bf16[32,3072]{1,0:T(8,128)(2,1)S(1)}, u32[]{:S(2)}, u32[]{:S(2)}) collective-permute-start(bf16[32,3072]{1,0:T(8,128)(2,1)S(1)} %get-tuple-element.46), channel_id=1, source_target_pairs={{0,2},{1,3},{2,0},{3,1},{4,6},{5,7},{6,4},{7,5},{8,10},{9,11},{10,... | collective-permute-start | bytes 589832 | tf_op jit(solution)/shard_map/ppermute | solution.py:355
  6.2 9.4 %collective-permute-start.2 = (bf16[32,3072]{1,0:T(8,128)(2,1)S(1)}, bf16[32,3072]{1,0:T(8,128)(2,1)S(1)}, u32[]{:S(2)}, u32[]{:S(2)}) collective-permute-start(bf16[32,3072]{1,0:T(8,128)(2,1)S(1)} %get-tuple-element.47), channel_id=1, source_target_pairs={{0,3},{1,2},{2,1},{3,0},{4,7},{5,6},{6,5},{7,4},{8,11},{9,10},{10,... | collective-permute-start | bytes 589832 | tf_op jit(solution)/shard_map/ppermute | solution.py:355
  7.9 12.5 %all-to-all-start = ((s32[8,1,9]{2,1,0:T(1,128)}), s32[8,1,9]{2,1,0:T(1,128)S(1)}, u32[]{:S(2)}, u32[]{:S(2)}) async-start(s32[8,1,9]{2,1,0:T(1,128)} %bitcast.5), calls=%async_computation | async-start | bytes 8192 | tf_op jit(solution)/shard_map/all_to_all | solution.py:446
  22.2 6.3 %collective-permute-start.3 = (bf16[9,32,256]{2,1,0:T(8,128)(2,1)S(1)}, bf16[9,32,256]{2,1,0:T(8,128)(2,1)S(1)}, u32[]{:S(2)}, u32[]{:S(2)}) collective-permute-start(bf16[9,32,256]{2,1,0:T(8,128)(2,1)S(1)} %get-tuple-element.49), channel_id=1, source_target_pairs={{0,4},{4,0},{8,12},{12,8},{16,20},{20,16},{24,28},{28,24},{1,5},{5... | collective-permute-start | bytes 442376 | tf_op jit(solution)/shard_map/ppermute | solution.py:355
  22.8 8.8 %collective-permute-start.4 = (bf16[9,32,256]{2,1,0:T(8,128)(2,1)S(1)}, bf16[9,32,256]{2,1,0:T(8,128)(2,1)S(1)}, u32[]{:S(2)}, u32[]{:S(2)}) collective-permute-start(bf16[9,32,256]{2,1,0:T(8,128)(2,1)S(1)} %get-tuple-element.50), channel_id=1, source_target_pairs={{0,12},{4,8},{8,4},{12,0},{16,28},{20,24},{24,20},{28,16},{1,13},{... | collective-permute-start | bytes 442376 | tf_op jit(solution)/shard_map/ppermute | solution.py:355
  24.3 11.1 %collective-permute-start.6 = (bf16[9,32,256]{2,1,0:T(8,128)(2,1)S(1)}, bf16[9,32,256]{2,1,0:T(8,128)(2,1)S(1)}, u32[]{:S(2)}, u32[]{:S(2)}) collective-permute-start(bf16[9,32,256]{2,1,0:T(8,128)(2,1)S(1)} %get-tuple-element.55), channel_id=1, source_target_pairs={{0,8},{4,12},{8,0},{12,4},{16,24},{20,28},{24,16},{28,20},{1,9},{5... | collective-permute-start | bytes 442376 | tf_op jit(solution)/shard_map/ppermute | solution.py:355
  25.8 13.1 %collective-permute-start.7 = (bf16[9,32,256]{2,1,0:T(8,128)(2,1)S(1)}, bf16[9,32,256]{2,1,0:T(8,128)(2,1)S(1)}, u32[]{:S(2)}, u32[]{:S(2)}) collective-permute-start(bf16[9,32,256]{2,1,0:T(8,128)(2,1)S(1)} %get-tuple-element.56), channel_id=1, source_target_pairs={{0,16},{4,20},{8,24},{12,28},{16,0},{20,4},{24,8},{28,12},{1,17},{... | collective-permute-start | bytes 442376 | tf_op jit(solution)/shard_map/ppermute | solution.py:355
  26.3 5.7 %collective-permute-start.5 = (bf16[9,32,256]{2,1,0:T(8,128)(2,1)S(1)}, bf16[9,32,256]{2,1,0:T(8,128)(2,1)S(1)}, u32[]{:S(2)}, u32[]{:S(2)}) collective-permute-start(bf16[9,32,256]{2,1,0:T(8,128)(2,1)S(1)} %get-tuple-element.51), channel_id=1, source_target_pairs={{0,2},{1,3},{2,0},{3,1},{4,6},{5,7},{6,4},{7,5},{8,10},{9,11},{10,... | collective-permute-start | bytes 442376 | tf_op jit(solution)/shard_map/ppermute | solution.py:355
  28.6 10.3 %collective-permute-start.8 = (bf16[9,32,256]{2,1,0:T(8,128)(2,1)S(1)}, bf16[9,32,256]{2,1,0:T(8,128)(2,1)S(1)}, u32[]{:S(2)}, u32[]{:S(2)}) collective-permute-start(bf16[9,32,256]{2,1,0:T(8,128)(2,1)S(1)} %get-tuple-element.57), channel_id=1, source_target_pairs={{0,24},{4,28},{8,16},{12,20},{16,8},{20,12},{24,0},{28,4},{1,25},{... | collective-permute-start | bytes 442376 | tf_op jit(solution)/shard_map/ppermute | solution.py:355
  32.1 7.6 %collective-permute-start.9 = (bf16[18,32,256]{2,1,0:T(8,128)(2,1)S(1)}, bf16[18,32,256]{2,1,0:T(8,128)(2,1)S(1)}, u32[]{:S(2)}, u32[]{:S(2)}) collective-permute-start(bf16[18,32,256]{2,1,0:T(8,128)(2,1)S(1)} %join.3), channel_id=1, source_target_pairs={{0,2},{1,3},{2,0},{3,1},{4,6},{5,7},{6,4},{7,5},{8,10},{9,11},{10,... | collective-permute-start | bytes 884744 | tf_op jit(solution)/shard_map/ppermute | solution.py:355
  39.7 10.1 %collective-permute-start.11 = (bf16[31,32,256]{2,1,0:T(8,128)(2,1)S(1)}, bf16[31,32,256]{2,1,0:T(8,128)(2,1)S(1)}, u32[]{:S(2)}, u32[]{:S(2)}) collective-permute-start(bf16[31,32,256]{2,1,0:T(8,128)(2,1)S(1)} %join.4), channel_id=1, source_target_pairs={{0,2},{1,3},{2,0},{3,1},{4,6},{5,7},{6,4},{7,5},{8,10},{9,11},{10,... | collective-permute-start | bytes 1523720 | tf_op jit(solution)/shard_map/ppermute | solution.py:355
  41.2 12.5 %collective-permute-start.13 = (bf16[9,32,256]{2,1,0:T(8,128)(2,1)S(1)}, bf16[9,32,256]{2,1,0:T(8,128)(2,1)S(1)}, u32[]{:S(2)}, u32[]{:S(2)}) collective-permute-start(bf16[9,32,256]{2,1,0:T(8,128)(2,1)S(1)} %get-tuple-element.65), channel_id=1, source_target_pairs={{0,20},{4,16},{8,28},{12,24},{16,4},{20,0},{24,12},{28,8},{1,21},{... | collective-permute-start | bytes 442376 | tf_op jit(solution)/shard_map/ppermute | solution.py:355
  43.0 10.8 %collective-permute-start.14 = (bf16[9,32,256]{2,1,0:T(8,128)(2,1)S(1)}, bf16[9,32,256]{2,1,0:T(8,128)(2,1)S(1)}, u32[]{:S(2)}, u32[]{:S(2)}) collective-permute-start(bf16[9,32,256]{2,1,0:T(8,128)(2,1)S(1)} %get-tuple-element.67), channel_id=1, source_target_pairs={{0,28},{4,24},{8,20},{12,16},{16,12},{20,8},{24,4},{28,0},{1,29},{... | collective-permute-start | bytes 442376 | tf_op jit(solution)/shard_map/ppermute | solution.py:355
  49.9 4.9 %collective-permute-start.12 = (bf16[58,32,256]{2,1,0:T(8,128)(2,1)S(1)}, bf16[58,32,256]{2,1,0:T(8,128)(2,1)S(1)}, u32[]{:S(2)}, u32[]{:S(2)}) collective-permute-start(bf16[58,32,256]{2,1,0:T(8,128)(2,1)S(1)} %pad_maximum_fusion.refs_2_), channel_id=1, source_target_pairs={{0,1},{1,0},{2,3},{3,2},{4,5},{5,4},{6,7},{7,6},{8,9},{9,8},{10,11... | collective-permute-start | bytes 2850824 | tf_op jit(solution)/shard_map/ppermute | solution.py:355
  54.1 6.8 %collective-permute-start.15 = (bf16[18,32,256]{2,1,0:T(8,128)(2,1)S(1)}, bf16[18,32,256]{2,1,0:T(8,128)(2,1)S(1)}, u32[]{:S(2)}, u32[]{:S(2)}) collective-permute-start(bf16[18,32,256]{2,1,0:T(8,128)(2,1)S(1)} %join.5), channel_id=1, source_target_pairs={{0,2},{1,3},{2,0},{3,1},{4,6},{5,7},{6,4},{7,5},{8,10},{9,11},{10,... | collective-permute-start | bytes 884744 | tf_op jit(solution)/shard_map/ppermute | solution.py:355
  54.8 10.0 %collective-permute-start.10 = (bf16[54,32,256]{2,1,0:T(8,128)(2,1)S(1)}, bf16[54,32,256]{2,1,0:T(8,128)(2,1)S(1)}, u32[]{:S(2)}, u32[]{:S(2)}) collective-permute-start(bf16[54,32,256]{2,1,0:T(8,128)(2,1)S(1)} %constant_dynamic-update-slice_fusion.refs_0_), channel_id=1, source_target_pairs={{0,1},{1,0},{2,3},{3,2},{4,5},{5,4},{6,7},{7,6},{8,9},{9,8},{10,11... | collective-permute-start | bytes 2654216 | tf_op jit(solution)/shard_map/ppermute | solution.py:355
  54.9 6.1 %collective-permute-start.18 = (bf16[4,32,256]{2,1,0:T(8,128)(2,1)S(1)}, bf16[4,32,256]{2,1,0:T(8,128)(2,1)S(1)}, u32[]{:S(2)}, u32[]{:S(2)}) collective-permute-start(bf16[4,32,256]{2,1,0:T(8,128)(2,1)S(1)} %get-tuple-element.70), channel_id=1, source_target_pairs={{0,12},{4,8},{8,4},{12,0},{16,28},{20,24},{24,20},{28,16},{1,13},{... | collective-permute-start | bytes 196616 | tf_op jit(solution)/shard_map/ppermute | solution.py:355
  62.4 7.3 %collective-permute-start.20 = (bf16[4,32,256]{2,1,0:T(8,128)(2,1)S(1)}, bf16[4,32,256]{2,1,0:T(8,128)(2,1)S(1)}, u32[]{:S(2)}, u32[]{:S(2)}) collective-permute-start(bf16[4,32,256]{2,1,0:T(8,128)(2,1)S(1)} %get-tuple-element.71), channel_id=1, source_target_pairs={{0,16},{4,20},{8,24},{12,28},{16,0},{20,4},{24,8},{28,12},{1,17},{... | collective-permute-start | bytes 196616 | tf_op jit(solution)/shard_map/ppermute | solution.py:355
  74.6 9.4 %collective-permute-start.23 = (f32[64,512]{1,0:T(8,128)S(1)}, f32[64,512]{1,0:T(8,128)S(1)}, u32[]{:S(2)}, u32[]{:S(2)}) collective-permute-start(f32[64,512]{1,0:T(8,128)S(1)} %get-tuple-element.84), channel_id=1, source_target_pairs={{0,3},{1,2},{2,1},{3,0},{4,7},{5,6},{6,5},{7,4},{8,11},{9,10},{10,... | collective-permute-start | bytes 393224 | tf_op jit(solution)/shard_map/ppermute | solution.py:355
  76.0 8.0 %collective-permute-start.22 = (f32[64,512]{1,0:T(8,128)S(1)}, f32[64,512]{1,0:T(8,128)S(1)}, u32[]{:S(2)}, u32[]{:S(2)}) collective-permute-start(f32[64,512]{1,0:T(8,128)S(1)} %get-tuple-element.85), channel_id=1, source_target_pairs={{0,2},{1,3},{2,0},{3,1},{4,6},{5,7},{6,4},{7,5},{8,10},{9,11},{10,... | collective-permute-start | bytes 393224 | tf_op jit(solution)/shard_map/ppermute | solution.py:355
  76.5 7.5 %collective-permute-start.21 = (f32[64,512]{1,0:T(8,128)S(1)}, f32[64,512]{1,0:T(8,128)S(1)}, u32[]{:S(2)}, u32[]{:S(2)}) collective-permute-start(f32[64,512]{1,0:T(8,128)S(1)} %get-tuple-element.86), channel_id=1, source_target_pairs={{0,1},{1,0},{2,3},{3,2},{4,5},{5,4},{6,7},{7,6},{8,9},{9,8},{10,11... | collective-permute-start | bytes 393224 | tf_op jit(solution)/shard_map/ppermute | solution.py:355
  81.8 5.9 %collective-permute-start.26 = (f32[32,512]{1,0:T(8,128)S(1)}, f32[32,512]{1,0:T(8,128)S(1)}, u32[]{:S(2)}, u32[]{:S(2)}) collective-permute-start(f32[32,512]{1,0:T(8,128)S(1)} %get-tuple-element.88), channel_id=1, source_target_pairs={{0,3},{1,2},{2,1},{3,0},{4,7},{5,6},{6,5},{7,4},{8,11},{9,10},{10,... | collective-permute-start | bytes 196616 | tf_op jit(solution)/shard_map/ppermute | solution.py:355
  84.1 10.8 %all-to-all-start.1 = ((f32[32,1,128]{2,1,0:T(1,128)}), f32[32,1,128]{2,1,0:T(1,128)S(1)}, u32[]{:S(2)}, u32[]{:S(2)}) async-start(f32[32,1,128]{2,1,0:T(1,128)} %bitcast.12), calls=%async_computation.1 | async-start | bytes 32768 | tf_op jit(solution)/shard_map/all_to_all | solution.py:590
  (8 other events, 50.9 us)

commit v11 on v10

--- a/solution.py
+++ b/solution.py
@@ -256,21 +256,19 @@
 def first_kernel(
     slot_ref, user_ref, info_ref, x_ref, part_ref, gram_ref, y, mask, *refs
 ):
-    sent_ref, field_ref, first_ref, gram_out, p_hl, acc, held = refs[-7:]
+    field_ref, first_ref, gram_out, p_hl, acc, held = refs[-6:]
     gram = gram_ref[...]
-    for arrived_ref in refs[:-7]:
+    for arrived_ref in refs[:-6]:
         gram = gram + unpack(arrived_ref)
     gram_out[...] = gram
     start = x_ref[...].T
     load(p_hl, start)
     field = part_ref[...] - dense(p_hl, gram_out, start)
     field_ref[...] = field
-    put(info_ref[1], sent_ref, field)
     load(p_hl, field)
     sparse(False, slot_ref, user_ref, y, mask, p_hl, acc, held)
     first = confidence * acc[...].reshape(field.shape) + dense(p_hl, gram_out, field)
     first_ref[...] = first
-    put(info_ref[1], sent_ref, first, 1)
 
 
 def second_kernel(
@@ -281,7 +279,8 @@
     load(p_hl, first)
     sparse(False, slot_ref, user_ref, y, mask, p_hl, acc, held)
     second = confidence * acc[...].reshape(field.shape) + dense(p_hl, gram_ref, first)
-    put(info_ref[1], sent_ref, second)
+    for part, vector in enumerate((field, first, second)):
+        put(info_ref[1], sent_ref, vector, part)
 
     def total(left, right):
         return jnp.sum(left * right)
@@ -309,14 +308,13 @@
 
 
 def finish_kernel(share, info_ref, dots_ref, x_ref, *refs):
-    n_cols = (len(refs) - 5) // 2
-    x_out, r_out, field_ref, first_ref, second_ref = refs[2 * n_cols :]
+    n_cols = len(refs) - 5
+    x_out, r_out, field_ref, first_ref, second_ref = refs[n_cols:]
     width = field_ref.shape[1]
     for m in range(n_cols):
         place = info_ref[1] ^ m
-        field_ref[place] = refs[m][:width]
-        first_ref[place] = refs[m][width:]
-        second_ref[place] = refs[n_cols + m][...]
+        for part, ref in enumerate((field_ref, first_ref, second_ref)):
+            ref[place] = refs[m][part * width : (part + 1) * width]
     dots = dots_ref[...]
 
     def column(j):
@@ -563,19 +561,18 @@
         8 * 10**9,
     )(*lists, start, mask, *pieces)
     rest = [after(arrived, part)] if direct else []
-    pair = jax.ShapeDtypeStruct((n_cols, 2 * col_width, own_users), f32)
-    pair_sent, field, first, gram = call(
+    field, first, gram = call(
         first_kernel,
-        [pair, vector, vector, square],
+        [vector, vector, square],
         [smem] * 3 + [vmem] * (5 + len(rest)),
         "first",
         work,
         8 * 10**9,
     )(*lists, start, part, gram, y, mask, *rest)
-    second_sent, dots = call(
+    sent, dots = call(
         second_kernel,
         [
-            jax.ShapeDtypeStruct((n_cols, col_width, own_users), f32),
+            jax.ShapeDtypeStruct((n_cols, 3 * col_width, own_users), f32),
             jax.ShapeDtypeStruct((devices, 128), f32),
         ],
         [smem] * 3 + [vmem] * 5,
@@ -584,16 +581,14 @@
         8 * 10**9,
     )(*lists, field, first, gram, y, mask)
 
-    turned = swap(pair_sent)
-    dots = after(dots, *turned)
-    turned += swap(second_sent)
+    turned = swap(sent)
     dots = lax.all_to_all(dots, ("rows", "cols"), split_axis=0, concat_axis=0, tiled=True)
     result = jax.ShapeDtypeStruct((col_width, users), f32)
     return tuple(
         call(
             functools.partial(finish_kernel, share),
             [result, result],
-            [smem] + [vmem] * (2 + 2 * n_cols),
+            [smem] + [vmem] * (2 + n_cols),
             "finish",
             [pltpu.VMEM((n_cols, col_width, own_users), f32)] * 3,
             10**9,

time: 97.2 us -> 94.2 us (0.969)
  blocking collectives: 0 us -> 10.7 us
  waiting for transfers between devices: 27.7 us -> 20.8 us
  starting transfers between devices: 39.8 us -> 33.9 us
    all_to_all x0 -> x1, blocking collectives: none -> 10.7 us  [on_device(): lax.all_to_all(dots, ('rows', 'cols'), split_axis=0, concat_axis=0, tiled...]
    all_to_all x1 -> x0, waiting for transfers between devices: 7.04 us -> none  [on_device(): lax.all_to_all(dots, ('rows', 'cols'), split_axis=0, concat_axis=0, tiled...]
    all_to_all x1 -> x0, starting transfers between devices: 3.72 us -> none  [on_device(): lax.all_to_all(dots, ('rows', 'cols'), split_axis=0, concat_axis=0, tiled...]
    ppermute x27 -> x24, starting transfers between devices: 30 us -> 27.8 us  [flip(): return lax.ppermute(value, axis, [(i, i ^ bit) for i in range(size)])]
    ppermute x27 -> x24, waiting for transfers between devices: 15.9 us -> 16 us  [flip(): return lax.ppermute(value, axis, [(i, i ^ bit) for i in range(size)])]
  transfers between devices with their start and end apart: 29 -> 25, of which waited for: 11 -> 10; matrix products, arithmetic and copies ran while one was open for 2% -> 2% of each run, Pallas kernels for 16% -> 11%
where the time goes in v11:
time: 94.2 us; the launch traced here: 93.9 us
  starting transfers between devices  33.9 us (36%)
  Pallas kernels  23.8 us (25%)
  waiting for transfers between devices  20.8 us (22%)
  blocking collectives  10.7 us (11%)
  local copies, waits for them, and re-layouts  1.92 us (2%)
  between operations  1.57 us (2%)
  other arithmetic  1.26 us (1%)
    ppermute x24, starting transfers between devices, flip(): return lax.ppermute(value, axis, [(i, i ^ bit) for i in range(size)])  27.8 us
    ppermute x24, waiting for transfers between devices, flip(): return lax.ppermute(value, axis, [(i, i ^ bit) for i in range(size)])  16 us
    all_to_all x1, blocking collectives, on_device(): lax.all_to_all(dots, ('rows', 'cols'), split_axis=0, concat_axis=0, tiled...  10.7 us
    all_to_all x1, starting transfers between devices, on_device(): lax.all_to_all(requests, 'rows', split_axis=0, concat_axis=0, tiled=True)  6.07 us
    pallas_call x1, Pallas kernels, on_device(): call(functools.partial(start_kernel, n_cols, slots), [vector, held], [sme...  4.95 us
    all_to_all x1, waiting for transfers between devices, on_device(): lax.all_to_all(requests, 'rows', split_axis=0, concat_axis=0, tiled=True)  4.76 us
    pallas_call x1, Pallas kernels, on_device(): call(first_kernel, [vector, vector, square], [smem] * 3 + [vmem] * (5 + l...  4.68 us
    pallas_call x1, Pallas kernels, on_device(): call(second_kernel, [jax.ShapeDtypeStruct((n_cols, 3 * col_width, own_use...  4.66 us
  transfers between devices with their start and end apart: 25, of which 10 were waited for; matrix products, arithmetic and copies ran while one was open for 2% of the time, Pallas kernels for 11%

profile of v11, /device:TPU:0, one launch (start us, length us, event | category | flops | bytes accessed | tf_op | source)
XLA Modules:
  0.0 93.9 jit_solution(12937923667297273267)
XLA Ops:
  1.4 1.7 %prepare.1 = (bf16[32,3072]{1,0:T(8,128)(2,1)S(1)}, bf16[32,3072]{1,0:T(8,128)(2,1)S(1)}, bf16[32,3072]{1,0:T(8,128)(2,1)S(1)}, bf16[32,3072]{1,0:T(8,128)(2,1)S(1)}) custom-call(s32[3]{0:T(128)S(1)} %pad_add_fusion.info_ref, f32[32,2048]{1,0:T(8,128)} %x_ref.1, bf16[32,8192]{1,0:T(8,128)(2,1)} %items_ref.1), custom_call_target="tpu_custom_call" | custom-call | flops 1000000000 | tf_op jit(solution)/shard_map/prepare/pallas_call | solution.py:411
  3.6 2.6 %collective-permute-start.1 = (bf16[32,3072]{1,0:T(8,128)(2,1)S(1)}, bf16[32,3072]{1,0:T(8,128)(2,1)S(1)}, u32[]{:S(2)}, u32[]{:S(2)}) collective-permute-start(bf16[32,3072]{1,0:T(8,128)(2,1)S(1)} %get-tuple-element.44), channel_id=1, source_target_pairs={{0,2},{1,3},{2,0},{3,1},{4,6},{5,7},{6,4},{7,5},{8,10},{9,11},{10,... | collective-permute-start | bytes 589832 | tf_op jit(solution)/shard_map/ppermute | solution.py:353
  7.9 6.1 %all-to-all-start = ((s32[8,1,9]{2,1,0:T(1,128)}), s32[8,1,9]{2,1,0:T(1,128)S(1)}, u32[]{:S(2)}, u32[]{:S(2)}) async-start(s32[8,1,9]{2,1,0:T(1,128)} %bitcast.5), calls=%async_computation | async-start | bytes 8192 | tf_op jit(solution)/shard_map/all_to_all | solution.py:444
  14.0 1.6 %collective-permute-done.2.refs_3_ = bf16[32,3072]{1,0:T(8,128)(2,1)S(1)} collective-permute-done((bf16[32,3072]{1,0:T(8,128)(2,1)S(1)}, bf16[32,3072]{1,0:T(8,128)(2,1)S(1)}, u32[]{:S(2)}, u32[]{:S(2)}) %collective-permute-start.2) | collective-permute-done | bytes 196640 | tf_op jit(solution)/shard_map/ppermute | solution.py:353
  15.6 4.8 %all-to-all-done = s32[8,1,9]{2,1,0:T(1,128)S(1)} async-done(((s32[8,1,9]{2,1,0:T(1,128)}), s32[8,1,9]{2,1,0:T(1,128)S(1)}, u32[]{:S(2)}, u32[]{:S(2)}) %all-to-all-start) | async-done | bytes 320 | tf_op jit(solution)/shard_map/all_to_all | solution.py:444
  22.8 1.5 %collective-permute-start.4 = (bf16[9,32,256]{2,1,0:T(8,128)(2,1)S(1)}, bf16[9,32,256]{2,1,0:T(8,128)(2,1)S(1)}, u32[]{:S(2)}, u32[]{:S(2)}) collective-permute-start(bf16[9,32,256]{2,1,0:T(8,128)(2,1)S(1)} %get-tuple-element.48), channel_id=1, source_target_pairs={{0,12},{4,8},{8,4},{12,0},{16,28},{20,24},{24,20},{28,16},{1,13},{... | collective-permute-start | bytes 442376 | tf_op jit(solution)/shard_map/ppermute | solution.py:353
  24.3 1.5 %collective-permute-start.6 = (bf16[9,32,256]{2,1,0:T(8,128)(2,1)S(1)}, bf16[9,32,256]{2,1,0:T(8,128)(2,1)S(1)}, u32[]{:S(2)}, u32[]{:S(2)}) collective-permute-start(bf16[9,32,256]{2,1,0:T(8,128)(2,1)S(1)} %get-tuple-element.53), channel_id=1, source_target_pairs={{0,8},{4,12},{8,0},{12,4},{16,24},{20,28},{24,16},{28,20},{1,9},{5... | collective-permute-start | bytes 442376 | tf_op jit(solution)/shard_map/ppermute | solution.py:353
  26.3 1.5 %collective-permute-start.5 = (bf16[9,32,256]{2,1,0:T(8,128)(2,1)S(1)}, bf16[9,32,256]{2,1,0:T(8,128)(2,1)S(1)}, u32[]{:S(2)}, u32[]{:S(2)}) collective-permute-start(bf16[9,32,256]{2,1,0:T(8,128)(2,1)S(1)} %get-tuple-element.49), channel_id=1, source_target_pairs={{0,2},{1,3},{2,0},{3,1},{4,6},{5,7},{6,4},{7,5},{8,10},{9,11},{10,... | collective-permute-start | bytes 442376 | tf_op jit(solution)/shard_map/ppermute | solution.py:353
  28.6 1.7 %collective-permute-start.8 = (bf16[9,32,256]{2,1,0:T(8,128)(2,1)S(1)}, bf16[9,32,256]{2,1,0:T(8,128)(2,1)S(1)}, u32[]{:S(2)}, u32[]{:S(2)}) collective-permute-start(bf16[9,32,256]{2,1,0:T(8,128)(2,1)S(1)} %get-tuple-element.55), channel_id=1, source_target_pairs={{0,24},{4,28},{8,16},{12,20},{16,8},{20,12},{24,0},{28,4},{1,25},{... | collective-permute-start | bytes 442376 | tf_op jit(solution)/shard_map/ppermute | solution.py:353
  32.1 1.5 %collective-permute-start.9 = (bf16[18,32,256]{2,1,0:T(8,128)(2,1)S(1)}, bf16[18,32,256]{2,1,0:T(8,128)(2,1)S(1)}, u32[]{:S(2)}, u32[]{:S(2)}) collective-permute-start(bf16[18,32,256]{2,1,0:T(8,128)(2,1)S(1)} %join.3), channel_id=1, source_target_pairs={{0,2},{1,3},{2,0},{3,1},{4,6},{5,7},{6,4},{7,5},{8,10},{9,11},{10,... | collective-permute-start | bytes 884744 | tf_op jit(solution)/shard_map/ppermute | solution.py:353
  35.4 3.5 %collective-permute-done.7.refs_1_ = bf16[9,32,256]{2,1,0:T(8,128)(2,1)S(1)} collective-permute-done((bf16[9,32,256]{2,1,0:T(8,128)(2,1)S(1)}, bf16[9,32,256]{2,1,0:T(8,128)(2,1)S(1)}, u32[]{:S(2)}, u32[]{:S(2)}) %collective-permute-start.7) | collective-permute-done | bytes 147488 | tf_op jit(solution)/shard_map/ppermute | solution.py:353
  39.7 1.6 %collective-permute-start.11 = (bf16[31,32,256]{2,1,0:T(8,128)(2,1)S(1)}, bf16[31,32,256]{2,1,0:T(8,128)(2,1)S(1)}, u32[]{:S(2)}, u32[]{:S(2)}) collective-permute-start(bf16[31,32,256]{2,1,0:T(8,128)(2,1)S(1)} %join.4), channel_id=1, source_target_pairs={{0,2},{1,3},{2,0},{3,1},{4,6},{5,7},{6,4},{7,5},{8,10},{9,11},{10,... | collective-permute-start | bytes 1523720 | tf_op jit(solution)/shard_map/ppermute | solution.py:353
  41.2 1.8 %collective-permute-start.13 = (bf16[9,32,256]{2,1,0:T(8,128)(2,1)S(1)}, bf16[9,32,256]{2,1,0:T(8,128)(2,1)S(1)}, u32[]{:S(2)}, u32[]{:S(2)}) collective-permute-start(bf16[9,32,256]{2,1,0:T(8,128)(2,1)S(1)} %get-tuple-element.63), channel_id=1, source_target_pairs={{0,20},{4,16},{8,28},{12,24},{16,4},{20,0},{24,12},{28,8},{1,21},{... | collective-permute-start | bytes 442376 | tf_op jit(solution)/shard_map/ppermute | solution.py:353
  43.0 3.6 %collective-permute-start.14 = (bf16[9,32,256]{2,1,0:T(8,128)(2,1)S(1)}, bf16[9,32,256]{2,1,0:T(8,128)(2,1)S(1)}, u32[]{:S(2)}, u32[]{:S(2)}) collective-permute-start(bf16[9,32,256]{2,1,0:T(8,128)(2,1)S(1)} %get-tuple-element.65), channel_id=1, source_target_pairs={{0,28},{4,24},{8,20},{12,16},{16,12},{20,8},{24,4},{28,0},{1,29},{... | collective-permute-start | bytes 442376 | tf_op jit(solution)/shard_map/ppermute | solution.py:353
  46.6 2.2 %mask.1 = bf16[72,64,256]{2,1,0:T(8,128)(2,1)S(1)} custom-call(s32[3]{0:T(128)S(1)} %pad_add_fusion.info_ref, bf16[72,256,256]{2,1,0:T(8,128)(2,1)} %mask_hbm.1), custom_call_target="tpu_custom_call" | custom-call | flops 1000000000 | tf_op jit(solution)/shard_map/mask/pallas_call | solution.py:511
  50.0 3.7 %collective-permute-done.13.refs_0_ = bf16[9,32,256]{2,1,0:T(8,128)(2,1)S(1)} collective-permute-done((bf16[9,32,256]{2,1,0:T(8,128)(2,1)S(1)}, bf16[9,32,256]{2,1,0:T(8,128)(2,1)S(1)}, u32[]{:S(2)}, u32[]{:S(2)}) %collective-permute-start.13) | collective-permute-done | bytes 147488 | tf_op jit(solution)/shard_map/ppermute | solution.py:353
  54.9 3.1 %collective-permute-start.18 = (bf16[4,32,256]{2,1,0:T(8,128)(2,1)S(1)}, bf16[4,32,256]{2,1,0:T(8,128)(2,1)S(1)}, u32[]{:S(2)}, u32[]{:S(2)}) collective-permute-start(bf16[4,32,256]{2,1,0:T(8,128)(2,1)S(1)} %get-tuple-element.68), channel_id=1, source_target_pairs={{0,12},{4,8},{8,4},{12,0},{16,28},{20,24},{24,20},{28,16},{1,13},{... | collective-permute-start | bytes 196616 | tf_op jit(solution)/shard_map/ppermute | solution.py:353
  58.6 2.3 %collective-permute-done.15 = bf16[18,32,256]{2,1,0:T(8,128)(2,1)S(1)} collective-permute-done((bf16[18,32,256]{2,1,0:T(8,128)(2,1)S(1)}, bf16[18,32,256]{2,1,0:T(8,128)(2,1)S(1)}, u32[]{:S(2)}, u32[]{:S(2)}) %collective-permute-start.15) | collective-permute-done | bytes 294944 | tf_op jit(solution)/shard_map/ppermute | solution.py:353
  62.4 2.4 %collective-permute-start.20 = (bf16[4,32,256]{2,1,0:T(8,128)(2,1)S(1)}, bf16[4,32,256]{2,1,0:T(8,128)(2,1)S(1)}, u32[]{:S(2)}, u32[]{:S(2)}) collective-permute-start(bf16[4,32,256]{2,1,0:T(8,128)(2,1)S(1)} %get-tuple-element.69), channel_id=1, source_target_pairs={{0,16},{4,20},{8,24},{12,28},{16,0},{20,4},{24,8},{28,12},{1,17},{... | collective-permute-start | bytes 196616 | tf_op jit(solution)/shard_map/ppermute | solution.py:353
  64.8 5.0 %start.1 = (f32[512,128]{1,0:T(8,128)S(1)}, bf16[72,128,256]{2,1,0:T(8,128)(2,1)S(1)}) custom-call(s32[72]{0:T(128)S(1)} %get-tuple-element.89.slot_ref, s32[72]{0:T(128)S(1)} %get-tuple-element.88.user_ref, s32[3]{0:T(128)S(1)} %pad_add_fusion.info_ref, f32[128,512]{1,0:T(8,128)S(1)} %get-tuple-element.52.x_ref, bf16[72,64,256]{2,1,0:T(8,128)(2,1)S(1)} %mask.1, ...), custom_call_target="tpu_custom_call" | custom-call | flops 8000000000 | tf_op jit(solution)/shard_map/start/pallas_call | solution.py:555
  69.8 4.7 %first.1 = (f32[512,128]{1,0:T(8,128)S(1)}, f32[512,128]{1,0:T(8,128)S(1)}, f32[128,128]{1,0:T(8,128)S(1)}) custom-call(s32[72]{0:T(128)S(1)} %get-tuple-element.89.slot_ref, s32[72]{0:T(128)S(1)} %get-tuple-element.88.user_ref, s32[3]{0:T(128)S(1)} %pad_add_fusion.info_ref, f32[128,512]{1,0:T(8,128)S(1)} %get-tuple-element.52.x_ref, ...), custom_call_target="tpu_custom_call" | custom-call | flops 8000000000 | tf_op jit(solution)/shard_map/first/pallas_call | solution.py:564
  74.5 4.7 %second.1 = (f32[4,96,512]{2,1,0:T(8,128)S(1)}, f32[32,128]{1,0:T(8,128)S(1)}) custom-call(s32[72]{0:T(128)S(1)} %get-tuple-element.89.slot_ref, s32[72]{0:T(128)S(1)} %get-tuple-element.88.user_ref, s32[3]{0:T(128)S(1)} %pad_add_fusion.info_ref, f32[512,128]{1,0:T(8,128)S(1)} %get-tuple-element.75.field_ref, f32[512,128]{1,0:T(8,128)S(1)} %get-tuple-element.76.first_ref, ...), custom_call_target="tpu_custom_call" | custom-call | flops 8000000000 | tf_op jit(solution)/shard_map/second/pallas_call | solution.py:572
  81.1 10.7 %all_to_all.19 = f32[32,1,128]{2,1,0:T(1,128)S(1)} all-to-all(f32[32,1,128]{2,1,0:T(1,128)S(1)} %bitcast.23), channel_id=1, replica_groups=mesh['rows'=8,'cols'=4] {'rows','cols'}, dimensions={0} | all-to-all | bytes 32768 | tf_op jit(solution)/shard_map/all_to_all | solution.py:585
  91.9 2.0 %finish.1 = (f32[32,2048]{1,0:T(8,128)}, f32[32,2048]{1,0:T(8,128)}) custom-call(s32[3]{0:T(128)S(1)} %pad_add_fusion.info_ref, f32[32,128]{1,0:T(8,128)S(1)} %bitcast.24, f32[32,2048]{1,0:T(8,128)S(1)} %copy-done.1, f32[96,512]{1,0:T(8,128)S(1)} %get-tuple-element.83.refs_0_, f32[96,512]{1,0:T(8,128)S(1)} %collective-permute-done.21.refs_1_, ...), custom_call_target="tpu_custom_call" | custom-call | flops 1000000000 | tf_op jit(solution)/shard_map/finish/pallas_call | solution.py:588
  (65 shorter events, 16.7 us)
Async XLA Ops:
  3.1 10.9 %collective-permute-start = (bf16[32,3072]{1,0:T(8,128)(2,1)S(1)}, bf16[32,3072]{1,0:T(8,128)(2,1)S(1)}, u32[]{:S(2)}, u32[]{:S(2)}) collective-permute-start(bf16[32,3072]{1,0:T(8,128)(2,1)S(1)} %get-tuple-element.43), channel_id=1, source_target_pairs={{0,1},{1,0},{2,3},{3,2},{4,5},{5,4},{6,7},{7,6},{8,9},{9,8},{10,11... | collective-permute-start | bytes 589832 | tf_op jit(solution)/shard_map/ppermute | solution.py:353
  3.6 10.4 %collective-permute-start.1 = (bf16[32,3072]{1,0:T(8,128)(2,1)S(1)}, bf16[32,3072]{1,0:T(8,128)(2,1)S(1)}, u32[]{:S(2)}, u32[]{:S(2)}) collective-permute-start(bf16[32,3072]{1,0:T(8,128)(2,1)S(1)} %get-tuple-element.44), channel_id=1, source_target_pairs={{0,2},{1,3},{2,0},{3,1},{4,6},{5,7},{6,4},{7,5},{8,10},{9,11},{10,... | collective-permute-start | bytes 589832 | tf_op jit(solution)/shard_map/ppermute | solution.py:353
  6.2 9.4 %collective-permute-start.2 = (bf16[32,3072]{1,0:T(8,128)(2,1)S(1)}, bf16[32,3072]{1,0:T(8,128)(2,1)S(1)}, u32[]{:S(2)}, u32[]{:S(2)}) collective-permute-start(bf16[32,3072]{1,0:T(8,128)(2,1)S(1)} %get-tuple-element.45), channel_id=1, source_target_pairs={{0,3},{1,2},{2,1},{3,0},{4,7},{5,6},{6,5},{7,4},{8,11},{9,10},{10,... | collective-permute-start | bytes 589832 | tf_op jit(solution)/shard_map/ppermute | solution.py:353
  7.9 12.5 %all-to-all-start = ((s32[8,1,9]{2,1,0:T(1,128)}), s32[8,1,9]{2,1,0:T(1,128)S(1)}, u32[]{:S(2)}, u32[]{:S(2)}) async-start(s32[8,1,9]{2,1,0:T(1,128)} %bitcast.5), calls=%async_computation | async-start | bytes 8192 | tf_op jit(solution)/shard_map/all_to_all | solution.py:444
  22.2 6.3 %collective-permute-start.3 = (bf16[9,32,256]{2,1,0:T(8,128)(2,1)S(1)}, bf16[9,32,256]{2,1,0:T(8,128)(2,1)S(1)}, u32[]{:S(2)}, u32[]{:S(2)}) collective-permute-start(bf16[9,32,256]{2,1,0:T(8,128)(2,1)S(1)} %get-tuple-element.47), channel_id=1, source_target_pairs={{0,4},{4,0},{8,12},{12,8},{16,20},{20,16},{24,28},{28,24},{1,5},{5... | collective-permute-start | bytes 442376 | tf_op jit(solution)/shard_map/ppermute | solution.py:353
  22.8 8.8 %collective-permute-start.4 = (bf16[9,32,256]{2,1,0:T(8,128)(2,1)S(1)}, bf16[9,32,256]{2,1,0:T(8,128)(2,1)S(1)}, u32[]{:S(2)}, u32[]{:S(2)}) collective-permute-start(bf16[9,32,256]{2,1,0:T(8,128)(2,1)S(1)} %get-tuple-element.48), channel_id=1, source_target_pairs={{0,12},{4,8},{8,4},{12,0},{16,28},{20,24},{24,20},{28,16},{1,13},{... | collective-permute-start | bytes 442376 | tf_op jit(solution)/shard_map/ppermute | solution.py:353
  24.3 11.1 %collective-permute-start.6 = (bf16[9,32,256]{2,1,0:T(8,128)(2,1)S(1)}, bf16[9,32,256]{2,1,0:T(8,128)(2,1)S(1)}, u32[]{:S(2)}, u32[]{:S(2)}) collective-permute-start(bf16[9,32,256]{2,1,0:T(8,128)(2,1)S(1)} %get-tuple-element.53), channel_id=1, source_target_pairs={{0,8},{4,12},{8,0},{12,4},{16,24},{20,28},{24,16},{28,20},{1,9},{5... | collective-permute-start | bytes 442376 | tf_op jit(solution)/shard_map/ppermute | solution.py:353
  25.8 13.1 %collective-permute-start.7 = (bf16[9,32,256]{2,1,0:T(8,128)(2,1)S(1)}, bf16[9,32,256]{2,1,0:T(8,128)(2,1)S(1)}, u32[]{:S(2)}, u32[]{:S(2)}) collective-permute-start(bf16[9,32,256]{2,1,0:T(8,128)(2,1)S(1)} %get-tuple-element.54), channel_id=1, source_target_pairs={{0,16},{4,20},{8,24},{12,28},{16,0},{20,4},{24,8},{28,12},{1,17},{... | collective-permute-start | bytes 442376 | tf_op jit(solution)/shard_map/ppermute | solution.py:353
  26.3 5.7 %collective-permute-start.5 = (bf16[9,32,256]{2,1,0:T(8,128)(2,1)S(1)}, bf16[9,32,256]{2,1,0:T(8,128)(2,1)S(1)}, u32[]{:S(2)}, u32[]{:S(2)}) collective-permute-start(bf16[9,32,256]{2,1,0:T(8,128)(2,1)S(1)} %get-tuple-element.49), channel_id=1, source_target_pairs={{0,2},{1,3},{2,0},{3,1},{4,6},{5,7},{6,4},{7,5},{8,10},{9,11},{10,... | collective-permute-start | bytes 442376 | tf_op jit(solution)/shard_map/ppermute | solution.py:353
  28.6 10.3 %collective-permute-start.8 = (bf16[9,32,256]{2,1,0:T(8,128)(2,1)S(1)}, bf16[9,32,256]{2,1,0:T(8,128)(2,1)S(1)}, u32[]{:S(2)}, u32[]{:S(2)}) collective-permute-start(bf16[9,32,256]{2,1,0:T(8,128)(2,1)S(1)} %get-tuple-element.55), channel_id=1, source_target_pairs={{0,24},{4,28},{8,16},{12,20},{16,8},{20,12},{24,0},{28,4},{1,25},{... | collective-permute-start | bytes 442376 | tf_op jit(solution)/shard_map/ppermute | solution.py:353
  32.1 7.6 %collective-permute-start.9 = (bf16[18,32,256]{2,1,0:T(8,128)(2,1)S(1)}, bf16[18,32,256]{2,1,0:T(8,128)(2,1)S(1)}, u32[]{:S(2)}, u32[]{:S(2)}) collective-permute-start(bf16[18,32,256]{2,1,0:T(8,128)(2,1)S(1)} %join.3), channel_id=1, source_target_pairs={{0,2},{1,3},{2,0},{3,1},{4,6},{5,7},{6,4},{7,5},{8,10},{9,11},{10,... | collective-permute-start | bytes 884744 | tf_op jit(solution)/shard_map/ppermute | solution.py:353
  39.7 10.1 %collective-permute-start.11 = (bf16[31,32,256]{2,1,0:T(8,128)(2,1)S(1)}, bf16[31,32,256]{2,1,0:T(8,128)(2,1)S(1)}, u32[]{:S(2)}, u32[]{:S(2)}) collective-permute-start(bf16[31,32,256]{2,1,0:T(8,128)(2,1)S(1)} %join.4), channel_id=1, source_target_pairs={{0,2},{1,3},{2,0},{3,1},{4,6},{5,7},{6,4},{7,5},{8,10},{9,11},{10,... | collective-permute-start | bytes 1523720 | tf_op jit(solution)/shard_map/ppermute | solution.py:353
  41.2 12.5 %collective-permute-start.13 = (bf16[9,32,256]{2,1,0:T(8,128)(2,1)S(1)}, bf16[9,32,256]{2,1,0:T(8,128)(2,1)S(1)}, u32[]{:S(2)}, u32[]{:S(2)}) collective-permute-start(bf16[9,32,256]{2,1,0:T(8,128)(2,1)S(1)} %get-tuple-element.63), channel_id=1, source_target_pairs={{0,20},{4,16},{8,28},{12,24},{16,4},{20,0},{24,12},{28,8},{1,21},{... | collective-permute-start | bytes 442376 | tf_op jit(solution)/shard_map/ppermute | solution.py:353
  43.0 10.8 %collective-permute-start.14 = (bf16[9,32,256]{2,1,0:T(8,128)(2,1)S(1)}, bf16[9,32,256]{2,1,0:T(8,128)(2,1)S(1)}, u32[]{:S(2)}, u32[]{:S(2)}) collective-permute-start(bf16[9,32,256]{2,1,0:T(8,128)(2,1)S(1)} %get-tuple-element.65), channel_id=1, source_target_pairs={{0,28},{4,24},{8,20},{12,16},{16,12},{20,8},{24,4},{28,0},{1,29},{... | collective-permute-start | bytes 442376 | tf_op jit(solution)/shard_map/ppermute | solution.py:353
  49.9 4.9 %collective-permute-start.12 = (bf16[58,32,256]{2,1,0:T(8,128)(2,1)S(1)}, bf16[58,32,256]{2,1,0:T(8,128)(2,1)S(1)}, u32[]{:S(2)}, u32[]{:S(2)}) collective-permute-start(bf16[58,32,256]{2,1,0:T(8,128)(2,1)S(1)} %pad_maximum_fusion.refs_2_), channel_id=1, source_target_pairs={{0,1},{1,0},{2,3},{3,2},{4,5},{5,4},{6,7},{7,6},{8,9},{9,8},{10,11... | collective-permute-start | bytes 2850824 | tf_op jit(solution)/shard_map/ppermute | solution.py:353
  54.1 6.8 %collective-permute-start.15 = (bf16[18,32,256]{2,1,0:T(8,128)(2,1)S(1)}, bf16[18,32,256]{2,1,0:T(8,128)(2,1)S(1)}, u32[]{:S(2)}, u32[]{:S(2)}) collective-permute-start(bf16[18,32,256]{2,1,0:T(8,128)(2,1)S(1)} %join.5), channel_id=1, source_target_pairs={{0,2},{1,3},{2,0},{3,1},{4,6},{5,7},{6,4},{7,5},{8,10},{9,11},{10,... | collective-permute-start | bytes 884744 | tf_op jit(solution)/shard_map/ppermute | solution.py:353
  54.8 10.0 %collective-permute-start.10 = (bf16[54,32,256]{2,1,0:T(8,128)(2,1)S(1)}, bf16[54,32,256]{2,1,0:T(8,128)(2,1)S(1)}, u32[]{:S(2)}, u32[]{:S(2)}) collective-permute-start(bf16[54,32,256]{2,1,0:T(8,128)(2,1)S(1)} %constant_dynamic-update-slice_fusion.refs_0_), channel_id=1, source_target_pairs={{0,1},{1,0},{2,3},{3,2},{4,5},{5,4},{6,7},{7,6},{8,9},{9,8},{10,11... | collective-permute-start | bytes 2654216 | tf_op jit(solution)/shard_map/ppermute | solution.py:353
  54.9 6.1 %collective-permute-start.18 = (bf16[4,32,256]{2,1,0:T(8,128)(2,1)S(1)}, bf16[4,32,256]{2,1,0:T(8,128)(2,1)S(1)}, u32[]{:S(2)}, u32[]{:S(2)}) collective-permute-start(bf16[4,32,256]{2,1,0:T(8,128)(2,1)S(1)} %get-tuple-element.68), channel_id=1, source_target_pairs={{0,12},{4,8},{8,4},{12,0},{16,28},{20,24},{24,20},{28,16},{1,13},{... | collective-permute-start | bytes 196616 | tf_op jit(solution)/shard_map/ppermute | solution.py:353
  58.0 4.3 %collective-permute-start.17 = (bf16[4,32,256]{2,1,0:T(8,128)(2,1)S(1)}, bf16[4,32,256]{2,1,0:T(8,128)(2,1)S(1)}, u32[]{:S(2)}, u32[]{:S(2)}) collective-permute-start(bf16[4,32,256]{2,1,0:T(8,128)(2,1)S(1)} %get-tuple-element.68), channel_id=1, source_target_pairs={{0,8},{4,12},{8,0},{12,4},{16,24},{20,28},{24,16},{28,20},{1,9},{5... | collective-permute-start | bytes 196616 | tf_op jit(solution)/shard_map/ppermute | solution.py:353
  58.0 4.3 %collective-permute-start.16 = (bf16[4,32,256]{2,1,0:T(8,128)(2,1)S(1)}, bf16[4,32,256]{2,1,0:T(8,128)(2,1)S(1)}, u32[]{:S(2)}, u32[]{:S(2)}) collective-permute-start(bf16[4,32,256]{2,1,0:T(8,128)(2,1)S(1)} %get-tuple-element.68), channel_id=1, source_target_pairs={{0,4},{4,0},{8,12},{12,8},{16,20},{20,16},{24,28},{28,24},{1,5},{5... | collective-permute-start | bytes 196616 | tf_op jit(solution)/shard_map/ppermute | solution.py:353
  62.4 7.3 %collective-permute-start.20 = (bf16[4,32,256]{2,1,0:T(8,128)(2,1)S(1)}, bf16[4,32,256]{2,1,0:T(8,128)(2,1)S(1)}, u32[]{:S(2)}, u32[]{:S(2)}) collective-permute-start(bf16[4,32,256]{2,1,0:T(8,128)(2,1)S(1)} %get-tuple-element.69), channel_id=1, source_target_pairs={{0,16},{4,20},{8,24},{12,28},{16,0},{20,4},{24,8},{28,12},{1,17},{... | collective-permute-start | bytes 196616 | tf_op jit(solution)/shard_map/ppermute | solution.py:353
  79.2 12.7 %collective-permute-start.23 = (f32[96,512]{1,0:T(8,128)S(1)}, f32[96,512]{1,0:T(8,128)S(1)}, u32[]{:S(2)}, u32[]{:S(2)}) collective-permute-start(f32[96,512]{1,0:T(8,128)S(1)} %get-tuple-element.80), channel_id=1, source_target_pairs={{0,3},{1,2},{2,1},{3,0},{4,7},{5,6},{6,5},{7,4},{8,11},{9,10},{10,... | collective-permute-start | bytes 589832 | tf_op jit(solution)/shard_map/ppermute | solution.py:353
  80.6 11.3 %collective-permute-start.22 = (f32[96,512]{1,0:T(8,128)S(1)}, f32[96,512]{1,0:T(8,128)S(1)}, u32[]{:S(2)}, u32[]{:S(2)}) collective-permute-start(f32[96,512]{1,0:T(8,128)S(1)} %get-tuple-element.81), channel_id=1, source_target_pairs={{0,2},{1,3},{2,0},{3,1},{4,6},{5,7},{6,4},{7,5},{8,10},{9,11},{10,... | collective-permute-start | bytes 589832 | tf_op jit(solution)/shard_map/ppermute | solution.py:353
  81.1 10.8 %collective-permute-start.21 = (f32[96,512]{1,0:T(8,128)S(1)}, f32[96,512]{1,0:T(8,128)S(1)}, u32[]{:S(2)}, u32[]{:S(2)}) collective-permute-start(f32[96,512]{1,0:T(8,128)S(1)} %get-tuple-element.82), channel_id=1, source_target_pairs={{0,1},{1,0},{2,3},{3,2},{4,5},{5,4},{6,7},{7,6},{8,9},{9,8},{10,11... | collective-permute-start | bytes 589832 | tf_op jit(solution)/shard_map/ppermute | solution.py:353
  (4 other events, 33.4 us)

commit v12 on v11

--- a/solution.py
+++ b/solution.py
@@ -9,7 +9,7 @@
 
 ridge = 0.5
 confidence = 40.0
-UNROLL = 18
+UNROLL = 12
 LIMIT = 24 * 1024 * 1024
 f32 = jnp.float32
 bf16 = jnp.bfloat16
@@ -213,7 +213,7 @@
         add(group - 1, terms)
         return carry
 
-    lax.fori_loop(1, groups, step, 0)
+    lax.fori_loop(1, groups, step, 0, unroll=True)
     add(groups - 1, collect(groups - 1))
 
 
@@ -253,32 +253,25 @@
     part_ref[...] = acc[...].reshape(part_ref.shape)
 
 
-def first_kernel(
+def iterate_kernel(
     slot_ref, user_ref, info_ref, x_ref, part_ref, gram_ref, y, mask, *refs
 ):
-    field_ref, first_ref, gram_out, p_hl, acc, held = refs[-6:]
-    gram = gram_ref[...]
-    for arrived_ref in refs[:-6]:
-        gram = gram + unpack(arrived_ref)
-    gram_out[...] = gram
+    sent_ref, dots_ref, p_hl, acc, held, gram, field_ref, first_ref = refs[-8:]
+    gram[...] = gram_ref[...]
+    for arrived_ref in refs[:-8]:
+        gram[...] += unpack(arrived_ref)
+
+    def image(vector):
+        load(p_hl, vector)
+        sparse(False, slot_ref, user_ref, y, mask, p_hl, acc, held)
+        return confidence * acc[...].reshape(vector.shape) + dense(p_hl, gram, vector)
+
     start = x_ref[...].T
     load(p_hl, start)
-    field = part_ref[...] - dense(p_hl, gram_out, start)
-    field_ref[...] = field
-    load(p_hl, field)
-    sparse(False, slot_ref, user_ref, y, mask, p_hl, acc, held)
-    first = confidence * acc[...].reshape(field.shape) + dense(p_hl, gram_out, field)
-    first_ref[...] = first
-
-
-def second_kernel(
-    slot_ref, user_ref, info_ref, field_ref, first_ref, gram_ref, y, mask, sent_ref, dots_ref, p_hl, acc, held
-):
-    field = field_ref[...]
-    first = first_ref[...]
-    load(p_hl, first)
-    sparse(False, slot_ref, user_ref, y, mask, p_hl, acc, held)
-    second = confidence * acc[...].reshape(field.shape) + dense(p_hl, gram_ref, first)
+    field_ref[...] = part_ref[...] - dense(p_hl, gram, start)
+    first_ref[...] = image(field_ref[...])
+    second = image(first_ref[...])
+    field, first = field_ref[...], first_ref[...]
     for part, vector in enumerate((field, first, second)):
         put(info_ref[1], sent_ref, vector, part)
 
@@ -561,25 +554,22 @@
         8 * 10**9,
     )(*lists, start, mask, *pieces)
     rest = [after(arrived, part)] if direct else []
-    field, first, gram = call(
-        first_kernel,
-        [vector, vector, square],
-        [smem] * 3 + [vmem] * (5 + len(rest)),
-        "first",
-        work,
-        8 * 10**9,
-    )(*lists, start, part, gram, y, mask, *rest)
     sent, dots = call(
-        second_kernel,
+        iterate_kernel,
         [
             jax.ShapeDtypeStruct((n_cols, 3 * col_width, own_users), f32),
             jax.ShapeDtypeStruct((devices, 128), f32),
         ],
-        [smem] * 3 + [vmem] * 5,
-        "second",
-        work,
-        8 * 10**9,
-    )(*lists, field, first, gram, y, mask)
+        [smem] * 3 + [vmem] * (5 + len(rest)),
+        "iterate",
+        work
+        + [
+            pltpu.VMEM((width, width), f32),
+            pltpu.VMEM((own_users, width), f32),
+            pltpu.VMEM((own_users, width), f32),
+        ],
+        16 * 10**9,
+    )(*lists, start, part, gram, y, mask, *rest)
 
     turned = swap(sent)
     dots = lax.all_to_all(dots, ("rows", "cols"), split_axis=0, concat_axis=0, tiled=True)

time: 94.2 us -> 91.8 us (0.975)
  Pallas kernels: 23.8 us -> 21.4 us
    pallas_call x2 -> x1, Pallas kernels: 9.34 us -> 7.38 us  [on_device(): call(iterate_kernel, [jax.ShapeDtypeStruct((n_cols, 3 * col_width, own_us...]
  transfers between devices with their start and end apart: 25 -> 25, of which waited for: 10 -> 10; matrix products, arithmetic and copies ran while one was open for 2% -> 2% of each run, Pallas kernels for 11% -> 10%
where the time goes in v12:
time: 91.8 us; the launch traced here: 91.5 us
  starting transfers between devices  33.9 us (37%)
  Pallas kernels  21.4 us (23%)
  waiting for transfers between devices  20.8 us (23%)
  blocking collectives  10.7 us (12%)
  local copies, waits for them, and re-layouts  1.92 us (2%)
  between operations  1.57 us (2%)
  other arithmetic  1.26 us (1%)
    ppermute x24, starting transfers between devices, flip(): return lax.ppermute(value, axis, [(i, i ^ bit) for i in range(size)])  27.8 us
    ppermute x24, waiting for transfers between devices, flip(): return lax.ppermute(value, axis, [(i, i ^ bit) for i in range(size)])  16 us
    all_to_all x1, blocking collectives, on_device(): lax.all_to_all(dots, ('rows', 'cols'), split_axis=0, concat_axis=0, tiled...  10.7 us
    pallas_call x1, Pallas kernels, on_device(): call(iterate_kernel, [jax.ShapeDtypeStruct((n_cols, 3 * col_width, own_us...  7.38 us
    all_to_all x1, starting transfers between devices, on_device(): lax.all_to_all(requests, 'rows', split_axis=0, concat_axis=0, tiled=True)  6.07 us
    all_to_all x1, waiting for transfers between devices, on_device(): lax.all_to_all(requests, 'rows', split_axis=0, concat_axis=0, tiled=True)  4.76 us
    pallas_call x1, Pallas kernels, on_device(): call(functools.partial(start_kernel, n_cols, slots), [vector, held], [sme...  4.55 us
    pallas_call x1, Pallas kernels, slice_mask(): call(mask_kernel, [strengths], [smem, anywhere], 'mask', [pltpu.Semaphore...  2.22 us
  transfers between devices with their start and end apart: 25, of which 10 were waited for; matrix products, arithmetic and copies ran while one was open for 2% of the time, Pallas kernels for 10%

profile of v12, /device:TPU:0, one launch (start us, length us, event | category | flops | bytes accessed | tf_op | source)
XLA Modules:
  0.0 91.5 jit_solution(8147781466030422458)
XLA Ops:
  1.4 1.7 %prepare.1 = (bf16[32,3072]{1,0:T(8,128)(2,1)S(1)}, bf16[32,3072]{1,0:T(8,128)(2,1)S(1)}, bf16[32,3072]{1,0:T(8,128)(2,1)S(1)}, bf16[32,3072]{1,0:T(8,128)(2,1)S(1)}) custom-call(s32[3]{0:T(128)S(1)} %pad_add_fusion.info_ref, f32[32,2048]{1,0:T(8,128)} %x_ref.1, bf16[32,8192]{1,0:T(8,128)(2,1)} %items_ref.1), custom_call_target="tpu_custom_call" | custom-call | flops 1000000000 | tf_op jit(solution)/shard_map/prepare/pallas_call | solution.py:404
  3.6 2.6 %collective-permute-start.1 = (bf16[32,3072]{1,0:T(8,128)(2,1)S(1)}, bf16[32,3072]{1,0:T(8,128)(2,1)S(1)}, u32[]{:S(2)}, u32[]{:S(2)}) collective-permute-start(bf16[32,3072]{1,0:T(8,128)(2,1)S(1)} %get-tuple-element.41), channel_id=1, source_target_pairs={{0,2},{1,3},{2,0},{3,1},{4,6},{5,7},{6,4},{7,5},{8,10},{9,11},{10,... | collective-permute-start | bytes 589832 | tf_op jit(solution)/shard_map/ppermute | solution.py:346
  7.9 6.1 %all-to-all-start = ((s32[8,1,9]{2,1,0:T(1,128)}), s32[8,1,9]{2,1,0:T(1,128)S(1)}, u32[]{:S(2)}, u32[]{:S(2)}) async-start(s32[8,1,9]{2,1,0:T(1,128)} %bitcast.5), calls=%async_computation | async-start | bytes 8192 | tf_op jit(solution)/shard_map/all_to_all | solution.py:437
  14.0 1.6 %collective-permute-done.2.refs_3_ = bf16[32,3072]{1,0:T(8,128)(2,1)S(1)} collective-permute-done((bf16[32,3072]{1,0:T(8,128)(2,1)S(1)}, bf16[32,3072]{1,0:T(8,128)(2,1)S(1)}, u32[]{:S(2)}, u32[]{:S(2)}) %collective-permute-start.2) | collective-permute-done | bytes 196640 | tf_op jit(solution)/shard_map/ppermute | solution.py:346
  15.6 4.8 %all-to-all-done = s32[8,1,9]{2,1,0:T(1,128)S(1)} async-done(((s32[8,1,9]{2,1,0:T(1,128)}), s32[8,1,9]{2,1,0:T(1,128)S(1)}, u32[]{:S(2)}, u32[]{:S(2)}) %all-to-all-start) | async-done | bytes 320 | tf_op jit(solution)/shard_map/all_to_all | solution.py:437
  22.8 1.5 %collective-permute-start.4 = (bf16[9,32,256]{2,1,0:T(8,128)(2,1)S(1)}, bf16[9,32,256]{2,1,0:T(8,128)(2,1)S(1)}, u32[]{:S(2)}, u32[]{:S(2)}) collective-permute-start(bf16[9,32,256]{2,1,0:T(8,128)(2,1)S(1)} %get-tuple-element.45), channel_id=1, source_target_pairs={{0,12},{4,8},{8,4},{12,0},{16,28},{20,24},{24,20},{28,16},{1,13},{... | collective-permute-start | bytes 442376 | tf_op jit(solution)/shard_map/ppermute | solution.py:346
  24.3 1.5 %collective-permute-start.6 = (bf16[9,32,256]{2,1,0:T(8,128)(2,1)S(1)}, bf16[9,32,256]{2,1,0:T(8,128)(2,1)S(1)}, u32[]{:S(2)}, u32[]{:S(2)}) collective-permute-start(bf16[9,32,256]{2,1,0:T(8,128)(2,1)S(1)} %get-tuple-element.50), channel_id=1, source_target_pairs={{0,8},{4,12},{8,0},{12,4},{16,24},{20,28},{24,16},{28,20},{1,9},{5... | collective-permute-start | bytes 442376 | tf_op jit(solution)/shard_map/ppermute | solution.py:346
  26.3 1.5 %collective-permute-start.5 = (bf16[9,32,256]{2,1,0:T(8,128)(2,1)S(1)}, bf16[9,32,256]{2,1,0:T(8,128)(2,1)S(1)}, u32[]{:S(2)}, u32[]{:S(2)}) collective-permute-start(bf16[9,32,256]{2,1,0:T(8,128)(2,1)S(1)} %get-tuple-element.46), channel_id=1, source_target_pairs={{0,2},{1,3},{2,0},{3,1},{4,6},{5,7},{6,4},{7,5},{8,10},{9,11},{10,... | collective-permute-start | bytes 442376 | tf_op jit(solution)/shard_map/ppermute | solution.py:346
  28.6 1.7 %collective-permute-start.8 = (bf16[9,32,256]{2,1,0:T(8,128)(2,1)S(1)}, bf16[9,32,256]{2,1,0:T(8,128)(2,1)S(1)}, u32[]{:S(2)}, u32[]{:S(2)}) collective-permute-start(bf16[9,32,256]{2,1,0:T(8,128)(2,1)S(1)} %get-tuple-element.52), channel_id=1, source_target_pairs={{0,24},{4,28},{8,16},{12,20},{16,8},{20,12},{24,0},{28,4},{1,25},{... | collective-permute-start | bytes 442376 | tf_op jit(solution)/shard_map/ppermute | solution.py:346
  30.2 1.4 %collective-permute-done.4.refs_1_ = bf16[9,32,256]{2,1,0:T(8,128)(2,1)S(1)} collective-permute-done((bf16[9,32,256]{2,1,0:T(8,128)(2,1)S(1)}, bf16[9,32,256]{2,1,0:T(8,128)(2,1)S(1)}, u32[]{:S(2)}, u32[]{:S(2)}) %collective-permute-start.4) | collective-permute-done | bytes 147488 | tf_op jit(solution)/shard_map/ppermute | solution.py:346
  32.1 1.5 %collective-permute-start.9 = (bf16[18,32,256]{2,1,0:T(8,128)(2,1)S(1)}, bf16[18,32,256]{2,1,0:T(8,128)(2,1)S(1)}, u32[]{:S(2)}, u32[]{:S(2)}) collective-permute-start(bf16[18,32,256]{2,1,0:T(8,128)(2,1)S(1)} %join.3), channel_id=1, source_target_pairs={{0,2},{1,3},{2,0},{3,1},{4,6},{5,7},{6,4},{7,5},{8,10},{9,11},{10,... | collective-permute-start | bytes 884744 | tf_op jit(solution)/shard_map/ppermute | solution.py:346
  35.4 3.5 %collective-permute-done.7.refs_1_ = bf16[9,32,256]{2,1,0:T(8,128)(2,1)S(1)} collective-permute-done((bf16[9,32,256]{2,1,0:T(8,128)(2,1)S(1)}, bf16[9,32,256]{2,1,0:T(8,128)(2,1)S(1)}, u32[]{:S(2)}, u32[]{:S(2)}) %collective-permute-start.7) | collective-permute-done | bytes 147488 | tf_op jit(solution)/shard_map/ppermute | solution.py:346
  39.7 1.6 %collective-permute-start.11 = (bf16[31,32,256]{2,1,0:T(8,128)(2,1)S(1)}, bf16[31,32,256]{2,1,0:T(8,128)(2,1)S(1)}, u32[]{:S(2)}, u32[]{:S(2)}) collective-permute-start(bf16[31,32,256]{2,1,0:T(8,128)(2,1)S(1)} %join.4), channel_id=1, source_target_pairs={{0,2},{1,3},{2,0},{3,1},{4,6},{5,7},{6,4},{7,5},{8,10},{9,11},{10,... | collective-permute-start | bytes 1523720 | tf_op jit(solution)/shard_map/ppermute | solution.py:346
  41.2 1.8 %collective-permute-start.13 = (bf16[9,32,256]{2,1,0:T(8,128)(2,1)S(1)}, bf16[9,32,256]{2,1,0:T(8,128)(2,1)S(1)}, u32[]{:S(2)}, u32[]{:S(2)}) collective-permute-start(bf16[9,32,256]{2,1,0:T(8,128)(2,1)S(1)} %get-tuple-element.60), channel_id=1, source_target_pairs={{0,20},{4,16},{8,28},{12,24},{16,4},{20,0},{24,12},{28,8},{1,21},{... | collective-permute-start | bytes 442376 | tf_op jit(solution)/shard_map/ppermute | solution.py:346
  43.0 3.6 %collective-permute-start.14 = (bf16[9,32,256]{2,1,0:T(8,128)(2,1)S(1)}, bf16[9,32,256]{2,1,0:T(8,128)(2,1)S(1)}, u32[]{:S(2)}, u32[]{:S(2)}) collective-permute-start(bf16[9,32,256]{2,1,0:T(8,128)(2,1)S(1)} %get-tuple-element.62), channel_id=1, source_target_pairs={{0,28},{4,24},{8,20},{12,16},{16,12},{20,8},{24,4},{28,0},{1,29},{... | collective-permute-start | bytes 442376 | tf_op jit(solution)/shard_map/ppermute | solution.py:346
  46.6 2.2 %mask.1 = bf16[72,64,256]{2,1,0:T(8,128)(2,1)S(1)} custom-call(s32[3]{0:T(128)S(1)} %pad_add_fusion.info_ref, bf16[72,256,256]{2,1,0:T(8,128)(2,1)} %mask_hbm.1), custom_call_target="tpu_custom_call" | custom-call | flops 1000000000 | tf_op jit(solution)/shard_map/mask/pallas_call | solution.py:504
  50.0 3.7 %collective-permute-done.13.refs_0_ = bf16[9,32,256]{2,1,0:T(8,128)(2,1)S(1)} collective-permute-done((bf16[9,32,256]{2,1,0:T(8,128)(2,1)S(1)}, bf16[9,32,256]{2,1,0:T(8,128)(2,1)S(1)}, u32[]{:S(2)}, u32[]{:S(2)}) %collective-permute-start.13) | collective-permute-done | bytes 147488 | tf_op jit(solution)/shard_map/ppermute | solution.py:346
  54.9 3.1 %collective-permute-start.18 = (bf16[4,32,256]{2,1,0:T(8,128)(2,1)S(1)}, bf16[4,32,256]{2,1,0:T(8,128)(2,1)S(1)}, u32[]{:S(2)}, u32[]{:S(2)}) collective-permute-start(bf16[4,32,256]{2,1,0:T(8,128)(2,1)S(1)} %get-tuple-element.65), channel_id=1, source_target_pairs={{0,12},{4,8},{8,4},{12,0},{16,28},{20,24},{24,20},{28,16},{1,13},{... | collective-permute-start | bytes 196616 | tf_op jit(solution)/shard_map/ppermute | solution.py:346
  58.6 2.3 %collective-permute-done.15 = bf16[18,32,256]{2,1,0:T(8,128)(2,1)S(1)} collective-permute-done((bf16[18,32,256]{2,1,0:T(8,128)(2,1)S(1)}, bf16[18,32,256]{2,1,0:T(8,128)(2,1)S(1)}, u32[]{:S(2)}, u32[]{:S(2)}) %collective-permute-start.15) | collective-permute-done | bytes 294944 | tf_op jit(solution)/shard_map/ppermute | solution.py:346
  62.4 2.4 %collective-permute-start.20 = (bf16[4,32,256]{2,1,0:T(8,128)(2,1)S(1)}, bf16[4,32,256]{2,1,0:T(8,128)(2,1)S(1)}, u32[]{:S(2)}, u32[]{:S(2)}) collective-permute-start(bf16[4,32,256]{2,1,0:T(8,128)(2,1)S(1)} %get-tuple-element.66), channel_id=1, source_target_pairs={{0,16},{4,20},{8,24},{12,28},{16,0},{20,4},{24,8},{28,12},{1,17},{... | collective-permute-start | bytes 196616 | tf_op jit(solution)/shard_map/ppermute | solution.py:346
  64.8 4.6 %start.1 = (f32[512,128]{1,0:T(8,128)S(1)}, bf16[72,128,256]{2,1,0:T(8,128)(2,1)S(1)}) custom-call(s32[72]{0:T(128)S(1)} %get-tuple-element.83.slot_ref, s32[72]{0:T(128)S(1)} %get-tuple-element.82.user_ref, s32[3]{0:T(128)S(1)} %pad_add_fusion.info_ref, f32[128,512]{1,0:T(8,128)S(1)} %get-tuple-element.49.x_ref, bf16[72,64,256]{2,1,0:T(8,128)(2,1)S(1)} %mask.1, ...), custom_call_target="tpu_custom_call" | custom-call | flops 8000000000 | tf_op jit(solution)/shard_map/start/pallas_call | solution.py:548
  69.4 7.4 %iterate.1 = (f32[4,96,512]{2,1,0:T(8,128)S(1)}, f32[32,128]{1,0:T(8,128)S(1)}) custom-call(s32[72]{0:T(128)S(1)} %get-tuple-element.83.slot_ref, s32[72]{0:T(128)S(1)} %get-tuple-element.82.user_ref, s32[3]{0:T(128)S(1)} %pad_add_fusion.info_ref, f32[128,512]{1,0:T(8,128)S(1)} %get-tuple-element.49.x_ref, f32[512,128]{1,0:T(8,128)S(1)} %get-tuple-element.68.part_ref, ...), custom_call_target="tpu_custom_call" | custom-call | flops 16000000000 | tf_op jit(solution)/shard_map/iterate/pallas_call | solution.py:557
  78.8 10.7 %all_to_all.19 = f32[32,1,128]{2,1,0:T(1,128)S(1)} all-to-all(f32[32,1,128]{2,1,0:T(1,128)S(1)} %bitcast.23), channel_id=1, replica_groups=mesh['rows'=8,'cols'=4] {'rows','cols'}, dimensions={0} | all-to-all | bytes 32768 | tf_op jit(solution)/shard_map/all_to_all | solution.py:575
  89.5 2.0 %finish.1 = (f32[32,2048]{1,0:T(8,128)}, f32[32,2048]{1,0:T(8,128)}) custom-call(s32[3]{0:T(128)S(1)} %pad_add_fusion.info_ref, f32[32,128]{1,0:T(8,128)S(1)} %bitcast.24, f32[32,2048]{1,0:T(8,128)S(1)} %copy-done.1, f32[96,512]{1,0:T(8,128)S(1)} %get-tuple-element.77.refs_0_, f32[96,512]{1,0:T(8,128)S(1)} %collective-permute-done.21.refs_1_, ...), custom_call_target="tpu_custom_call" | custom-call | flops 1000000000 | tf_op jit(solution)/shard_map/finish/pallas_call | solution.py:578
  (64 shorter events, 15.3 us)
Async XLA Ops:
  3.1 10.9 %collective-permute-start = (bf16[32,3072]{1,0:T(8,128)(2,1)S(1)}, bf16[32,3072]{1,0:T(8,128)(2,1)S(1)}, u32[]{:S(2)}, u32[]{:S(2)}) collective-permute-start(bf16[32,3072]{1,0:T(8,128)(2,1)S(1)} %get-tuple-element.40), channel_id=1, source_target_pairs={{0,1},{1,0},{2,3},{3,2},{4,5},{5,4},{6,7},{7,6},{8,9},{9,8},{10,11... | collective-permute-start | bytes 589832 | tf_op jit(solution)/shard_map/ppermute | solution.py:346
  3.6 10.4 %collective-permute-start.1 = (bf16[32,3072]{1,0:T(8,128)(2,1)S(1)}, bf16[32,3072]{1,0:T(8,128)(2,1)S(1)}, u32[]{:S(2)}, u32[]{:S(2)}) collective-permute-start(bf16[32,3072]{1,0:T(8,128)(2,1)S(1)} %get-tuple-element.41), channel_id=1, source_target_pairs={{0,2},{1,3},{2,0},{3,1},{4,6},{5,7},{6,4},{7,5},{8,10},{9,11},{10,... | collective-permute-start | bytes 589832 | tf_op jit(solution)/shard_map/ppermute | solution.py:346
  6.2 9.4 %collective-permute-start.2 = (bf16[32,3072]{1,0:T(8,128)(2,1)S(1)}, bf16[32,3072]{1,0:T(8,128)(2,1)S(1)}, u32[]{:S(2)}, u32[]{:S(2)}) collective-permute-start(bf16[32,3072]{1,0:T(8,128)(2,1)S(1)} %get-tuple-element.42), channel_id=1, source_target_pairs={{0,3},{1,2},{2,1},{3,0},{4,7},{5,6},{6,5},{7,4},{8,11},{9,10},{10,... | collective-permute-start | bytes 589832 | tf_op jit(solution)/shard_map/ppermute | solution.py:346
  7.9 12.5 %all-to-all-start = ((s32[8,1,9]{2,1,0:T(1,128)}), s32[8,1,9]{2,1,0:T(1,128)S(1)}, u32[]{:S(2)}, u32[]{:S(2)}) async-start(s32[8,1,9]{2,1,0:T(1,128)} %bitcast.5), calls=%async_computation | async-start | bytes 8192 | tf_op jit(solution)/shard_map/all_to_all | solution.py:437
  22.2 6.3 %collective-permute-start.3 = (bf16[9,32,256]{2,1,0:T(8,128)(2,1)S(1)}, bf16[9,32,256]{2,1,0:T(8,128)(2,1)S(1)}, u32[]{:S(2)}, u32[]{:S(2)}) collective-permute-start(bf16[9,32,256]{2,1,0:T(8,128)(2,1)S(1)} %get-tuple-element.44), channel_id=1, source_target_pairs={{0,4},{4,0},{8,12},{12,8},{16,20},{20,16},{24,28},{28,24},{1,5},{5... | collective-permute-start | bytes 442376 | tf_op jit(solution)/shard_map/ppermute | solution.py:346
  22.8 8.8 %collective-permute-start.4 = (bf16[9,32,256]{2,1,0:T(8,128)(2,1)S(1)}, bf16[9,32,256]{2,1,0:T(8,128)(2,1)S(1)}, u32[]{:S(2)}, u32[]{:S(2)}) collective-permute-start(bf16[9,32,256]{2,1,0:T(8,128)(2,1)S(1)} %get-tuple-element.45), channel_id=1, source_target_pairs={{0,12},{4,8},{8,4},{12,0},{16,28},{20,24},{24,20},{28,16},{1,13},{... | collective-permute-start | bytes 442376 | tf_op jit(solution)/shard_map/ppermute | solution.py:346
  24.3 11.1 %collective-permute-start.6 = (bf16[9,32,256]{2,1,0:T(8,128)(2,1)S(1)}, bf16[9,32,256]{2,1,0:T(8,128)(2,1)S(1)}, u32[]{:S(2)}, u32[]{:S(2)}) collective-permute-start(bf16[9,32,256]{2,1,0:T(8,128)(2,1)S(1)} %get-tuple-element.50), channel_id=1, source_target_pairs={{0,8},{4,12},{8,0},{12,4},{16,24},{20,28},{24,16},{28,20},{1,9},{5... | collective-permute-start | bytes 442376 | tf_op jit(solution)/shard_map/ppermute | solution.py:346
  25.8 13.1 %collective-permute-start.7 = (bf16[9,32,256]{2,1,0:T(8,128)(2,1)S(1)}, bf16[9,32,256]{2,1,0:T(8,128)(2,1)S(1)}, u32[]{:S(2)}, u32[]{:S(2)}) collective-permute-start(bf16[9,32,256]{2,1,0:T(8,128)(2,1)S(1)} %get-tuple-element.51), channel_id=1, source_target_pairs={{0,16},{4,20},{8,24},{12,28},{16,0},{20,4},{24,8},{28,12},{1,17},{... | collective-permute-start | bytes 442376 | tf_op jit(solution)/shard_map/ppermute | solution.py:346
  26.3 5.7 %collective-permute-start.5 = (bf16[9,32,256]{2,1,0:T(8,128)(2,1)S(1)}, bf16[9,32,256]{2,1,0:T(8,128)(2,1)S(1)}, u32[]{:S(2)}, u32[]{:S(2)}) collective-permute-start(bf16[9,32,256]{2,1,0:T(8,128)(2,1)S(1)} %get-tuple-element.46), channel_id=1, source_target_pairs={{0,2},{1,3},{2,0},{3,1},{4,6},{5,7},{6,4},{7,5},{8,10},{9,11},{10,... | collective-permute-start | bytes 442376 | tf_op jit(solution)/shard_map/ppermute | solution.py:346
  28.6 10.3 %collective-permute-start.8 = (bf16[9,32,256]{2,1,0:T(8,128)(2,1)S(1)}, bf16[9,32,256]{2,1,0:T(8,128)(2,1)S(1)}, u32[]{:S(2)}, u32[]{:S(2)}) collective-permute-start(bf16[9,32,256]{2,1,0:T(8,128)(2,1)S(1)} %get-tuple-element.52), channel_id=1, source_target_pairs={{0,24},{4,28},{8,16},{12,20},{16,8},{20,12},{24,0},{28,4},{1,25},{... | collective-permute-start | bytes 442376 | tf_op jit(solution)/shard_map/ppermute | solution.py:346
  32.1 7.6 %collective-permute-start.9 = (bf16[18,32,256]{2,1,0:T(8,128)(2,1)S(1)}, bf16[18,32,256]{2,1,0:T(8,128)(2,1)S(1)}, u32[]{:S(2)}, u32[]{:S(2)}) collective-permute-start(bf16[18,32,256]{2,1,0:T(8,128)(2,1)S(1)} %join.3), channel_id=1, source_target_pairs={{0,2},{1,3},{2,0},{3,1},{4,6},{5,7},{6,4},{7,5},{8,10},{9,11},{10,... | collective-permute-start | bytes 884744 | tf_op jit(solution)/shard_map/ppermute | solution.py:346
  39.7 10.1 %collective-permute-start.11 = (bf16[31,32,256]{2,1,0:T(8,128)(2,1)S(1)}, bf16[31,32,256]{2,1,0:T(8,128)(2,1)S(1)}, u32[]{:S(2)}, u32[]{:S(2)}) collective-permute-start(bf16[31,32,256]{2,1,0:T(8,128)(2,1)S(1)} %join.4), channel_id=1, source_target_pairs={{0,2},{1,3},{2,0},{3,1},{4,6},{5,7},{6,4},{7,5},{8,10},{9,11},{10,... | collective-permute-start | bytes 1523720 | tf_op jit(solution)/shard_map/ppermute | solution.py:346
  41.2 12.5 %collective-permute-start.13 = (bf16[9,32,256]{2,1,0:T(8,128)(2,1)S(1)}, bf16[9,32,256]{2,1,0:T(8,128)(2,1)S(1)}, u32[]{:S(2)}, u32[]{:S(2)}) collective-permute-start(bf16[9,32,256]{2,1,0:T(8,128)(2,1)S(1)} %get-tuple-element.60), channel_id=1, source_target_pairs={{0,20},{4,16},{8,28},{12,24},{16,4},{20,0},{24,12},{28,8},{1,21},{... | collective-permute-start | bytes 442376 | tf_op jit(solution)/shard_map/ppermute | solution.py:346
  43.0 10.8 %collective-permute-start.14 = (bf16[9,32,256]{2,1,0:T(8,128)(2,1)S(1)}, bf16[9,32,256]{2,1,0:T(8,128)(2,1)S(1)}, u32[]{:S(2)}, u32[]{:S(2)}) collective-permute-start(bf16[9,32,256]{2,1,0:T(8,128)(2,1)S(1)} %get-tuple-element.62), channel_id=1, source_target_pairs={{0,28},{4,24},{8,20},{12,16},{16,12},{20,8},{24,4},{28,0},{1,29},{... | collective-permute-start | bytes 442376 | tf_op jit(solution)/shard_map/ppermute | solution.py:346
  49.9 4.9 %collective-permute-start.12 = (bf16[58,32,256]{2,1,0:T(8,128)(2,1)S(1)}, bf16[58,32,256]{2,1,0:T(8,128)(2,1)S(1)}, u32[]{:S(2)}, u32[]{:S(2)}) collective-permute-start(bf16[58,32,256]{2,1,0:T(8,128)(2,1)S(1)} %pad_maximum_fusion.refs_2_), channel_id=1, source_target_pairs={{0,1},{1,0},{2,3},{3,2},{4,5},{5,4},{6,7},{7,6},{8,9},{9,8},{10,11... | collective-permute-start | bytes 2850824 | tf_op jit(solution)/shard_map/ppermute | solution.py:346
  54.1 6.8 %collective-permute-start.15 = (bf16[18,32,256]{2,1,0:T(8,128)(2,1)S(1)}, bf16[18,32,256]{2,1,0:T(8,128)(2,1)S(1)}, u32[]{:S(2)}, u32[]{:S(2)}) collective-permute-start(bf16[18,32,256]{2,1,0:T(8,128)(2,1)S(1)} %join.5), channel_id=1, source_target_pairs={{0,2},{1,3},{2,0},{3,1},{4,6},{5,7},{6,4},{7,5},{8,10},{9,11},{10,... | collective-permute-start | bytes 884744 | tf_op jit(solution)/shard_map/ppermute | solution.py:346
  54.8 10.0 %collective-permute-start.10 = (bf16[54,32,256]{2,1,0:T(8,128)(2,1)S(1)}, bf16[54,32,256]{2,1,0:T(8,128)(2,1)S(1)}, u32[]{:S(2)}, u32[]{:S(2)}) collective-permute-start(bf16[54,32,256]{2,1,0:T(8,128)(2,1)S(1)} %constant_dynamic-update-slice_fusion.refs_0_), channel_id=1, source_target_pairs={{0,1},{1,0},{2,3},{3,2},{4,5},{5,4},{6,7},{7,6},{8,9},{9,8},{10,11... | collective-permute-start | bytes 2654216 | tf_op jit(solution)/shard_map/ppermute | solution.py:346
  54.9 6.1 %collective-permute-start.18 = (bf16[4,32,256]{2,1,0:T(8,128)(2,1)S(1)}, bf16[4,32,256]{2,1,0:T(8,128)(2,1)S(1)}, u32[]{:S(2)}, u32[]{:S(2)}) collective-permute-start(bf16[4,32,256]{2,1,0:T(8,128)(2,1)S(1)} %get-tuple-element.65), channel_id=1, source_target_pairs={{0,12},{4,8},{8,4},{12,0},{16,28},{20,24},{24,20},{28,16},{1,13},{... | collective-permute-start | bytes 196616 | tf_op jit(solution)/shard_map/ppermute | solution.py:346
  58.0 4.3 %collective-permute-start.17 = (bf16[4,32,256]{2,1,0:T(8,128)(2,1)S(1)}, bf16[4,32,256]{2,1,0:T(8,128)(2,1)S(1)}, u32[]{:S(2)}, u32[]{:S(2)}) collective-permute-start(bf16[4,32,256]{2,1,0:T(8,128)(2,1)S(1)} %get-tuple-element.65), channel_id=1, source_target_pairs={{0,8},{4,12},{8,0},{12,4},{16,24},{20,28},{24,16},{28,20},{1,9},{5... | collective-permute-start | bytes 196616 | tf_op jit(solution)/shard_map/ppermute | solution.py:346
  58.0 4.3 %collective-permute-start.16 = (bf16[4,32,256]{2,1,0:T(8,128)(2,1)S(1)}, bf16[4,32,256]{2,1,0:T(8,128)(2,1)S(1)}, u32[]{:S(2)}, u32[]{:S(2)}) collective-permute-start(bf16[4,32,256]{2,1,0:T(8,128)(2,1)S(1)} %get-tuple-element.65), channel_id=1, source_target_pairs={{0,4},{4,0},{8,12},{12,8},{16,20},{20,16},{24,28},{28,24},{1,5},{5... | collective-permute-start | bytes 196616 | tf_op jit(solution)/shard_map/ppermute | solution.py:346
  62.4 6.9 %collective-permute-start.20 = (bf16[4,32,256]{2,1,0:T(8,128)(2,1)S(1)}, bf16[4,32,256]{2,1,0:T(8,128)(2,1)S(1)}, u32[]{:S(2)}, u32[]{:S(2)}) collective-permute-start(bf16[4,32,256]{2,1,0:T(8,128)(2,1)S(1)} %get-tuple-element.66), channel_id=1, source_target_pairs={{0,16},{4,20},{8,24},{12,28},{16,0},{20,4},{24,8},{28,12},{1,17},{... | collective-permute-start | bytes 196616 | tf_op jit(solution)/shard_map/ppermute | solution.py:346
  76.8 12.7 %collective-permute-start.23 = (f32[96,512]{1,0:T(8,128)S(1)}, f32[96,512]{1,0:T(8,128)S(1)}, u32[]{:S(2)}, u32[]{:S(2)}) collective-permute-start(f32[96,512]{1,0:T(8,128)S(1)} %get-tuple-element.74), channel_id=1, source_target_pairs={{0,3},{1,2},{2,1},{3,0},{4,7},{5,6},{6,5},{7,4},{8,11},{9,10},{10,... | collective-permute-start | bytes 589832 | tf_op jit(solution)/shard_map/ppermute | solution.py:346
  78.2 11.3 %collective-permute-start.22 = (f32[96,512]{1,0:T(8,128)S(1)}, f32[96,512]{1,0:T(8,128)S(1)}, u32[]{:S(2)}, u32[]{:S(2)}) collective-permute-start(f32[96,512]{1,0:T(8,128)S(1)} %get-tuple-element.75), channel_id=1, source_target_pairs={{0,2},{1,3},{2,0},{3,1},{4,6},{5,7},{6,4},{7,5},{8,10},{9,11},{10,... | collective-permute-start | bytes 589832 | tf_op jit(solution)/shard_map/ppermute | solution.py:346
  78.7 10.8 %collective-permute-start.21 = (f32[96,512]{1,0:T(8,128)S(1)}, f32[96,512]{1,0:T(8,128)S(1)}, u32[]{:S(2)}, u32[]{:S(2)}) collective-permute-start(f32[96,512]{1,0:T(8,128)S(1)} %get-tuple-element.76), channel_id=1, source_target_pairs={{0,1},{1,0},{2,3},{3,2},{4,5},{5,4},{6,7},{7,6},{8,9},{9,8},{10,11... | collective-permute-start | bytes 589832 | tf_op jit(solution)/shard_map/ppermute | solution.py:346
  (4 other events, 36.1 us)

commit v13 on v12

--- a/solution.py
+++ b/solution.py
@@ -9,7 +9,7 @@
 
 ridge = 0.5
 confidence = 40.0
-UNROLL = 12
+UNROLL = 8
 LIMIT = 24 * 1024 * 1024
 f32 = jnp.float32
 bf16 = jnp.bfloat16
@@ -73,7 +73,11 @@
     lax.fori_loop(info_ref[0], tiles, clear, 0)
 
 
-def pick_kernel(direct, info_ref, wanted_ref, items_ref, *out_refs):
+def pick_kernel(direct, info_ref, wanted_ref, items_hbm, *refs):
+    out_refs, (items_ref, sem) = refs[:-2], refs[-2:]
+    copy = pltpu.make_async_copy(items_hbm, items_ref, sem)
+    copy.start()
+    copy.wait()
     capacity = wanted_ref.shape[1]
     side = out_refs[0].shape[2]
     for o, out_ref in enumerate(out_refs):
@@ -450,10 +454,15 @@
         [jax.ShapeDtypeStruct((capacity, col_width, side), bf16)] * row_devs
         if direct
         else [jax.ShapeDtypeStruct((row_devs * capacity, col_width, side), bf16)],
-        [smem, smem, vmem],
+        [smem, smem, anywhere],
         "pick",
-        flops=10**9,
-    )(after(info, *shared), wanted, item_factors)
+        [pltpu.VMEM(item_factors.shape, bf16), pltpu.SemaphoreType.DMA],
+        10**9,
+    )(
+        after(info, *shared),
+        wanted,
+        pltpu.with_memory_space_constraint(item_factors, pltpu.HBM),
+    )
 
     def join(*arrays):
         return jnp.concatenate(arrays, axis=0)

time: 91.8 us -> 91.7 us (level)
  local copies, waits for them, and re-layouts: 1.92 us -> 0.87 us
  Pallas kernels: 21.4 us -> 22.4 us
    unnamed x9 -> x7, local copies, waits for them, and re-layouts: 1.1 us -> 0.06 us
    pallas_call x1, Pallas kernels: 0.77 us -> 1.8 us  [on_device(): call(functools.partial(pick_kernel, direct), [jax.ShapeDtypeStruct((capac...]
  transfers between devices with their start and end apart: 25 -> 25, of which waited for: 10 -> 10; matrix products, arithmetic and copies ran while one was open for 2% -> 2% of each run, Pallas kernels for 10% -> 11%
where the time goes in v13:
time: 91.7 us; the launch traced here: 91.4 us
  starting transfers between devices  33.9 us (37%)
  Pallas kernels  22.4 us (24%)
  waiting for transfers between devices  20.8 us (23%)
  blocking collectives  10.7 us (12%)
  between operations  1.57 us (2%)
  other arithmetic  1.26 us (1%)
    ppermute x24, starting transfers between devices, flip(): return lax.ppermute(value, axis, [(i, i ^ bit) for i in range(size)])  27.8 us
    ppermute x24, waiting for transfers between devices, flip(): return lax.ppermute(value, axis, [(i, i ^ bit) for i in range(size)])  16 us
    all_to_all x1, blocking collectives, on_device(): lax.all_to_all(dots, ('rows', 'cols'), split_axis=0, concat_axis=0, tiled...  10.7 us
    pallas_call x1, Pallas kernels, on_device(): call(iterate_kernel, [jax.ShapeDtypeStruct((n_cols, 3 * col_width, own_us...  7.19 us
    all_to_all x1, starting transfers between devices, on_device(): lax.all_to_all(requests, 'rows', split_axis=0, concat_axis=0, tiled=True)  6.07 us
    all_to_all x1, waiting for transfers between devices, on_device(): lax.all_to_all(requests, 'rows', split_axis=0, concat_axis=0, tiled=True)  4.76 us
    pallas_call x1, Pallas kernels, on_device(): call(functools.partial(start_kernel, n_cols, slots), [vector, held], [sme...  4.66 us
    pallas_call x1, Pallas kernels, slice_mask(): call(mask_kernel, [strengths], [smem, anywhere], 'mask', [pltpu.Semaphore...  2.23 us
  transfers between devices with their start and end apart: 25, of which 10 were waited for; matrix products, arithmetic and copies ran while one was open for 2% of the time, Pallas kernels for 11%

profile of v13, /device:TPU:0, one launch (start us, length us, event | category | flops | bytes accessed | tf_op | source)
XLA Modules:
  0.0 91.4 jit_solution(11748993208565078622)
XLA Ops:
  1.4 1.7 %prepare.1 = (bf16[32,3072]{1,0:T(8,128)(2,1)S(1)}, bf16[32,3072]{1,0:T(8,128)(2,1)S(1)}, bf16[32,3072]{1,0:T(8,128)(2,1)S(1)}, bf16[32,3072]{1,0:T(8,128)(2,1)S(1)}) custom-call(s32[3]{0:T(128)S(1)} %pad_add_fusion.info_ref, f32[32,2048]{1,0:T(8,128)} %x_ref.1, bf16[32,8192]{1,0:T(8,128)(2,1)} %items_hbm.3), custom_call_target="tpu_custom_call" | custom-call | flops 1000000000 | tf_op jit(solution)/shard_map/prepare/pallas_call | solution.py:408
  3.6 2.6 %collective-permute-start.1 = (bf16[32,3072]{1,0:T(8,128)(2,1)S(1)}, bf16[32,3072]{1,0:T(8,128)(2,1)S(1)}, u32[]{:S(2)}, u32[]{:S(2)}) collective-permute-start(bf16[32,3072]{1,0:T(8,128)(2,1)S(1)} %get-tuple-element.41), channel_id=1, source_target_pairs={{0,2},{1,3},{2,0},{3,1},{4,6},{5,7},{6,4},{7,5},{8,10},{9,11},{10,... | collective-permute-start | bytes 589832 | tf_op jit(solution)/shard_map/ppermute | solution.py:350
  7.9 6.1 %all-to-all-start = ((s32[8,1,9]{2,1,0:T(1,128)}), s32[8,1,9]{2,1,0:T(1,128)S(1)}, u32[]{:S(2)}, u32[]{:S(2)}) async-start(s32[8,1,9]{2,1,0:T(1,128)} %bitcast.5), calls=%async_computation | async-start | bytes 8192 | tf_op jit(solution)/shard_map/all_to_all | solution.py:441
  14.0 1.6 %collective-permute-done.2.refs_3_ = bf16[32,3072]{1,0:T(8,128)(2,1)S(1)} collective-permute-done((bf16[32,3072]{1,0:T(8,128)(2,1)S(1)}, bf16[32,3072]{1,0:T(8,128)(2,1)S(1)}, u32[]{:S(2)}, u32[]{:S(2)}) %collective-permute-start.2) | collective-permute-done | bytes 196640 | tf_op jit(solution)/shard_map/ppermute | solution.py:350
  15.6 4.8 %all-to-all-done = s32[8,1,9]{2,1,0:T(1,128)S(1)} async-done(((s32[8,1,9]{2,1,0:T(1,128)}), s32[8,1,9]{2,1,0:T(1,128)S(1)}, u32[]{:S(2)}, u32[]{:S(2)}) %all-to-all-start) | async-done | bytes 320 | tf_op jit(solution)/shard_map/all_to_all | solution.py:441
  20.4 1.8 %pick.1 = (bf16[9,32,256]{2,1,0:T(8,128)(2,1)S(1)}, bf16[9,32,256]{2,1,0:T(8,128)(2,1)S(1)}, bf16[9,32,256]{2,1,0:T(8,128)(2,1)S(1)}, bf16[9,32,256]{2,1,0:T(8,1...) custom-call(s32[3]{0:T(128)S(1)} %pad_add_fusion.info_ref, ...), custom_call_target="tpu_custom_call" | custom-call | flops 1000000000 | tf_op jit(solution)/shard_map/pick/pallas_call | solution.py:452
  22.8 1.4 %collective-permute-start.4 = (bf16[9,32,256]{2,1,0:T(8,128)(2,1)S(1)}, bf16[9,32,256]{2,1,0:T(8,128)(2,1)S(1)}, u32[]{:S(2)}, u32[]{:S(2)}) collective-permute-start(bf16[9,32,256]{2,1,0:T(8,128)(2,1)S(1)} %get-tuple-element.45), channel_id=1, source_target_pairs={{0,12},{4,8},{8,4},{12,0},{16,28},{20,24},{24,20},{28,16},{1,13},{... | collective-permute-start | bytes 442376 | tf_op jit(solution)/shard_map/ppermute | solution.py:350
  24.3 1.5 %collective-permute-start.6 = (bf16[9,32,256]{2,1,0:T(8,128)(2,1)S(1)}, bf16[9,32,256]{2,1,0:T(8,128)(2,1)S(1)}, u32[]{:S(2)}, u32[]{:S(2)}) collective-permute-start(bf16[9,32,256]{2,1,0:T(8,128)(2,1)S(1)} %get-tuple-element.50), channel_id=1, source_target_pairs={{0,8},{4,12},{8,0},{12,4},{16,24},{20,28},{24,16},{28,20},{1,9},{5... | collective-permute-start | bytes 442376 | tf_op jit(solution)/shard_map/ppermute | solution.py:350
  26.3 1.5 %collective-permute-start.5 = (bf16[9,32,256]{2,1,0:T(8,128)(2,1)S(1)}, bf16[9,32,256]{2,1,0:T(8,128)(2,1)S(1)}, u32[]{:S(2)}, u32[]{:S(2)}) collective-permute-start(bf16[9,32,256]{2,1,0:T(8,128)(2,1)S(1)} %get-tuple-element.46), channel_id=1, source_target_pairs={{0,2},{1,3},{2,0},{3,1},{4,6},{5,7},{6,4},{7,5},{8,10},{9,11},{10,... | collective-permute-start | bytes 442376 | tf_op jit(solution)/shard_map/ppermute | solution.py:350
  28.5 1.7 %collective-permute-start.8 = (bf16[9,32,256]{2,1,0:T(8,128)(2,1)S(1)}, bf16[9,32,256]{2,1,0:T(8,128)(2,1)S(1)}, u32[]{:S(2)}, u32[]{:S(2)}) collective-permute-start(bf16[9,32,256]{2,1,0:T(8,128)(2,1)S(1)} %get-tuple-element.52), channel_id=1, source_target_pairs={{0,24},{4,28},{8,16},{12,20},{16,8},{20,12},{24,0},{28,4},{1,25},{... | collective-permute-start | bytes 442376 | tf_op jit(solution)/shard_map/ppermute | solution.py:350
  32.1 1.5 %collective-permute-start.9 = (bf16[18,32,256]{2,1,0:T(8,128)(2,1)S(1)}, bf16[18,32,256]{2,1,0:T(8,128)(2,1)S(1)}, u32[]{:S(2)}, u32[]{:S(2)}) collective-permute-start(bf16[18,32,256]{2,1,0:T(8,128)(2,1)S(1)} %join.3), channel_id=1, source_target_pairs={{0,2},{1,3},{2,0},{3,1},{4,6},{5,7},{6,4},{7,5},{8,10},{9,11},{10,... | collective-permute-start | bytes 884744 | tf_op jit(solution)/shard_map/ppermute | solution.py:350
  35.4 3.5 %collective-permute-done.7.refs_1_ = bf16[9,32,256]{2,1,0:T(8,128)(2,1)S(1)} collective-permute-done((bf16[9,32,256]{2,1,0:T(8,128)(2,1)S(1)}, bf16[9,32,256]{2,1,0:T(8,128)(2,1)S(1)}, u32[]{:S(2)}, u32[]{:S(2)}) %collective-permute-start.7) | collective-permute-done | bytes 147488 | tf_op jit(solution)/shard_map/ppermute | solution.py:350
  39.7 1.6 %collective-permute-start.11 = (bf16[31,32,256]{2,1,0:T(8,128)(2,1)S(1)}, bf16[31,32,256]{2,1,0:T(8,128)(2,1)S(1)}, u32[]{:S(2)}, u32[]{:S(2)}) collective-permute-start(bf16[31,32,256]{2,1,0:T(8,128)(2,1)S(1)} %join.4), channel_id=1, source_target_pairs={{0,2},{1,3},{2,0},{3,1},{4,6},{5,7},{6,4},{7,5},{8,10},{9,11},{10,... | collective-permute-start | bytes 1523720 | tf_op jit(solution)/shard_map/ppermute | solution.py:350
  41.2 1.8 %collective-permute-start.13 = (bf16[9,32,256]{2,1,0:T(8,128)(2,1)S(1)}, bf16[9,32,256]{2,1,0:T(8,128)(2,1)S(1)}, u32[]{:S(2)}, u32[]{:S(2)}) collective-permute-start(bf16[9,32,256]{2,1,0:T(8,128)(2,1)S(1)} %get-tuple-element.60), channel_id=1, source_target_pairs={{0,20},{4,16},{8,28},{12,24},{16,4},{20,0},{24,12},{28,8},{1,21},{... | collective-permute-start | bytes 442376 | tf_op jit(solution)/shard_map/ppermute | solution.py:350
  43.0 3.6 %collective-permute-start.14 = (bf16[9,32,256]{2,1,0:T(8,128)(2,1)S(1)}, bf16[9,32,256]{2,1,0:T(8,128)(2,1)S(1)}, u32[]{:S(2)}, u32[]{:S(2)}) collective-permute-start(bf16[9,32,256]{2,1,0:T(8,128)(2,1)S(1)} %get-tuple-element.62), channel_id=1, source_target_pairs={{0,28},{4,24},{8,20},{12,16},{16,12},{20,8},{24,4},{28,0},{1,29},{... | collective-permute-start | bytes 442376 | tf_op jit(solution)/shard_map/ppermute | solution.py:350
  46.6 2.2 %mask.1 = bf16[72,64,256]{2,1,0:T(8,128)(2,1)S(1)} custom-call(s32[3]{0:T(128)S(1)} %pad_add_fusion.info_ref, bf16[72,256,256]{2,1,0:T(8,128)(2,1)} %mask_hbm.1), custom_call_target="tpu_custom_call" | custom-call | flops 1000000000 | tf_op jit(solution)/shard_map/mask/pallas_call | solution.py:513
  50.0 3.7 %collective-permute-done.13.refs_0_ = bf16[9,32,256]{2,1,0:T(8,128)(2,1)S(1)} collective-permute-done((bf16[9,32,256]{2,1,0:T(8,128)(2,1)S(1)}, bf16[9,32,256]{2,1,0:T(8,128)(2,1)S(1)}, u32[]{:S(2)}, u32[]{:S(2)}) %collective-permute-start.13) | collective-permute-done | bytes 147488 | tf_op jit(solution)/shard_map/ppermute | solution.py:350
  54.9 3.1 %collective-permute-start.18 = (bf16[4,32,256]{2,1,0:T(8,128)(2,1)S(1)}, bf16[4,32,256]{2,1,0:T(8,128)(2,1)S(1)}, u32[]{:S(2)}, u32[]{:S(2)}) collective-permute-start(bf16[4,32,256]{2,1,0:T(8,128)(2,1)S(1)} %get-tuple-element.65), channel_id=1, source_target_pairs={{0,12},{4,8},{8,4},{12,0},{16,28},{20,24},{24,20},{28,16},{1,13},{... | collective-permute-start | bytes 196616 | tf_op jit(solution)/shard_map/ppermute | solution.py:350
  58.6 2.3 %collective-permute-done.15 = bf16[18,32,256]{2,1,0:T(8,128)(2,1)S(1)} collective-permute-done((bf16[18,32,256]{2,1,0:T(8,128)(2,1)S(1)}, bf16[18,32,256]{2,1,0:T(8,128)(2,1)S(1)}, u32[]{:S(2)}, u32[]{:S(2)}) %collective-permute-start.15) | collective-permute-done | bytes 294944 | tf_op jit(solution)/shard_map/ppermute | solution.py:350
  62.4 2.4 %collective-permute-start.20 = (bf16[4,32,256]{2,1,0:T(8,128)(2,1)S(1)}, bf16[4,32,256]{2,1,0:T(8,128)(2,1)S(1)}, u32[]{:S(2)}, u32[]{:S(2)}) collective-permute-start(bf16[4,32,256]{2,1,0:T(8,128)(2,1)S(1)} %get-tuple-element.66), channel_id=1, source_target_pairs={{0,16},{4,20},{8,24},{12,28},{16,0},{20,4},{24,8},{28,12},{1,17},{... | collective-permute-start | bytes 196616 | tf_op jit(solution)/shard_map/ppermute | solution.py:350
  64.8 4.7 %start.1 = (f32[512,128]{1,0:T(8,128)S(1)}, bf16[72,128,256]{2,1,0:T(8,128)(2,1)S(1)}) custom-call(s32[72]{0:T(128)S(1)} %get-tuple-element.83.slot_ref, s32[72]{0:T(128)S(1)} %get-tuple-element.82.user_ref, s32[3]{0:T(128)S(1)} %pad_add_fusion.info_ref, f32[128,512]{1,0:T(8,128)S(1)} %get-tuple-element.49.x_ref, bf16[72,64,256]{2,1,0:T(8,128)(2,1)S(1)} %mask.1, ...), custom_call_target="tpu_custom_call" | custom-call | flops 8000000000 | tf_op jit(solution)/shard_map/start/pallas_call | solution.py:557
  69.5 7.2 %iterate.1 = (f32[4,96,512]{2,1,0:T(8,128)S(1)}, f32[32,128]{1,0:T(8,128)S(1)}) custom-call(s32[72]{0:T(128)S(1)} %get-tuple-element.83.slot_ref, s32[72]{0:T(128)S(1)} %get-tuple-element.82.user_ref, s32[3]{0:T(128)S(1)} %pad_add_fusion.info_ref, f32[128,512]{1,0:T(8,128)S(1)} %get-tuple-element.49.x_ref, f32[512,128]{1,0:T(8,128)S(1)} %get-tuple-element.68.part_ref, ...), custom_call_target="tpu_custom_call" | custom-call | flops 16000000000 | tf_op jit(solution)/shard_map/iterate/pallas_call | solution.py:566
  78.7 10.7 %all_to_all.19 = f32[32,1,128]{2,1,0:T(1,128)S(1)} all-to-all(f32[32,1,128]{2,1,0:T(1,128)S(1)} %bitcast.23), channel_id=1, replica_groups=mesh['rows'=8,'cols'=4] {'rows','cols'}, dimensions={0} | all-to-all | bytes 32768 | tf_op jit(solution)/shard_map/all_to_all | solution.py:584
  89.4 2.0 %finish.1 = (f32[32,2048]{1,0:T(8,128)}, f32[32,2048]{1,0:T(8,128)}) custom-call(s32[3]{0:T(128)S(1)} %pad_add_fusion.info_ref, f32[32,128]{1,0:T(8,128)S(1)} %bitcast.24, f32[32,2048]{1,0:T(8,128)S(1)} %copy-done, f32[96,512]{1,0:T(8,128)S(1)} %get-tuple-element.77.refs_0_, f32[96,512]{1,0:T(8,128)S(1)} %collective-permute-done.21.refs_1_, ...), custom_call_target="tpu_custom_call" | custom-call | flops 1000000000 | tf_op jit(solution)/shard_map/finish/pallas_call | solution.py:587
  (62 shorter events, 14.9 us)
Async XLA Ops:
  3.1 10.9 %collective-permute-start = (bf16[32,3072]{1,0:T(8,128)(2,1)S(1)}, bf16[32,3072]{1,0:T(8,128)(2,1)S(1)}, u32[]{:S(2)}, u32[]{:S(2)}) collective-permute-start(bf16[32,3072]{1,0:T(8,128)(2,1)S(1)} %get-tuple-element.40), channel_id=1, source_target_pairs={{0,1},{1,0},{2,3},{3,2},{4,5},{5,4},{6,7},{7,6},{8,9},{9,8},{10,11... | collective-permute-start | bytes 589832 | tf_op jit(solution)/shard_map/ppermute | solution.py:350
  3.6 10.4 %collective-permute-start.1 = (bf16[32,3072]{1,0:T(8,128)(2,1)S(1)}, bf16[32,3072]{1,0:T(8,128)(2,1)S(1)}, u32[]{:S(2)}, u32[]{:S(2)}) collective-permute-start(bf16[32,3072]{1,0:T(8,128)(2,1)S(1)} %get-tuple-element.41), channel_id=1, source_target_pairs={{0,2},{1,3},{2,0},{3,1},{4,6},{5,7},{6,4},{7,5},{8,10},{9,11},{10,... | collective-permute-start | bytes 589832 | tf_op jit(solution)/shard_map/ppermute | solution.py:350
  6.2 9.4 %collective-permute-start.2 = (bf16[32,3072]{1,0:T(8,128)(2,1)S(1)}, bf16[32,3072]{1,0:T(8,128)(2,1)S(1)}, u32[]{:S(2)}, u32[]{:S(2)}) collective-permute-start(bf16[32,3072]{1,0:T(8,128)(2,1)S(1)} %get-tuple-element.42), channel_id=1, source_target_pairs={{0,3},{1,2},{2,1},{3,0},{4,7},{5,6},{6,5},{7,4},{8,11},{9,10},{10,... | collective-permute-start | bytes 589832 | tf_op jit(solution)/shard_map/ppermute | solution.py:350
  7.9 12.5 %all-to-all-start = ((s32[8,1,9]{2,1,0:T(1,128)}), s32[8,1,9]{2,1,0:T(1,128)S(1)}, u32[]{:S(2)}, u32[]{:S(2)}) async-start(s32[8,1,9]{2,1,0:T(1,128)} %bitcast.5), calls=%async_computation | async-start | bytes 8192 | tf_op jit(solution)/shard_map/all_to_all | solution.py:441
  22.2 6.3 %collective-permute-start.3 = (bf16[9,32,256]{2,1,0:T(8,128)(2,1)S(1)}, bf16[9,32,256]{2,1,0:T(8,128)(2,1)S(1)}, u32[]{:S(2)}, u32[]{:S(2)}) collective-permute-start(bf16[9,32,256]{2,1,0:T(8,128)(2,1)S(1)} %get-tuple-element.44), channel_id=1, source_target_pairs={{0,4},{4,0},{8,12},{12,8},{16,20},{20,16},{24,28},{28,24},{1,5},{5... | collective-permute-start | bytes 442376 | tf_op jit(solution)/shard_map/ppermute | solution.py:350
  22.8 8.8 %collective-permute-start.4 = (bf16[9,32,256]{2,1,0:T(8,128)(2,1)S(1)}, bf16[9,32,256]{2,1,0:T(8,128)(2,1)S(1)}, u32[]{:S(2)}, u32[]{:S(2)}) collective-permute-start(bf16[9,32,256]{2,1,0:T(8,128)(2,1)S(1)} %get-tuple-element.45), channel_id=1, source_target_pairs={{0,12},{4,8},{8,4},{12,0},{16,28},{20,24},{24,20},{28,16},{1,13},{... | collective-permute-start | bytes 442376 | tf_op jit(solution)/shard_map/ppermute | solution.py:350
  24.3 11.1 %collective-permute-start.6 = (bf16[9,32,256]{2,1,0:T(8,128)(2,1)S(1)}, bf16[9,32,256]{2,1,0:T(8,128)(2,1)S(1)}, u32[]{:S(2)}, u32[]{:S(2)}) collective-permute-start(bf16[9,32,256]{2,1,0:T(8,128)(2,1)S(1)} %get-tuple-element.50), channel_id=1, source_target_pairs={{0,8},{4,12},{8,0},{12,4},{16,24},{20,28},{24,16},{28,20},{1,9},{5... | collective-permute-start | bytes 442376 | tf_op jit(solution)/shard_map/ppermute | solution.py:350
  25.8 13.1 %collective-permute-start.7 = (bf16[9,32,256]{2,1,0:T(8,128)(2,1)S(1)}, bf16[9,32,256]{2,1,0:T(8,128)(2,1)S(1)}, u32[]{:S(2)}, u32[]{:S(2)}) collective-permute-start(bf16[9,32,256]{2,1,0:T(8,128)(2,1)S(1)} %get-tuple-element.51), channel_id=1, source_target_pairs={{0,16},{4,20},{8,24},{12,28},{16,0},{20,4},{24,8},{28,12},{1,17},{... | collective-permute-start | bytes 442376 | tf_op jit(solution)/shard_map/ppermute | solution.py:350
  26.3 5.7 %collective-permute-start.5 = (bf16[9,32,256]{2,1,0:T(8,128)(2,1)S(1)}, bf16[9,32,256]{2,1,0:T(8,128)(2,1)S(1)}, u32[]{:S(2)}, u32[]{:S(2)}) collective-permute-start(bf16[9,32,256]{2,1,0:T(8,128)(2,1)S(1)} %get-tuple-element.46), channel_id=1, source_target_pairs={{0,2},{1,3},{2,0},{3,1},{4,6},{5,7},{6,4},{7,5},{8,10},{9,11},{10,... | collective-permute-start | bytes 442376 | tf_op jit(solution)/shard_map/ppermute | solution.py:350
  28.5 10.3 %collective-permute-start.8 = (bf16[9,32,256]{2,1,0:T(8,128)(2,1)S(1)}, bf16[9,32,256]{2,1,0:T(8,128)(2,1)S(1)}, u32[]{:S(2)}, u32[]{:S(2)}) collective-permute-start(bf16[9,32,256]{2,1,0:T(8,128)(2,1)S(1)} %get-tuple-element.52), channel_id=1, source_target_pairs={{0,24},{4,28},{8,16},{12,20},{16,8},{20,12},{24,0},{28,4},{1,25},{... | collective-permute-start | bytes 442376 | tf_op jit(solution)/shard_map/ppermute | solution.py:350
  32.1 7.6 %collective-permute-start.9 = (bf16[18,32,256]{2,1,0:T(8,128)(2,1)S(1)}, bf16[18,32,256]{2,1,0:T(8,128)(2,1)S(1)}, u32[]{:S(2)}, u32[]{:S(2)}) collective-permute-start(bf16[18,32,256]{2,1,0:T(8,128)(2,1)S(1)} %join.3), channel_id=1, source_target_pairs={{0,2},{1,3},{2,0},{3,1},{4,6},{5,7},{6,4},{7,5},{8,10},{9,11},{10,... | collective-permute-start | bytes 884744 | tf_op jit(solution)/shard_map/ppermute | solution.py:350
  39.7 10.1 %collective-permute-start.11 = (bf16[31,32,256]{2,1,0:T(8,128)(2,1)S(1)}, bf16[31,32,256]{2,1,0:T(8,128)(2,1)S(1)}, u32[]{:S(2)}, u32[]{:S(2)}) collective-permute-start(bf16[31,32,256]{2,1,0:T(8,128)(2,1)S(1)} %join.4), channel_id=1, source_target_pairs={{0,2},{1,3},{2,0},{3,1},{4,6},{5,7},{6,4},{7,5},{8,10},{9,11},{10,... | collective-permute-start | bytes 1523720 | tf_op jit(solution)/shard_map/ppermute | solution.py:350
  41.2 12.5 %collective-permute-start.13 = (bf16[9,32,256]{2,1,0:T(8,128)(2,1)S(1)}, bf16[9,32,256]{2,1,0:T(8,128)(2,1)S(1)}, u32[]{:S(2)}, u32[]{:S(2)}) collective-permute-start(bf16[9,32,256]{2,1,0:T(8,128)(2,1)S(1)} %get-tuple-element.60), channel_id=1, source_target_pairs={{0,20},{4,16},{8,28},{12,24},{16,4},{20,0},{24,12},{28,8},{1,21},{... | collective-permute-start | bytes 442376 | tf_op jit(solution)/shard_map/ppermute | solution.py:350
  43.0 10.8 %collective-permute-start.14 = (bf16[9,32,256]{2,1,0:T(8,128)(2,1)S(1)}, bf16[9,32,256]{2,1,0:T(8,128)(2,1)S(1)}, u32[]{:S(2)}, u32[]{:S(2)}) collective-permute-start(bf16[9,32,256]{2,1,0:T(8,128)(2,1)S(1)} %get-tuple-element.62), channel_id=1, source_target_pairs={{0,28},{4,24},{8,20},{12,16},{16,12},{20,8},{24,4},{28,0},{1,29},{... | collective-permute-start | bytes 442376 | tf_op jit(solution)/shard_map/ppermute | solution.py:350
  49.9 4.9 %collective-permute-start.12 = (bf16[58,32,256]{2,1,0:T(8,128)(2,1)S(1)}, bf16[58,32,256]{2,1,0:T(8,128)(2,1)S(1)}, u32[]{:S(2)}, u32[]{:S(2)}) collective-permute-start(bf16[58,32,256]{2,1,0:T(8,128)(2,1)S(1)} %pad_maximum_fusion.refs_2_), channel_id=1, source_target_pairs={{0,1},{1,0},{2,3},{3,2},{4,5},{5,4},{6,7},{7,6},{8,9},{9,8},{10,11... | collective-permute-start | bytes 2850824 | tf_op jit(solution)/shard_map/ppermute | solution.py:350
  54.1 6.8 %collective-permute-start.15 = (bf16[18,32,256]{2,1,0:T(8,128)(2,1)S(1)}, bf16[18,32,256]{2,1,0:T(8,128)(2,1)S(1)}, u32[]{:S(2)}, u32[]{:S(2)}) collective-permute-start(bf16[18,32,256]{2,1,0:T(8,128)(2,1)S(1)} %join.5), channel_id=1, source_target_pairs={{0,2},{1,3},{2,0},{3,1},{4,6},{5,7},{6,4},{7,5},{8,10},{9,11},{10,... | collective-permute-start | bytes 884744 | tf_op jit(solution)/shard_map/ppermute | solution.py:350
  54.8 10.0 %collective-permute-start.10 = (bf16[54,32,256]{2,1,0:T(8,128)(2,1)S(1)}, bf16[54,32,256]{2,1,0:T(8,128)(2,1)S(1)}, u32[]{:S(2)}, u32[]{:S(2)}) collective-permute-start(bf16[54,32,256]{2,1,0:T(8,128)(2,1)S(1)} %constant_dynamic-update-slice_fusion.refs_0_), channel_id=1, source_target_pairs={{0,1},{1,0},{2,3},{3,2},{4,5},{5,4},{6,7},{7,6},{8,9},{9,8},{10,11... | collective-permute-start | bytes 2654216 | tf_op jit(solution)/shard_map/ppermute | solution.py:350
  54.9 6.1 %collective-permute-start.18 = (bf16[4,32,256]{2,1,0:T(8,128)(2,1)S(1)}, bf16[4,32,256]{2,1,0:T(8,128)(2,1)S(1)}, u32[]{:S(2)}, u32[]{:S(2)}) collective-permute-start(bf16[4,32,256]{2,1,0:T(8,128)(2,1)S(1)} %get-tuple-element.65), channel_id=1, source_target_pairs={{0,12},{4,8},{8,4},{12,0},{16,28},{20,24},{24,20},{28,16},{1,13},{... | collective-permute-start | bytes 196616 | tf_op jit(solution)/shard_map/ppermute | solution.py:350
  58.0 4.3 %collective-permute-start.17 = (bf16[4,32,256]{2,1,0:T(8,128)(2,1)S(1)}, bf16[4,32,256]{2,1,0:T(8,128)(2,1)S(1)}, u32[]{:S(2)}, u32[]{:S(2)}) collective-permute-start(bf16[4,32,256]{2,1,0:T(8,128)(2,1)S(1)} %get-tuple-element.65), channel_id=1, source_target_pairs={{0,8},{4,12},{8,0},{12,4},{16,24},{20,28},{24,16},{28,20},{1,9},{5... | collective-permute-start | bytes 196616 | tf_op jit(solution)/shard_map/ppermute | solution.py:350
  58.0 4.3 %collective-permute-start.16 = (bf16[4,32,256]{2,1,0:T(8,128)(2,1)S(1)}, bf16[4,32,256]{2,1,0:T(8,128)(2,1)S(1)}, u32[]{:S(2)}, u32[]{:S(2)}) collective-permute-start(bf16[4,32,256]{2,1,0:T(8,128)(2,1)S(1)} %get-tuple-element.65), channel_id=1, source_target_pairs={{0,4},{4,0},{8,12},{12,8},{16,20},{20,16},{24,28},{28,24},{1,5},{5... | collective-permute-start | bytes 196616 | tf_op jit(solution)/shard_map/ppermute | solution.py:350
  62.4 7.0 %collective-permute-start.20 = (bf16[4,32,256]{2,1,0:T(8,128)(2,1)S(1)}, bf16[4,32,256]{2,1,0:T(8,128)(2,1)S(1)}, u32[]{:S(2)}, u32[]{:S(2)}) collective-permute-start(bf16[4,32,256]{2,1,0:T(8,128)(2,1)S(1)} %get-tuple-element.66), channel_id=1, source_target_pairs={{0,16},{4,20},{8,24},{12,28},{16,0},{20,4},{24,8},{28,12},{1,17},{... | collective-permute-start | bytes 196616 | tf_op jit(solution)/shard_map/ppermute | solution.py:350
  76.7 12.6 %collective-permute-start.23 = (f32[96,512]{1,0:T(8,128)S(1)}, f32[96,512]{1,0:T(8,128)S(1)}, u32[]{:S(2)}, u32[]{:S(2)}) collective-permute-start(f32[96,512]{1,0:T(8,128)S(1)} %get-tuple-element.74), channel_id=1, source_target_pairs={{0,3},{1,2},{2,1},{3,0},{4,7},{5,6},{6,5},{7,4},{8,11},{9,10},{10,... | collective-permute-start | bytes 589832 | tf_op jit(solution)/shard_map/ppermute | solution.py:350
  78.1 11.3 %collective-permute-start.22 = (f32[96,512]{1,0:T(8,128)S(1)}, f32[96,512]{1,0:T(8,128)S(1)}, u32[]{:S(2)}, u32[]{:S(2)}) collective-permute-start(f32[96,512]{1,0:T(8,128)S(1)} %get-tuple-element.75), channel_id=1, source_target_pairs={{0,2},{1,3},{2,0},{3,1},{4,6},{5,7},{6,4},{7,5},{8,10},{9,11},{10,... | collective-permute-start | bytes 589832 | tf_op jit(solution)/shard_map/ppermute | solution.py:350
  78.6 10.7 %collective-permute-start.21 = (f32[96,512]{1,0:T(8,128)S(1)}, f32[96,512]{1,0:T(8,128)S(1)}, u32[]{:S(2)}, u32[]{:S(2)}) collective-permute-start(f32[96,512]{1,0:T(8,128)S(1)} %get-tuple-element.76), channel_id=1, source_target_pairs={{0,1},{1,0},{2,3},{3,2},{4,5},{5,4},{6,7},{7,6},{8,9},{9,8},{10,11... | collective-permute-start | bytes 589832 | tf_op jit(solution)/shard_map/ppermute | solution.py:350
  (3 other events, 34.9 us)

commit v14 on v13

--- a/solution.py
+++ b/solution.py
@@ -459,7 +459,7 @@
         [pltpu.VMEM(item_factors.shape, bf16), pltpu.SemaphoreType.DMA],
         10**9,
     )(
-        after(info, *shared),
+        after(info, shared[1]),
         wanted,
         pltpu.with_memory_space_constraint(item_factors, pltpu.HBM),
     )

time: 91.7 us -> 96.3 us (1.050)
  waiting for transfers between devices: 20.8 us -> 23.9 us
    all_to_all x1, waiting for transfers between devices: 4.76 us -> 6.38 us  [on_device(): lax.all_to_all(requests, 'rows', split_axis=0, concat_axis=0, tiled=True)]
    ppermute x24, waiting for transfers between devices: 16 us -> 17.6 us  [flip(): return lax.ppermute(value, axis, [(i, i ^ bit) for i in range(size)])]
  transfers between devices with their start and end apart: 25 -> 25, of which waited for: 10 -> 10; matrix products, arithmetic and copies ran while one was open for 2% -> 2% of each run, Pallas kernels for 11% -> 10%
where the time goes in v14:
time: 96.3 us; the launch traced here: 96 us
  starting transfers between devices  34.8 us (36%)
  waiting for transfers between devices  23.9 us (25%)
  Pallas kernels  22.5 us (23%)
  blocking collectives  11.1 us (12%)
  between operations  1.55 us (2%)
  other arithmetic  1.26 us (1%)
    ppermute x24, starting transfers between devices, flip(): return lax.ppermute(value, axis, [(i, i ^ bit) for i in range(size)])  27.9 us
    ppermute x24, waiting for transfers between devices, flip(): return lax.ppermute(value, axis, [(i, i ^ bit) for i in range(size)])  17.6 us
    all_to_all x1, blocking collectives, on_device(): lax.all_to_all(dots, ('rows', 'cols'), split_axis=0, concat_axis=0, tiled...  11.1 us
    pallas_call x1, Pallas kernels, on_device(): call(iterate_kernel, [jax.ShapeDtypeStruct((n_cols, 3 * col_width, own_us...  7.19 us
    all_to_all x1, starting transfers between devices, on_device(): lax.all_to_all(requests, 'rows', split_axis=0, concat_axis=0, tiled=True)  6.85 us
    all_to_all x1, waiting for transfers between devices, on_device(): lax.all_to_all(requests, 'rows', split_axis=0, concat_axis=0, tiled=True)  6.38 us
    pallas_call x1, Pallas kernels, on_device(): call(functools.partial(start_kernel, n_cols, slots), [vector, held], [sme...  4.66 us
    pallas_call x1, Pallas kernels, slice_mask(): call(mask_kernel, [strengths], [smem, anywhere], 'mask', [pltpu.Semaphore...  2.28 us
  transfers between devices with their start and end apart: 25, of which 10 were waited for; matrix products, arithmetic and copies ran while one was open for 2% of the time, Pallas kernels for 10%

profile of v14, /device:TPU:0, one launch (start us, length us, event | category | flops | bytes accessed | tf_op | source)
XLA Modules:
  0.0 96.0 jit_solution(15634259020151327519)
XLA Ops:
  1.4 1.7 %prepare.1 = (bf16[32,3072]{1,0:T(8,128)(2,1)S(1)}, bf16[32,3072]{1,0:T(8,128)(2,1)S(1)}, bf16[32,3072]{1,0:T(8,128)(2,1)S(1)}, bf16[32,3072]{1,0:T(8,128)(2,1)S(1)}) custom-call(s32[3]{0:T(128)S(1)} %pad_add_fusion.info_ref, f32[32,2048]{1,0:T(8,128)} %x_ref.1, bf16[32,8192]{1,0:T(8,128)(2,1)} %items_hbm.3), custom_call_target="tpu_custom_call" | custom-call | flops 1000000000 | tf_op jit(solution)/shard_map/prepare/pallas_call | solution.py:408
  5.3 6.9 %all-to-all-start = ((s32[8,1,9]{2,1,0:T(1,128)}), s32[8,1,9]{2,1,0:T(1,128)S(1)}, u32[]{:S(2)}, u32[]{:S(2)}) async-start(s32[8,1,9]{2,1,0:T(1,128)} %bitcast.5), calls=%async_computation | async-start | bytes 8192 | tf_op jit(solution)/shard_map/all_to_all | solution.py:441
  12.2 6.4 %all-to-all-done = s32[8,1,9]{2,1,0:T(1,128)S(1)} async-done(((s32[8,1,9]{2,1,0:T(1,128)}), s32[8,1,9]{2,1,0:T(1,128)S(1)}, u32[]{:S(2)}, u32[]{:S(2)}) %all-to-all-start) | async-done | bytes 320 | tf_op jit(solution)/shard_map/all_to_all | solution.py:441
  18.5 1.8 %pick.1 = (bf16[9,32,256]{2,1,0:T(8,128)(2,1)S(1)}, bf16[9,32,256]{2,1,0:T(8,128)(2,1)S(1)}, bf16[9,32,256]{2,1,0:T(8,128)(2,1)S(1)}, bf16[9,32,256]{2,1,0:T(8,1...) custom-call(s32[3]{0:T(128)S(1)} %pad_add_fusion.info_ref, ...), custom_call_target="tpu_custom_call" | custom-call | flops 1000000000 | tf_op jit(solution)/shard_map/pick/pallas_call | solution.py:452
  21.0 1.5 %collective-permute-start.2 = (bf16[9,32,256]{2,1,0:T(8,128)(2,1)S(1)}, bf16[9,32,256]{2,1,0:T(8,128)(2,1)S(1)}, u32[]{:S(2)}, u32[]{:S(2)}) collective-permute-start(bf16[9,32,256]{2,1,0:T(8,128)(2,1)S(1)} %get-tuple-element.43), channel_id=1, source_target_pairs={{0,12},{4,8},{8,4},{12,0},{16,28},{20,24},{24,20},{28,16},{1,13},{... | collective-permute-start | bytes 442376 | tf_op jit(solution)/shard_map/ppermute | solution.py:350
  22.4 1.5 %collective-permute-start.3 = (bf16[9,32,256]{2,1,0:T(8,128)(2,1)S(1)}, bf16[9,32,256]{2,1,0:T(8,128)(2,1)S(1)}, u32[]{:S(2)}, u32[]{:S(2)}) collective-permute-start(bf16[9,32,256]{2,1,0:T(8,128)(2,1)S(1)} %get-tuple-element.44), channel_id=1, source_target_pairs={{0,2},{1,3},{2,0},{3,1},{4,6},{5,7},{6,4},{7,5},{8,10},{9,11},{10,... | collective-permute-start | bytes 442376 | tf_op jit(solution)/shard_map/ppermute | solution.py:350
  24.5 3.9 %collective-permute-done.1.refs_0_ = bf16[9,32,256]{2,1,0:T(8,128)(2,1)S(1)} collective-permute-done((bf16[9,32,256]{2,1,0:T(8,128)(2,1)S(1)}, bf16[9,32,256]{2,1,0:T(8,128)(2,1)S(1)}, u32[]{:S(2)}, u32[]{:S(2)}) %collective-permute-start.1) | collective-permute-done | bytes 147488 | tf_op jit(solution)/shard_map/ppermute | solution.py:350
  29.5 3.3 %collective-permute-start.8 = (bf16[9,32,256]{2,1,0:T(8,128)(2,1)S(1)}, bf16[9,32,256]{2,1,0:T(8,128)(2,1)S(1)}, u32[]{:S(2)}, u32[]{:S(2)}) collective-permute-start(bf16[9,32,256]{2,1,0:T(8,128)(2,1)S(1)} %get-tuple-element.52), channel_id=1, source_target_pairs={{0,24},{4,28},{8,16},{12,20},{16,8},{20,12},{24,0},{28,4},{1,25},{... | collective-permute-start | bytes 442376 | tf_op jit(solution)/shard_map/ppermute | solution.py:350
  33.2 1.7 %collective-permute-start.9 = (bf16[18,32,256]{2,1,0:T(8,128)(2,1)S(1)}, bf16[18,32,256]{2,1,0:T(8,128)(2,1)S(1)}, u32[]{:S(2)}, u32[]{:S(2)}) collective-permute-start(bf16[18,32,256]{2,1,0:T(8,128)(2,1)S(1)} %join.3), channel_id=1, source_target_pairs={{0,2},{1,3},{2,0},{3,1},{4,6},{5,7},{6,4},{7,5},{8,10},{9,11},{10,... | collective-permute-start | bytes 884744 | tf_op jit(solution)/shard_map/ppermute | solution.py:350
  34.9 1.7 %collective-permute-done.5.refs_3_ = bf16[32,3072]{1,0:T(8,128)(2,1)S(1)} collective-permute-done((bf16[32,3072]{1,0:T(8,128)(2,1)S(1)}, bf16[32,3072]{1,0:T(8,128)(2,1)S(1)}, u32[]{:S(2)}, u32[]{:S(2)}) %collective-permute-start.5) | collective-permute-done | bytes 196640 | tf_op jit(solution)/shard_map/ppermute | solution.py:350
  37.9 3.2 %collective-permute-done.7.refs_1_ = bf16[9,32,256]{2,1,0:T(8,128)(2,1)S(1)} collective-permute-done((bf16[9,32,256]{2,1,0:T(8,128)(2,1)S(1)}, bf16[9,32,256]{2,1,0:T(8,128)(2,1)S(1)}, u32[]{:S(2)}, u32[]{:S(2)}) %collective-permute-start.7) | collective-permute-done | bytes 147488 | tf_op jit(solution)/shard_map/ppermute | solution.py:350
  43.0 2.0 %collective-permute-start.13 = (bf16[9,32,256]{2,1,0:T(8,128)(2,1)S(1)}, bf16[9,32,256]{2,1,0:T(8,128)(2,1)S(1)}, u32[]{:S(2)}, u32[]{:S(2)}) collective-permute-start(bf16[9,32,256]{2,1,0:T(8,128)(2,1)S(1)} %get-tuple-element.60), channel_id=1, source_target_pairs={{0,20},{4,16},{8,28},{12,24},{16,4},{20,0},{24,12},{28,8},{1,21},{... | collective-permute-start | bytes 442376 | tf_op jit(solution)/shard_map/ppermute | solution.py:350
  45.0 3.7 %collective-permute-start.14 = (bf16[9,32,256]{2,1,0:T(8,128)(2,1)S(1)}, bf16[9,32,256]{2,1,0:T(8,128)(2,1)S(1)}, u32[]{:S(2)}, u32[]{:S(2)}) collective-permute-start(bf16[9,32,256]{2,1,0:T(8,128)(2,1)S(1)} %get-tuple-element.62), channel_id=1, source_target_pairs={{0,28},{4,24},{8,20},{12,16},{16,12},{20,8},{24,4},{28,0},{1,29},{... | collective-permute-start | bytes 442376 | tf_op jit(solution)/shard_map/ppermute | solution.py:350
  48.7 2.3 %mask.1 = bf16[72,64,256]{2,1,0:T(8,128)(2,1)S(1)} custom-call(s32[3]{0:T(128)S(1)} %pad_add_fusion.info_ref, bf16[72,256,256]{2,1,0:T(8,128)(2,1)} %mask_hbm.1), custom_call_target="tpu_custom_call" | custom-call | flops 1000000000 | tf_op jit(solution)/shard_map/mask/pallas_call | solution.py:513
  51.0 3.0 %collective-permute-done.11.refs_0_ = bf16[31,32,256]{2,1,0:T(8,128)(2,1)S(1)} collective-permute-done((bf16[31,32,256]{2,1,0:T(8,128)(2,1)S(1)}, bf16[31,32,256]{2,1,0:T(8,128)(2,1)S(1)}, u32[]{:S(2)}, u32[]{:S(2)}) %collective-permute-start.11) | collective-permute-done | bytes 507936 | tf_op jit(solution)/shard_map/ppermute | solution.py:350
  54.3 2.5 %collective-permute-done.13.refs_0_ = bf16[9,32,256]{2,1,0:T(8,128)(2,1)S(1)} collective-permute-done((bf16[9,32,256]{2,1,0:T(8,128)(2,1)S(1)}, bf16[9,32,256]{2,1,0:T(8,128)(2,1)S(1)}, u32[]{:S(2)}, u32[]{:S(2)}) %collective-permute-start.13) | collective-permute-done | bytes 147488 | tf_op jit(solution)/shard_map/ppermute | solution.py:350
  57.2 1.7 %collective-permute-start.15 = (bf16[18,32,256]{2,1,0:T(8,128)(2,1)S(1)}, bf16[18,32,256]{2,1,0:T(8,128)(2,1)S(1)}, u32[]{:S(2)}, u32[]{:S(2)}) collective-permute-start(bf16[18,32,256]{2,1,0:T(8,128)(2,1)S(1)} %join.5), channel_id=1, source_target_pairs={{0,2},{1,3},{2,0},{3,1},{4,6},{5,7},{6,4},{7,5},{8,10},{9,11},{10,... | collective-permute-start | bytes 884744 | tf_op jit(solution)/shard_map/ppermute | solution.py:350
  58.9 2.2 %collective-permute-start.18 = (bf16[4,32,256]{2,1,0:T(8,128)(2,1)S(1)}, bf16[4,32,256]{2,1,0:T(8,128)(2,1)S(1)}, u32[]{:S(2)}, u32[]{:S(2)}) collective-permute-start(bf16[4,32,256]{2,1,0:T(8,128)(2,1)S(1)} %get-tuple-element.65), channel_id=1, source_target_pairs={{0,12},{4,8},{8,4},{12,0},{16,28},{20,24},{24,20},{28,16},{1,13},{... | collective-permute-start | bytes 196616 | tf_op jit(solution)/shard_map/ppermute | solution.py:350
  62.5 1.6 %collective-permute-done.15 = bf16[18,32,256]{2,1,0:T(8,128)(2,1)S(1)} collective-permute-done((bf16[18,32,256]{2,1,0:T(8,128)(2,1)S(1)}, bf16[18,32,256]{2,1,0:T(8,128)(2,1)S(1)}, u32[]{:S(2)}, u32[]{:S(2)}) %collective-permute-start.15) | collective-permute-done | bytes 294944 | tf_op jit(solution)/shard_map/ppermute | solution.py:350
  65.9 3.0 %collective-permute-start.20 = (bf16[4,32,256]{2,1,0:T(8,128)(2,1)S(1)}, bf16[4,32,256]{2,1,0:T(8,128)(2,1)S(1)}, u32[]{:S(2)}, u32[]{:S(2)}) collective-permute-start(bf16[4,32,256]{2,1,0:T(8,128)(2,1)S(1)} %get-tuple-element.66), channel_id=1, source_target_pairs={{0,16},{4,20},{8,24},{12,28},{16,0},{20,4},{24,8},{28,12},{1,17},{... | collective-permute-start | bytes 196616 | tf_op jit(solution)/shard_map/ppermute | solution.py:350
  68.9 4.7 %start.1 = (f32[512,128]{1,0:T(8,128)S(1)}, bf16[72,128,256]{2,1,0:T(8,128)(2,1)S(1)}) custom-call(s32[72]{0:T(128)S(1)} %get-tuple-element.83.slot_ref, s32[72]{0:T(128)S(1)} %get-tuple-element.82.user_ref, s32[3]{0:T(128)S(1)} %pad_add_fusion.info_ref, f32[128,512]{1,0:T(8,128)S(1)} %get-tuple-element.49.x_ref, bf16[72,64,256]{2,1,0:T(8,128)(2,1)S(1)} %mask.1, ...), custom_call_target="tpu_custom_call" | custom-call | flops 8000000000 | tf_op jit(solution)/shard_map/start/pallas_call | solution.py:557
  73.6 7.2 %iterate.1 = (f32[4,96,512]{2,1,0:T(8,128)S(1)}, f32[32,128]{1,0:T(8,128)S(1)}) custom-call(s32[72]{0:T(128)S(1)} %get-tuple-element.83.slot_ref, s32[72]{0:T(128)S(1)} %get-tuple-element.82.user_ref, s32[3]{0:T(128)S(1)} %pad_add_fusion.info_ref, f32[128,512]{1,0:T(8,128)S(1)} %get-tuple-element.49.x_ref, f32[512,128]{1,0:T(8,128)S(1)} %get-tuple-element.68.part_ref, ...), custom_call_target="tpu_custom_call" | custom-call | flops 16000000000 | tf_op jit(solution)/shard_map/iterate/pallas_call | solution.py:566
  82.8 11.1 %all_to_all.19 = f32[32,1,128]{2,1,0:T(1,128)S(1)} all-to-all(f32[32,1,128]{2,1,0:T(1,128)S(1)} %bitcast.23), channel_id=1, replica_groups=mesh['rows'=8,'cols'=4] {'rows','cols'}, dimensions={0} | all-to-all | bytes 32768 | tf_op jit(solution)/shard_map/all_to_all | solution.py:584
  94.0 2.0 %finish.1 = (f32[32,2048]{1,0:T(8,128)}, f32[32,2048]{1,0:T(8,128)}) custom-call(s32[3]{0:T(128)S(1)} %pad_add_fusion.info_ref, f32[32,128]{1,0:T(8,128)S(1)} %bitcast.24, f32[32,2048]{1,0:T(8,128)S(1)} %copy-done, f32[96,512]{1,0:T(8,128)S(1)} %get-tuple-element.77.refs_0_, f32[96,512]{1,0:T(8,128)S(1)} %collective-permute-done.21.refs_1_, ...), custom_call_target="tpu_custom_call" | custom-call | flops 1000000000 | tf_op jit(solution)/shard_map/finish/pallas_call | solution.py:587
  (62 shorter events, 13.9 us)
Async XLA Ops:
  3.1 9.0 %collective-permute-start = (bf16[32,3072]{1,0:T(8,128)(2,1)S(1)}, bf16[32,3072]{1,0:T(8,128)(2,1)S(1)}, u32[]{:S(2)}, u32[]{:S(2)}) collective-permute-start(bf16[32,3072]{1,0:T(8,128)(2,1)S(1)} %get-tuple-element.40), channel_id=1, source_target_pairs={{0,1},{1,0},{2,3},{3,2},{4,5},{5,4},{6,7},{7,6},{8,9},{9,8},{10,11... | collective-permute-start | bytes 589832 | tf_op jit(solution)/shard_map/ppermute | solution.py:350
  5.3 13.2 %all-to-all-start = ((s32[8,1,9]{2,1,0:T(1,128)}), s32[8,1,9]{2,1,0:T(1,128)S(1)}, u32[]{:S(2)}, u32[]{:S(2)}) async-start(s32[8,1,9]{2,1,0:T(1,128)} %bitcast.5), calls=%async_computation | async-start | bytes 8192 | tf_op jit(solution)/shard_map/all_to_all | solution.py:441
  20.3 8.0 %collective-permute-start.1 = (bf16[9,32,256]{2,1,0:T(8,128)(2,1)S(1)}, bf16[9,32,256]{2,1,0:T(8,128)(2,1)S(1)}, u32[]{:S(2)}, u32[]{:S(2)}) collective-permute-start(bf16[9,32,256]{2,1,0:T(8,128)(2,1)S(1)} %get-tuple-element.42), channel_id=1, source_target_pairs={{0,4},{4,0},{8,12},{12,8},{16,20},{20,16},{24,28},{28,24},{1,5},{5... | collective-permute-start | bytes 442376 | tf_op jit(solution)/shard_map/ppermute | solution.py:350
  21.0 8.0 %collective-permute-start.2 = (bf16[9,32,256]{2,1,0:T(8,128)(2,1)S(1)}, bf16[9,32,256]{2,1,0:T(8,128)(2,1)S(1)}, u32[]{:S(2)}, u32[]{:S(2)}) collective-permute-start(bf16[9,32,256]{2,1,0:T(8,128)(2,1)S(1)} %get-tuple-element.43), channel_id=1, source_target_pairs={{0,12},{4,8},{8,4},{12,0},{16,28},{20,24},{24,20},{28,16},{1,13},{... | collective-permute-start | bytes 442376 | tf_op jit(solution)/shard_map/ppermute | solution.py:350
  22.4 7.1 %collective-permute-start.3 = (bf16[9,32,256]{2,1,0:T(8,128)(2,1)S(1)}, bf16[9,32,256]{2,1,0:T(8,128)(2,1)S(1)}, u32[]{:S(2)}, u32[]{:S(2)}) collective-permute-start(bf16[9,32,256]{2,1,0:T(8,128)(2,1)S(1)} %get-tuple-element.44), channel_id=1, source_target_pairs={{0,2},{1,3},{2,0},{3,1},{4,6},{5,7},{6,4},{7,5},{8,10},{9,11},{10,... | collective-permute-start | bytes 442376 | tf_op jit(solution)/shard_map/ppermute | solution.py:350
  23.9 9.3 %collective-permute-start.4 = (bf16[32,3072]{1,0:T(8,128)(2,1)S(1)}, bf16[32,3072]{1,0:T(8,128)(2,1)S(1)}, u32[]{:S(2)}, u32[]{:S(2)}) collective-permute-start(bf16[32,3072]{1,0:T(8,128)(2,1)S(1)} %get-tuple-element.47), channel_id=1, source_target_pairs={{0,2},{1,3},{2,0},{3,1},{4,6},{5,7},{6,4},{7,5},{8,10},{9,11},{10,... | collective-permute-start | bytes 589832 | tf_op jit(solution)/shard_map/ppermute | solution.py:350
  24.4 12.2 %collective-permute-start.5 = (bf16[32,3072]{1,0:T(8,128)(2,1)S(1)}, bf16[32,3072]{1,0:T(8,128)(2,1)S(1)}, u32[]{:S(2)}, u32[]{:S(2)}) collective-permute-start(bf16[32,3072]{1,0:T(8,128)(2,1)S(1)} %get-tuple-element.48), channel_id=1, source_target_pairs={{0,3},{1,2},{2,1},{3,0},{4,7},{5,6},{6,5},{7,4},{8,11},{9,10},{10,... | collective-permute-start | bytes 589832 | tf_op jit(solution)/shard_map/ppermute | solution.py:350
  28.4 9.5 %collective-permute-start.6 = (bf16[9,32,256]{2,1,0:T(8,128)(2,1)S(1)}, bf16[9,32,256]{2,1,0:T(8,128)(2,1)S(1)}, u32[]{:S(2)}, u32[]{:S(2)}) collective-permute-start(bf16[9,32,256]{2,1,0:T(8,128)(2,1)S(1)} %get-tuple-element.50), channel_id=1, source_target_pairs={{0,8},{4,12},{8,0},{12,4},{16,24},{20,28},{24,16},{28,20},{1,9},{5... | collective-permute-start | bytes 442376 | tf_op jit(solution)/shard_map/ppermute | solution.py:350
  28.9 12.2 %collective-permute-start.7 = (bf16[9,32,256]{2,1,0:T(8,128)(2,1)S(1)}, bf16[9,32,256]{2,1,0:T(8,128)(2,1)S(1)}, u32[]{:S(2)}, u32[]{:S(2)}) collective-permute-start(bf16[9,32,256]{2,1,0:T(8,128)(2,1)S(1)} %get-tuple-element.51), channel_id=1, source_target_pairs={{0,16},{4,20},{8,24},{12,28},{16,0},{20,4},{24,8},{28,12},{1,17},{... | collective-permute-start | bytes 442376 | tf_op jit(solution)/shard_map/ppermute | solution.py:350
  29.5 11.6 %collective-permute-start.8 = (bf16[9,32,256]{2,1,0:T(8,128)(2,1)S(1)}, bf16[9,32,256]{2,1,0:T(8,128)(2,1)S(1)}, u32[]{:S(2)}, u32[]{:S(2)}) collective-permute-start(bf16[9,32,256]{2,1,0:T(8,128)(2,1)S(1)} %get-tuple-element.52), channel_id=1, source_target_pairs={{0,24},{4,28},{8,16},{12,20},{16,8},{20,12},{24,0},{28,4},{1,25},{... | collective-permute-start | bytes 442376 | tf_op jit(solution)/shard_map/ppermute | solution.py:350
  33.2 8.7 %collective-permute-start.9 = (bf16[18,32,256]{2,1,0:T(8,128)(2,1)S(1)}, bf16[18,32,256]{2,1,0:T(8,128)(2,1)S(1)}, u32[]{:S(2)}, u32[]{:S(2)}) collective-permute-start(bf16[18,32,256]{2,1,0:T(8,128)(2,1)S(1)} %join.3), channel_id=1, source_target_pairs={{0,2},{1,3},{2,0},{3,1},{4,6},{5,7},{6,4},{7,5},{8,10},{9,11},{10,... | collective-permute-start | bytes 884744 | tf_op jit(solution)/shard_map/ppermute | solution.py:350
  41.9 12.1 %collective-permute-start.11 = (bf16[31,32,256]{2,1,0:T(8,128)(2,1)S(1)}, bf16[31,32,256]{2,1,0:T(8,128)(2,1)S(1)}, u32[]{:S(2)}, u32[]{:S(2)}) collective-permute-start(bf16[31,32,256]{2,1,0:T(8,128)(2,1)S(1)} %join.4), channel_id=1, source_target_pairs={{0,2},{1,3},{2,0},{3,1},{4,6},{5,7},{6,4},{7,5},{8,10},{9,11},{10,... | collective-permute-start | bytes 1523720 | tf_op jit(solution)/shard_map/ppermute | solution.py:350
  43.0 13.8 %collective-permute-start.13 = (bf16[9,32,256]{2,1,0:T(8,128)(2,1)S(1)}, bf16[9,32,256]{2,1,0:T(8,128)(2,1)S(1)}, u32[]{:S(2)}, u32[]{:S(2)}) collective-permute-start(bf16[9,32,256]{2,1,0:T(8,128)(2,1)S(1)} %get-tuple-element.60), channel_id=1, source_target_pairs={{0,20},{4,16},{8,28},{12,24},{16,4},{20,0},{24,12},{28,8},{1,21},{... | collective-permute-start | bytes 442376 | tf_op jit(solution)/shard_map/ppermute | solution.py:350
  45.0 11.8 %collective-permute-start.14 = (bf16[9,32,256]{2,1,0:T(8,128)(2,1)S(1)}, bf16[9,32,256]{2,1,0:T(8,128)(2,1)S(1)}, u32[]{:S(2)}, u32[]{:S(2)}) collective-permute-start(bf16[9,32,256]{2,1,0:T(8,128)(2,1)S(1)} %get-tuple-element.62), channel_id=1, source_target_pairs={{0,28},{4,24},{8,20},{12,16},{16,12},{20,8},{24,4},{28,0},{1,29},{... | collective-permute-start | bytes 442376 | tf_op jit(solution)/shard_map/ppermute | solution.py:350
  54.2 4.6 %collective-permute-start.12 = (bf16[58,32,256]{2,1,0:T(8,128)(2,1)S(1)}, bf16[58,32,256]{2,1,0:T(8,128)(2,1)S(1)}, u32[]{:S(2)}, u32[]{:S(2)}) collective-permute-start(bf16[58,32,256]{2,1,0:T(8,128)(2,1)S(1)} %pad_maximum_fusion.refs_2_), channel_id=1, source_target_pairs={{0,1},{1,0},{2,3},{3,2},{4,5},{5,4},{6,7},{7,6},{8,9},{9,8},{10,11... | collective-permute-start | bytes 2850824 | tf_op jit(solution)/shard_map/ppermute | solution.py:350
  57.2 7.0 %collective-permute-start.15 = (bf16[18,32,256]{2,1,0:T(8,128)(2,1)S(1)}, bf16[18,32,256]{2,1,0:T(8,128)(2,1)S(1)}, u32[]{:S(2)}, u32[]{:S(2)}) collective-permute-start(bf16[18,32,256]{2,1,0:T(8,128)(2,1)S(1)} %join.5), channel_id=1, source_target_pairs={{0,2},{1,3},{2,0},{3,1},{4,6},{5,7},{6,4},{7,5},{8,10},{9,11},{10,... | collective-permute-start | bytes 884744 | tf_op jit(solution)/shard_map/ppermute | solution.py:350
  58.8 10.1 %collective-permute-start.10 = (bf16[54,32,256]{2,1,0:T(8,128)(2,1)S(1)}, bf16[54,32,256]{2,1,0:T(8,128)(2,1)S(1)}, u32[]{:S(2)}, u32[]{:S(2)}) collective-permute-start(bf16[54,32,256]{2,1,0:T(8,128)(2,1)S(1)} %constant_dynamic-update-slice_fusion.refs_0_), channel_id=1, source_target_pairs={{0,1},{1,0},{2,3},{3,2},{4,5},{5,4},{6,7},{7,6},{8,9},{9,8},{10,11... | collective-permute-start | bytes 2654216 | tf_op jit(solution)/shard_map/ppermute | solution.py:350
  58.9 5.5 %collective-permute-start.18 = (bf16[4,32,256]{2,1,0:T(8,128)(2,1)S(1)}, bf16[4,32,256]{2,1,0:T(8,128)(2,1)S(1)}, u32[]{:S(2)}, u32[]{:S(2)}) collective-permute-start(bf16[4,32,256]{2,1,0:T(8,128)(2,1)S(1)} %get-tuple-element.65), channel_id=1, source_target_pairs={{0,12},{4,8},{8,4},{12,0},{16,28},{20,24},{24,20},{28,16},{1,13},{... | collective-permute-start | bytes 196616 | tf_op jit(solution)/shard_map/ppermute | solution.py:350
  61.1 4.3 %collective-permute-start.17 = (bf16[4,32,256]{2,1,0:T(8,128)(2,1)S(1)}, bf16[4,32,256]{2,1,0:T(8,128)(2,1)S(1)}, u32[]{:S(2)}, u32[]{:S(2)}) collective-permute-start(bf16[4,32,256]{2,1,0:T(8,128)(2,1)S(1)} %get-tuple-element.65), channel_id=1, source_target_pairs={{0,8},{4,12},{8,0},{12,4},{16,24},{20,28},{24,16},{28,20},{1,9},{5... | collective-permute-start | bytes 196616 | tf_op jit(solution)/shard_map/ppermute | solution.py:350
  61.1 4.6 %collective-permute-start.16 = (bf16[4,32,256]{2,1,0:T(8,128)(2,1)S(1)}, bf16[4,32,256]{2,1,0:T(8,128)(2,1)S(1)}, u32[]{:S(2)}, u32[]{:S(2)}) collective-permute-start(bf16[4,32,256]{2,1,0:T(8,128)(2,1)S(1)} %get-tuple-element.65), channel_id=1, source_target_pairs={{0,4},{4,0},{8,12},{12,8},{16,20},{20,16},{24,28},{28,24},{1,5},{5... | collective-permute-start | bytes 196616 | tf_op jit(solution)/shard_map/ppermute | solution.py:350
  65.9 7.7 %collective-permute-start.20 = (bf16[4,32,256]{2,1,0:T(8,128)(2,1)S(1)}, bf16[4,32,256]{2,1,0:T(8,128)(2,1)S(1)}, u32[]{:S(2)}, u32[]{:S(2)}) collective-permute-start(bf16[4,32,256]{2,1,0:T(8,128)(2,1)S(1)} %get-tuple-element.66), channel_id=1, source_target_pairs={{0,16},{4,20},{8,24},{12,28},{16,0},{20,4},{24,8},{28,12},{1,17},{... | collective-permute-start | bytes 196616 | tf_op jit(solution)/shard_map/ppermute | solution.py:350
  80.9 13.1 %collective-permute-start.23 = (f32[96,512]{1,0:T(8,128)S(1)}, f32[96,512]{1,0:T(8,128)S(1)}, u32[]{:S(2)}, u32[]{:S(2)}) collective-permute-start(f32[96,512]{1,0:T(8,128)S(1)} %get-tuple-element.74), channel_id=1, source_target_pairs={{0,3},{1,2},{2,1},{3,0},{4,7},{5,6},{6,5},{7,4},{8,11},{9,10},{10,... | collective-permute-start | bytes 589832 | tf_op jit(solution)/shard_map/ppermute | solution.py:350
  81.3 12.6 %collective-permute-start.22 = (f32[96,512]{1,0:T(8,128)S(1)}, f32[96,512]{1,0:T(8,128)S(1)}, u32[]{:S(2)}, u32[]{:S(2)}) collective-permute-start(f32[96,512]{1,0:T(8,128)S(1)} %get-tuple-element.75), channel_id=1, source_target_pairs={{0,2},{1,3},{2,0},{3,1},{4,6},{5,7},{6,4},{7,5},{8,10},{9,11},{10,... | collective-permute-start | bytes 589832 | tf_op jit(solution)/shard_map/ppermute | solution.py:350
  82.8 11.2 %collective-permute-start.21 = (f32[96,512]{1,0:T(8,128)S(1)}, f32[96,512]{1,0:T(8,128)S(1)}, u32[]{:S(2)}, u32[]{:S(2)}) collective-permute-start(f32[96,512]{1,0:T(8,128)S(1)} %get-tuple-element.76), channel_id=1, source_target_pairs={{0,1},{1,0},{2,3},{3,2},{4,5},{5,4},{6,7},{7,6},{8,9},{9,8},{10,11... | collective-permute-start | bytes 589832 | tf_op jit(solution)/shard_map/ppermute | solution.py:350
  (3 other events, 35.2 us)

commit v15 on v13

--- a/solution.py
+++ b/solution.py
@@ -305,13 +305,10 @@
 
 
 def finish_kernel(share, info_ref, dots_ref, x_ref, *refs):
-    n_cols = len(refs) - 5
-    x_out, r_out, field_ref, first_ref, second_ref = refs[n_cols:]
-    width = field_ref.shape[1]
-    for m in range(n_cols):
-        place = info_ref[1] ^ m
-        for part, ref in enumerate((field_ref, first_ref, second_ref)):
-            ref[place] = refs[m][part * width : (part + 1) * width]
+    pieces, (x_out, r_out) = refs[:-2], refs[-2:]
+    own = info_ref[1]
+    odd = own % 2 == 1
+    width = x_ref.shape[0]
     dots = dots_ref[...]
 
     def column(j):
@@ -331,18 +328,24 @@
     alpha1 = rr1 / (curved + 2.0 * beta * crossed + beta * beta * ab)
     along = alpha0 + alpha1 * (1.0 + beta)
     across = alpha1 * alpha0
-    blocks = x_ref.shape[1] // (share * n_cols)
-    for b in range(blocks):
-
-        def gather(ref):
-            return jnp.concatenate(
-                [ref[m, :, b * share : (b + 1) * share] for m in range(n_cols)], axis=1
-            )
-
-        field, first, second = gather(field_ref), gather(first_ref), gather(second_ref)
-        here = slice(b * share * n_cols, (b + 1) * share * n_cols)
-        x_out[:, here] = x_ref[:, here] + along * field - across * first
-        r_out[:, here] = field - along * first + across * second
+    n_cols = len(pieces)
+    for b in range(x_ref.shape[1] // (share * n_cols)):
+        for k in range(0, n_cols, 2):
+
+            def pair(part):
+                left, right = (
+                    ref[part * width : (part + 1) * width, b * share : (b + 1) * share]
+                    for ref in pieces[k : k + 2]
+                )
+                return jnp.concatenate(
+                    [jnp.where(odd, right, left), jnp.where(odd, left, right)], axis=1
+                )
+
+            field, first, second = pair(0), pair(1), pair(2)
+            place = (b * n_cols + ((own // 2) ^ (k // 2)) * 2) * share
+            here = pl.ds(pl.multiple_of(place, 2 * share), 2 * share)
+            x_out[:, here] = x_ref[:, here] + along * field - across * first
+            r_out[:, here] = field - along * first + across * second
 
 
 def flip(value, axis, bit):
@@ -589,7 +592,7 @@
             [result, result],
             [smem] + [vmem] * (2 + n_cols),
             "finish",
-            [pltpu.VMEM((n_cols, col_width, own_users), f32)] * 3,
+            (),
             10**9,
         )(info, dots, user_factors, *turned)
     )

time: 91.7 us -> 91.7 us (level)
  no operation moved by 1% of the time
where the time goes in v15:
time: 91.7 us; the launch traced here: 91.4 us
  starting transfers between devices  33.9 us (37%)
  Pallas kernels  22.4 us (24%)
  waiting for transfers between devices  20.8 us (23%)
  blocking collectives  10.7 us (12%)
  between operations  1.57 us (2%)
  other arithmetic  1.26 us (1%)
    ppermute x24, starting transfers between devices, flip(): return lax.ppermute(value, axis, [(i, i ^ bit) for i in range(size)])  27.8 us
    ppermute x24, waiting for transfers between devices, flip(): return lax.ppermute(value, axis, [(i, i ^ bit) for i in range(size)])  16 us
    all_to_all x1, blocking collectives, on_device(): lax.all_to_all(dots, ('rows', 'cols'), split_axis=0, concat_axis=0, tiled...  10.7 us
    pallas_call x1, Pallas kernels, on_device(): call(iterate_kernel, [jax.ShapeDtypeStruct((n_cols, 3 * col_width, own_us...  7.19 us
    all_to_all x1, starting transfers between devices, on_device(): lax.all_to_all(requests, 'rows', split_axis=0, concat_axis=0, tiled=True)  6.07 us
    all_to_all x1, waiting for transfers between devices, on_device(): lax.all_to_all(requests, 'rows', split_axis=0, concat_axis=0, tiled=True)  4.76 us
    pallas_call x1, Pallas kernels, on_device(): call(functools.partial(start_kernel, n_cols, slots), [vector, held], [sme...  4.66 us
    pallas_call x1, Pallas kernels, slice_mask(): call(mask_kernel, [strengths], [smem, anywhere], 'mask', [pltpu.Semaphore...  2.23 us
  transfers between devices with their start and end apart: 25, of which 10 were waited for; matrix products, arithmetic and copies ran while one was open for 2% of the time, Pallas kernels for 11%

profile of v15, /device:TPU:0, one launch (start us, length us, event | category | flops | bytes accessed | tf_op | source)
XLA Modules:
  0.0 91.4 jit_solution(6360171648717432750)
XLA Ops:
  1.4 1.7 %prepare.1 = (bf16[32,3072]{1,0:T(8,128)(2,1)S(1)}, bf16[32,3072]{1,0:T(8,128)(2,1)S(1)}, bf16[32,3072]{1,0:T(8,128)(2,1)S(1)}, bf16[32,3072]{1,0:T(8,128)(2,1)S(1)}) custom-call(s32[3]{0:T(128)S(1)} %pad_add_fusion.info_ref, f32[32,2048]{1,0:T(8,128)} %x_ref.1, bf16[32,8192]{1,0:T(8,128)(2,1)} %items_hbm.3), custom_call_target="tpu_custom_call" | custom-call | flops 1000000000 | tf_op jit(solution)/shard_map/prepare/pallas_call | solution.py:411
  3.6 2.6 %collective-permute-start.1 = (bf16[32,3072]{1,0:T(8,128)(2,1)S(1)}, bf16[32,3072]{1,0:T(8,128)(2,1)S(1)}, u32[]{:S(2)}, u32[]{:S(2)}) collective-permute-start(bf16[32,3072]{1,0:T(8,128)(2,1)S(1)} %get-tuple-element.41), channel_id=1, source_target_pairs={{0,2},{1,3},{2,0},{3,1},{4,6},{5,7},{6,4},{7,5},{8,10},{9,11},{10,... | collective-permute-start | bytes 589832 | tf_op jit(solution)/shard_map/ppermute | solution.py:353
  7.9 6.1 %all-to-all-start = ((s32[8,1,9]{2,1,0:T(1,128)}), s32[8,1,9]{2,1,0:T(1,128)S(1)}, u32[]{:S(2)}, u32[]{:S(2)}) async-start(s32[8,1,9]{2,1,0:T(1,128)} %bitcast.5), calls=%async_computation | async-start | bytes 8192 | tf_op jit(solution)/shard_map/all_to_all | solution.py:444
  14.0 1.6 %collective-permute-done.2.refs_3_ = bf16[32,3072]{1,0:T(8,128)(2,1)S(1)} collective-permute-done((bf16[32,3072]{1,0:T(8,128)(2,1)S(1)}, bf16[32,3072]{1,0:T(8,128)(2,1)S(1)}, u32[]{:S(2)}, u32[]{:S(2)}) %collective-permute-start.2) | collective-permute-done | bytes 196640 | tf_op jit(solution)/shard_map/ppermute | solution.py:353
  15.6 4.8 %all-to-all-done = s32[8,1,9]{2,1,0:T(1,128)S(1)} async-done(((s32[8,1,9]{2,1,0:T(1,128)}), s32[8,1,9]{2,1,0:T(1,128)S(1)}, u32[]{:S(2)}, u32[]{:S(2)}) %all-to-all-start) | async-done | bytes 320 | tf_op jit(solution)/shard_map/all_to_all | solution.py:444
  20.4 1.8 %pick.1 = (bf16[9,32,256]{2,1,0:T(8,128)(2,1)S(1)}, bf16[9,32,256]{2,1,0:T(8,128)(2,1)S(1)}, bf16[9,32,256]{2,1,0:T(8,128)(2,1)S(1)}, bf16[9,32,256]{2,1,0:T(8,1...) custom-call(s32[3]{0:T(128)S(1)} %pad_add_fusion.info_ref, ...), custom_call_target="tpu_custom_call" | custom-call | flops 1000000000 | tf_op jit(solution)/shard_map/pick/pallas_call | solution.py:455
  22.8 1.5 %collective-permute-start.4 = (bf16[9,32,256]{2,1,0:T(8,128)(2,1)S(1)}, bf16[9,32,256]{2,1,0:T(8,128)(2,1)S(1)}, u32[]{:S(2)}, u32[]{:S(2)}) collective-permute-start(bf16[9,32,256]{2,1,0:T(8,128)(2,1)S(1)} %get-tuple-element.45), channel_id=1, source_target_pairs={{0,12},{4,8},{8,4},{12,0},{16,28},{20,24},{24,20},{28,16},{1,13},{... | collective-permute-start | bytes 442376 | tf_op jit(solution)/shard_map/ppermute | solution.py:353
  24.3 1.5 %collective-permute-start.6 = (bf16[9,32,256]{2,1,0:T(8,128)(2,1)S(1)}, bf16[9,32,256]{2,1,0:T(8,128)(2,1)S(1)}, u32[]{:S(2)}, u32[]{:S(2)}) collective-permute-start(bf16[9,32,256]{2,1,0:T(8,128)(2,1)S(1)} %get-tuple-element.50), channel_id=1, source_target_pairs={{0,8},{4,12},{8,0},{12,4},{16,24},{20,28},{24,16},{28,20},{1,9},{5... | collective-permute-start | bytes 442376 | tf_op jit(solution)/shard_map/ppermute | solution.py:353
  26.3 1.5 %collective-permute-start.5 = (bf16[9,32,256]{2,1,0:T(8,128)(2,1)S(1)}, bf16[9,32,256]{2,1,0:T(8,128)(2,1)S(1)}, u32[]{:S(2)}, u32[]{:S(2)}) collective-permute-start(bf16[9,32,256]{2,1,0:T(8,128)(2,1)S(1)} %get-tuple-element.46), channel_id=1, source_target_pairs={{0,2},{1,3},{2,0},{3,1},{4,6},{5,7},{6,4},{7,5},{8,10},{9,11},{10,... | collective-permute-start | bytes 442376 | tf_op jit(solution)/shard_map/ppermute | solution.py:353
  28.5 1.7 %collective-permute-start.8 = (bf16[9,32,256]{2,1,0:T(8,128)(2,1)S(1)}, bf16[9,32,256]{2,1,0:T(8,128)(2,1)S(1)}, u32[]{:S(2)}, u32[]{:S(2)}) collective-permute-start(bf16[9,32,256]{2,1,0:T(8,128)(2,1)S(1)} %get-tuple-element.52), channel_id=1, source_target_pairs={{0,24},{4,28},{8,16},{12,20},{16,8},{20,12},{24,0},{28,4},{1,25},{... | collective-permute-start | bytes 442376 | tf_op jit(solution)/shard_map/ppermute | solution.py:353
  32.1 1.5 %collective-permute-start.9 = (bf16[18,32,256]{2,1,0:T(8,128)(2,1)S(1)}, bf16[18,32,256]{2,1,0:T(8,128)(2,1)S(1)}, u32[]{:S(2)}, u32[]{:S(2)}) collective-permute-start(bf16[18,32,256]{2,1,0:T(8,128)(2,1)S(1)} %join.3), channel_id=1, source_target_pairs={{0,2},{1,3},{2,0},{3,1},{4,6},{5,7},{6,4},{7,5},{8,10},{9,11},{10,... | collective-permute-start | bytes 884744 | tf_op jit(solution)/shard_map/ppermute | solution.py:353
  35.4 3.5 %collective-permute-done.7.refs_1_ = bf16[9,32,256]{2,1,0:T(8,128)(2,1)S(1)} collective-permute-done((bf16[9,32,256]{2,1,0:T(8,128)(2,1)S(1)}, bf16[9,32,256]{2,1,0:T(8,128)(2,1)S(1)}, u32[]{:S(2)}, u32[]{:S(2)}) %collective-permute-start.7) | collective-permute-done | bytes 147488 | tf_op jit(solution)/shard_map/ppermute | solution.py:353
  39.7 1.6 %collective-permute-start.11 = (bf16[31,32,256]{2,1,0:T(8,128)(2,1)S(1)}, bf16[31,32,256]{2,1,0:T(8,128)(2,1)S(1)}, u32[]{:S(2)}, u32[]{:S(2)}) collective-permute-start(bf16[31,32,256]{2,1,0:T(8,128)(2,1)S(1)} %join.4), channel_id=1, source_target_pairs={{0,2},{1,3},{2,0},{3,1},{4,6},{5,7},{6,4},{7,5},{8,10},{9,11},{10,... | collective-permute-start | bytes 1523720 | tf_op jit(solution)/shard_map/ppermute | solution.py:353
  41.2 1.8 %collective-permute-start.13 = (bf16[9,32,256]{2,1,0:T(8,128)(2,1)S(1)}, bf16[9,32,256]{2,1,0:T(8,128)(2,1)S(1)}, u32[]{:S(2)}, u32[]{:S(2)}) collective-permute-start(bf16[9,32,256]{2,1,0:T(8,128)(2,1)S(1)} %get-tuple-element.60), channel_id=1, source_target_pairs={{0,20},{4,16},{8,28},{12,24},{16,4},{20,0},{24,12},{28,8},{1,21},{... | collective-permute-start | bytes 442376 | tf_op jit(solution)/shard_map/ppermute | solution.py:353
  43.0 3.6 %collective-permute-start.14 = (bf16[9,32,256]{2,1,0:T(8,128)(2,1)S(1)}, bf16[9,32,256]{2,1,0:T(8,128)(2,1)S(1)}, u32[]{:S(2)}, u32[]{:S(2)}) collective-permute-start(bf16[9,32,256]{2,1,0:T(8,128)(2,1)S(1)} %get-tuple-element.62), channel_id=1, source_target_pairs={{0,28},{4,24},{8,20},{12,16},{16,12},{20,8},{24,4},{28,0},{1,29},{... | collective-permute-start | bytes 442376 | tf_op jit(solution)/shard_map/ppermute | solution.py:353
  46.6 2.2 %mask.1 = bf16[72,64,256]{2,1,0:T(8,128)(2,1)S(1)} custom-call(s32[3]{0:T(128)S(1)} %pad_add_fusion.info_ref, bf16[72,256,256]{2,1,0:T(8,128)(2,1)} %mask_hbm.1), custom_call_target="tpu_custom_call" | custom-call | flops 1000000000 | tf_op jit(solution)/shard_map/mask/pallas_call | solution.py:516
  50.0 3.7 %collective-permute-done.13.refs_0_ = bf16[9,32,256]{2,1,0:T(8,128)(2,1)S(1)} collective-permute-done((bf16[9,32,256]{2,1,0:T(8,128)(2,1)S(1)}, bf16[9,32,256]{2,1,0:T(8,128)(2,1)S(1)}, u32[]{:S(2)}, u32[]{:S(2)}) %collective-permute-start.13) | collective-permute-done | bytes 147488 | tf_op jit(solution)/shard_map/ppermute | solution.py:353
  54.9 3.2 %collective-permute-start.18 = (bf16[4,32,256]{2,1,0:T(8,128)(2,1)S(1)}, bf16[4,32,256]{2,1,0:T(8,128)(2,1)S(1)}, u32[]{:S(2)}, u32[]{:S(2)}) collective-permute-start(bf16[4,32,256]{2,1,0:T(8,128)(2,1)S(1)} %get-tuple-element.65), channel_id=1, source_target_pairs={{0,12},{4,8},{8,4},{12,0},{16,28},{20,24},{24,20},{28,16},{1,13},{... | collective-permute-start | bytes 196616 | tf_op jit(solution)/shard_map/ppermute | solution.py:353
  58.7 2.3 %collective-permute-done.15 = bf16[18,32,256]{2,1,0:T(8,128)(2,1)S(1)} collective-permute-done((bf16[18,32,256]{2,1,0:T(8,128)(2,1)S(1)}, bf16[18,32,256]{2,1,0:T(8,128)(2,1)S(1)}, u32[]{:S(2)}, u32[]{:S(2)}) %collective-permute-start.15) | collective-permute-done | bytes 294944 | tf_op jit(solution)/shard_map/ppermute | solution.py:353
  62.5 2.3 %collective-permute-start.20 = (bf16[4,32,256]{2,1,0:T(8,128)(2,1)S(1)}, bf16[4,32,256]{2,1,0:T(8,128)(2,1)S(1)}, u32[]{:S(2)}, u32[]{:S(2)}) collective-permute-start(bf16[4,32,256]{2,1,0:T(8,128)(2,1)S(1)} %get-tuple-element.66), channel_id=1, source_target_pairs={{0,16},{4,20},{8,24},{12,28},{16,0},{20,4},{24,8},{28,12},{1,17},{... | collective-permute-start | bytes 196616 | tf_op jit(solution)/shard_map/ppermute | solution.py:353
  64.8 4.7 %start.1 = (f32[512,128]{1,0:T(8,128)S(1)}, bf16[72,128,256]{2,1,0:T(8,128)(2,1)S(1)}) custom-call(s32[72]{0:T(128)S(1)} %get-tuple-element.83.slot_ref, s32[72]{0:T(128)S(1)} %get-tuple-element.82.user_ref, s32[3]{0:T(128)S(1)} %pad_add_fusion.info_ref, f32[128,512]{1,0:T(8,128)S(1)} %get-tuple-element.49.x_ref, bf16[72,64,256]{2,1,0:T(8,128)(2,1)S(1)} %mask.1, ...), custom_call_target="tpu_custom_call" | custom-call | flops 8000000000 | tf_op jit(solution)/shard_map/start/pallas_call | solution.py:560
  69.5 7.2 %iterate.1 = (f32[4,96,512]{2,1,0:T(8,128)S(1)}, f32[32,128]{1,0:T(8,128)S(1)}) custom-call(s32[72]{0:T(128)S(1)} %get-tuple-element.83.slot_ref, s32[72]{0:T(128)S(1)} %get-tuple-element.82.user_ref, s32[3]{0:T(128)S(1)} %pad_add_fusion.info_ref, f32[128,512]{1,0:T(8,128)S(1)} %get-tuple-element.49.x_ref, f32[512,128]{1,0:T(8,128)S(1)} %get-tuple-element.68.part_ref, ...), custom_call_target="tpu_custom_call" | custom-call | flops 16000000000 | tf_op jit(solution)/shard_map/iterate/pallas_call | solution.py:569
  78.7 10.7 %all_to_all.19 = f32[32,1,128]{2,1,0:T(1,128)S(1)} all-to-all(f32[32,1,128]{2,1,0:T(1,128)S(1)} %bitcast.23), channel_id=1, replica_groups=mesh['rows'=8,'cols'=4] {'rows','cols'}, dimensions={0} | all-to-all | bytes 32768 | tf_op jit(solution)/shard_map/all_to_all | solution.py:587
  89.4 2.0 %finish.1 = (f32[32,2048]{1,0:T(8,128)}, f32[32,2048]{1,0:T(8,128)}) custom-call(s32[3]{0:T(128)S(1)} %pad_add_fusion.info_ref, f32[32,128]{1,0:T(8,128)S(1)} %bitcast.24, f32[32,2048]{1,0:T(8,128)S(1)} %copy-done, f32[96,512]{1,0:T(8,128)S(1)} %get-tuple-element.77.refs_0_, f32[96,512]{1,0:T(8,128)S(1)} %collective-permute-done.21.refs_1_, ...), custom_call_target="tpu_custom_call" | custom-call | flops 1000000000 | tf_op jit(solution)/shard_map/finish/pallas_call | solution.py:590
  (62 shorter events, 14.9 us)
Async XLA Ops:
  3.1 10.9 %collective-permute-start = (bf16[32,3072]{1,0:T(8,128)(2,1)S(1)}, bf16[32,3072]{1,0:T(8,128)(2,1)S(1)}, u32[]{:S(2)}, u32[]{:S(2)}) collective-permute-start(bf16[32,3072]{1,0:T(8,128)(2,1)S(1)} %get-tuple-element.40), channel_id=1, source_target_pairs={{0,1},{1,0},{2,3},{3,2},{4,5},{5,4},{6,7},{7,6},{8,9},{9,8},{10,11... | collective-permute-start | bytes 589832 | tf_op jit(solution)/shard_map/ppermute | solution.py:353
  3.6 10.4 %collective-permute-start.1 = (bf16[32,3072]{1,0:T(8,128)(2,1)S(1)}, bf16[32,3072]{1,0:T(8,128)(2,1)S(1)}, u32[]{:S(2)}, u32[]{:S(2)}) collective-permute-start(bf16[32,3072]{1,0:T(8,128)(2,1)S(1)} %get-tuple-element.41), channel_id=1, source_target_pairs={{0,2},{1,3},{2,0},{3,1},{4,6},{5,7},{6,4},{7,5},{8,10},{9,11},{10,... | collective-permute-start | bytes 589832 | tf_op jit(solution)/shard_map/ppermute | solution.py:353
  6.2 9.4 %collective-permute-start.2 = (bf16[32,3072]{1,0:T(8,128)(2,1)S(1)}, bf16[32,3072]{1,0:T(8,128)(2,1)S(1)}, u32[]{:S(2)}, u32[]{:S(2)}) collective-permute-start(bf16[32,3072]{1,0:T(8,128)(2,1)S(1)} %get-tuple-element.42), channel_id=1, source_target_pairs={{0,3},{1,2},{2,1},{3,0},{4,7},{5,6},{6,5},{7,4},{8,11},{9,10},{10,... | collective-permute-start | bytes 589832 | tf_op jit(solution)/shard_map/ppermute | solution.py:353
  7.9 12.5 %all-to-all-start = ((s32[8,1,9]{2,1,0:T(1,128)}), s32[8,1,9]{2,1,0:T(1,128)S(1)}, u32[]{:S(2)}, u32[]{:S(2)}) async-start(s32[8,1,9]{2,1,0:T(1,128)} %bitcast.5), calls=%async_computation | async-start | bytes 8192 | tf_op jit(solution)/shard_map/all_to_all | solution.py:444
  22.2 6.3 %collective-permute-start.3 = (bf16[9,32,256]{2,1,0:T(8,128)(2,1)S(1)}, bf16[9,32,256]{2,1,0:T(8,128)(2,1)S(1)}, u32[]{:S(2)}, u32[]{:S(2)}) collective-permute-start(bf16[9,32,256]{2,1,0:T(8,128)(2,1)S(1)} %get-tuple-element.44), channel_id=1, source_target_pairs={{0,4},{4,0},{8,12},{12,8},{16,20},{20,16},{24,28},{28,24},{1,5},{5... | collective-permute-start | bytes 442376 | tf_op jit(solution)/shard_map/ppermute | solution.py:353
  22.8 8.8 %collective-permute-start.4 = (bf16[9,32,256]{2,1,0:T(8,128)(2,1)S(1)}, bf16[9,32,256]{2,1,0:T(8,128)(2,1)S(1)}, u32[]{:S(2)}, u32[]{:S(2)}) collective-permute-start(bf16[9,32,256]{2,1,0:T(8,128)(2,1)S(1)} %get-tuple-element.45), channel_id=1, source_target_pairs={{0,12},{4,8},{8,4},{12,0},{16,28},{20,24},{24,20},{28,16},{1,13},{... | collective-permute-start | bytes 442376 | tf_op jit(solution)/shard_map/ppermute | solution.py:353
  24.3 11.1 %collective-permute-start.6 = (bf16[9,32,256]{2,1,0:T(8,128)(2,1)S(1)}, bf16[9,32,256]{2,1,0:T(8,128)(2,1)S(1)}, u32[]{:S(2)}, u32[]{:S(2)}) collective-permute-start(bf16[9,32,256]{2,1,0:T(8,128)(2,1)S(1)} %get-tuple-element.50), channel_id=1, source_target_pairs={{0,8},{4,12},{8,0},{12,4},{16,24},{20,28},{24,16},{28,20},{1,9},{5... | collective-permute-start | bytes 442376 | tf_op jit(solution)/shard_map/ppermute | solution.py:353
  25.8 13.1 %collective-permute-start.7 = (bf16[9,32,256]{2,1,0:T(8,128)(2,1)S(1)}, bf16[9,32,256]{2,1,0:T(8,128)(2,1)S(1)}, u32[]{:S(2)}, u32[]{:S(2)}) collective-permute-start(bf16[9,32,256]{2,1,0:T(8,128)(2,1)S(1)} %get-tuple-element.51), channel_id=1, source_target_pairs={{0,16},{4,20},{8,24},{12,28},{16,0},{20,4},{24,8},{28,12},{1,17},{... | collective-permute-start | bytes 442376 | tf_op jit(solution)/shard_map/ppermute | solution.py:353
  26.3 5.7 %collective-permute-start.5 = (bf16[9,32,256]{2,1,0:T(8,128)(2,1)S(1)}, bf16[9,32,256]{2,1,0:T(8,128)(2,1)S(1)}, u32[]{:S(2)}, u32[]{:S(2)}) collective-permute-start(bf16[9,32,256]{2,1,0:T(8,128)(2,1)S(1)} %get-tuple-element.46), channel_id=1, source_target_pairs={{0,2},{1,3},{2,0},{3,1},{4,6},{5,7},{6,4},{7,5},{8,10},{9,11},{10,... | collective-permute-start | bytes 442376 | tf_op jit(solution)/shard_map/ppermute | solution.py:353
  28.5 10.3 %collective-permute-start.8 = (bf16[9,32,256]{2,1,0:T(8,128)(2,1)S(1)}, bf16[9,32,256]{2,1,0:T(8,128)(2,1)S(1)}, u32[]{:S(2)}, u32[]{:S(2)}) collective-permute-start(bf16[9,32,256]{2,1,0:T(8,128)(2,1)S(1)} %get-tuple-element.52), channel_id=1, source_target_pairs={{0,24},{4,28},{8,16},{12,20},{16,8},{20,12},{24,0},{28,4},{1,25},{... | collective-permute-start | bytes 442376 | tf_op jit(solution)/shard_map/ppermute | solution.py:353
  32.1 7.6 %collective-permute-start.9 = (bf16[18,32,256]{2,1,0:T(8,128)(2,1)S(1)}, bf16[18,32,256]{2,1,0:T(8,128)(2,1)S(1)}, u32[]{:S(2)}, u32[]{:S(2)}) collective-permute-start(bf16[18,32,256]{2,1,0:T(8,128)(2,1)S(1)} %join.3), channel_id=1, source_target_pairs={{0,2},{1,3},{2,0},{3,1},{4,6},{5,7},{6,4},{7,5},{8,10},{9,11},{10,... | collective-permute-start | bytes 884744 | tf_op jit(solution)/shard_map/ppermute | solution.py:353
  39.7 10.1 %collective-permute-start.11 = (bf16[31,32,256]{2,1,0:T(8,128)(2,1)S(1)}, bf16[31,32,256]{2,1,0:T(8,128)(2,1)S(1)}, u32[]{:S(2)}, u32[]{:S(2)}) collective-permute-start(bf16[31,32,256]{2,1,0:T(8,128)(2,1)S(1)} %join.4), channel_id=1, source_target_pairs={{0,2},{1,3},{2,0},{3,1},{4,6},{5,7},{6,4},{7,5},{8,10},{9,11},{10,... | collective-permute-start | bytes 1523720 | tf_op jit(solution)/shard_map/ppermute | solution.py:353
  41.2 12.5 %collective-permute-start.13 = (bf16[9,32,256]{2,1,0:T(8,128)(2,1)S(1)}, bf16[9,32,256]{2,1,0:T(8,128)(2,1)S(1)}, u32[]{:S(2)}, u32[]{:S(2)}) collective-permute-start(bf16[9,32,256]{2,1,0:T(8,128)(2,1)S(1)} %get-tuple-element.60), channel_id=1, source_target_pairs={{0,20},{4,16},{8,28},{12,24},{16,4},{20,0},{24,12},{28,8},{1,21},{... | collective-permute-start | bytes 442376 | tf_op jit(solution)/shard_map/ppermute | solution.py:353
  43.0 10.8 %collective-permute-start.14 = (bf16[9,32,256]{2,1,0:T(8,128)(2,1)S(1)}, bf16[9,32,256]{2,1,0:T(8,128)(2,1)S(1)}, u32[]{:S(2)}, u32[]{:S(2)}) collective-permute-start(bf16[9,32,256]{2,1,0:T(8,128)(2,1)S(1)} %get-tuple-element.62), channel_id=1, source_target_pairs={{0,28},{4,24},{8,20},{12,16},{16,12},{20,8},{24,4},{28,0},{1,29},{... | collective-permute-start | bytes 442376 | tf_op jit(solution)/shard_map/ppermute | solution.py:353
  49.9 4.9 %collective-permute-start.12 = (bf16[58,32,256]{2,1,0:T(8,128)(2,1)S(1)}, bf16[58,32,256]{2,1,0:T(8,128)(2,1)S(1)}, u32[]{:S(2)}, u32[]{:S(2)}) collective-permute-start(bf16[58,32,256]{2,1,0:T(8,128)(2,1)S(1)} %pad_maximum_fusion.refs_2_), channel_id=1, source_target_pairs={{0,1},{1,0},{2,3},{3,2},{4,5},{5,4},{6,7},{7,6},{8,9},{9,8},{10,11... | collective-permute-start | bytes 2850824 | tf_op jit(solution)/shard_map/ppermute | solution.py:353
  54.1 6.8 %collective-permute-start.15 = (bf16[18,32,256]{2,1,0:T(8,128)(2,1)S(1)}, bf16[18,32,256]{2,1,0:T(8,128)(2,1)S(1)}, u32[]{:S(2)}, u32[]{:S(2)}) collective-permute-start(bf16[18,32,256]{2,1,0:T(8,128)(2,1)S(1)} %join.5), channel_id=1, source_target_pairs={{0,2},{1,3},{2,0},{3,1},{4,6},{5,7},{6,4},{7,5},{8,10},{9,11},{10,... | collective-permute-start | bytes 884744 | tf_op jit(solution)/shard_map/ppermute | solution.py:353
  54.8 10.0 %collective-permute-start.10 = (bf16[54,32,256]{2,1,0:T(8,128)(2,1)S(1)}, bf16[54,32,256]{2,1,0:T(8,128)(2,1)S(1)}, u32[]{:S(2)}, u32[]{:S(2)}) collective-permute-start(bf16[54,32,256]{2,1,0:T(8,128)(2,1)S(1)} %constant_dynamic-update-slice_fusion.refs_0_), channel_id=1, source_target_pairs={{0,1},{1,0},{2,3},{3,2},{4,5},{5,4},{6,7},{7,6},{8,9},{9,8},{10,11... | collective-permute-start | bytes 2654216 | tf_op jit(solution)/shard_map/ppermute | solution.py:353
  54.9 6.1 %collective-permute-start.18 = (bf16[4,32,256]{2,1,0:T(8,128)(2,1)S(1)}, bf16[4,32,256]{2,1,0:T(8,128)(2,1)S(1)}, u32[]{:S(2)}, u32[]{:S(2)}) collective-permute-start(bf16[4,32,256]{2,1,0:T(8,128)(2,1)S(1)} %get-tuple-element.65), channel_id=1, source_target_pairs={{0,12},{4,8},{8,4},{12,0},{16,28},{20,24},{24,20},{28,16},{1,13},{... | collective-permute-start | bytes 196616 | tf_op jit(solution)/shard_map/ppermute | solution.py:353
  58.0 4.3 %collective-permute-start.17 = (bf16[4,32,256]{2,1,0:T(8,128)(2,1)S(1)}, bf16[4,32,256]{2,1,0:T(8,128)(2,1)S(1)}, u32[]{:S(2)}, u32[]{:S(2)}) collective-permute-start(bf16[4,32,256]{2,1,0:T(8,128)(2,1)S(1)} %get-tuple-element.65), channel_id=1, source_target_pairs={{0,8},{4,12},{8,0},{12,4},{16,24},{20,28},{24,16},{28,20},{1,9},{5... | collective-permute-start | bytes 196616 | tf_op jit(solution)/shard_map/ppermute | solution.py:353
  58.0 4.3 %collective-permute-start.16 = (bf16[4,32,256]{2,1,0:T(8,128)(2,1)S(1)}, bf16[4,32,256]{2,1,0:T(8,128)(2,1)S(1)}, u32[]{:S(2)}, u32[]{:S(2)}) collective-permute-start(bf16[4,32,256]{2,1,0:T(8,128)(2,1)S(1)} %get-tuple-element.65), channel_id=1, source_target_pairs={{0,4},{4,0},{8,12},{12,8},{16,20},{20,16},{24,28},{28,24},{1,5},{5... | collective-permute-start | bytes 196616 | tf_op jit(solution)/shard_map/ppermute | solution.py:353
  62.5 7.0 %collective-permute-start.20 = (bf16[4,32,256]{2,1,0:T(8,128)(2,1)S(1)}, bf16[4,32,256]{2,1,0:T(8,128)(2,1)S(1)}, u32[]{:S(2)}, u32[]{:S(2)}) collective-permute-start(bf16[4,32,256]{2,1,0:T(8,128)(2,1)S(1)} %get-tuple-element.66), channel_id=1, source_target_pairs={{0,16},{4,20},{8,24},{12,28},{16,0},{20,4},{24,8},{28,12},{1,17},{... | collective-permute-start | bytes 196616 | tf_op jit(solution)/shard_map/ppermute | solution.py:353
  76.7 12.6 %collective-permute-start.23 = (f32[96,512]{1,0:T(8,128)S(1)}, f32[96,512]{1,0:T(8,128)S(1)}, u32[]{:S(2)}, u32[]{:S(2)}) collective-permute-start(f32[96,512]{1,0:T(8,128)S(1)} %get-tuple-element.74), channel_id=1, source_target_pairs={{0,3},{1,2},{2,1},{3,0},{4,7},{5,6},{6,5},{7,4},{8,11},{9,10},{10,... | collective-permute-start | bytes 589832 | tf_op jit(solution)/shard_map/ppermute | solution.py:353
  78.1 11.3 %collective-permute-start.22 = (f32[96,512]{1,0:T(8,128)S(1)}, f32[96,512]{1,0:T(8,128)S(1)}, u32[]{:S(2)}, u32[]{:S(2)}) collective-permute-start(f32[96,512]{1,0:T(8,128)S(1)} %get-tuple-element.75), channel_id=1, source_target_pairs={{0,2},{1,3},{2,0},{3,1},{4,6},{5,7},{6,4},{7,5},{8,10},{9,11},{10,... | collective-permute-start | bytes 589832 | tf_op jit(solution)/shard_map/ppermute | solution.py:353
  78.6 10.8 %collective-permute-start.21 = (f32[96,512]{1,0:T(8,128)S(1)}, f32[96,512]{1,0:T(8,128)S(1)}, u32[]{:S(2)}, u32[]{:S(2)}) collective-permute-start(f32[96,512]{1,0:T(8,128)S(1)} %get-tuple-element.76), channel_id=1, source_target_pairs={{0,1},{1,0},{2,3},{3,2},{4,5},{5,4},{6,7},{7,6},{8,9},{9,8},{10,11... | collective-permute-start | bytes 589832 | tf_op jit(solution)/shard_map/ppermute | solution.py:353
  (3 other events, 34.9 us)
